TPU v7x, 32 devices: a whole 2x2x4 slice. The times are simulated.
32 devices in a mesh: ens: 2 (over x), lon: 16 (over z, y, core).
Axes of the slice: x: 2, y: 2, z: 4, core: 2. Of those that a mesh axis runs over, the one named last changes fastest.
Arguments:
- state: bfloat16 [256, 4, 64, 256], P(('ens', 'lon')), parts along dimension 0, may hold values from -24 to 24
- obs_index: int32 [8192], P(('ens', 'lon')), parts along dimension 0, may hold values from 0 to 511
- obs_value: float32 [8192], P(('ens', 'lon')), parts along dimension 0, may hold values from -20 to 20
- obs_var: float32 [8192], P(('ens', 'lon')), parts along dimension 0, may hold values from 0.5 to 2
Outputs:
- analysis: bfloat16 [256, 4, 64, 256], P(('ens', 'lon')), parts along dimension 0
There are 2 independent parts, one for each index of `ens`. A program takes and returns all parts, laid end to end along the dimension named above; each array names one. Nothing has to cross between parts.
Inputs may be any that keep to these rules, and one draw needn't show every extreme that they name: `obs_index`: a column of the device's own strip.
All inputs are finite; a program needn't handle non-finite values.
Results may differ from a plain program's by a relative error of at most 0.0029.
Values may be sent and summed in bfloat16 or wider, within the bound.
No kernel may reach another device: no remote copies, remote signals or barrier semaphores. Data moves between devices by JAX's collectives and lax.ppermute only.
A program may use at most 128 MiB of HBM per device.

v0:
```python
import jax
import jax.numpy as jnp
from jax import lax
from jax.sharding import PartitionSpec as P

REGION = 8
HALO = 4
SWEEPS = 4


EPS = 0.05


def with_halo(cells, sides, width):
    for axis, dim in sides:
        count = lax.axis_size(axis)
        head = lax.slice_in_dim(cells, 0, width, axis=dim)
        tail = lax.slice_in_dim(cells, cells.shape[dim] - width, cells.shape[dim], axis=dim)
        cells = jnp.concatenate(
            [
                lax.ppermute(tail, axis, [(i, (i + 1) % count) for i in range(count)]),
                cells,
                lax.ppermute(head, axis, [((i + 1) % count, i) for i in range(count)]),
            ],
            axis=dim,
        )
    return cells


def taper():
    place = jnp.arange(REGION + 2 * HALO)
    dist = jnp.maximum(0, jnp.maximum(HALO - place, place - (HALO + REGION - 1)))
    line = 1.0 - dist.astype(jnp.float32) / (HALO + 1)
    return line[:, None] * line[None, :]


def windows(block):
    lon_len, nvar, lat_len, members = block.shape
    lon_blocks = lon_len // REGION
    lat_blocks = lat_len // REGION
    split = block.reshape(lon_blocks, REGION, nvar, lat_blocks, REGION, members)
    split = jnp.concatenate([split[:-1], split[1:]], axis=1)
    return jnp.concatenate([split[:, :, :, :-1], split[:, :, :, 1:]], axis=4)


def gram_part(win, lower, upper):
    rho = taper()
    weighted = (win.astype(jnp.float32) * rho[None, lower:upper, None, None, :, None]).astype(
        jnp.bfloat16
    )
    return jnp.einsum("apvbqm,apvbqn->abmn", weighted, win, preferred_element_type=jnp.float32)


def analyse(win, mis_win, scale, gram):
    rho = taper()
    members = win.shape[-1]
    diag = jnp.diagonal(gram, axis1=2, axis2=3)
    cost = (diag[..., :, None] + diag[..., None, :] - 2.0 * gram) / (win.shape[2] * jnp.sum(rho))
    like = scale * jnp.einsum("apxbqm,pq->abm", mis_win, rho, precision=lax.Precision.HIGHEST)
    logw = like - jax.nn.logsumexp(like, axis=-1, keepdims=True)
    pot_g = jnp.zeros(like.shape, jnp.float32)
    pot_f = pot_g
    for sweep in range(SWEEPS):
        pot_f = EPS * logw - EPS * jax.nn.logsumexp((pot_g[..., None, :] - cost) / EPS, axis=-1)
        pot_g = -EPS * jnp.log(1.0 * members) - EPS * jax.nn.logsumexp(
            (pot_f[..., :, None] - cost) / EPS, axis=-2
        )
    transport = (
        members * jnp.exp((pot_f[..., :, None] + pot_g[..., None, :] - cost) / EPS)
    ).astype(jnp.bfloat16)
    own = win[:, HALO : HALO + REGION, :, :, HALO : HALO + REGION, :]
    result = jnp.einsum("apvbqi,abij->apvbqj", own, transport, preferred_element_type=jnp.float32)
    return result.astype(jnp.bfloat16)


def tempering(partial_value, count):
    return count / lax.psum(partial_value, "lon")


def on_device(state, obs_index, obs_value, obs_var):
    lon_dev, nvar, lat, members = state.shape
    nobs_dev = obs_index.shape[0]
    count = nobs_dev * lax.axis_size("lon")
    span = REGION + 2 * HALO
    rows = state[:, 0].reshape(lon_dev * lat, members)
    seen = jnp.take(rows, obs_index, axis=0).astype(jnp.float32)
    centre = jnp.mean(seen, axis=1)
    spread = jnp.sum((seen - centre[:, None]) ** 2, axis=1) / (members - 1)
    partial_value = jnp.sum((obs_value - centre) ** 2 / (obs_var + spread))
    factor = -0.5 * tempering(partial_value, count)
    padded = with_halo(state, (("lon", 0),), HALO)
    terms = factor * (obs_value[:, None] - seen) ** 2 / obs_var[:, None]
    local = jax.ops.segment_sum(terms, obs_index, num_segments=lon_dev * lat)
    misfit = with_halo(local.reshape(lon_dev, lat, members), (("lon", 0),), HALO)
    scale = 1.0
    state_pad = jnp.pad(padded, ((0, 0), (0, 0), (HALO, HALO), (0, 0)))
    mis_pad = jnp.pad(misfit, ((0, 0), (HALO, HALO), (0, 0)))[:, None]
    win = windows(state_pad)
    gram = gram_part(win, 0, span)
    result = analyse(win, windows(mis_pad), scale, gram)
    return result.reshape(lon_dev, nvar, lat, members)


def solution(mesh):
    return jax.shard_map(
        on_device,
        mesh=mesh,
        in_specs=(
            P(("ens", "lon"), None, None, None),
            P(("ens", "lon")),
            P(("ens", "lon")),
            P(("ens", "lon")),
        ),
        out_specs=P(("ens", "lon"), None, None, None),
        check_vma=False,
    )
```

profile of v0, /device:TPU:0, one launch (start us, length us, event | category | flops | bytes accessed | tf_op | source)
XLA Modules:
  0.0 95.9 jit_solution(521357441232246632)
XLA Ops:
  0.0 1.3 %fusion.64 = (bf16[4,4,64,256]{3,2,1,0:T(8,128)(2,1)S(1)}, bf16[4,4,64,256]{3,2,1,0:T(8,128)(2,1)S(1)}) fusion(bf16[8,4,64,256]{3,2,1,0:T(8,128)(2,1)} %param.4), kind=kLoop, calls=%fused_computation.137 | loop fusion | bytes 2097152 | tf_op jit(solution)/shard_map/slice | solution.py:18
  1.3 5.5 %collective-permute-start.3 = (bf16[4,4,64,256]{3,2,1,0:T(8,128)(2,1)S(1)}, bf16[4,4,64,256]{3,2,1,0:T(8,128)(2,1)S(1)}, u32[]{:S(2)}, u32[]{:S(2)}) collective-permute-start(bf16[4,4,64,256]{3,2,1,0:T(8,128)(2,1)S(1)} %get-tuple-element.14), channel_id=1, source_target_pairs={{1,0},{2,1},{3,2},{4,3},{5,4},{6,5},{7,6},{8,7},{9,8},{10,9},{11,1... | collective-permute-start | bytes 1572872 | tf_op jit(solution)/shard_map/ppermute | solution.py:23
  6.9 1.2 %gather_fusion = bf16[256,256]{1,0:T(8,128)(2,1)S(1)} fusion(bf16[512,256]{1,0:T(8,128)(2,1)S(1)} %bitcast.68, s32[1024]{0:T(1024)S(1)} %pad_clamp_fusion), kind=kCustom, calls=%fused_computation | custom fusion | bytes 263168 | tf_op jit(solution)/shard_map/jit(_take)/gather | solution.py:86
  8.0 0.2 convert_reduce_fusion
  8.2 0.2 fusion.41
  8.5 0.6 fusion.55
  9.1 34.6 %psum.7 = f32[]{:T(128)} all-reduce(f32[]{:T(128)} %fusion.55), channel_id=1, replica_groups=mesh['ens'=2,'lon'=16] {'lon'}, use_global_device_ids=true, to_apply=%region_3.4 | all-reduce | flops 1 | bytes 8 | tf_op jit(solution)/shard_map/psum | solution.py:77
  44.4 2.2 %scatter_custom_fusion = f32[512,256]{1,0:T(8,128)S(1)} fusion(s32[256]{0:T(256)S(1)} %copy-done.7, f32[]{:T(128)} %constant.24.clone.1, f32[256]{0:T(256)S(1)} %copy-done.5, f32[256]{0:T(256)S(1)} %copy-done.6, f32[]{:T(128)S(6)} %mul_shard_map.6, bf16[256,256]{1,0:T(8,128)(2,1)S(1)} %gather_fusion, pred[256]{0:T(512)(128)(4,1)S(1)} %compare_and_fusion), kind=kCustom, calls=%fused_computation.88 | custom fusion | flops 458752 | bytes 657928 | tf_op jit(solution)/shard_map/scatter-add | solution.py:93
  46.6 0.7 fusion.65
  47.4 0.5 collective-permute-start
  47.9 0.8 broadcast_multiply_fusion
  49.4 2.2 %collective-permute-done.1 = f32[4,64,256]{2,1,0:T(8,128)S(1)} collective-permute-done((f32[4,64,256]{2,1,0:T(8,128)}, f32[4,64,256]{2,1,0:T(8,128)S(1)}, u32[]{:S(2)}, u32[]{:S(2)}) %collective-permute-start.1) | collective-permute-done | bytes 262176 | tf_op jit(solution)/shard_map/ppermute | solution.py:23
  51.6 4.3 %collective-permute-done = f32[4,64,256]{2,1,0:T(8,128)S(1)} collective-permute-done((f32[4,64,256]{2,1,0:T(8,128)S(1)}, f32[4,64,256]{2,1,0:T(8,128)S(1)}, u32[]{:S(2)}, u32[]{:S(2)}) %collective-permute-start) | collective-permute-done | bytes 262176 | tf_op jit(solution)/shard_map/ppermute | solution.py:21
  55.9 0.1 select_maximum_fusion
  56.1 0.1 slice_bitcast_fusion.3
  56.2 0.1 fusion.32
  56.3 1.2 %fusion.13 = f32[1,8,256,1]{2,0,1,3:T(1,128)S(1)} fusion(f32[16,16,1,1]{1,2,3,0:T(1,128)S(1)} %bitcast.72, f32[1,8,1,9,8,256]{5,4,3,1,2,0:T(8,128)S(1)} %get-tuple-element.12, f32[1,8,1,9,8,256]{5,4,3,1,2,0:T(8,128)S(1)} %get-tuple-element.11, f32[1,16,1,8,8,256]{5,4,3,1,2,0:T(8,128)S(1)} %fusion.32), kind=kOutput, calls=%fused_computation.26 | convolution fusion | flops 7340032 | bytes 2237440 | tf_op jit(solution)/shard_map/apxbqm,pq->abm/dot_general | solution.py:59
  57.5 0.1 bitcast_reduce_fusion
  57.6 0.2 fusion.52
  57.8 1.4 %fusion.9 = bf16[16,4,72,256]{3,2,1,0:T(8,128)(2,1)S(1)} fusion(bf16[4,4,64,256]{3,2,1,0:T(8,128)(2,1)S(1)} %collective-permute-done.3, bf16[8,4,64,256]{3,2,1,0:T(8,128)(2,1)S(1)} %copy-done.4, bf16[4,4,64,256]{3,2,1,0:T(8,128)(2,1)S(1)} %collective-permute-done.2), kind=kLoop, calls=%fused_computation.18 | loop fusion | flops 14155776 | bytes 4456448 | tf_op jit(solution)/shard_map/concatenate | solution.py:19
  59.2 0.2 slice_bitcast_fusion.1
  59.4 0.5 fusion.10
  59.9 0.6 copy_bitcast_fusion
  60.5 0.9 copy-done
  61.4 0.5 copy-done.2
  61.9 2.0 %fusion.25 = f32[8,256,256]{2,1,0:T(8,128)S(1)} fusion(bf16[1,16,4,8,8,256]{5,4,3,2,1,0:T(8,128)(2,1)S(1)} %get-tuple-element.8, bf16[1,16,4,8,8,256]{5,4,3,2,1,0:T(8,128)(2,1)S(1)} %get-tuple-element.7, bf16[16,4,8,8,256]{4,3,1,0,2:T(8,128)(2,1)S(1)} %get-tuple-element.19, bf16[16,4,8,8,256]{4,3,1,0,2:T(8,128)(2,1)S(1)} %get-tuple-element.20, ...), kind=kOutput, calls=%fused_computation.59 | convolution fusion | flops 1094713344 | bytes 10486784 | tf_op jit(solution)/shard_map/apvbqm,apvbqn->abmn/dot_general | solution.py:51
  63.9 16.4 %copy.10 = f32[8,256,256]{0,2,1:T(8,128)} copy(f32[8,256,256]{2,1,0:T(8,128)S(1)} %fusion.25) | data formatting | bytes 4194304 | tf_op jit(solution)/shard_map/apvbqm,apvbqn->abmn/dot_general | solution.py:51
  80.3 2.3 %gather_fusion.1 = f32[256,8]{1,0:T(8,128)S(1)} fusion(f32[8,256,256]{0,2,1:T(8,128)} %copy.10, s32[256]{0:T(256)S(1)} %bitcast.67), kind=kCustom, calls=%fused_computation.1 | custom fusion | bytes 18432 | tf_op jit(solution)/shard_map/jit(diagonal)/gather | solution.py:57
  82.6 0.9 fusion.17
  83.5 0.8 exponential_reduce_fusion.7
  84.4 0.4 fusion.18
  84.8 0.5 exponential_reduce_fusion.6
  85.3 0.4 fusion.19
  85.8 0.9 exponential_reduce_fusion.5
  86.7 0.4 fusion.20
  87.1 0.5 exponential_reduce_fusion.4
  87.6 0.4 fusion.21
  88.1 0.9 exponential_reduce_fusion.3
  89.0 0.4 fusion.22
  89.4 0.5 exponential_reduce_fusion.2
  89.9 0.4 fusion.23
  90.3 0.9 exponential_reduce_fusion.1
  91.3 0.4 fusion.24
  91.7 0.5 exponential_reduce_fusion
  92.2 0.7 copy-done.1
  92.9 0.6 copy-done.3
  93.5 1.3 %fusion.30 = bf16[1,8,4,8,8,256]{5,4,2,1,3,0:T(8,128)(2,1)S(1)} fusion(f32[8,256,256]{2,1,0:T(8,128)S(1)} %get-tuple-element.6, f32[8,256]{1,0:T(8,128)S(1)} %multiply_subtract_fusion, f32[8,256]{1,0:T(8,128)S(1)} %multiply_subtract_fusion.1, bf16[1,16,4,8,8,256]{5,4,3,2,1,0:T(8,128)(2,1)S(1)} %copy-done.1, bf16[1,16,4,8,8,256]{5,4,3,2,1,0:T(8,128)(2,1)S(1)} %copy-done.3), kind=kOutput, calls=%fused_computation.61 | convolution fusion | flops 273678336 | bytes 7356416 | tf_op jit(solution)/shard_map/apvbqi,abij->apvbqj/dot_general | solution.py:72
  94.8 1.1 %copy.50 = bf16[1,8,4,8,8,256]{5,4,3,2,1,0:T(8,128)(2,1)} copy(bf16[1,8,4,8,8,256]{5,4,2,1,3,0:T(8,128)(2,1)S(1)} %fusion.30) | data formatting | bytes 2097152 | tf_op jit(solution)/shard_map/convert_element_type | solution.py:73
  (43 shorter events, 0.5 us)
Async XLA Ops:
  0.0 6.9 %slice-start = ((bf16[8,4,64,256]{3,2,1,0:T(8,128)(2,1)}), bf16[8,1,64,256]{3,2,1,0:T(8,128)(2,1)S(1)}, s32[]{:S(2)}) async-start(bf16[8,4,64,256]{3,2,1,0:T(8,128)(2,1)} %param.4), calls=%async_computation | async-start | bytes 524288 | tf_op jit(solution)/shard_map/slice | solution.py:85
  0.0 6.8 %copy-start.7 = (s32[256]{0:T(256)S(1)}, s32[256]{0:T(256)}, u32[]{:S(2)}) copy-start(s32[256]{0:T(256)} %param.5) | copy-start | bytes 3076
  0.0 8.4 %copy-start.5 = (f32[256]{0:T(256)S(1)}, f32[256]{0:T(256)}, u32[]{:S(2)}) copy-start(f32[256]{0:T(256)} %param.7) | copy-start | bytes 3076
  0.0 8.4 %copy-start.6 = (f32[256]{0:T(256)S(1)}, f32[256]{0:T(256)}, u32[]{:S(2)}) copy-start(f32[256]{0:T(256)} %param.6) | copy-start | bytes 3076
  1.3 56.5 %collective-permute-start.3 = (bf16[4,4,64,256]{3,2,1,0:T(8,128)(2,1)S(1)}, bf16[4,4,64,256]{3,2,1,0:T(8,128)(2,1)S(1)}, u32[]{:S(2)}, u32[]{:S(2)}) collective-permute-start(bf16[4,4,64,256]{3,2,1,0:T(8,128)(2,1)S(1)} %get-tuple-element.14), channel_id=1, source_target_pairs={{1,0},{2,1},{3,2},{4,3},{5,4},{6,5},{7,6},{8,7},{9,8},{10,9},{11,1... | collective-permute-start | bytes 1572872 | tf_op jit(solution)/shard_map/ppermute | solution.py:23
  9.1 48.7 %collective-permute-start.2 = (bf16[4,4,64,256]{3,2,1,0:T(8,128)(2,1)S(1)}, bf16[4,4,64,256]{3,2,1,0:T(8,128)(2,1)S(1)}, u32[]{:S(2)}, u32[]{:S(2)}) collective-permute-start(bf16[4,4,64,256]{3,2,1,0:T(8,128)(2,1)S(1)} %get-tuple-element.13), channel_id=1, source_target_pairs={{0,1},{1,2},{2,3},{3,4},{4,5},{5,6},{6,7},{7,8},{8,9},{9,10},{10,1... | collective-permute-start | bytes 1572872 | tf_op jit(solution)/shard_map/ppermute | solution.py:21
  47.4 4.2 %collective-permute-start.1 = (f32[4,64,256]{2,1,0:T(8,128)}, f32[4,64,256]{2,1,0:T(8,128)S(1)}, u32[]{:S(2)}, u32[]{:S(2)}) collective-permute-start(f32[4,64,256]{2,1,0:T(8,128)} %bitcast.3), channel_id=1, source_target_pairs={{1,0},{2,1},{3,2},{4,3},{5,4},{6,5},{7,6},{8,7},{9,8},{10,9},{11,1... | collective-permute-start | bytes 786440 | tf_op jit(solution)/shard_map/ppermute | solution.py:23
  47.4 8.5 %collective-permute-start = (f32[4,64,256]{2,1,0:T(8,128)S(1)}, f32[4,64,256]{2,1,0:T(8,128)S(1)}, u32[]{:S(2)}, u32[]{:S(2)}) collective-permute-start(f32[4,64,256]{2,1,0:T(8,128)S(1)} %bitcast.70), channel_id=1, source_target_pairs={{0,1},{1,2},{2,3},{3,4},{4,5},{5,6},{6,7},{7,8},{8,9},{9,10},{10,1... | collective-permute-start | bytes 786440 | tf_op jit(solution)/shard_map/ppermute | solution.py:21
  56.1 1.7 %copy-start.4 = (bf16[8,4,64,256]{3,2,1,0:T(8,128)(2,1)S(1)}, bf16[8,4,64,256]{3,2,1,0:T(8,128)(2,1)}, u32[]{:S(2)}) copy-start(bf16[8,4,64,256]{3,2,1,0:T(8,128)(2,1)} %param.4) | copy-start | bytes 3145732
  59.9 1.5 %copy-start = (bf16[1,16,4,8,8,256]{5,4,3,2,1,0:T(8,128)(2,1)}, bf16[1,16,4,8,8,256]{5,4,3,2,1,0:T(8,128)(2,1)S(1)}, u32[]{:S(2)}) copy-start(bf16[1,16,4,8,8,256]{5,4,3,2,1,0:T(8,128)(2,1)S(1)} %get-tuple-element.7) | copy-start | bytes 6291460
  59.9 2.0 %copy-start.2 = (bf16[1,16,4,8,8,256]{5,4,3,2,1,0:T(8,128)(2,1)}, bf16[1,16,4,8,8,256]{5,4,3,2,1,0:T(8,128)(2,1)S(1)}, u32[]{:S(2)}) copy-start(bf16[1,16,4,8,8,256]{5,4,3,2,1,0:T(8,128)(2,1)S(1)} %get-tuple-element.8) | copy-start | bytes 6291460
  91.3 1.6 %copy-start.1 = (bf16[1,16,4,8,8,256]{5,4,3,2,1,0:T(8,128)(2,1)S(1)}, bf16[1,16,4,8,8,256]{5,4,3,2,1,0:T(8,128)(2,1)}, u32[]{:S(2)}) copy-start(bf16[1,16,4,8,8,256]{5,4,3,2,1,0:T(8,128)(2,1)} %copy-done) | copy-start | bytes 6291460
  91.3 2.2 %copy-start.3 = (bf16[1,16,4,8,8,256]{5,4,3,2,1,0:T(8,128)(2,1)S(1)}, bf16[1,16,4,8,8,256]{5,4,3,2,1,0:T(8,128)(2,1)}, u32[]{:S(2)}) copy-start(bf16[1,16,4,8,8,256]{5,4,3,2,1,0:T(8,128)(2,1)} %copy-done.2) | copy-start | bytes 6291460
where the time goes:
time: 96.1 us; the launch traced here: 95.9 us
  blocking collectives  34.6 us (36%)
  local copies, waits for them, and re-layouts  26.6 us (28%)
  other arithmetic  15.9 us (17%)
  waiting for transfers between devices  6.56 us (7%)
  starting transfers between devices  6.01 us (6%)
  matrix products  4.46 us (5%)
  between operations  1.75 us (2%)
    psum x1, blocking collectives, tempering(): return count / lax.psum(partial_value, 'lon')  34.6 us
    dot_general x1, local copies, waits for them, and re-layouts, gram_part(): jnp.einsum('apvbqm,apvbqn->abmn', weighted, win, preferred_element_type=j...  16.4 us
    ppermute x2, starting transfers between devices, with_halo(): lax.ppermute(head, axis, [((i + 1) % count, i) for i in range(count)])  5.5 us
    ppermute x2, waiting for transfers between devices, with_halo(): lax.ppermute(tail, axis, [(i, (i + 1) % count) for i in range(count)])  4.33 us
    reduce_sum x4, other arithmetic, analyse(): jax.nn.logsumexp((pot_g[..., None, :] - cost) / EPS, axis=-1)  3.45 us
    unnamed x16, local copies, waits for them, and re-layouts  2.76 us
    gather x2, local copies, waits for them, and re-layouts, analyse(): diag = jnp.diagonal(gram, axis1=2, axis2=3)  2.38 us
    scatter-add x1, other arithmetic, on_device(): local = jax.ops.segment_sum(terms, obs_index, num_segments=lon_dev * lat)  2.24 us
  transfers between devices with their start and end apart: 4, of which 2 were waited for; matrix products, arithmetic and copies ran while one was open for 8% of the time, Pallas kernels for 0%

commit v1 on v0

v1 whole, which is shorter than its diff:
```python
import functools

import jax
import jax.numpy as jnp
from jax import lax
from jax.experimental import pallas as pl
from jax.experimental.pallas import tpu as pltpu
from jax.sharding import PartitionSpec as P

REGION = 8
HALO = 4
SWEEPS = 4
EPS = 0.05
TILE = 8
PAIR = 2
LOG2E = 1.4426950408889634
LIFT = 100.0
ROWS = 32

HIGH = lax.Precision.HIGHEST


def line_weight(place):
    dist = jnp.maximum(0.0, jnp.maximum(HALO - place, place - (HALO + REGION - 1)))
    inside = (place >= 0) & (place < REGION + 2 * HALO)
    return jnp.where(inside, 1.0 - dist / (HALO + 1), 0.0)


def obs_kernel(cells_ref, index_ref, value_ref, var_ref, own_ref, left_ref, right_ref, part_ref):
    lon_dev, _, lat, members = cells_ref.shape
    nobs = index_ref.shape[1]
    rows = cells_ref[:, 0].reshape(lon_dev * lat, members)
    index = index_ref[...]
    sub = lax.broadcasted_iota(jnp.int32, (TILE, nobs), 0)
    table = jnp.where(
        sub == 0,
        index.astype(jnp.float32),
        jnp.where(sub == 1, value_ref[...], var_ref[...]),
    ).T
    index_col = table[:, 0:1].astype(jnp.int32)
    value = table[:, 1:2]
    var = table[:, 2:3]
    pick = index_col == lax.broadcasted_iota(jnp.int32, (nobs, lon_dev * lat), 1)
    pick = jnp.where(pick, 1.0, 0.0).astype(jnp.bfloat16)
    seen = jnp.dot(pick, rows, preferred_element_type=jnp.float32)
    centre = jnp.sum(seen, axis=1, keepdims=True) * (1.0 / members)
    spread = jnp.sum((seen - centre) ** 2, axis=1, keepdims=True) * (1.0 / (members - 1))
    innovation = (value - centre) ** 2 / (var + spread)
    part_ref[...] = jnp.broadcast_to(jnp.sum(innovation, axis=0, keepdims=True), part_ref.shape)
    terms = (value - seen) ** 2 * (1.0 / var)
    lon = (index // lat).astype(jnp.float32)
    along = index.astype(jnp.float32) - lon * lat
    for ref, shift in ((own_ref, HALO), (left_ref, HALO + REGION), (right_ref, HALO - REGION)):
        blocks = ref.shape[0]
        block = lax.broadcasted_iota(jnp.int32, (blocks, nobs), 0).astype(jnp.float32)
        weight = line_weight(lon + shift) * line_weight(along - REGION * block + HALO)
        ref[...] = jnp.dot(weight, terms, precision=HIGH, preferred_element_type=jnp.float32)


def observe(state, obs_index, obs_value, obs_var):
    lon_dev, _, lat, members = state.shape
    nobs = obs_index.shape[0]
    blocks = lat // REGION
    row = pl.BlockSpec((1, nobs), lambda i: (0, 0))
    like = jax.ShapeDtypeStruct((blocks, members), jnp.float32)
    like_spec = pl.BlockSpec((blocks, members), lambda i: (0, 0))
    return pl.pallas_call(
        obs_kernel,
        grid=(1,),
        in_specs=[pl.BlockSpec((lon_dev, 1, lat, members), lambda i: (0, 0, 0, 0)), row, row, row],
        out_specs=[like_spec] * 3 + [pl.BlockSpec((8, 128), lambda i: (0, 0))],
        out_shape=[like] * 3 + [jax.ShapeDtypeStruct((8, 128), jnp.float32)],
        compiler_params=pltpu.CompilerParams(vmem_limit_bytes=32 * 2**20),
        name="observe",
    )(state, obs_index[None], obs_value[None], obs_var[None])


def gram_of(before, here, after, places, step, steps):
    columns, nvar, _, members = here.shape
    wide = here.astype(jnp.float32)
    low, high = wide[:, :, :TILE], wide[:, :, TILE:]
    prev = before[:, :, TILE:].astype(jnp.float32)
    nxt = after[:, :, :TILE].astype(jnp.float32)
    prev = jnp.where(step == 0, 0.0, prev)
    nxt = jnp.where(step == steps - 1, 0.0, nxt)
    row = lax.broadcasted_iota(jnp.int32, (1, 1, TILE, members), 2)
    upper = row < HALO
    rowf = row.astype(jnp.float32)
    edge = line_weight(jnp.where(upper, rowf + (HALO + REGION), rowf - HALO))
    grams = []
    for own, following, preceding in ((low, high, prev), (high, nxt, low)):
        margin = jnp.where(upper, following, preceding)
        win = jnp.concatenate([own, margin], axis=2)
        weighted = []
        for column, place in enumerate(places):
            dist = max(0, HALO - place, place - (HALO + REGION - 1))
            weight = jnp.float32(1.0) - jnp.float32(dist) / jnp.float32(HALO + 1)
            weighted.append(
                jnp.concatenate([own[column] * weight, margin[column] * (edge[0] * weight)], axis=1)
            )
        weighted = jnp.stack(weighted)
        shape = (columns * nvar * 2 * TILE, members)
        grams.append(
            lax.dot_general(
                weighted.astype(jnp.bfloat16).reshape(shape),
                win.astype(jnp.bfloat16).reshape(shape),
                (((0,), (0,)), ((), ())),
                preferred_element_type=jnp.float32,
            )
        )
    return grams


def own_gram_kernel(before_ref, here_ref, after_ref, gram_ref):
    step, steps = pl.program_id(0), pl.num_programs(0)
    places = range(HALO, HALO + here_ref.shape[0])
    grams = gram_of(before_ref[...], here_ref[...], after_ref[...], places, step, steps)
    for region in range(PAIR):
        gram_ref[region] = grams[region]


def lat_specs(columns, nvar, members, steps):
    shape = (columns, nvar, PAIR * TILE, members)
    return [
        pl.BlockSpec(shape, lambda i: (0, 0, jnp.maximum(i - 1, 0), 0)),
        pl.BlockSpec(shape, lambda i: (0, 0, i, 0)),
        pl.BlockSpec(shape, lambda i: (0, 0, jnp.minimum(i + 1, steps - 1), 0)),
    ]


def own_gram(state):
    lon_dev, nvar, lat, members = state.shape
    steps = lat // (PAIR * TILE)
    return pl.pallas_call(
        own_gram_kernel,
        grid=(steps,),
        in_specs=lat_specs(lon_dev, nvar, members, steps),
        out_specs=pl.BlockSpec((PAIR, members, members), lambda i: (i, 0, 0)),
        out_shape=jax.ShapeDtypeStruct((steps * PAIR, members, members), jnp.float32),
        compiler_params=pltpu.CompilerParams(vmem_limit_bytes=48 * 2**20),
        name="own_gram",
    )(state, state, state)


def diagonal(gram_ref, region):
    members = gram_ref.shape[-1]
    across, down = None, []
    for start in range(0, members, ROWS):
        gram = gram_ref[region, start : start + ROWS, :]
        i = lax.broadcasted_iota(jnp.int32, gram.shape, 0) + start
        j = lax.broadcasted_iota(jnp.int32, gram.shape, 1)
        kept = jnp.where(i == j, gram, 0.0)
        down.append(jnp.sum(kept, axis=1, keepdims=True))
        part = jnp.sum(kept.reshape(ROWS // TILE, TILE, members), axis=0)
        across = part if across is None else across + part
    return jnp.sum(across, axis=0, keepdims=True), down


def transport_scaled(gram_ref, plan_ref, out_ref, region, weight, scale):
    members = gram_ref.shape[-1]
    across, down = diagonal(gram_ref, region)
    across = 0.5 * LIFT - across * scale
    starts = range(0, members, ROWS)
    lift = 2.0**LIFT
    factor = None
    least_row = least_col = grown_row = grown_col = None
    grown_rows = [None] * len(starts)
    for sweep in range(SWEEPS):
        total = None
        for at, start in enumerate(starts):
            rows = slice(start, start + ROWS)
            if sweep == 0:
                plan = jnp.exp2(
                    gram_ref[region, rows, :] * (2.0 * scale)
                    + (0.5 * LIFT - down[at] * scale)
                    + across
                )
            else:
                plan = plan_ref[region, rows, :] * factor
            mass = jnp.sum(plan, axis=1, keepdims=True)
            ratio = weight[rows] * (lift / mass)
            plan = plan * ratio
            plan_ref[region, rows, :] = plan
            part = jnp.sum(plan.reshape(ROWS // TILE, TILE, members), axis=0)
            total = part if total is None else total + part
            grow = jnp.maximum(ratio, 1.0)
            grown_rows[at] = grow if sweep == 0 else grown_rows[at] * grow
            least_row = mass if least_row is None else jnp.minimum(least_row, mass)
        total = jnp.sum(total, axis=0, keepdims=True)
        factor = (lift / members) / total
        grow = jnp.maximum(factor, 1.0)
        grown_col = grow if sweep == 0 else grown_col * grow
        least_col = total if sweep == 0 else jnp.minimum(least_col, total)
    final = 1.0 / total
    for start in starts:
        rows = slice(start, start + ROWS)
        out_ref[region, rows, :] = (plan_ref[region, rows, :] * final).astype(jnp.bfloat16)
    for grow in grown_rows:
        grown_row = grow if grown_row is None else jnp.maximum(grown_row, grow)
    least = jnp.minimum(jnp.min(least_row), jnp.min(least_col))
    most = jnp.max(grown_row) * jnp.max(grown_col)
    return least, most * 2.0**-94


def transport_logs(gram_ref, cost_ref, out_ref, region, logw, scale):
    members = gram_ref.shape[-1]
    across, down = diagonal(gram_ref, region)
    starts = range(0, members, ROWS)
    for at, start in enumerate(starts):
        rows = slice(start, start + ROWS)
        cost_ref[region, rows, :] = (
            down[at] * scale + across * scale - gram_ref[region, rows, :] * (2.0 * scale)
        )
    pot_g = jnp.zeros((1, members), jnp.float32)
    cost = cost_ref[region]
    for sweep in range(SWEEPS):
        term = pot_g - cost
        top = jnp.max(term, axis=1, keepdims=True)
        pot_f = logw - top - jnp.log(jnp.sum(jnp.exp2(term - top), axis=1, keepdims=True)) * LOG2E
        term = pot_f - cost
        top = jnp.max(term, axis=0, keepdims=True)
        pot_g = -jnp.log(1.0 * members) * LOG2E - top
        pot_g = pot_g - jnp.log(jnp.sum(jnp.exp2(term - top), axis=0, keepdims=True)) * LOG2E
    plan = members * jnp.exp2(pot_f + pot_g - cost)
    out_ref[region] = plan.astype(jnp.bfloat16)


def analysis_kernel(count, scale, *refs):
    lefts, rights = refs[0:3], refs[3:6]
    own_ref, gram_in_ref, like_refs, total_ref = refs[6], refs[7], refs[8:11], refs[11]
    out_ref, gram_ref, plan_ref, move_ref = refs[12:16]
    step, steps = pl.program_id(0), pl.num_programs(0)
    columns = lefts[0].shape[0]
    left = gram_of(*[r[...] for r in lefts], range(columns), step, steps)
    right = gram_of(
        *[r[...] for r in rights], range(HALO + REGION, HALO + REGION + columns), step, steps
    )
    for region in range(PAIR):
        gram_ref[region] = gram_in_ref[region] + left[region] + right[region]
    beta = count / total_ref[0:1, 0:1]
    like = -0.5 * beta * (like_refs[0][0] + like_refs[1][0] + like_refs[2][0])
    like = like - jnp.max(like, axis=1, keepdims=True)
    weight = jnp.exp(like)
    norm = jnp.sum(weight, axis=1, keepdims=True)
    weight = weight / norm
    logw = (like - jnp.log(norm)) * LOG2E
    pad = jnp.zeros((TILE - 2 * PAIR,) + like.shape[1:], jnp.float32)
    table = jnp.concatenate([weight, logw, pad], axis=0).T
    checks = [
        transport_scaled(gram_ref, plan_ref, move_ref, r, table[:, r : r + 1], scale)
        for r in range(PAIR)
    ]
    for region, (least, most) in enumerate(checks):

        @pl.when(jnp.logical_not(least >= most))
        def _():
            lw = table[:, PAIR + region : PAIR + region + 1]
            transport_logs(gram_ref, plan_ref, move_ref, region, lw, scale)

    lon_dev, nvar, _, members = own_ref.shape
    own = own_ref[...].astype(jnp.float32)
    parts = []
    for region in range(PAIR):
        cells = own[:, :, region * TILE : (region + 1) * TILE].astype(jnp.bfloat16)
        cells = cells.reshape(lon_dev * nvar * TILE, members)
        moved = jnp.dot(cells, move_ref[region], preferred_element_type=jnp.float32)
        parts.append(moved.reshape(lon_dev, nvar, TILE, members))
    out_ref[...] = jnp.concatenate(parts, axis=2).astype(jnp.bfloat16)


def analyse(state, left, right, gram, likes, total, count):
    lon_dev, nvar, lat, members = state.shape
    steps = lat // (PAIR * TILE)
    offsets = range(REGION + 2 * HALO)
    line = [1.0 - max(0, HALO - p, p - (HALO + REGION - 1)) / (HALO + 1) for p in offsets]
    scale = LOG2E / EPS / (nvar * sum(line) ** 2)
    halo_specs = lat_specs(left.shape[0], nvar, members, steps)
    strip = pl.BlockSpec((lon_dev, nvar, PAIR * TILE, members), lambda i: (0, 0, i, 0))
    like_spec = pl.BlockSpec((1, PAIR, members), lambda i: (i, 0, 0))
    return pl.pallas_call(
        functools.partial(analysis_kernel, count, scale),
        grid=(steps,),
        in_specs=halo_specs
        + halo_specs
        + [strip, pl.BlockSpec((PAIR, members, members), lambda i: (i, 0, 0))]
        + [like_spec] * 3
        + [pl.BlockSpec(total.shape, lambda i: (0, 0))],
        out_specs=strip,
        out_shape=jax.ShapeDtypeStruct(state.shape, state.dtype),
        scratch_shapes=[
            pltpu.VMEM((PAIR, members, members), jnp.float32),
            pltpu.VMEM((PAIR, members, members), jnp.float32),
            pltpu.VMEM((PAIR, members, members), jnp.bfloat16),
        ],
        compiler_params=pltpu.CompilerParams(vmem_limit_bytes=48 * 2**20),
        name="analyse",
    )(left, left, left, right, right, right, state, gram,
      *[x.reshape(steps, PAIR, members) for x in likes], total)


def sum_over(value, axis):
    count = lax.axis_size(axis)
    if count & (count - 1):
        return lax.psum(value, axis)
    hop = 1
    while hop < count:
        value = value + lax.ppermute(value, axis, [(i, i ^ hop) for i in range(count)])
        hop *= 2
    return value


def on_device(state, obs_index, obs_value, obs_var):
    lon_dev = state.shape[0]
    count = lax.axis_size("lon")
    to_right = [(i, (i + 1) % count) for i in range(count)]
    to_left = [((i + 1) % count, i) for i in range(count)]
    left = lax.ppermute(state[lon_dev - HALO :], "lon", to_right)
    right = lax.ppermute(state[:HALO], "lon", to_left)
    own, for_left, for_right, part = observe(state, obs_index, obs_value, obs_var)
    total = sum_over(part, "lon")
    from_left = lax.ppermute(for_right, "lon", to_right)
    from_right = lax.ppermute(for_left, "lon", to_left)
    gram = own_gram(state)
    nobs = float(obs_index.shape[0] * count)
    return analyse(state, left, right, gram, (own, from_left, from_right), total, nobs)


def solution(mesh):
    return jax.shard_map(
        on_device,
        mesh=mesh,
        in_specs=(
            P(("ens", "lon"), None, None, None),
            P(("ens", "lon")),
            P(("ens", "lon")),
            P(("ens", "lon")),
        ),
        out_specs=P(("ens", "lon"), None, None, None),
        check_vma=False,
    )
```

time: 96.1 us -> 51.4 us (0.53)
  blocking collectives: 34.6 us -> 0 us
  Pallas kernels: 0 us -> 27.4 us
  local copies, waits for them, and re-layouts: 26.6 us -> 2.41 us
  other arithmetic: 15.9 us -> 0.01 us
  starting transfers between devices: 6.01 us -> 18.6 us
  matrix products: 4.46 us -> 0 us
  waiting for transfers between devices: 6.56 us -> 2.78 us
  between operations: 1.75 us -> 0.1 us
    psum x1 -> x0, blocking collectives: 34.6 us -> none  [tempering(): return count / lax.psum(partial_value, 'lon')]
    pallas_call x0 -> x3, Pallas kernels: none -> 27.4 us  [the longest x1 24.8 us: analyse(): pl.pallas_call(functools.partial(analysis_kernel, count, scale), grid=(st...]
    dot_general x1 -> x0, local copies, waits for them, and re-layouts: 16.4 us -> none  [gram_part(): jnp.einsum('apvbqm,apvbqn->abmn', weighted, win, preferred_element_type=j...]
    ppermute x4 -> x8, starting transfers between devices: 6.01 us -> 18.6 us  [the longest x4 8.66 us: sum_over(): lax.ppermute(value, axis, [(i, i ^ hop) for i in range(count)])]
    reduce_sum x12 -> x0, other arithmetic: 6.74 us -> none  [the longest x4 3.45 us: analyse(): jax.nn.logsumexp((pot_g[..., None, :] - cost) / EPS, axis=-1)]
    dot_general x3 -> x0, matrix products: 4.46 us -> none  [the longest x1 1.95 us: gram_part(): jnp.einsum('apvbqm,apvbqn->abmn', weighted, win, preferred_element_type=j...]
    ppermute x4 -> x8, waiting for transfers between devices: 6.56 us -> 2.78 us  [the longest x4 2.77 us: sum_over(): lax.ppermute(value, axis, [(i, i ^ hop) for i in range(count)])]
    reduce_max x9 -> x0, other arithmetic: 3.63 us -> none  [the longest x4 2.07 us: analyse(): jax.nn.logsumexp((pot_g[..., None, :] - cost) / EPS, axis=-1)]
  transfers between devices with their start and end apart: 4 -> 8, of which waited for: 2 -> 2; matrix products, arithmetic and copies ran while one was open for 8% -> 0% of each run, Pallas kernels for 0% -> 5%
where the time goes in v1:
time: 51.4 us; the launch traced here: 51.3 us
  Pallas kernels  27.4 us (53%)
  starting transfers between devices  18.6 us (36%)
  waiting for transfers between devices  2.78 us (5%)
  local copies, waits for them, and re-layouts  2.41 us (5%)
    pallas_call x1, Pallas kernels, analyse(): pl.pallas_call(functools.partial(analysis_kernel, count, scale), grid=(st...  24.8 us
    ppermute x4, starting transfers between devices, sum_over(): lax.ppermute(value, axis, [(i, i ^ hop) for i in range(count)])  8.66 us
    ppermute x1, starting transfers between devices, on_device(): right = lax.ppermute(state[:HALO], 'lon', to_left)  5.45 us
    ppermute x1, starting transfers between devices, on_device(): from_right = lax.ppermute(for_left, 'lon', to_left)  4.32 us
    ppermute x4, waiting for transfers between devices, sum_over(): lax.ppermute(value, axis, [(i, i ^ hop) for i in range(count)])  2.77 us
    slice x1, local copies, waits for them, and re-layouts, on_device(): right = lax.ppermute(state[:HALO], 'lon', to_left)  2.36 us
    pallas_call x1, Pallas kernels, own_gram(): pl.pallas_call(own_gram_kernel, grid=(steps,), in_specs=lat_specs(lon_dev...  1.66 us
  transfers between devices with their start and end apart: 8, of which 2 were waited for; matrix products, arithmetic and copies ran while one was open for 0% of the time, Pallas kernels for 5%

profile of v1, /device:TPU:0, one launch (start us, length us, event | category | flops | bytes accessed | tf_op | source)
XLA Modules:
  0.0 51.3 jit_solution(4928962474897847036)
XLA Ops:
  0.0 0.0 copy-start
  0.0 0.0 copy-start.3
  0.0 0.0 copy-start.2
  0.0 0.0 copy-start.1
  0.0 2.4 %fusion = (bf16[4,4,64,256]{3,2,1,0:T(8,128)(2,1)}, bf16[4,4,64,256]{3,2,1,0:T(8,128)(2,1)}) fusion(bf16[8,4,64,256]{3,2,1,0:T(8,128)(2,1)} %refs_6_.1), kind=kLoop, calls=%fused_computation | loop fusion | bytes 2097152 | tf_op jit(solution)/shard_map/slice | solution.py:318
  2.4 5.5 %collective-permute-start.1 = (bf16[4,4,64,256]{3,2,1,0:T(8,128)(2,1)}, bf16[4,4,64,256]{3,2,1,0:T(8,128)(2,1)}, u32[]{:S(2)}, u32[]{:S(2)}) collective-permute-start(bf16[4,4,64,256]{3,2,1,0:T(8,128)(2,1)} %get-tuple-element.13), channel_id=1, source_target_pairs={{1,0},{2,1},{3,2},{4,3},{5,4},{6,5},{7,6},{8,7},{9,8},{10,9},{11,1... | collective-permute-start | bytes 1572872 | tf_op jit(solution)/shard_map/ppermute | solution.py:318
  7.8 0.0 collective-permute-start
  7.8 0.0 copy-done
  7.8 0.0 copy-done.3
  7.8 0.0 copy-done.2
  7.8 0.0 copy-done.1
  7.9 0.9 %observe.1 = (f32[8,256]{1,0:T(8,128)S(1)}, f32[8,256]{1,0:T(8,128)S(1)}, f32[8,256]{1,0:T(8,128)S(1)}, f32[8,128]{1,0:T(8,128)S(1)}) custom-call(bf16[8,4,64,256]{3,2,1,0:T(8,128)(2,1)S(1)} %copy-done, s32[1,256]{1,0:T(1,128)S(1)} %bitcast.3, f32[1,256]{1,0:T(1,128)S(1)} %bitcast.4, f32[1,256]{1,0:T(1,128)S(1)} %bitcast.5), custom_call_target="tpu_custom_call" | custom-call | tf_op jit(solution)/shard_map/observe/pallas_call | solution.py:67
  8.8 0.0 collective-permute-start.4
  8.8 1.2 %collective-permute-done.4 = f32[8,128]{1,0:T(8,128)S(1)} collective-permute-done((f32[8,128]{1,0:T(8,128)S(1)}, f32[8,128]{1,0:T(8,128)S(1)}, u32[]{:S(2)}, u32[]{:S(2)}) %collective-permute-start.4) | collective-permute-done | bytes 4128 | tf_op jit(solution)/shard_map/ppermute | solution.py:307
  10.0 0.0 collective-permute-start.5
  10.0 0.2 collective-permute-start.2
  10.1 4.3 %collective-permute-start.3 = (f32[8,256]{1,0:T(8,128)S(1)}, f32[8,256]{1,0:T(8,128)S(1)}, u32[]{:S(2)}, u32[]{:S(2)}) collective-permute-start(f32[8,256]{1,0:T(8,128)S(1)} %get-tuple-element.11), channel_id=1, source_target_pairs={{1,0},{2,1},{3,2},{4,3},{5,4},{6,5},{7,6},{8,7},{9,8},{10,9},{11,1... | collective-permute-start | bytes 24584 | tf_op jit(solution)/shard_map/ppermute | solution.py:322
  14.5 0.0 collective-permute-done.5
  14.5 5.6 %collective-permute-start.6 = (f32[8,128]{1,0:T(8,128)S(1)}, f32[8,128]{1,0:T(8,128)S(1)}, u32[]{:S(2)}, u32[]{:S(2)}) collective-permute-start(f32[8,128]{1,0:T(8,128)S(1)} %add.13), channel_id=1, source_target_pairs={{0,4},{1,5},{2,6},{3,7},{4,0},{5,1},{6,2},{7,3},{8,12},{9,13},{10,... | collective-permute-start | bytes 12296 | tf_op jit(solution)/shard_map/ppermute | solution.py:307
  20.1 1.6 %collective-permute-done.6 = f32[8,128]{1,0:T(8,128)S(1)} collective-permute-done((f32[8,128]{1,0:T(8,128)S(1)}, f32[8,128]{1,0:T(8,128)S(1)}, u32[]{:S(2)}, u32[]{:S(2)}) %collective-permute-start.6) | collective-permute-done | bytes 4128 | tf_op jit(solution)/shard_map/ppermute | solution.py:307
  21.7 3.0 %collective-permute-start.7 = (f32[8,128]{1,0:T(8,128)S(1)}, f32[8,128]{1,0:T(8,128)S(1)}, u32[]{:S(2)}, u32[]{:S(2)}) collective-permute-start(f32[8,128]{1,0:T(8,128)S(1)} %add.14), channel_id=1, source_target_pairs={{0,8},{1,9},{2,10},{3,11},{4,12},{5,13},{6,14},{7,15},{8,0},{9,1},... | collective-permute-start | bytes 12296 | tf_op jit(solution)/shard_map/ppermute | solution.py:307
  24.7 1.7 %own_gram.1.refs_7_ = f32[8,256,256]{2,1,0:T(8,128)S(1)} custom-call(bf16[8,4,64,256]{3,2,1,0:T(8,128)(2,1)S(1)} %copy-done, bf16[8,4,64,256]{3,2,1,0:T(8,128)(2,1)S(1)} %copy-done, bf16[8,4,64,256]{3,2,1,0:T(8,128)(2,1)S(1)} %copy-done), custom_call_target="tpu_custom_call" | custom-call | tf_op jit(solution)/shard_map/own_gram/pallas_call | solution.py:134
  26.4 0.0 collective-permute-done.2
  26.4 0.0 collective-permute-done.3
  26.5 0.0 collective-permute-done.7
  26.5 0.0 collective-permute-done.1.refs_3_.refs_4_.refs_5_
  26.5 0.0 collective-permute-done.refs_0_.refs_1_.refs_2_
  26.5 24.8 %analyse.1 = bf16[8,4,64,256]{3,2,1,0:T(8,128)(2,1)} custom-call(bf16[4,4,64,256]{3,2,1,0:T(8,128)(2,1)} %collective-permute-done.refs_0_.refs_1_.refs_2_, bf16[4,4,64,256]{3,2,1,0:T(8,128)(2,1)} %collective-permute-done.refs_0_.refs_1_.refs_2_, bf16[4,4,64,256]{3,2,1,0:T(8,128)(2,1)} %collective-permute-done.refs_0_.refs_1_.refs_2_, ...), custom_call_target="tpu_custom_call" | custom-call | tf_op jit(solution)/shard_map/analyse/pallas_call | solution.py:280
  (7 shorter events, 0.0 us)
Async XLA Ops:
  0.0 7.8 %copy-start = (bf16[8,4,64,256]{3,2,1,0:T(8,128)(2,1)S(1)}, bf16[8,4,64,256]{3,2,1,0:T(8,128)(2,1)}, u32[]{:S(2)}) copy-start(bf16[8,4,64,256]{3,2,1,0:T(8,128)(2,1)} %refs_6_.1) | copy-start | bytes 3145732
  0.0 7.8 %copy-start.3 = (f32[256]{0:T(256)S(1)}, f32[256]{0:T(256)}, u32[]{:S(2)}) copy-start(f32[256]{0:T(256)} %param.7) | copy-start | bytes 3076
  0.0 7.8 %copy-start.2 = (f32[256]{0:T(256)S(1)}, f32[256]{0:T(256)}, u32[]{:S(2)}) copy-start(f32[256]{0:T(256)} %param.6) | copy-start | bytes 3076
  0.0 7.8 %copy-start.1 = (s32[256]{0:T(256)S(1)}, s32[256]{0:T(256)}, u32[]{:S(2)}) copy-start(s32[256]{0:T(256)} %param.5) | copy-start | bytes 3076
  2.4 24.1 %collective-permute-start.1 = (bf16[4,4,64,256]{3,2,1,0:T(8,128)(2,1)}, bf16[4,4,64,256]{3,2,1,0:T(8,128)(2,1)}, u32[]{:S(2)}, u32[]{:S(2)}) collective-permute-start(bf16[4,4,64,256]{3,2,1,0:T(8,128)(2,1)} %get-tuple-element.13), channel_id=1, source_target_pairs={{1,0},{2,1},{3,2},{4,3},{5,4},{6,5},{7,6},{8,7},{9,8},{10,9},{11,1... | collective-permute-start | bytes 1572872 | tf_op jit(solution)/shard_map/ppermute | solution.py:318
  7.8 18.7 %collective-permute-start = (bf16[4,4,64,256]{3,2,1,0:T(8,128)(2,1)}, bf16[4,4,64,256]{3,2,1,0:T(8,128)(2,1)}, u32[]{:S(2)}, u32[]{:S(2)}) collective-permute-start(bf16[4,4,64,256]{3,2,1,0:T(8,128)(2,1)} %get-tuple-element.14), channel_id=1, source_target_pairs={{0,1},{1,2},{2,3},{3,4},{4,5},{5,6},{6,7},{7,8},{8,9},{9,10},{10,1... | collective-permute-start | bytes 1572872 | tf_op jit(solution)/shard_map/ppermute | solution.py:317
  8.8 1.2 %collective-permute-start.4 = (f32[8,128]{1,0:T(8,128)S(1)}, f32[8,128]{1,0:T(8,128)S(1)}, u32[]{:S(2)}, u32[]{:S(2)}) collective-permute-start(f32[8,128]{1,0:T(8,128)S(1)} %get-tuple-element.12), channel_id=1, source_target_pairs={{0,1},{1,0},{2,3},{3,2},{4,5},{5,4},{6,7},{7,6},{8,9},{9,8},{10,11... | collective-permute-start | bytes 12296 | tf_op jit(solution)/shard_map/ppermute | solution.py:307
  10.0 4.5 %collective-permute-start.5 = (f32[8,128]{1,0:T(8,128)S(1)}, f32[8,128]{1,0:T(8,128)S(1)}, u32[]{:S(2)}, u32[]{:S(2)}) collective-permute-start(f32[8,128]{1,0:T(8,128)S(1)} %add.12), channel_id=1, source_target_pairs={{0,2},{1,3},{2,0},{3,1},{4,6},{5,7},{6,4},{7,5},{8,10},{9,11},{10,... | collective-permute-start | bytes 12296 | tf_op jit(solution)/shard_map/ppermute | solution.py:307
  10.0 16.4 %collective-permute-start.2 = (f32[8,256]{1,0:T(8,128)S(1)}, f32[8,256]{1,0:T(8,128)S(1)}, u32[]{:S(2)}, u32[]{:S(2)}) collective-permute-start(f32[8,256]{1,0:T(8,128)S(1)} %get-tuple-element.10), channel_id=1, source_target_pairs={{0,1},{1,2},{2,3},{3,4},{4,5},{5,6},{6,7},{7,8},{8,9},{9,10},{10,1... | collective-permute-start | bytes 24584 | tf_op jit(solution)/shard_map/ppermute | solution.py:321
  10.1 16.3 %collective-permute-start.3 = (f32[8,256]{1,0:T(8,128)S(1)}, f32[8,256]{1,0:T(8,128)S(1)}, u32[]{:S(2)}, u32[]{:S(2)}) collective-permute-start(f32[8,256]{1,0:T(8,128)S(1)} %get-tuple-element.11), channel_id=1, source_target_pairs={{1,0},{2,1},{3,2},{4,3},{5,4},{6,5},{7,6},{8,7},{9,8},{10,9},{11,1... | collective-permute-start | bytes 24584 | tf_op jit(solution)/shard_map/ppermute | solution.py:322
  14.5 7.2 %collective-permute-start.6 = (f32[8,128]{1,0:T(8,128)S(1)}, f32[8,128]{1,0:T(8,128)S(1)}, u32[]{:S(2)}, u32[]{:S(2)}) collective-permute-start(f32[8,128]{1,0:T(8,128)S(1)} %add.13), channel_id=1, source_target_pairs={{0,4},{1,5},{2,6},{3,7},{4,0},{5,1},{6,2},{7,3},{8,12},{9,13},{10,... | collective-permute-start | bytes 12296 | tf_op jit(solution)/shard_map/ppermute | solution.py:307
  21.7 4.8 %collective-permute-start.7 = (f32[8,128]{1,0:T(8,128)S(1)}, f32[8,128]{1,0:T(8,128)S(1)}, u32[]{:S(2)}, u32[]{:S(2)}) collective-permute-start(f32[8,128]{1,0:T(8,128)S(1)} %add.14), channel_id=1, source_target_pairs={{0,8},{1,9},{2,10},{3,11},{4,12},{5,13},{6,14},{7,15},{8,0},{9,1},... | collective-permute-start | bytes 12296 | tf_op jit(solution)/shard_map/ppermute | solution.py:307

commit v2 on v1

v2 whole, which is shorter than its diff:
```python
import functools
import math

import jax
import jax.numpy as jnp
from jax import lax
from jax.experimental import pallas as pl
from jax.experimental.pallas import tpu as pltpu
from jax.sharding import PartitionSpec as P

REGION = 8
HALO = 4
SWEEPS = 4
EPS = 0.05
TILE = 8
PAIR = 2
LOG2E = 1.4426950408889634
ROWS = 32
GROUP = 4
LIFT, START, MASS = 20, -10, 60

HIGH = lax.Precision.HIGHEST


def line_weight(place):
    dist = jnp.maximum(0.0, jnp.maximum(HALO - place, place - (HALO + REGION - 1)))
    inside = (place >= 0) & (place < REGION + 2 * HALO)
    return jnp.where(inside, 1.0 - dist / (HALO + 1), 0.0)


def obs_kernel(cells_ref, index_ref, value_ref, var_ref, own_ref, left_ref, right_ref, part_ref):
    lon_dev, _, lat, members = cells_ref.shape
    nobs = index_ref.shape[1]
    rows = cells_ref[:, 0].reshape(lon_dev * lat, members)
    index = index_ref[...]
    sub = lax.broadcasted_iota(jnp.int32, (TILE, nobs), 0)
    table = jnp.where(
        sub == 0,
        index.astype(jnp.float32),
        jnp.where(sub == 1, value_ref[...], var_ref[...]),
    ).T
    index_col = table[:, 0:1].astype(jnp.int32)
    value = table[:, 1:2]
    var = table[:, 2:3]
    pick = index_col == lax.broadcasted_iota(jnp.int32, (nobs, lon_dev * lat), 1)
    pick = jnp.where(pick, 1.0, 0.0).astype(jnp.bfloat16)
    seen = jnp.dot(pick, rows, preferred_element_type=jnp.float32)
    centre = jnp.sum(seen, axis=1, keepdims=True) * (1.0 / members)
    spread = jnp.sum((seen - centre) ** 2, axis=1, keepdims=True) * (1.0 / (members - 1))
    innovation = (value - centre) ** 2 / (var + spread)
    part_ref[...] = jnp.broadcast_to(jnp.sum(innovation, axis=0, keepdims=True), part_ref.shape)
    terms = (value - seen) ** 2 * (1.0 / var)
    lon = (index // lat).astype(jnp.float32)
    along = index.astype(jnp.float32) - lon * lat
    for ref, shift in ((own_ref, HALO), (left_ref, HALO + REGION), (right_ref, HALO - REGION)):
        blocks = ref.shape[0]
        block = lax.broadcasted_iota(jnp.int32, (blocks, nobs), 0).astype(jnp.float32)
        weight = line_weight(lon + shift) * line_weight(along - REGION * block + HALO)
        ref[...] = jnp.dot(weight, terms, precision=HIGH, preferred_element_type=jnp.float32)


def observe(state, obs_index, obs_value, obs_var):
    lon_dev, _, lat, members = state.shape
    nobs = obs_index.shape[0]
    blocks = lat // REGION
    row = pl.BlockSpec((1, nobs), lambda i: (0, 0))
    like = jax.ShapeDtypeStruct((blocks, members), jnp.float32)
    like_spec = pl.BlockSpec((blocks, members), lambda i: (0, 0))
    return pl.pallas_call(
        obs_kernel,
        grid=(1,),
        in_specs=[pl.BlockSpec((lon_dev, 1, lat, members), lambda i: (0, 0, 0, 0)), row, row, row],
        out_specs=[like_spec] * 3 + [pl.BlockSpec((8, 128), lambda i: (0, 0))],
        out_shape=[like] * 3 + [jax.ShapeDtypeStruct((8, 128), jnp.float32)],
        compiler_params=pltpu.CompilerParams(vmem_limit_bytes=32 * 2**20),
        name="observe",
    )(state, obs_index[None], obs_value[None], obs_var[None])


def pair_tiles(ref, step, steps):
    size = PAIR * TILE

    def load(at):
        return ref[:, :, pl.ds(pl.multiple_of(at * size, size), size), :].astype(jnp.float32)

    here = load(step)
    before = load(jnp.maximum(step - 1, 0))[:, :, TILE:]
    after = load(jnp.minimum(step + 1, steps - 1))[:, :, :TILE]
    before = jnp.where(step == 0, 0.0, before)
    after = jnp.where(step == steps - 1, 0.0, after)
    return before, here[:, :, :TILE], here[:, :, TILE:], after


def gram_of(tiles, places):
    before, low, high, after = tiles
    columns, nvar, _, members = low.shape
    row = lax.broadcasted_iota(jnp.int32, (1, TILE, members), 1)
    upper = row < HALO
    rowf = row.astype(jnp.float32)
    edge = line_weight(jnp.where(upper, rowf + (HALO + REGION), rowf - HALO))
    grams = []
    for own, following, preceding in ((low, high, before), (high, after, low)):
        margin = jnp.where(upper, following, preceding)
        win = jnp.concatenate([own, margin], axis=2)
        weighted = []
        for column, place in enumerate(places):
            dist = max(0, HALO - place, place - (HALO + REGION - 1))
            if dist:
                weight = jnp.float32(1.0) - jnp.float32(dist) / jnp.float32(HALO + 1)
                parts = [own[column] * weight, margin[column] * (edge * weight)]
            else:
                parts = [own[column], margin[column] * edge]
            weighted.append(jnp.concatenate(parts, axis=1))
        weighted = jnp.stack(weighted)
        shape = (columns * nvar * 2 * TILE, members)
        grams.append(
            lax.dot_general(
                weighted.astype(jnp.bfloat16).reshape(shape),
                win.astype(jnp.bfloat16).reshape(shape),
                (((0,), (0,)), ((), ())),
                preferred_element_type=jnp.float32,
            )
        )
    return grams


def own_gram_kernel(state_ref, gram_ref):
    step, steps = pl.program_id(0), pl.num_programs(0)
    places = range(HALO, HALO + state_ref.shape[0])
    grams = gram_of(pair_tiles(state_ref, step, steps), places)
    for region in range(PAIR):
        gram_ref[region] = grams[region]


def own_gram(state):
    lon_dev, nvar, lat, members = state.shape
    steps = lat // (PAIR * TILE)
    return pl.pallas_call(
        own_gram_kernel,
        grid=(steps,),
        in_specs=[pl.BlockSpec(state.shape, lambda i: (0, 0, 0, 0))],
        out_specs=pl.BlockSpec((PAIR, members, members), lambda i: (i, 0, 0)),
        out_shape=jax.ShapeDtypeStruct((steps * PAIR, members, members), jnp.float32),
        compiler_params=pltpu.CompilerParams(vmem_limit_bytes=48 * 2**20),
        name="own_gram",
    )(state)


def halves(ref, region, rows):
    members = ref.shape[-1]
    return [ref[region, rows, at : at + 128] for at in range(0, members, 128)]


def diagonal(gram_ref, region):
    members = gram_ref.shape[-1]
    across = [None] * (members // 128)
    down = []
    for start in range(0, members, ROWS):
        lane = start // 128
        gram = gram_ref[region, pl.ds(start, ROWS), lane * 128 : lane * 128 + 128]
        i = lax.broadcasted_iota(jnp.int32, gram.shape, 0) + start
        j = lax.broadcasted_iota(jnp.int32, gram.shape, 1) + lane * 128
        kept = jnp.where(i == j, gram, 0.0)
        down.append(jnp.broadcast_to(jnp.sum(kept, axis=1, keepdims=True), gram.shape))
        part = jnp.sum(kept.reshape(ROWS // TILE, TILE, 128), axis=0)
        across[lane] = part if across[lane] is None else across[lane] + part
    return [jnp.sum(x, axis=0, keepdims=True) for x in across], down


def sweep_rows(parts, weight, totals):
    scaled, mass = parts
    mass = jnp.broadcast_to(jnp.sum(mass, axis=1, keepdims=True), weight.shape)
    near = pl.reciprocal(mass, approx=True)
    ratio = weight * (near * (2.0 - mass * near))
    for lane, part in enumerate(scaled):
        part = jnp.sum((part * ratio).reshape(ROWS // TILE, TILE, 128), axis=0)
        totals[lane] = part if totals[lane] is None else totals[lane] + part
    return mass, ratio


def fold(values, op):
    out = values[0]
    for value in values[1:]:
        out = op(out, value)
    return out


def sweeps_scaled(regions, gram_ref, kernel_ref, ratio_ref, weight_ref, scale):
    members = gram_ref.shape[-1]
    starts = range(0, members, ROWS)
    lanes = range(members // 128)
    least_row, most_row, least_col, cols = [], [], [], []
    share = 2.0**MASS / members

    def settle(totals):
        totals = [jnp.sum(x, axis=0, keepdims=True) for x in totals]
        return totals, fold(totals, jnp.minimum)

    for region in regions:
        across, down = diagonal(gram_ref, region)
        across = [0.5 * LIFT - x * scale for x in across]
        totals = [None] * len(lanes)
        masses = []
        for at, start in enumerate(starts):
            rows = pl.ds(start, ROWS)
            base = 0.5 * LIFT - down[at] * scale
            kernel = [
                jnp.exp2(g * (2.0 * scale) + base + x)
                for g, x in zip(halves(gram_ref, region, rows), across)
            ]
            for lane, part in enumerate(kernel):
                kernel_ref[region, rows, lane * 128 : lane * 128 + 128] = part
            mass, _ = sweep_rows(
                (kernel, fold(kernel, jnp.add) * 2.0**START), weight_ref[region, rows, :], totals
            )
            masses.append(mass)
        least_row.append(fold(masses, jnp.minimum))
        most_row.append(fold(masses, jnp.maximum))
        totals, least = settle(totals)
        least_col.append(least)
        cols.append(totals)

    def sweep(last, carry):
        least_row, least_col, cols = carry
        rows_out, least_out, cols_out = [], [], []
        for region, lrow, lcol, col in zip(regions, least_row, least_col, cols):
            factor = [share / x for x in col]
            totals = [None] * len(lanes)
            for start in starts:
                rows = pl.ds(start, ROWS)
                kernel = halves(kernel_ref, region, rows)
                mass = fold([k * f for k, f in zip(kernel, factor)], jnp.add)
                mass, ratio = sweep_rows((kernel, mass), weight_ref[region, rows, :], totals)
                if last:
                    ratio_ref[region, rows, :] = ratio
                lrow = jnp.minimum(lrow, mass)
            totals, least = settle(totals)
            rows_out.append(lrow)
            least_out.append(jnp.minimum(lcol, least))
            cols_out.append(totals)
        return rows_out, least_out, cols_out

    carry = least_row, least_col, cols
    carry = lax.fori_loop(0, SWEEPS - 2, lambda i, c: sweep(False, c), carry)
    least_row, least_col, cols = sweep(True, carry)
    factors = [[1.0 / x for x in col] for col in cols]
    return (
        factors,
        fold(least_row, jnp.minimum),
        fold(least_col, jnp.minimum),
        fold(most_row, jnp.maximum),
    )


def transport_scaled(region, factor, kernel_ref, ratio_ref):
    members = kernel_ref.shape[-1]
    parts = []
    for start in range(0, members, ROWS):
        rows = pl.ds(start, ROWS)
        ratio = ratio_ref[region, rows, :]
        row = [k * ratio * f for k, f in zip(halves(kernel_ref, region, rows), factor)]
        parts.append(jnp.concatenate(row, axis=1).astype(jnp.bfloat16))
    return jnp.concatenate(parts, axis=0)


def transport_logs(region, gram_ref, logw, scale):
    members = gram_ref.shape[-1]
    gram = gram_ref[region]
    i = lax.broadcasted_iota(jnp.int32, gram.shape, 0)
    j = lax.broadcasted_iota(jnp.int32, gram.shape, 1)
    kept = jnp.where(i == j, gram, 0.0)
    down = jnp.sum(kept, axis=1, keepdims=True)
    across = jnp.sum(kept, axis=0, keepdims=True)
    cost = (down + across - 2.0 * gram) * scale
    logw = jnp.sum(jnp.where(i == j, logw, 0.0), axis=1, keepdims=True)
    pot_g = jnp.zeros((1, members), jnp.float32)
    for sweep in range(SWEEPS):
        term = pot_g - cost
        top = jnp.max(term, axis=1, keepdims=True)
        pot_f = logw - top - jnp.log(jnp.sum(jnp.exp2(term - top), axis=1, keepdims=True)) * LOG2E
        term = pot_f - cost
        top = jnp.max(term, axis=0, keepdims=True)
        pot_g = -math.log2(members) - top
        pot_g = pot_g - jnp.log(jnp.sum(jnp.exp2(term - top), axis=0, keepdims=True)) * LOG2E
    return (members * jnp.exp2(pot_f + pot_g - cost)).astype(jnp.bfloat16)


def transform(state_ref, pair, moves):
    lon_dev, nvar, _, members = state_ref.shape
    size = PAIR * TILE
    own = state_ref[:, :, pl.ds(pl.multiple_of(pair * size, size), size), :].astype(jnp.float32)
    parts = []
    for region, move in enumerate(moves):
        cells = own[:, :, region * TILE : (region + 1) * TILE].astype(jnp.bfloat16)
        cells = cells.reshape(lon_dev * nvar * TILE, members)
        moved = jnp.dot(cells, move, preferred_element_type=jnp.float32)
        parts.append(moved.reshape(lon_dev, nvar, TILE, members))
    return jnp.concatenate(parts, axis=2).astype(jnp.bfloat16)


def analysis_kernel(count, scale, *refs):
    left_ref, right_ref, state_ref, gram_in_ref = refs[0:4]
    like_refs, total_ref, out_ref = refs[4:7], refs[7], refs[8]
    gram_ref, kernel_ref, ratio_ref, weight_ref, logw_ref, result_ref, sems = refs[9:]
    columns = left_ref.shape[0]
    regions, members = gram_in_ref.shape[0], gram_in_ref.shape[-1]
    pairs = regions // PAIR
    size = PAIR * TILE

    total = jnp.sum(total_ref[...], axis=0, keepdims=True)[:, 0:1] * (1.0 / TILE)
    like = -0.5 * (count / total) * (like_refs[0][...] + like_refs[1][...] + like_refs[2][...])
    like = like - jnp.max(like, axis=1, keepdims=True)
    logw = (like - jnp.log(jnp.sum(jnp.exp(like), axis=1, keepdims=True))) * LOG2E
    logw_ref[...] = logw
    weight = jnp.exp2(logw + MASS).T
    for region in range(regions):
        weight_ref[region] = jnp.broadcast_to(weight[:, region : region + 1], (members, 128))

    def send(pair):
        at = pl.ds(pl.multiple_of(pair * size, size), size)
        return pltpu.make_async_copy(result_ref.at[pair], out_ref.at[:, :, at, :], sems.at[pair])

    def halo_grams(pair, carry):
        left = pair_tiles(left_ref, pair, pairs)
        right = pair_tiles(right_ref, pair, pairs)
        both = [jnp.concatenate([x, y], axis=0) for x, y in zip(left, right)]
        far = HALO + REGION
        grams = gram_of(both, list(range(columns)) + list(range(far, far + columns)))
        for at in range(PAIR):
            region = pair * PAIR + at
            gram_ref[region] = gram_in_ref[region] + grams[at]
        return carry

    lax.fori_loop(0, pairs, halo_grams, 0)

    def group(at, carry):
        least_row, least_col, most_row = carry
        first = at * GROUP
        factors, row, col, most = sweeps_scaled(
            [first + r for r in range(GROUP)], gram_ref, kernel_ref, ratio_ref, weight_ref, scale
        )
        for pair in range(GROUP // PAIR):
            moves = [
                transport_scaled(first + r, factors[r], kernel_ref, ratio_ref)
                for r in range(pair * PAIR, (pair + 1) * PAIR)
            ]
            where = at * (GROUP // PAIR) + pair
            result_ref[where] = transform(state_ref, where, moves)
            send(where).start()
        return (
            jnp.minimum(least_row, row),
            jnp.minimum(least_col, col),
            jnp.maximum(most_row, most),
        )

    high = jnp.full((ROWS, 128), 1e30, jnp.float32)
    least_row, least_col, most_row = lax.fori_loop(
        0, regions // GROUP, group, (high, high[:1], jnp.zeros((ROWS, 128), jnp.float32))
    )

    def drain(pair, carry):
        send(pair).wait()
        return carry

    lax.fori_loop(0, pairs, drain, 0)
    row, col, most = jnp.min(least_row), jnp.min(least_col), jnp.max(most_row)
    sound = (row >= 2.0**-24) & (col >= 2.0**-30) & (most <= 2.0**20) & (row * col >= 2.0**-34)

    @pl.when(jnp.logical_not(sound))
    def _():
        def again(pair, carry):
            moves = []
            for at in range(PAIR):
                region = pair * PAIR + at
                moves.append(transport_logs(region, gram_ref, logw_ref[pl.ds(region, 1), :], scale))
            result_ref[pair] = transform(state_ref, pair, moves)
            copy = send(pair)
            copy.start()
            copy.wait()
            return carry

        lax.fori_loop(0, pairs, again, 0)


def analyse(state, left, right, gram, likes, total, count):
    lon_dev, nvar, lat, members = state.shape
    regions = lat // REGION
    offsets = range(REGION + 2 * HALO)
    line = [1.0 - max(0, HALO - p, p - (HALO + REGION - 1)) / (HALO + 1) for p in offsets]
    scale = LOG2E / EPS / (nvar * sum(line) ** 2)
    vmem = pl.BlockSpec(memory_space=pltpu.VMEM)
    return pl.pallas_call(
        functools.partial(analysis_kernel, count, scale),
        in_specs=[vmem] * 8,
        out_specs=pl.BlockSpec(memory_space=pl.ANY),
        out_shape=jax.ShapeDtypeStruct(state.shape, state.dtype),
        scratch_shapes=[
            pltpu.VMEM((regions, members, members), jnp.float32),
            pltpu.VMEM((regions, members, members), jnp.float32),
            pltpu.VMEM((regions, members, 128), jnp.float32),
            pltpu.VMEM((regions, members, 128), jnp.float32),
            pltpu.VMEM((regions, members), jnp.float32),
            pltpu.VMEM((regions // PAIR, lon_dev, nvar, PAIR * TILE, members), jnp.bfloat16),
            pltpu.SemaphoreType.DMA((regions // PAIR,)),
        ],
        compiler_params=pltpu.CompilerParams(vmem_limit_bytes=48 * 2**20),
        name="analyse",
    )(left, right, state, gram, *likes, total)


def on_device(state, obs_index, obs_value, obs_var):
    lon_dev = state.shape[0]
    count = lax.axis_size("lon")
    to_right = [(i, (i + 1) % count) for i in range(count)]
    to_left = [((i + 1) % count, i) for i in range(count)]
    left = lax.ppermute(state[lon_dev - HALO :], "lon", to_right)
    right = lax.ppermute(state[:HALO], "lon", to_left)
    own, for_left, for_right, part = observe(state, obs_index, obs_value, obs_var)
    total = lax.all_gather(part, "lon", tiled=True)
    from_left = lax.ppermute(for_right, "lon", to_right)
    from_right = lax.ppermute(for_left, "lon", to_left)
    gram = own_gram(state)
    nobs = float(obs_index.shape[0] * count)
    return analyse(state, left, right, gram, (own, from_left, from_right), total, nobs)


def solution(mesh):
    return jax.shard_map(
        on_device,
        mesh=mesh,
        in_specs=(
            P(("ens", "lon"), None, None, None),
            P(("ens", "lon")),
            P(("ens", "lon")),
            P(("ens", "lon")),
        ),
        out_specs=P(("ens", "lon"), None, None, None),
        check_vma=False,
    )
```

time: 51.4 us -> 48 us (0.934)
  the two profiles are of different devices: /device:TPU:0 before, /device:TPU:1 now
where the time goes in v2:
time: 48 us; the launch traced here: 47.7 us
  blocking collectives  21.9 us (46%)
  Pallas kernels  18.8 us (39%)
  starting transfers between devices  5.59 us (12%)
  local copies, waits for them, and re-layouts  1.37 us (3%)
    all_gather x1, blocking collectives, on_device(): total = lax.all_gather(part, 'lon', tiled=True)  21.9 us
    pallas_call x1, Pallas kernels, analyse(): pl.pallas_call(functools.partial(analysis_kernel, count, scale), in_specs...  16.5 us
    ppermute x1, starting transfers between devices, on_device(): left = lax.ppermute(state[lon_dev - HALO:], 'lon', to_right)  2.65 us
    ppermute x1, starting transfers between devices, on_device(): from_right = lax.ppermute(for_left, 'lon', to_left)  2.38 us
    pallas_call x1, Pallas kernels, own_gram(): pl.pallas_call(own_gram_kernel, grid=(steps,), in_specs=[pl.BlockSpec(sta...  1.4 us
    slice x1, local copies, waits for them, and re-layouts, on_device(): right = lax.ppermute(state[:HALO], 'lon', to_left)  1.35 us
  transfers between devices with their start and end apart: 4, of which 0 were waited for; matrix products, arithmetic and copies ran while one was open for 0% of the time, Pallas kernels for 5%

profile of v2, /device:TPU:1, one launch (start us, length us, event | category | flops | bytes accessed | tf_op | source)
XLA Modules:
  0.0 47.7 jit_solution(1660947649042243769)
XLA Ops:
  0.0 0.0 copy-start
  0.0 0.0 copy-start.3
  0.0 0.0 copy-start.2
  0.0 0.0 copy-start.1
  0.0 1.4 %fusion = (bf16[4,4,64,256]{3,2,1,0:T(8,128)(2,1)S(1)}, bf16[4,4,64,256]{3,2,1,0:T(8,128)(2,1)S(1)}) fusion(bf16[8,4,64,256]{3,2,1,0:T(8,128)(2,1)} %refs_2_.1), kind=kLoop, calls=%fused_computation | loop fusion | bytes 2097152 | tf_op jit(solution)/shard_map/slice | solution.py:417
  1.4 0.1 collective-permute-start.1
  1.5 2.6 %collective-permute-start = (bf16[4,4,64,256]{3,2,1,0:T(8,128)(2,1)S(1)}, bf16[4,4,64,256]{3,2,1,0:T(8,128)(2,1)S(1)}, u32[]{:S(2)}, u32[]{:S(2)}) collective-permute-start(bf16[4,4,64,256]{3,2,1,0:T(8,128)(2,1)S(1)} %get-tuple-element.14), channel_id=1, source_target_pairs={{0,1},{1,2},{2,3},{3,4},{4,5},{5,6},{6,7},{7,8},{8,9},{9,10},{10,1... | collective-permute-start | bytes 1572872 | tf_op jit(solution)/shard_map/ppermute | solution.py:416
  4.1 0.0 copy-done
  4.1 0.0 copy-done.3
  4.1 0.0 copy-done.2
  4.1 0.0 copy-done.1
  4.1 0.9 %observe.1 = (f32[8,256]{1,0:T(8,128)S(1)}, f32[8,256]{1,0:T(8,128)S(1)}, f32[8,256]{1,0:T(8,128)S(1)}, f32[8,128]{1,0:T(8,128)S(1)}) custom-call(bf16[8,4,64,256]{3,2,1,0:T(8,128)(2,1)S(1)} %copy-done, s32[1,256]{1,0:T(1,128)S(1)} %bitcast.3, f32[1,256]{1,0:T(1,128)S(1)} %bitcast.4, f32[1,256]{1,0:T(1,128)S(1)} %bitcast.5), custom_call_target="tpu_custom_call" | custom-call | tf_op jit(solution)/shard_map/observe/pallas_call | solution.py:69
  5.1 0.5 collective-permute-start.2
  5.5 2.4 %collective-permute-start.3 = (f32[8,256]{1,0:T(8,128)S(1)}, f32[8,256]{1,0:T(8,128)S(1)}, u32[]{:S(2)}, u32[]{:S(2)}) collective-permute-start(f32[8,256]{1,0:T(8,128)S(1)} %get-tuple-element.11), channel_id=1, source_target_pairs={{1,0},{2,1},{3,2},{4,3},{5,4},{6,5},{7,6},{8,7},{9,8},{10,9},{11,1... | collective-permute-start | bytes 24584 | tf_op jit(solution)/shard_map/ppermute | solution.py:421
  7.9 21.9 %all_gather.3.refs_7_ = f32[128,128]{1,0:T(8,128)S(1)} all-gather(f32[8,128]{1,0:T(8,128)S(1)} %get-tuple-element.12), channel_id=1, replica_groups=mesh['ens'=2,'lon'=16] {'lon'}, dimensions={0}, use_global_device_ids=true | all-gather | bytes 69632 | tf_op jit(solution)/shard_map/all_gather | solution.py:419
  29.8 1.4 %own_gram.1.refs_3_ = f32[8,256,256]{2,1,0:T(8,128)S(1)} custom-call(bf16[8,4,64,256]{3,2,1,0:T(8,128)(2,1)S(1)} %copy-done), custom_call_target="tpu_custom_call" | custom-call | tf_op jit(solution)/shard_map/own_gram/pallas_call | solution.py:138
  31.2 0.0 collective-permute-done.2.refs_5_
  31.2 0.0 collective-permute-done.3.refs_6_
  31.2 0.0 collective-permute-done.1.refs_1_
  31.2 0.0 collective-permute-done.refs_0_
  31.3 16.5 %analyse.1 = bf16[8,4,64,256]{3,2,1,0:T(8,128)(2,1)} custom-call(bf16[4,4,64,256]{3,2,1,0:T(8,128)(2,1)S(1)} %collective-permute-done.refs_0_, bf16[4,4,64,256]{3,2,1,0:T(8,128)(2,1)S(1)} %collective-permute-done.1.refs_1_, bf16[8,4,64,256]{3,2,1,0:T(8,128)(2,1)S(1)} %copy-done, f32[8,256,256]{2,1,0:T(8,128)S(1)} %own_gram.1.refs_3_, ...), custom_call_target="tpu_custom_call" | custom-call | tf_op jit(solution)/shard_map/analyse/pallas_call | solution.py:392
Async XLA Ops:
  0.0 4.1 %copy-start = (bf16[8,4,64,256]{3,2,1,0:T(8,128)(2,1)S(1)}, bf16[8,4,64,256]{3,2,1,0:T(8,128)(2,1)}, u32[]{:S(2)}) copy-start(bf16[8,4,64,256]{3,2,1,0:T(8,128)(2,1)} %refs_2_.1) | copy-start | bytes 3145732
  0.0 4.1 %copy-start.3 = (f32[256]{0:T(256)S(1)}, f32[256]{0:T(256)}, u32[]{:S(2)}) copy-start(f32[256]{0:T(256)} %param.7) | copy-start | bytes 3076
  0.0 4.1 %copy-start.2 = (f32[256]{0:T(256)S(1)}, f32[256]{0:T(256)}, u32[]{:S(2)}) copy-start(f32[256]{0:T(256)} %param.6) | copy-start | bytes 3076
  0.0 4.1 %copy-start.1 = (s32[256]{0:T(256)S(1)}, s32[256]{0:T(256)}, u32[]{:S(2)}) copy-start(s32[256]{0:T(256)} %param.5) | copy-start | bytes 3076
  1.4 29.9 %collective-permute-start.1 = (bf16[4,4,64,256]{3,2,1,0:T(8,128)(2,1)S(1)}, bf16[4,4,64,256]{3,2,1,0:T(8,128)(2,1)S(1)}, u32[]{:S(2)}, u32[]{:S(2)}) collective-permute-start(bf16[4,4,64,256]{3,2,1,0:T(8,128)(2,1)S(1)} %get-tuple-element.13), channel_id=1, source_target_pairs={{1,0},{2,1},{3,2},{4,3},{5,4},{6,5},{7,6},{8,7},{9,8},{10,9},{11,1... | collective-permute-start | bytes 1572872 | tf_op jit(solution)/shard_map/ppermute | solution.py:417
  1.5 29.8 %collective-permute-start = (bf16[4,4,64,256]{3,2,1,0:T(8,128)(2,1)S(1)}, bf16[4,4,64,256]{3,2,1,0:T(8,128)(2,1)S(1)}, u32[]{:S(2)}, u32[]{:S(2)}) collective-permute-start(bf16[4,4,64,256]{3,2,1,0:T(8,128)(2,1)S(1)} %get-tuple-element.14), channel_id=1, source_target_pairs={{0,1},{1,2},{2,3},{3,4},{4,5},{5,6},{6,7},{7,8},{8,9},{9,10},{10,1... | collective-permute-start | bytes 1572872 | tf_op jit(solution)/shard_map/ppermute | solution.py:416
  5.1 26.1 %collective-permute-start.2 = (f32[8,256]{1,0:T(8,128)S(1)}, f32[8,256]{1,0:T(8,128)S(1)}, u32[]{:S(2)}, u32[]{:S(2)}) collective-permute-start(f32[8,256]{1,0:T(8,128)S(1)} %get-tuple-element.10), channel_id=1, source_target_pairs={{0,1},{1,2},{2,3},{3,4},{4,5},{5,6},{6,7},{7,8},{8,9},{9,10},{10,1... | collective-permute-start | bytes 24584 | tf_op jit(solution)/shard_map/ppermute | solution.py:420
  5.5 25.7 %collective-permute-start.3 = (f32[8,256]{1,0:T(8,128)S(1)}, f32[8,256]{1,0:T(8,128)S(1)}, u32[]{:S(2)}, u32[]{:S(2)}) collective-permute-start(f32[8,256]{1,0:T(8,128)S(1)} %get-tuple-element.11), channel_id=1, source_target_pairs={{1,0},{2,1},{3,2},{4,3},{5,4},{6,5},{7,6},{8,7},{9,8},{10,9},{11,1... | collective-permute-start | bytes 24584 | tf_op jit(solution)/shard_map/ppermute | solution.py:421

commit v3 on v2

--- a/solution.py
+++ b/solution.py
@@ -28,7 +28,7 @@
     return jnp.where(inside, 1.0 - dist / (HALO + 1), 0.0)
 
 
-def obs_kernel(cells_ref, index_ref, value_ref, var_ref, own_ref, left_ref, right_ref, part_ref):
+def obs_kernel(odd_ref, cells_ref, index_ref, value_ref, var_ref, own_ref, near_ref, far_ref):
     lon_dev, _, lat, members = cells_ref.shape
     nobs = index_ref.shape[1]
     rows = cells_ref[:, 0].reshape(lon_dev * lat, members)
@@ -48,33 +48,48 @@
     centre = jnp.sum(seen, axis=1, keepdims=True) * (1.0 / members)
     spread = jnp.sum((seen - centre) ** 2, axis=1, keepdims=True) * (1.0 / (members - 1))
     innovation = (value - centre) ** 2 / (var + spread)
-    part_ref[...] = jnp.broadcast_to(jnp.sum(innovation, axis=0, keepdims=True), part_ref.shape)
+    blocks, members = own_ref.shape
+    part = jnp.broadcast_to(jnp.sum(innovation, axis=0, keepdims=True), (TILE, members))
+    near_ref[blocks:, :] = part
     terms = (value - seen) ** 2 * (1.0 / var)
     lon = (index // lat).astype(jnp.float32)
     along = index.astype(jnp.float32) - lon * lat
-    for ref, shift in ((own_ref, HALO), (left_ref, HALO + REGION), (right_ref, HALO - REGION)):
-        blocks = ref.shape[0]
-        block = lax.broadcasted_iota(jnp.int32, (blocks, nobs), 0).astype(jnp.float32)
-        weight = line_weight(lon + shift) * line_weight(along - REGION * block + HALO)
-        ref[...] = jnp.dot(weight, terms, precision=HIGH, preferred_element_type=jnp.float32)
-
-
-def observe(state, obs_index, obs_value, obs_var):
+    block = lax.broadcasted_iota(jnp.int32, (blocks, nobs), 0).astype(jnp.float32)
+    across = line_weight(along - REGION * block + HALO)
+    side = jnp.where(odd_ref[0] == 1, float(REGION), float(-REGION))
+    weights = [line_weight(lon + (HALO + shift)) * across for shift in (0.0, side, -side)]
+    like = jnp.dot(
+        jnp.concatenate(weights, axis=0), terms, precision=HIGH, preferred_element_type=jnp.float32
+    )
+    own_ref[...] = like[:blocks]
+    near_ref[:blocks, :] = like[blocks : 2 * blocks]
+    far_ref[...] = like[2 * blocks :]
+
+
+def observe(odd, state, obs_index, obs_value, obs_var):
     lon_dev, _, lat, members = state.shape
     nobs = obs_index.shape[0]
     blocks = lat // REGION
     row = pl.BlockSpec((1, nobs), lambda i: (0, 0))
     like = jax.ShapeDtypeStruct((blocks, members), jnp.float32)
     like_spec = pl.BlockSpec((blocks, members), lambda i: (0, 0))
+    more = jax.ShapeDtypeStruct((blocks + TILE, members), jnp.float32)
+    more_spec = pl.BlockSpec((blocks + TILE, members), lambda i: (0, 0))
     return pl.pallas_call(
         obs_kernel,
         grid=(1,),
-        in_specs=[pl.BlockSpec((lon_dev, 1, lat, members), lambda i: (0, 0, 0, 0)), row, row, row],
-        out_specs=[like_spec] * 3 + [pl.BlockSpec((8, 128), lambda i: (0, 0))],
-        out_shape=[like] * 3 + [jax.ShapeDtypeStruct((8, 128), jnp.float32)],
+        in_specs=[
+            pl.BlockSpec(memory_space=pltpu.SMEM),
+            pl.BlockSpec((lon_dev, 1, lat, members), lambda i: (0, 0, 0, 0)),
+            row,
+            row,
+            row,
+        ],
+        out_specs=[like_spec, more_spec, like_spec],
+        out_shape=[like, more, like],
         compiler_params=pltpu.CompilerParams(vmem_limit_bytes=32 * 2**20),
         name="observe",
-    )(state, obs_index[None], obs_value[None], obs_var[None])
+    )(odd, state, obs_index[None], obs_value[None], obs_var[None])
 
 
 def pair_tiles(ref, step, steps):
@@ -91,7 +106,12 @@
     return before, here[:, :, :TILE], here[:, :, TILE:], after
 
 
-def gram_of(tiles, places):
+def halo_weights(to_left):
+    steps = [jnp.float32(1.0) - jnp.float32(d) / jnp.float32(HALO + 1) for d in range(HALO, 0, -1)]
+    return [jnp.where(to_left, x, y) for x, y in zip(steps, steps[::-1])]
+
+
+def gram_of(tiles, weights):
     before, low, high, after = tiles
     columns, nvar, _, members = low.shape
     row = lax.broadcasted_iota(jnp.int32, (1, TILE, members), 1)
@@ -103,13 +123,11 @@
         margin = jnp.where(upper, following, preceding)
         win = jnp.concatenate([own, margin], axis=2)
         weighted = []
-        for column, place in enumerate(places):
-            dist = max(0, HALO - place, place - (HALO + REGION - 1))
-            if dist:
-                weight = jnp.float32(1.0) - jnp.float32(dist) / jnp.float32(HALO + 1)
+        for column, weight in enumerate(weights):
+            if weight is None:
+                parts = [own[column], margin[column] * edge]
+            else:
                 parts = [own[column] * weight, margin[column] * (edge * weight)]
-            else:
-                parts = [own[column], margin[column] * edge]
             weighted.append(jnp.concatenate(parts, axis=1))
         weighted = jnp.stack(weighted)
         shape = (columns * nvar * 2 * TILE, members)
@@ -124,26 +142,31 @@
     return grams
 
 
-def own_gram_kernel(state_ref, gram_ref):
+def own_gram_kernel(odd_ref, state_ref, near_ref, gram_ref):
     step, steps = pl.program_id(0), pl.num_programs(0)
-    places = range(HALO, HALO + state_ref.shape[0])
-    grams = gram_of(pair_tiles(state_ref, step, steps), places)
+    tiles = zip(pair_tiles(state_ref, step, steps), pair_tiles(near_ref, step, steps))
+    tiles = [jnp.concatenate([x, y], axis=0) for x, y in tiles]
+    grams = gram_of(tiles, [None] * state_ref.shape[0] + halo_weights(odd_ref[0] == 1))
     for region in range(PAIR):
         gram_ref[region] = grams[region]
 
 
-def own_gram(state):
+def own_gram(odd, state, near):
     lon_dev, nvar, lat, members = state.shape
     steps = lat // (PAIR * TILE)
     return pl.pallas_call(
         own_gram_kernel,
         grid=(steps,),
-        in_specs=[pl.BlockSpec(state.shape, lambda i: (0, 0, 0, 0))],
+        in_specs=[
+            pl.BlockSpec(memory_space=pltpu.SMEM),
+            pl.BlockSpec(state.shape, lambda i: (0, 0, 0, 0)),
+            pl.BlockSpec(near.shape, lambda i: (0, 0, 0, 0)),
+        ],
         out_specs=pl.BlockSpec((PAIR, members, members), lambda i: (i, 0, 0)),
         out_shape=jax.ShapeDtypeStruct((steps * PAIR, members, members), jnp.float32),
         compiler_params=pltpu.CompilerParams(vmem_limit_bytes=48 * 2**20),
         name="own_gram",
-    )(state)
+    )(odd, state, near)
 
 
 def halves(ref, region, rows):
@@ -299,16 +322,16 @@
 
 
 def analysis_kernel(count, scale, *refs):
-    left_ref, right_ref, state_ref, gram_in_ref = refs[0:4]
-    like_refs, total_ref, out_ref = refs[4:7], refs[7], refs[8]
+    odd_ref, halo_ref, state_ref, gram_in_ref = refs[0:4]
+    own_ref, near_ref, far_ref, sum_ref, out_ref = refs[4:9]
     gram_ref, kernel_ref, ratio_ref, weight_ref, logw_ref, result_ref, sems = refs[9:]
-    columns = left_ref.shape[0]
     regions, members = gram_in_ref.shape[0], gram_in_ref.shape[-1]
     pairs = regions // PAIR
     size = PAIR * TILE
 
-    total = jnp.sum(total_ref[...], axis=0, keepdims=True)[:, 0:1] * (1.0 / TILE)
-    like = -0.5 * (count / total) * (like_refs[0][...] + like_refs[1][...] + like_refs[2][...])
+    total = sum_ref[0:1, 0:1] + far_ref[regions : regions + 1, 0:1]
+    like = own_ref[...] + near_ref[:regions, :] + far_ref[:regions, :]
+    like = -0.5 * (count / total) * like
     like = like - jnp.max(like, axis=1, keepdims=True)
     logw = (like - jnp.log(jnp.sum(jnp.exp(like), axis=1, keepdims=True))) * LOG2E
     logw_ref[...] = logw
@@ -321,11 +344,7 @@
         return pltpu.make_async_copy(result_ref.at[pair], out_ref.at[:, :, at, :], sems.at[pair])
 
     def halo_grams(pair, carry):
-        left = pair_tiles(left_ref, pair, pairs)
-        right = pair_tiles(right_ref, pair, pairs)
-        both = [jnp.concatenate([x, y], axis=0) for x, y in zip(left, right)]
-        far = HALO + REGION
-        grams = gram_of(both, list(range(columns)) + list(range(far, far + columns)))
+        grams = gram_of(pair_tiles(halo_ref, pair, pairs), halo_weights(odd_ref[0] == 0))
         for at in range(PAIR):
             region = pair * PAIR + at
             gram_ref[region] = gram_in_ref[region] + grams[at]
@@ -382,7 +401,7 @@
         lax.fori_loop(0, pairs, again, 0)
 
 
-def analyse(state, left, right, gram, likes, total, count):
+def analyse(odd, halo, state, gram, own, near, far, total, count):
     lon_dev, nvar, lat, members = state.shape
     regions = lat // REGION
     offsets = range(REGION + 2 * HALO)
@@ -391,7 +410,7 @@
     vmem = pl.BlockSpec(memory_space=pltpu.VMEM)
     return pl.pallas_call(
         functools.partial(analysis_kernel, count, scale),
-        in_specs=[vmem] * 8,
+        in_specs=[pl.BlockSpec(memory_space=pltpu.SMEM)] + [vmem] * 7,
         out_specs=pl.BlockSpec(memory_space=pl.ANY),
         out_shape=jax.ShapeDtypeStruct(state.shape, state.dtype),
         scratch_shapes=[
@@ -405,23 +424,32 @@
         ],
         compiler_params=pltpu.CompilerParams(vmem_limit_bytes=48 * 2**20),
         name="analyse",
-    )(left, right, state, gram, *likes, total)
+    )(odd, halo, state, gram, own, near, far, total)
 
 
 def on_device(state, obs_index, obs_value, obs_var):
     lon_dev = state.shape[0]
     count = lax.axis_size("lon")
-    to_right = [(i, (i + 1) % count) for i in range(count)]
-    to_left = [((i + 1) % count, i) for i in range(count)]
-    left = lax.ppermute(state[lon_dev - HALO :], "lon", to_right)
-    right = lax.ppermute(state[:HALO], "lon", to_left)
-    own, for_left, for_right, part = observe(state, obs_index, obs_value, obs_var)
-    total = lax.all_gather(part, "lon", tiled=True)
-    from_left = lax.ppermute(for_right, "lon", to_right)
-    from_right = lax.ppermute(for_left, "lon", to_left)
-    gram = own_gram(state)
+    odd = lax.axis_index("lon") % 2
+    near_pairs = [(i, i ^ 1) for i in range(count)]
+    far_pairs = [(i, (i + 1 if i % 2 else i - 1) % count) for i in range(count)]
+    for_far = lax.dynamic_slice_in_dim(state, odd * (lon_dev - HALO), HALO, axis=0)
+    for_near = lax.dynamic_slice_in_dim(state, (1 - odd) * (lon_dev - HALO), HALO, axis=0)
+    far = lax.ppermute(for_far, "lon", far_pairs)
+    near = lax.ppermute(for_near, "lon", near_pairs)
+    odd = odd.astype(jnp.int32).reshape(1)
+    own_like, near_like, far_like = observe(odd, state, obs_index, obs_value, obs_var)
+    blocks = own_like.shape[0]
+    got_near = lax.ppermute(near_like, "lon", near_pairs)
+    total = near_like[blocks:] + got_near[blocks:]
+    hop = 4
+    while hop < count:
+        total = total + lax.ppermute(total, "lon", [(i, i ^ hop) for i in range(count)])
+        hop *= 2
+    got_far = lax.ppermute(jnp.concatenate([far_like, total], axis=0), "lon", far_pairs)
+    gram = own_gram(odd, state, near)
     nobs = float(obs_index.shape[0] * count)
-    return analyse(state, left, right, gram, (own, from_left, from_right), total, nobs)
+    return analyse(odd, far, state, gram, own_like, got_near, got_far, total, nobs)
 
 
 def solution(mesh):

time: 48 us -> 41.2 us (0.86)
  the two profiles are of different devices: /device:TPU:1 before, /device:TPU:0 now
where the time goes in v3:
time: 41.2 us; the launch traced here: 41.1 us
  Pallas kernels  18.5 us (45%)
  waiting for transfers between devices  13.1 us (32%)
  starting transfers between devices  7.95 us (19%)
  local copies, waits for them, and re-layouts  1.4 us (3%)
    pallas_call x1, Pallas kernels, analyse(): pl.pallas_call(functools.partial(analysis_kernel, count, scale), in_specs...  16 us
    ppermute x2, waiting for transfers between devices, on_device(): lax.ppermute(total, 'lon', [(i, i ^ hop) for i in range(count)])  8.15 us
    ppermute x1, starting transfers between devices, on_device(): far = lax.ppermute(for_far, 'lon', far_pairs)  5.67 us
    ppermute x1, waiting for transfers between devices, on_device(): lax.ppermute(jnp.concatenate([far_like, total], axis=0), 'lon', far_pairs)  3.82 us
    pallas_call x1, Pallas kernels, own_gram(): pl.pallas_call(own_gram_kernel, grid=(steps,), in_specs=[pl.BlockSpec(mem...  1.72 us
    ppermute x2, starting transfers between devices, on_device(): lax.ppermute(total, 'lon', [(i, i ^ hop) for i in range(count)])  1.4 us
    dynamic_slice x1, local copies, waits for them, and re-layouts, on_device(): lax.dynamic_slice_in_dim(state, (1 - odd) * (lon_dev - HALO), HALO, axis=0)  1.39 us
    ppermute x1, waiting for transfers between devices, on_device(): got_near = lax.ppermute(near_like, 'lon', near_pairs)  1.17 us
  transfers between devices with their start and end apart: 6, of which 4 were waited for; matrix products, arithmetic and copies ran while one was open for 0% of the time, Pallas kernels for 6%

profile of v3, /device:TPU:0, one launch (start us, length us, event | category | flops | bytes accessed | tf_op | source)
XLA Modules:
  0.0 41.1 jit_solution(17178758158137642115)
XLA Ops:
  0.0 0.0 copy-start
  0.0 0.0 copy-start.3
  0.0 0.0 copy-start.2
  0.0 0.0 copy-start.1
  0.0 1.4 %constant_dynamic-slice_fusion = (bf16[4,4,64,256]{3,2,1,0:T(8,128)(2,1)S(1)}, bf16[4,4,64,256]{3,2,1,0:T(8,128)(2,1)S(1)}) fusion(bf16[8,4,64,256]{3,2,1,0:T(8,128)(2,1)} %refs_2_.1, s32[]{:T(128)S(6)} %select_n.15, s32[]{:T(128)S(6)} %select_n.14), kind=kLoop, calls=%fused_computation.2 | loop fusion | bytes 2097160 | tf_op jit(solution)/shard_map/dynamic_slice | solution.py:437
  1.4 0.5 %collective-permute-start.1 = (bf16[4,4,64,256]{3,2,1,0:T(8,128)(2,1)S(1)}, bf16[4,4,64,256]{3,2,1,0:T(8,128)(2,1)S(1)}, u32[]{:S(2)}, u32[]{:S(2)}) collective-permute-start(bf16[4,4,64,256]{3,2,1,0:T(8,128)(2,1)S(1)} %get-tuple-element.11), channel_id=1, source_target_pairs={{0,1},{1,0},{2,3},{3,2},{4,5},{5,4},{6,7},{7,6},{8,9},{9,8},{10,11... | collective-permute-start | bytes 1572872 | tf_op jit(solution)/shard_map/ppermute | solution.py:439
  2.0 5.7 %collective-permute-start = (bf16[4,4,64,256]{3,2,1,0:T(8,128)(2,1)S(1)}, bf16[4,4,64,256]{3,2,1,0:T(8,128)(2,1)S(1)}, u32[]{:S(2)}, u32[]{:S(2)}) collective-permute-start(bf16[4,4,64,256]{3,2,1,0:T(8,128)(2,1)S(1)} %get-tuple-element.12), channel_id=1, source_target_pairs={{0,15},{1,2},{2,1},{3,4},{4,3},{5,6},{6,5},{7,8},{8,7},{9,10},{10,... | collective-permute-start | bytes 1572872 | tf_op jit(solution)/shard_map/ppermute | solution.py:438
  7.6 0.0 copy-done
  7.6 0.0 copy-done.3
  7.6 0.0 copy-done.2
  7.6 0.0 copy-done.1
  7.6 0.8 %observe.1 = (f32[8,256]{1,0:T(8,128)S(1)}, f32[16,256]{1,0:T(8,128)S(1)}, f32[8,256]{1,0:T(8,128)S(1)}) custom-call(s32[1]{0:T(128)} %bitcast.odd_ref.refs_0_, bf16[8,4,64,256]{3,2,1,0:T(8,128)(2,1)S(1)} %copy-done, s32[1,256]{1,0:T(1,128)S(1)} %bitcast.4, f32[1,256]{1,0:T(1,128)S(1)} %bitcast.5, f32[1,256]{1,0:T(1,128)S(1)} %bitcast.6), custom_call_target="tpu_custom_call" | custom-call | tf_op jit(solution)/shard_map/observe/pallas_call | solution.py:78
  8.4 0.0 collective-permute-start.2
  8.4 1.2 %collective-permute-done.2.refs_5_ = f32[16,256]{1,0:T(8,128)S(1)} collective-permute-done((f32[16,256]{1,0:T(8,128)S(1)}, f32[16,256]{1,0:T(8,128)S(1)}, u32[]{:S(2)}, u32[]{:S(2)}) %collective-permute-start.2) | collective-permute-done | bytes 16416 | tf_op jit(solution)/shard_map/ppermute | solution.py:443
  9.6 0.0 collective-permute-start.3
  9.6 5.0 %collective-permute-done.3 = f32[8,256]{1,0:T(8,128)S(1)} collective-permute-done((f32[8,256]{1,0:T(8,128)S(1)}, f32[8,256]{1,0:T(8,128)S(1)}, u32[]{:S(2)}, u32[]{:S(2)}) %collective-permute-start.3) | collective-permute-done | bytes 8224 | tf_op jit(solution)/shard_map/ppermute | solution.py:447
  14.6 1.4 %collective-permute-start.4 = (f32[8,256]{1,0:T(8,128)S(1)}, f32[8,256]{1,0:T(8,128)S(1)}, u32[]{:S(2)}, u32[]{:S(2)}) collective-permute-start(f32[8,256]{1,0:T(8,128)S(1)} %add.23), channel_id=1, source_target_pairs={{0,8},{1,9},{2,10},{3,11},{4,12},{5,13},{6,14},{7,15},{8,0},{9,1},... | collective-permute-start | bytes 24584 | tf_op jit(solution)/shard_map/ppermute | solution.py:447
  16.0 3.2 %collective-permute-done.4 = f32[8,256]{1,0:T(8,128)S(1)} collective-permute-done((f32[8,256]{1,0:T(8,128)S(1)}, f32[8,256]{1,0:T(8,128)S(1)}, u32[]{:S(2)}, u32[]{:S(2)}) %collective-permute-start.4) | collective-permute-done | bytes 8224 | tf_op jit(solution)/shard_map/ppermute | solution.py:447
  19.2 0.3 collective-permute-start.5
  19.5 0.0 collective-permute-done.1.near_ref
  19.5 1.7 %own_gram.1.refs_3_ = f32[8,256,256]{2,1,0:T(8,128)S(1)} custom-call(s32[1]{0:T(128)} %bitcast.odd_ref.refs_0_, bf16[8,4,64,256]{3,2,1,0:T(8,128)(2,1)S(1)} %copy-done, bf16[4,4,64,256]{3,2,1,0:T(8,128)(2,1)S(1)} %collective-permute-done.1.near_ref), custom_call_target="tpu_custom_call" | custom-call | tf_op jit(solution)/shard_map/own_gram/pallas_call | solution.py:157
  21.2 3.8 %collective-permute-done.5.refs_6_ = f32[16,256]{1,0:T(8,128)S(1)} collective-permute-done((f32[16,256]{1,0:T(8,128)S(1)}, f32[16,256]{1,0:T(8,128)S(1)}, u32[]{:S(2)}, u32[]{:S(2)}) %collective-permute-start.5) | collective-permute-done | bytes 16416 | tf_op jit(solution)/shard_map/ppermute | solution.py:449
  25.0 0.0 collective-permute-done.refs_1_
  25.0 16.0 %analyse.1 = bf16[8,4,64,256]{3,2,1,0:T(8,128)(2,1)} custom-call(s32[1]{0:T(128)} %bitcast.odd_ref.refs_0_, bf16[4,4,64,256]{3,2,1,0:T(8,128)(2,1)S(1)} %collective-permute-done.refs_1_, bf16[8,4,64,256]{3,2,1,0:T(8,128)(2,1)S(1)} %copy-done, f32[8,256,256]{2,1,0:T(8,128)S(1)} %own_gram.1.refs_3_, f32[8,256]{1,0:T(8,128)S(1)} %get-tuple-element.8.refs_4_, ...), custom_call_target="tpu_custom_call" | custom-call | tf_op jit(solution)/shard_map/analyse/pallas_call | solution.py:411
  (4 shorter events, 0.0 us)
Async XLA Ops:
  0.0 7.6 %copy-start = (bf16[8,4,64,256]{3,2,1,0:T(8,128)(2,1)S(1)}, bf16[8,4,64,256]{3,2,1,0:T(8,128)(2,1)}, u32[]{:S(2)}) copy-start(bf16[8,4,64,256]{3,2,1,0:T(8,128)(2,1)} %refs_2_.1) | copy-start | bytes 3145732
  0.0 7.6 %copy-start.3 = (f32[256]{0:T(256)S(1)}, f32[256]{0:T(256)}, u32[]{:S(2)}) copy-start(f32[256]{0:T(256)} %param.7) | copy-start | bytes 3076
  0.0 7.6 %copy-start.2 = (f32[256]{0:T(256)S(1)}, f32[256]{0:T(256)}, u32[]{:S(2)}) copy-start(f32[256]{0:T(256)} %param.6) | copy-start | bytes 3076
  0.0 7.6 %copy-start.1 = (s32[256]{0:T(256)S(1)}, s32[256]{0:T(256)}, u32[]{:S(2)}) copy-start(s32[256]{0:T(256)} %param.5) | copy-start | bytes 3076
  1.4 18.1 %collective-permute-start.1 = (bf16[4,4,64,256]{3,2,1,0:T(8,128)(2,1)S(1)}, bf16[4,4,64,256]{3,2,1,0:T(8,128)(2,1)S(1)}, u32[]{:S(2)}, u32[]{:S(2)}) collective-permute-start(bf16[4,4,64,256]{3,2,1,0:T(8,128)(2,1)S(1)} %get-tuple-element.11), channel_id=1, source_target_pairs={{0,1},{1,0},{2,3},{3,2},{4,5},{5,4},{6,7},{7,6},{8,9},{9,8},{10,11... | collective-permute-start | bytes 1572872 | tf_op jit(solution)/shard_map/ppermute | solution.py:439
  2.0 23.1 %collective-permute-start = (bf16[4,4,64,256]{3,2,1,0:T(8,128)(2,1)S(1)}, bf16[4,4,64,256]{3,2,1,0:T(8,128)(2,1)S(1)}, u32[]{:S(2)}, u32[]{:S(2)}) collective-permute-start(bf16[4,4,64,256]{3,2,1,0:T(8,128)(2,1)S(1)} %get-tuple-element.12), channel_id=1, source_target_pairs={{0,15},{1,2},{2,1},{3,4},{4,3},{5,6},{6,5},{7,8},{8,7},{9,10},{10,... | collective-permute-start | bytes 1572872 | tf_op jit(solution)/shard_map/ppermute | solution.py:438
  8.4 1.2 %collective-permute-start.2 = (f32[16,256]{1,0:T(8,128)S(1)}, f32[16,256]{1,0:T(8,128)S(1)}, u32[]{:S(2)}, u32[]{:S(2)}) collective-permute-start(f32[16,256]{1,0:T(8,128)S(1)} %get-tuple-element.9), channel_id=1, source_target_pairs={{0,1},{1,0},{2,3},{3,2},{4,5},{5,4},{6,7},{7,6},{8,9},{9,8},{10,11... | collective-permute-start | bytes 49160 | tf_op jit(solution)/shard_map/ppermute | solution.py:443
  9.6 5.0 %collective-permute-start.3 = (f32[8,256]{1,0:T(8,128)S(1)}, f32[8,256]{1,0:T(8,128)S(1)}, u32[]{:S(2)}, u32[]{:S(2)}) collective-permute-start(f32[8,256]{1,0:T(8,128)S(1)} %slice_add_fusion), channel_id=1, source_target_pairs={{0,4},{1,5},{2,6},{3,7},{4,0},{5,1},{6,2},{7,3},{8,12},{9,13},{10,... | collective-permute-start | bytes 24584 | tf_op jit(solution)/shard_map/ppermute | solution.py:447
  14.6 4.5 %collective-permute-start.4 = (f32[8,256]{1,0:T(8,128)S(1)}, f32[8,256]{1,0:T(8,128)S(1)}, u32[]{:S(2)}, u32[]{:S(2)}) collective-permute-start(f32[8,256]{1,0:T(8,128)S(1)} %add.23), channel_id=1, source_target_pairs={{0,8},{1,9},{2,10},{3,11},{4,12},{5,13},{6,14},{7,15},{8,0},{9,1},... | collective-permute-start | bytes 24584 | tf_op jit(solution)/shard_map/ppermute | solution.py:447
  19.2 5.9 %collective-permute-start.5 = (f32[16,256]{1,0:T(8,128)S(1)}, f32[16,256]{1,0:T(8,128)S(1)}, u32[]{:S(2)}, u32[]{:S(2)}) collective-permute-start(f32[16,256]{1,0:T(8,128)S(1)} %pad_maximum_fusion), channel_id=1, source_target_pairs={{0,15},{1,2},{2,1},{3,4},{4,3},{5,6},{6,5},{7,8},{8,7},{9,10},{10,... | collective-permute-start | bytes 49160 | tf_op jit(solution)/shard_map/ppermute | solution.py:449

commit v4 on v3

--- a/solution.py
+++ b/solution.py
@@ -28,10 +28,22 @@
     return jnp.where(inside, 1.0 - dist / (HALO + 1), 0.0)
 
 
-def obs_kernel(odd_ref, cells_ref, index_ref, value_ref, var_ref, own_ref, near_ref, far_ref):
-    lon_dev, _, lat, members = cells_ref.shape
+def observe_kernel(*refs):
+    odd_ref, state_ref, index_ref, value_ref, var_ref = refs[:5]
+    own_ref, near_ref, far_ref, near_edge_ref, far_edge_ref, cells_ref, sems = refs[5:]
+    lon_dev, lat, members = cells_ref.shape
     nobs = index_ref.shape[1]
-    rows = cells_ref[:, 0].reshape(lon_dev * lat, members)
+    last = lon_dev - HALO
+    far_at = odd_ref[0] * last
+    copies = [
+        pltpu.make_async_copy(state_ref.at[:, 0], cells_ref, sems.at[0]),
+        pltpu.make_async_copy(state_ref.at[pl.ds(far_at, HALO)], far_edge_ref, sems.at[1]),
+        pltpu.make_async_copy(state_ref.at[pl.ds(last - far_at, HALO)], near_edge_ref, sems.at[2]),
+    ]
+    for copy in copies:
+        copy.start()
+    copies[0].wait()
+    rows = cells_ref[...].reshape(lon_dev * lat, members)
     index = index_ref[...]
     sub = lax.broadcasted_iota(jnp.int32, (TILE, nobs), 0)
     table = jnp.where(
@@ -64,30 +76,33 @@
     own_ref[...] = like[:blocks]
     near_ref[:blocks, :] = like[blocks : 2 * blocks]
     far_ref[...] = like[2 * blocks :]
+    for copy in copies[1:]:
+        copy.wait()
 
 
 def observe(odd, state, obs_index, obs_value, obs_var):
-    lon_dev, _, lat, members = state.shape
-    nobs = obs_index.shape[0]
+    lon_dev, nvar, lat, members = state.shape
     blocks = lat // REGION
-    row = pl.BlockSpec((1, nobs), lambda i: (0, 0))
     like = jax.ShapeDtypeStruct((blocks, members), jnp.float32)
-    like_spec = pl.BlockSpec((blocks, members), lambda i: (0, 0))
     more = jax.ShapeDtypeStruct((blocks + TILE, members), jnp.float32)
-    more_spec = pl.BlockSpec((blocks + TILE, members), lambda i: (0, 0))
+    edge = jax.ShapeDtypeStruct((HALO, nvar, lat, members), state.dtype)
+    vmem = pl.BlockSpec(memory_space=pltpu.VMEM)
     return pl.pallas_call(
-        obs_kernel,
-        grid=(1,),
+        observe_kernel,
         in_specs=[
             pl.BlockSpec(memory_space=pltpu.SMEM),
-            pl.BlockSpec((lon_dev, 1, lat, members), lambda i: (0, 0, 0, 0)),
-            row,
-            row,
-            row,
-        ],
-        out_specs=[like_spec, more_spec, like_spec],
-        out_shape=[like, more, like],
-        compiler_params=pltpu.CompilerParams(vmem_limit_bytes=32 * 2**20),
+            pl.BlockSpec(memory_space=pltpu.HBM),
+            vmem,
+            vmem,
+            vmem,
+        ],
+        out_specs=[vmem] * 5,
+        out_shape=[like, more, like, edge, edge],
+        scratch_shapes=[
+            pltpu.VMEM((lon_dev, lat, members), state.dtype),
+            pltpu.SemaphoreType.DMA((3,)),
+        ],
+        compiler_params=pltpu.CompilerParams(vmem_limit_bytes=24 * 2**20),
         name="observe",
     )(odd, state, obs_index[None], obs_value[None], obs_var[None])
 
@@ -164,7 +179,12 @@
         ],
         out_specs=pl.BlockSpec((PAIR, members, members), lambda i: (i, 0, 0)),
         out_shape=jax.ShapeDtypeStruct((steps * PAIR, members, members), jnp.float32),
-        compiler_params=pltpu.CompilerParams(vmem_limit_bytes=48 * 2**20),
+        compiler_params=pltpu.CompilerParams(vmem_limit_bytes=24 * 2**20),
+        cost_estimate=pl.CostEstimate(
+            flops=2 * (lon_dev + HALO) * nvar * 2 * lat * members**2,
+            bytes_accessed=2 * (state.size + near.size) + 4 * lat // REGION * members**2,
+            transcendentals=0,
+        ),
         name="own_gram",
     )(odd, state, near)
 
@@ -190,15 +210,53 @@
     return [jnp.sum(x, axis=0, keepdims=True) for x in across], down
 
 
-def sweep_rows(parts, weight, totals):
-    scaled, mass = parts
-    mass = jnp.broadcast_to(jnp.sum(mass, axis=1, keepdims=True), weight.shape)
-    near = pl.reciprocal(mass, approx=True)
-    ratio = weight * (near * (2.0 - mass * near))
-    for lane, part in enumerate(scaled):
-        part = jnp.sum((part * ratio).reshape(ROWS // TILE, TILE, 128), axis=0)
-        totals[lane] = part if totals[lane] is None else totals[lane] + part
-    return mass, ratio
+def prepare_kernel(scale, odd_ref, halo_ref, gram_in_ref, gram_ref, kernel_ref, most_ref):
+    step, steps = pl.program_id(0), pl.num_programs(0)
+    members = gram_ref.shape[-1]
+    grams = gram_of(pair_tiles(halo_ref, step, steps), halo_weights(odd_ref[0] == 0))
+    most = None
+    for region in range(PAIR):
+        gram_ref[region] = gram_in_ref[region] + grams[region]
+    for region in range(PAIR):
+        across, down = diagonal(gram_ref, region)
+        across = [0.5 * LIFT - x * scale for x in across]
+        for at, start in enumerate(range(0, members, ROWS)):
+            rows = pl.ds(start, ROWS)
+            base = 0.5 * LIFT - down[at] * scale
+            for lane, (gram, x) in enumerate(zip(halves(gram_ref, region, rows), across)):
+                part = jnp.exp2(gram * (2.0 * scale) + base + x)
+                kernel_ref[region, rows, lane * 128 : lane * 128 + 128] = part
+                most = part if most is None else jnp.maximum(most, part)
+    most_ref[0] = jnp.max(most.reshape(ROWS // TILE, TILE, 128), axis=0)
+
+
+def prepare(odd, halo, gram, scale):
+    regions, members, _ = gram.shape
+    steps = regions // PAIR
+    matrices = pl.BlockSpec((PAIR, members, members), lambda i: (i, 0, 0))
+    return pl.pallas_call(
+        functools.partial(prepare_kernel, scale),
+        grid=(steps,),
+        in_specs=[
+            pl.BlockSpec(memory_space=pltpu.SMEM),
+            pl.BlockSpec(halo.shape, lambda i: (0, 0, 0, 0)),
+            matrices,
+        ],
+        out_specs=[matrices, matrices, pl.BlockSpec((1, TILE, 128), lambda i: (i, 0, 0))],
+        out_shape=[
+            jax.ShapeDtypeStruct(gram.shape, jnp.float32),
+            jax.ShapeDtypeStruct(gram.shape, jnp.float32),
+            jax.ShapeDtypeStruct((steps, TILE, 128), jnp.float32),
+        ],
+        input_output_aliases={2: 0},
+        compiler_params=pltpu.CompilerParams(vmem_limit_bytes=24 * 2**20),
+        cost_estimate=pl.CostEstimate(
+            flops=2 * halo.size * 2 * members + 10 * gram.size,
+            bytes_accessed=2 * halo.size + 12 * gram.size,
+            transcendentals=gram.size,
+        ),
+        name="prepare",
+    )(odd, halo, gram)
 
 
 def fold(values, op):
@@ -208,71 +266,42 @@
     return out
 
 
-def sweeps_scaled(regions, gram_ref, kernel_ref, ratio_ref, weight_ref, scale):
-    members = gram_ref.shape[-1]
+def sweeps_scaled(regions, kernel_ref, ratio_ref, weight_ref):
+    members = kernel_ref.shape[-1]
     starts = range(0, members, ROWS)
     lanes = range(members // 128)
-    least_row, most_row, least_col, cols = [], [], [], []
     share = 2.0**MASS / members
 
-    def settle(totals):
-        totals = [jnp.sum(x, axis=0, keepdims=True) for x in totals]
-        return totals, fold(totals, jnp.minimum)
-
-    for region in regions:
-        across, down = diagonal(gram_ref, region)
-        across = [0.5 * LIFT - x * scale for x in across]
-        totals = [None] * len(lanes)
-        masses = []
-        for at, start in enumerate(starts):
-            rows = pl.ds(start, ROWS)
-            base = 0.5 * LIFT - down[at] * scale
-            kernel = [
-                jnp.exp2(g * (2.0 * scale) + base + x)
-                for g, x in zip(halves(gram_ref, region, rows), across)
-            ]
-            for lane, part in enumerate(kernel):
-                kernel_ref[region, rows, lane * 128 : lane * 128 + 128] = part
-            mass, _ = sweep_rows(
-                (kernel, fold(kernel, jnp.add) * 2.0**START), weight_ref[region, rows, :], totals
-            )
-            masses.append(mass)
-        least_row.append(fold(masses, jnp.minimum))
-        most_row.append(fold(masses, jnp.maximum))
-        totals, least = settle(totals)
-        least_col.append(least)
-        cols.append(totals)
-
     def sweep(last, carry):
-        least_row, least_col, cols = carry
-        rows_out, least_out, cols_out = [], [], []
-        for region, lrow, lcol, col in zip(regions, least_row, least_col, cols):
-            factor = [share / x for x in col]
-            totals = [None] * len(lanes)
+        least_row, least_col, factors = carry
+        rows_out, least_out, factors_out = [], [], []
+        for region, lrow, lcol, factor in zip(regions, least_row, least_col, factors):
+            totals = [None for _ in lanes]
             for start in starts:
                 rows = pl.ds(start, ROWS)
                 kernel = halves(kernel_ref, region, rows)
                 mass = fold([k * f for k, f in zip(kernel, factor)], jnp.add)
-                mass, ratio = sweep_rows((kernel, mass), weight_ref[region, rows, :], totals)
+                mass = jnp.broadcast_to(jnp.sum(mass, axis=1, keepdims=True), (ROWS, 128))
+                near = pl.reciprocal(mass, approx=True)
+                ratio = weight_ref[region, rows, :] * (near * (2.0 - mass * near))
+                for lane, part in enumerate(kernel):
+                    part = jnp.sum((part * ratio).reshape(ROWS // TILE, TILE, 128), axis=0)
+                    totals[lane] = part if totals[lane] is None else totals[lane] + part
                 if last:
                     ratio_ref[region, rows, :] = ratio
                 lrow = jnp.minimum(lrow, mass)
-            totals, least = settle(totals)
+            totals = [jnp.sum(x, axis=0, keepdims=True) for x in totals]
             rows_out.append(lrow)
-            least_out.append(jnp.minimum(lcol, least))
-            cols_out.append(totals)
-        return rows_out, least_out, cols_out
-
-    carry = least_row, least_col, cols
-    carry = lax.fori_loop(0, SWEEPS - 2, lambda i, c: sweep(False, c), carry)
-    least_row, least_col, cols = sweep(True, carry)
-    factors = [[1.0 / x for x in col] for col in cols]
-    return (
-        factors,
-        fold(least_row, jnp.minimum),
-        fold(least_col, jnp.minimum),
-        fold(most_row, jnp.maximum),
-    )
+            least_out.append(jnp.minimum(lcol, fold(totals, jnp.minimum)))
+            factors_out.append([(1.0 if last else share) / x for x in totals])
+        return rows_out, least_out, factors_out
+
+    high = jnp.full((ROWS, 128), 1e30, jnp.float32)
+    first = jnp.full((1, 128), 2.0**START, jnp.float32)
+    carry = [high for _ in regions], [high[:1] for _ in regions], [[first] * len(lanes) for _ in regions]
+    carry = lax.fori_loop(0, SWEEPS - 1, lambda i, c: sweep(False, c), carry)
+    least_row, least_col, factors = sweep(True, carry)
+    return factors, fold(least_row, jnp.minimum), fold(least_col, jnp.minimum)
 
 
 def transport_scaled(region, factor, kernel_ref, ratio_ref):
@@ -321,17 +350,16 @@
     return jnp.concatenate(parts, axis=2).astype(jnp.bfloat16)
 
 
-def analysis_kernel(count, scale, *refs):
-    odd_ref, halo_ref, state_ref, gram_in_ref = refs[0:4]
-    own_ref, near_ref, far_ref, sum_ref, out_ref = refs[4:9]
-    gram_ref, kernel_ref, ratio_ref, weight_ref, logw_ref, result_ref, sems = refs[9:]
-    regions, members = gram_in_ref.shape[0], gram_in_ref.shape[-1]
+def finish_kernel(count, scale, *refs):
+    state_ref, gram_ref, kernel_ref, most_ref = refs[0:4]
+    own_ref, near_ref, far_ref, total_ref, handed_ref, out_ref = refs[4:10]
+    ratio_ref, weight_ref, logw_ref, result_ref, sems = refs[10:]
+    regions, members = gram_ref.shape[0], gram_ref.shape[-1]
     pairs = regions // PAIR
     size = PAIR * TILE
 
-    total = sum_ref[0:1, 0:1] + far_ref[regions : regions + 1, 0:1]
     like = own_ref[...] + near_ref[:regions, :] + far_ref[:regions, :]
-    like = -0.5 * (count / total) * like
+    like = -0.5 * (count / (total_ref[0:1, 0:1] + handed_ref[0:1, 0:1])) * like
     like = like - jnp.max(like, axis=1, keepdims=True)
     logw = (like - jnp.log(jnp.sum(jnp.exp(like), axis=1, keepdims=True))) * LOG2E
     logw_ref[...] = logw
@@ -343,20 +371,10 @@
         at = pl.ds(pl.multiple_of(pair * size, size), size)
         return pltpu.make_async_copy(result_ref.at[pair], out_ref.at[:, :, at, :], sems.at[pair])
 
-    def halo_grams(pair, carry):
-        grams = gram_of(pair_tiles(halo_ref, pair, pairs), halo_weights(odd_ref[0] == 0))
-        for at in range(PAIR):
-            region = pair * PAIR + at
-            gram_ref[region] = gram_in_ref[region] + grams[at]
-        return carry
-
-    lax.fori_loop(0, pairs, halo_grams, 0)
-
     def group(at, carry):
-        least_row, least_col, most_row = carry
         first = at * GROUP
-        factors, row, col, most = sweeps_scaled(
-            [first + r for r in range(GROUP)], gram_ref, kernel_ref, ratio_ref, weight_ref, scale
+        factors, row, col = sweeps_scaled(
+            [first + r for r in range(GROUP)], kernel_ref, ratio_ref, weight_ref
         )
         for pair in range(GROUP // PAIR):
             moves = [
@@ -366,24 +384,18 @@
             where = at * (GROUP // PAIR) + pair
             result_ref[where] = transform(state_ref, where, moves)
             send(where).start()
-        return (
-            jnp.minimum(least_row, row),
-            jnp.minimum(least_col, col),
-            jnp.maximum(most_row, most),
-        )
+        return jnp.minimum(carry[0], row), jnp.minimum(carry[1], col)
 
     high = jnp.full((ROWS, 128), 1e30, jnp.float32)
-    least_row, least_col, most_row = lax.fori_loop(
-        0, regions // GROUP, group, (high, high[:1], jnp.zeros((ROWS, 128), jnp.float32))
-    )
+    least_row, least_col = lax.fori_loop(0, regions // GROUP, group, (high, high[:1]))
 
     def drain(pair, carry):
         send(pair).wait()
         return carry
 
     lax.fori_loop(0, pairs, drain, 0)
-    row, col, most = jnp.min(least_row), jnp.min(least_col), jnp.max(most_row)
-    sound = (row >= 2.0**-24) & (col >= 2.0**-30) & (most <= 2.0**20) & (row * col >= 2.0**-34)
+    row, col, most = jnp.min(least_row), jnp.min(least_col), jnp.max(most_ref[...])
+    sound = (row >= 2.0**-24) & (col >= 2.0**-30) & (most <= 2.0**30) & (row * col >= 2.0**-34)
 
     @pl.when(jnp.logical_not(sound))
     def _():
@@ -401,55 +413,67 @@
         lax.fori_loop(0, pairs, again, 0)
 
 
-def analyse(odd, halo, state, gram, own, near, far, total, count):
+def finish(state, gram, kernel, most, own, near, far, total, handed, count, scale):
     lon_dev, nvar, lat, members = state.shape
     regions = lat // REGION
-    offsets = range(REGION + 2 * HALO)
-    line = [1.0 - max(0, HALO - p, p - (HALO + REGION - 1)) / (HALO + 1) for p in offsets]
-    scale = LOG2E / EPS / (nvar * sum(line) ** 2)
     vmem = pl.BlockSpec(memory_space=pltpu.VMEM)
     return pl.pallas_call(
-        functools.partial(analysis_kernel, count, scale),
-        in_specs=[pl.BlockSpec(memory_space=pltpu.SMEM)] + [vmem] * 7,
+        functools.partial(finish_kernel, count, scale),
+        in_specs=[vmem] * 9,
         out_specs=pl.BlockSpec(memory_space=pl.ANY),
         out_shape=jax.ShapeDtypeStruct(state.shape, state.dtype),
         scratch_shapes=[
-            pltpu.VMEM((regions, members, members), jnp.float32),
-            pltpu.VMEM((regions, members, members), jnp.float32),
             pltpu.VMEM((regions, members, 128), jnp.float32),
             pltpu.VMEM((regions, members, 128), jnp.float32),
             pltpu.VMEM((regions, members), jnp.float32),
             pltpu.VMEM((regions // PAIR, lon_dev, nvar, PAIR * TILE, members), jnp.bfloat16),
             pltpu.SemaphoreType.DMA((regions // PAIR,)),
         ],
-        compiler_params=pltpu.CompilerParams(vmem_limit_bytes=48 * 2**20),
-        name="analyse",
-    )(odd, halo, state, gram, own, near, far, total)
+        compiler_params=pltpu.CompilerParams(vmem_limit_bytes=24 * 2**20),
+        name="finish",
+    )(state, gram, kernel, most, own, near, far, total, handed)
 
 
 def on_device(state, obs_index, obs_value, obs_var):
-    lon_dev = state.shape[0]
+    nvar = state.shape[1]
     count = lax.axis_size("lon")
-    odd = lax.axis_index("lon") % 2
+    place = lax.axis_index("lon")
+    odd = place & 1
     near_pairs = [(i, i ^ 1) for i in range(count)]
     far_pairs = [(i, (i + 1 if i % 2 else i - 1) % count) for i in range(count)]
-    for_far = lax.dynamic_slice_in_dim(state, odd * (lon_dev - HALO), HALO, axis=0)
-    for_near = lax.dynamic_slice_in_dim(state, (1 - odd) * (lon_dev - HALO), HALO, axis=0)
+    odd = odd.astype(jnp.int32).reshape(1)
+    own_like, near_like, far_like, for_near, for_far = observe(
+        odd, state, obs_index, obs_value, obs_var
+    )
     far = lax.ppermute(for_far, "lon", far_pairs)
     near = lax.ppermute(for_near, "lon", near_pairs)
-    odd = odd.astype(jnp.int32).reshape(1)
-    own_like, near_like, far_like = observe(odd, state, obs_index, obs_value, obs_var)
     blocks = own_like.shape[0]
     got_near = lax.ppermute(near_like, "lon", near_pairs)
-    total = near_like[blocks:] + got_near[blocks:]
-    hop = 4
-    while hop < count:
-        total = total + lax.ppermute(total, "lon", [(i, i ^ hop) for i in range(count)])
-        hop *= 2
-    got_far = lax.ppermute(jnp.concatenate([far_like, total], axis=0), "lon", far_pairs)
     gram = own_gram(odd, state, near)
+    if count % 4 == 0 and count & (count - 1) == 0:
+        leads = [i for i in range(count) if (i ^ i >> 1) & 1]
+        total = near_like[blocks:] + got_near[blocks:]
+        hop = 4
+        while hop < count:
+            total = total + lax.ppermute(total, "lon", [(i, i ^ hop) for i in leads])
+            hop *= 2
+        total, gram = lax.optimization_barrier((total, gram))
+        got_far = lax.ppermute(jnp.concatenate([far_like, total], axis=0), "lon", far_pairs)
+        lead = (place ^ place >> 1) & 1
+        total = jnp.where(lead == 1, total + got_far[blocks:], 0.0)
+        handed = lax.ppermute(total, "lon", [(i, i ^ 1) for i in leads])
+    else:
+        got_far = lax.ppermute(far_like, "lon", far_pairs)
+        total = lax.psum(near_like[blocks:], "lon")
+        handed = jnp.zeros_like(total)
+    offsets = range(REGION + 2 * HALO)
+    line = [1.0 - max(0, HALO - p, p - (HALO + REGION - 1)) / (HALO + 1) for p in offsets]
+    scale = LOG2E / EPS / (nvar * sum(line) ** 2)
+    gram, kernel, most = prepare(odd, far, gram, scale)
     nobs = float(obs_index.shape[0] * count)
-    return analyse(odd, far, state, gram, own_like, got_near, got_far, total, nobs)
+    return finish(
+        state, gram, kernel, most, own_like, got_near, got_far, total, handed, nobs, scale
+    )
 
 
 def solution(mesh):

time: 41.2 us -> 45.2 us (1.097)
  the two profiles are of different devices: /device:TPU:0 before, /device:TPU:1 now
where the time goes in v4:
time: 45.2 us; the launch traced here: 44.9 us
  Pallas kernels  21.3 us (47%)
  starting transfers between devices  15.9 us (35%)
  waiting for transfers between devices  4.23 us (9%)
  local copies, waits for them, and re-layouts  3.27 us (7%)
    pallas_call x1, Pallas kernels, finish(): pl.pallas_call(functools.partial(finish_kernel, count, scale), in_specs=[...  14.9 us
    ppermute x2, starting transfers between devices, on_device(): total = total + lax.ppermute(total, 'lon', [(i, i ^ hop) for i in leads])  7.4 us
    ppermute x1, starting transfers between devices, on_device(): lax.ppermute(jnp.concatenate([far_like, total], axis=0), 'lon', far_pairs)  4.04 us
    unnamed x10, local copies, waits for them, and re-layouts  3.27 us
    pallas_call x1, Pallas kernels, prepare(): pl.pallas_call(functools.partial(prepare_kernel, scale), grid=(steps,), i...  3.04 us
    ppermute x2, waiting for transfers between devices, on_device(): total = total + lax.ppermute(total, 'lon', [(i, i ^ hop) for i in leads])  2.8 us
    ppermute x1, starting transfers between devices, on_device(): far = lax.ppermute(for_far, 'lon', far_pairs)  2.63 us
    pallas_call x1, Pallas kernels, own_gram(): pl.pallas_call(own_gram_kernel, grid=(steps,), in_specs=[pl.BlockSpec(mem...  1.71 us
  transfers between devices with their start and end apart: 7, of which 3 were waited for; matrix products, arithmetic and copies ran while one was open for 0% of the time, Pallas kernels for 11%

profile of v4, /device:TPU:1, one launch (start us, length us, event | category | flops | bytes accessed | tf_op | source)
XLA Modules:
  0.0 44.9 jit_solution(639813085206818889)
XLA Ops:
  0.0 0.0 copy-start
  0.0 1.2 %copy-done = bf16[8,4,64,256]{3,2,1,0:T(8,128)(2,1)S(1)} copy-done((bf16[8,4,64,256]{3,2,1,0:T(8,128)(2,1)S(1)}, bf16[8,4,64,256]{3,2,1,0:T(8,128)(2,1)}, u32[]{:S(2)}) %copy-start) | copy-done | bytes 1048600
  1.2 0.0 copy-start.2
  1.2 0.7 %copy-done.2 = s32[256]{0:T(256)S(1)} copy-done((s32[256]{0:T(256)S(1)}, s32[256]{0:T(256)}, u32[]{:S(2)}) %copy-start.2) | copy-done | bytes 1048
  1.9 0.0 copy-start.3
  1.9 0.7 %copy-done.3 = f32[256]{0:T(256)S(1)} copy-done((f32[256]{0:T(256)S(1)}, f32[256]{0:T(256)}, u32[]{:S(2)}) %copy-start.3) | copy-done | bytes 1048
  2.6 0.0 copy-start.4
  2.6 0.7 %copy-done.4 = f32[256]{0:T(256)S(1)} copy-done((f32[256]{0:T(256)S(1)}, f32[256]{0:T(256)}, u32[]{:S(2)}) %copy-start.4) | copy-done | bytes 1048
  3.3 1.7 %observe.1 = (f32[8,256]{1,0:T(8,128)S(1)}, f32[16,256]{1,0:T(8,128)S(1)}, f32[8,256]{1,0:T(8,128)S(1)}, bf16[4,4,64,256]{3,2,1,0:T(8,128)(2,1)S(1)}, bf16[4,4,64,256]{3,2,1,0:T(8,128)(2,1)}) custom-call(s32[1]{0:T(128)} %bitcast.refs_0_.odd_ref, bf16[8,4,64,256]{3,2,1,0:T(8,128)(2,1)S(1)} %copy-done, s32[1,256]{1,0:T(1,128)S(1)} %bitcast.4, ...), custom_call_target="tpu_custom_call" | custom-call | tf_op jit(solution)/shard_map/observe/pallas_call | solution.py:90
  5.0 0.1 collective-permute-start.4
  5.1 0.5 %collective-permute-start.1 = (f32[16,256]{1,0:T(8,128)S(1)}, f32[16,256]{1,0:T(8,128)S(1)}, u32[]{:S(2)}, u32[]{:S(2)}) collective-permute-start(f32[16,256]{1,0:T(8,128)S(1)} %get-tuple-element.16), channel_id=1, source_target_pairs={{0,1},{1,0},{2,3},{3,2},{4,5},{5,4},{6,7},{7,6},{8,9},{9,8},{10,11... | collective-permute-start | bytes 49160 | tf_op jit(solution)/shard_map/ppermute | solution.py:451
  5.5 2.6 %collective-permute-start = (bf16[4,4,64,256]{3,2,1,0:T(8,128)(2,1)}, bf16[4,4,64,256]{3,2,1,0:T(8,128)(2,1)}, u32[]{:S(2)}, u32[]{:S(2)}) collective-permute-start(bf16[4,4,64,256]{3,2,1,0:T(8,128)(2,1)} %get-tuple-element.15), channel_id=1, source_target_pairs={{0,15},{1,2},{2,1},{3,4},{4,3},{5,6},{6,5},{7,8},{8,7},{9,10},{10,... | collective-permute-start | bytes 1572872 | tf_op jit(solution)/shard_map/ppermute | solution.py:448
  8.2 0.0 collective-permute-done.1.refs_5_
  8.2 3.2 %collective-permute-start.2 = (f32[8,256]{1,0:T(8,128)S(1)}, f32[8,256]{1,0:T(8,128)S(1)}, u32[]{:S(2)}, u32[]{:S(2)}) collective-permute-start(f32[8,256]{1,0:T(8,128)S(1)} %slice_add_fusion.1), channel_id=1, source_target_pairs={{1,5},{2,6},{5,1},{6,2},{9,13},{10,14},{13,9},{14,10},{17,21},{18,... | collective-permute-start | bytes 24584 | tf_op jit(solution)/shard_map/ppermute | solution.py:458
  11.4 1.7 %collective-permute-done.2 = f32[8,256]{1,0:T(8,128)S(1)} collective-permute-done((f32[8,256]{1,0:T(8,128)S(1)}, f32[8,256]{1,0:T(8,128)S(1)}, u32[]{:S(2)}, u32[]{:S(2)}) %collective-permute-start.2) | collective-permute-done | bytes 8224 | tf_op jit(solution)/shard_map/ppermute | solution.py:458
  13.1 4.2 %collective-permute-start.3 = (f32[8,256]{1,0:T(8,128)S(1)}, f32[8,256]{1,0:T(8,128)S(1)}, u32[]{:S(2)}, u32[]{:S(2)}) collective-permute-start(f32[8,256]{1,0:T(8,128)S(1)} %add.13), channel_id=1, source_target_pairs={{1,9},{2,10},{5,13},{6,14},{9,1},{10,2},{13,5},{14,6},{17,25},{18,... | collective-permute-start | bytes 24584 | tf_op jit(solution)/shard_map/ppermute | solution.py:458
  17.3 1.1 %collective-permute-done.3 = f32[8,256]{1,0:T(8,128)S(1)} collective-permute-done((f32[8,256]{1,0:T(8,128)S(1)}, f32[8,256]{1,0:T(8,128)S(1)}, u32[]{:S(2)}, u32[]{:S(2)}) %collective-permute-start.3) | collective-permute-done | bytes 8224 | tf_op jit(solution)/shard_map/ppermute | solution.py:458
  18.4 0.0 collective-permute-done.4.near_ref
  18.4 1.7 %own_gram.1.gram_in_ref = f32[8,256,256]{2,1,0:T(8,128)S(1)} custom-call(s32[1]{0:T(128)} %bitcast.refs_0_.odd_ref, bf16[8,4,64,256]{3,2,1,0:T(8,128)(2,1)S(1)} %copy-done, bf16[4,4,64,256]{3,2,1,0:T(8,128)(2,1)S(1)} %collective-permute-done.4.near_ref), custom_call_target="tpu_custom_call" | custom-call | flops 805306368 | bytes 3670016 | tf_op jit(solution)/shard_map/own_gram/pallas_call | solution.py:172
  20.1 0.0 copy-start.1
  20.1 4.0 %collective-permute-start.5 = (f32[16,256]{1,0:T(8,128)S(1)}, f32[16,256]{1,0:T(8,128)S(1)}, u32[]{:S(2)}, u32[]{:S(2)}) collective-permute-start(f32[16,256]{1,0:T(8,128)S(1)} %pad_maximum_fusion), channel_id=1, source_target_pairs={{0,15},{1,2},{2,1},{3,4},{4,3},{5,6},{6,5},{7,8},{8,7},{9,10},{10,... | collective-permute-start | bytes 49160 | tf_op jit(solution)/shard_map/ppermute | solution.py:461
  24.2 1.4 %collective-permute-done.5.refs_6_ = f32[16,256]{1,0:T(8,128)S(1)} collective-permute-done((f32[16,256]{1,0:T(8,128)S(1)}, f32[16,256]{1,0:T(8,128)S(1)}, u32[]{:S(2)}, u32[]{:S(2)}) %collective-permute-start.5) | collective-permute-done | bytes 16416 | tf_op jit(solution)/shard_map/ppermute | solution.py:461
  25.6 1.3 %collective-permute-start.6 = (f32[8,256]{1,0:T(8,128)S(1)}, f32[8,256]{1,0:T(8,128)S(1)}, u32[]{:S(2)}, u32[]{:S(2)}) collective-permute-start(f32[8,256]{1,0:T(8,128)S(1)} %fusion.refs_7_), channel_id=1, source_target_pairs={{1,0},{2,3},{5,4},{6,7},{9,8},{10,11},{13,12},{14,15},{17,16},{18,... | collective-permute-start | bytes 24584 | tf_op jit(solution)/shard_map/ppermute | solution.py:464
  26.9 0.0 collective-permute-done.halo_ref
  26.9 3.0 %prepare.1 = (f32[8,256,256]{2,1,0:T(8,128)S(1)}, f32[8,256,256]{2,1,0:T(8,128)S(1)}, f32[4,8,128]{2,1,0:T(8,128)S(1)}) custom-call(s32[1]{0:T(128)} %bitcast.refs_0_.odd_ref, bf16[4,4,64,256]{3,2,1,0:T(8,128)(2,1)} %collective-permute-done.halo_ref, f32[8,256,256]{2,1,0:T(8,128)S(1)} %own_gram.1.gram_in_ref), custom_call_target="tpu_custom_call", output_to_operand_aliasing={{0}: (2, {})} | custom-call | flops 273678336 | bytes 6815744 | tf_op jit(solution)/shard_map/prepare/pallas_call | solution.py:237
  30.0 0.0 collective-permute-done.6.refs_8_
  30.0 0.0 copy-done.1
  30.0 14.9 %finish.1 = bf16[8,4,64,256]{3,2,1,0:T(8,128)(2,1)} custom-call(bf16[8,4,64,256]{3,2,1,0:T(8,128)(2,1)S(1)} %copy-done.1, f32[8,256,256]{2,1,0:T(8,128)S(1)} %get-tuple-element.19.refs_1_, f32[8,256,256]{2,1,0:T(8,128)S(1)} %get-tuple-element.20.refs_2_, f32[4,8,128]{2,1,0:T(8,128)S(1)} %get-tuple-element.21.refs_3_, ...), custom_call_target="tpu_custom_call" | custom-call | tf_op jit(solution)/shard_map/finish/pallas_call | solution.py:420
  (5 shorter events, 0.0 us)
Async XLA Ops:
  0.0 1.2 %copy-start = (bf16[8,4,64,256]{3,2,1,0:T(8,128)(2,1)S(1)}, bf16[8,4,64,256]{3,2,1,0:T(8,128)(2,1)}, u32[]{:S(2)}) copy-start(bf16[8,4,64,256]{3,2,1,0:T(8,128)(2,1)} %refs_0_.1) | copy-start | bytes 3145732
  1.2 0.7 %copy-start.2 = (s32[256]{0:T(256)S(1)}, s32[256]{0:T(256)}, u32[]{:S(2)}) copy-start(s32[256]{0:T(256)} %param.5) | copy-start | bytes 3076
  1.9 0.7 %copy-start.3 = (f32[256]{0:T(256)S(1)}, f32[256]{0:T(256)}, u32[]{:S(2)}) copy-start(f32[256]{0:T(256)} %param.6) | copy-start | bytes 3076
  2.6 0.7 %copy-start.4 = (f32[256]{0:T(256)S(1)}, f32[256]{0:T(256)}, u32[]{:S(2)}) copy-start(f32[256]{0:T(256)} %param.7) | copy-start | bytes 3076
  5.0 13.4 %collective-permute-start.4 = (bf16[4,4,64,256]{3,2,1,0:T(8,128)(2,1)S(1)}, bf16[4,4,64,256]{3,2,1,0:T(8,128)(2,1)S(1)}, u32[]{:S(2)}, u32[]{:S(2)}) collective-permute-start(bf16[4,4,64,256]{3,2,1,0:T(8,128)(2,1)S(1)} %get-tuple-element.17), channel_id=1, source_target_pairs={{0,1},{1,0},{2,3},{3,2},{4,5},{5,4},{6,7},{7,6},{8,9},{9,8},{10,11... | collective-permute-start | bytes 1572872 | tf_op jit(solution)/shard_map/ppermute | solution.py:449
  5.1 3.1 %collective-permute-start.1 = (f32[16,256]{1,0:T(8,128)S(1)}, f32[16,256]{1,0:T(8,128)S(1)}, u32[]{:S(2)}, u32[]{:S(2)}) collective-permute-start(f32[16,256]{1,0:T(8,128)S(1)} %get-tuple-element.16), channel_id=1, source_target_pairs={{0,1},{1,0},{2,3},{3,2},{4,5},{5,4},{6,7},{7,6},{8,9},{9,8},{10,11... | collective-permute-start | bytes 49160 | tf_op jit(solution)/shard_map/ppermute | solution.py:451
  5.5 21.4 %collective-permute-start = (bf16[4,4,64,256]{3,2,1,0:T(8,128)(2,1)}, bf16[4,4,64,256]{3,2,1,0:T(8,128)(2,1)}, u32[]{:S(2)}, u32[]{:S(2)}) collective-permute-start(bf16[4,4,64,256]{3,2,1,0:T(8,128)(2,1)} %get-tuple-element.15), channel_id=1, source_target_pairs={{0,15},{1,2},{2,1},{3,4},{4,3},{5,6},{6,5},{7,8},{8,7},{9,10},{10,... | collective-permute-start | bytes 1572872 | tf_op jit(solution)/shard_map/ppermute | solution.py:448
  8.2 4.9 %collective-permute-start.2 = (f32[8,256]{1,0:T(8,128)S(1)}, f32[8,256]{1,0:T(8,128)S(1)}, u32[]{:S(2)}, u32[]{:S(2)}) collective-permute-start(f32[8,256]{1,0:T(8,128)S(1)} %slice_add_fusion.1), channel_id=1, source_target_pairs={{1,5},{2,6},{5,1},{6,2},{9,13},{10,14},{13,9},{14,10},{17,21},{18,... | collective-permute-start | bytes 24584 | tf_op jit(solution)/shard_map/ppermute | solution.py:458
  13.1 5.3 %collective-permute-start.3 = (f32[8,256]{1,0:T(8,128)S(1)}, f32[8,256]{1,0:T(8,128)S(1)}, u32[]{:S(2)}, u32[]{:S(2)}) collective-permute-start(f32[8,256]{1,0:T(8,128)S(1)} %add.13), channel_id=1, source_target_pairs={{1,9},{2,10},{5,13},{6,14},{9,1},{10,2},{13,5},{14,6},{17,25},{18,... | collective-permute-start | bytes 24584 | tf_op jit(solution)/shard_map/ppermute | solution.py:458
  20.1 9.8 %copy-start.1 = (bf16[8,4,64,256]{3,2,1,0:T(8,128)(2,1)S(1)}, bf16[8,4,64,256]{3,2,1,0:T(8,128)(2,1)}, u32[]{:S(2)}) copy-start(bf16[8,4,64,256]{3,2,1,0:T(8,128)(2,1)} %refs_0_.1) | copy-start | bytes 3145732
  20.1 5.5 %collective-permute-start.5 = (f32[16,256]{1,0:T(8,128)S(1)}, f32[16,256]{1,0:T(8,128)S(1)}, u32[]{:S(2)}, u32[]{:S(2)}) collective-permute-start(f32[16,256]{1,0:T(8,128)S(1)} %pad_maximum_fusion), channel_id=1, source_target_pairs={{0,15},{1,2},{2,1},{3,4},{4,3},{5,6},{6,5},{7,8},{8,7},{9,10},{10,... | collective-permute-start | bytes 49160 | tf_op jit(solution)/shard_map/ppermute | solution.py:461
  25.6 4.3 %collective-permute-start.6 = (f32[8,256]{1,0:T(8,128)S(1)}, f32[8,256]{1,0:T(8,128)S(1)}, u32[]{:S(2)}, u32[]{:S(2)}) collective-permute-start(f32[8,256]{1,0:T(8,128)S(1)} %fusion.refs_7_), channel_id=1, source_target_pairs={{1,0},{2,3},{5,4},{6,7},{9,8},{10,11},{13,12},{14,15},{17,16},{18,... | collective-permute-start | bytes 24584 | tf_op jit(solution)/shard_map/ppermute | solution.py:464

commit v5 on v3

--- a/solution.py
+++ b/solution.py
@@ -28,10 +28,28 @@
     return jnp.where(inside, 1.0 - dist / (HALO + 1), 0.0)
 
 
-def obs_kernel(odd_ref, cells_ref, index_ref, value_ref, var_ref, own_ref, near_ref, far_ref):
-    lon_dev, _, lat, members = cells_ref.shape
+def observe_kernel(*refs):
+    odd_ref, state_ref = refs[:2]
+    own_ref, near_ref, far_ref, near_edge_ref, far_edge_ref = refs[5:10]
+    cells_ref, index_ref, value_ref, var_ref, sems = refs[10:]
+    lon_dev, lat, members = cells_ref.shape
     nobs = index_ref.shape[1]
-    rows = cells_ref[:, 0].reshape(lon_dev * lat, members)
+    last = lon_dev - HALO
+    far_at = odd_ref[0] * last
+    copies = [
+        pltpu.make_async_copy(state_ref.at[:, 0], cells_ref, sems.at[0]),
+        pltpu.make_async_copy(state_ref.at[pl.ds(far_at, HALO)], far_edge_ref, sems.at[1]),
+        pltpu.make_async_copy(state_ref.at[pl.ds(last - far_at, HALO)], near_edge_ref, sems.at[2]),
+    ]
+    fetches = [
+        pltpu.make_async_copy(src, dst, sems.at[len(copies) + i])
+        for i, (src, dst) in enumerate(zip(refs[2:5], (index_ref, value_ref, var_ref)))
+    ]
+    for copy in fetches + copies:
+        copy.start()
+    for copy in fetches + copies[:1]:
+        copy.wait()
+    rows = cells_ref[...].reshape(lon_dev * lat, members)
     index = index_ref[...]
     sub = lax.broadcasted_iota(jnp.int32, (TILE, nobs), 0)
     table = jnp.where(
@@ -64,32 +82,36 @@
     own_ref[...] = like[:blocks]
     near_ref[:blocks, :] = like[blocks : 2 * blocks]
     far_ref[...] = like[2 * blocks :]
+    for copy in copies[1:]:
+        copy.wait()
 
 
 def observe(odd, state, obs_index, obs_value, obs_var):
-    lon_dev, _, lat, members = state.shape
-    nobs = obs_index.shape[0]
+    lon_dev, nvar, lat, members = state.shape
     blocks = lat // REGION
-    row = pl.BlockSpec((1, nobs), lambda i: (0, 0))
     like = jax.ShapeDtypeStruct((blocks, members), jnp.float32)
-    like_spec = pl.BlockSpec((blocks, members), lambda i: (0, 0))
     more = jax.ShapeDtypeStruct((blocks + TILE, members), jnp.float32)
-    more_spec = pl.BlockSpec((blocks + TILE, members), lambda i: (0, 0))
+    edge = jax.ShapeDtypeStruct((HALO, nvar, lat, members), state.dtype)
+    vmem = pl.BlockSpec(memory_space=pltpu.VMEM)
+    arrays = state, obs_index[None], obs_value[None], obs_var[None]
     return pl.pallas_call(
-        obs_kernel,
-        grid=(1,),
+        observe_kernel,
         in_specs=[
             pl.BlockSpec(memory_space=pltpu.SMEM),
-            pl.BlockSpec((lon_dev, 1, lat, members), lambda i: (0, 0, 0, 0)),
-            row,
-            row,
-            row,
+        ]
+        + [pl.BlockSpec(memory_space=pltpu.HBM)] * 4,
+        out_specs=[vmem] * 5,
+        out_shape=[like, more, like, edge, edge],
+        scratch_shapes=[
+            pltpu.VMEM((lon_dev, lat, members), state.dtype),
+            pltpu.VMEM((1, obs_index.size), jnp.int32),
+            pltpu.VMEM((1, obs_index.size), jnp.float32),
+            pltpu.VMEM((1, obs_index.size), jnp.float32),
+            pltpu.SemaphoreType.DMA((6,)),
         ],
-        out_specs=[like_spec, more_spec, like_spec],
-        out_shape=[like, more, like],
-        compiler_params=pltpu.CompilerParams(vmem_limit_bytes=32 * 2**20),
+        compiler_params=pltpu.CompilerParams(vmem_limit_bytes=24 * 2**20),
         name="observe",
-    )(odd, state, obs_index[None], obs_value[None], obs_var[None])
+    )(odd, *[pltpu.with_memory_space_constraint(x, pltpu.HBM) for x in arrays])
 
 
 def pair_tiles(ref, step, steps):
@@ -164,7 +186,12 @@
         ],
         out_specs=pl.BlockSpec((PAIR, members, members), lambda i: (i, 0, 0)),
         out_shape=jax.ShapeDtypeStruct((steps * PAIR, members, members), jnp.float32),
-        compiler_params=pltpu.CompilerParams(vmem_limit_bytes=48 * 2**20),
+        compiler_params=pltpu.CompilerParams(vmem_limit_bytes=24 * 2**20),
+        cost_estimate=pl.CostEstimate(
+            flops=2 * (lon_dev + HALO) * nvar * 2 * lat * members**2,
+            bytes_accessed=2 * (state.size + near.size) + 4 * lat // REGION * members**2,
+            transcendentals=0,
+        ),
         name="own_gram",
     )(odd, state, near)
 
@@ -322,15 +349,15 @@
 
 
 def analysis_kernel(count, scale, *refs):
-    odd_ref, halo_ref, state_ref, gram_in_ref = refs[0:4]
-    own_ref, near_ref, far_ref, sum_ref, out_ref = refs[4:9]
-    gram_ref, kernel_ref, ratio_ref, weight_ref, logw_ref, result_ref, sems = refs[9:]
+    flags_ref, close_ref, wide_ref, state_ref, gram_in_ref = refs[0:5]
+    own_ref, near_ref, far_close_ref, far_wide_ref, sum_ref, back_ref, out_ref = refs[5:12]
+    gram_ref, kernel_ref, ratio_ref, weight_ref, logw_ref, result_ref, sems = refs[12:]
     regions, members = gram_in_ref.shape[0], gram_in_ref.shape[-1]
     pairs = regions // PAIR
     size = PAIR * TILE
 
-    total = sum_ref[0:1, 0:1] + far_ref[regions : regions + 1, 0:1]
-    like = own_ref[...] + near_ref[:regions, :] + far_ref[:regions, :]
+    total = sum_ref[0:1, 0:1] + back_ref[0:1, 0:1]
+    like = own_ref[...] + near_ref[:regions, :] + far_close_ref[:regions, :] + far_wide_ref[...]
     like = -0.5 * (count / total) * like
     like = like - jnp.max(like, axis=1, keepdims=True)
     logw = (like - jnp.log(jnp.sum(jnp.exp(like), axis=1, keepdims=True))) * LOG2E
@@ -344,7 +371,9 @@
         return pltpu.make_async_copy(result_ref.at[pair], out_ref.at[:, :, at, :], sems.at[pair])
 
     def halo_grams(pair, carry):
-        grams = gram_of(pair_tiles(halo_ref, pair, pairs), halo_weights(odd_ref[0] == 0))
+        tiles = zip(pair_tiles(close_ref, pair, pairs), pair_tiles(wide_ref, pair, pairs))
+        tiles = [jnp.where(flags_ref[1] == 1, x, y) for x, y in tiles]
+        grams = gram_of(tiles, halo_weights(flags_ref[0] == 0))
         for at in range(PAIR):
             region = pair * PAIR + at
             gram_ref[region] = gram_in_ref[region] + grams[at]
@@ -401,7 +430,7 @@
         lax.fori_loop(0, pairs, again, 0)
 
 
-def analyse(odd, halo, state, gram, own, near, far, total, count):
+def analyse(flags, halos, state, gram, likes, totals, count):
     lon_dev, nvar, lat, members = state.shape
     regions = lat // REGION
     offsets = range(REGION + 2 * HALO)
@@ -410,7 +439,7 @@
     vmem = pl.BlockSpec(memory_space=pltpu.VMEM)
     return pl.pallas_call(
         functools.partial(analysis_kernel, count, scale),
-        in_specs=[pl.BlockSpec(memory_space=pltpu.SMEM)] + [vmem] * 7,
+        in_specs=[pl.BlockSpec(memory_space=pltpu.SMEM)] + [vmem] * 10,
         out_specs=pl.BlockSpec(memory_space=pl.ANY),
         out_shape=jax.ShapeDtypeStruct(state.shape, state.dtype),
         scratch_shapes=[
@@ -422,34 +451,50 @@
             pltpu.VMEM((regions // PAIR, lon_dev, nvar, PAIR * TILE, members), jnp.bfloat16),
             pltpu.SemaphoreType.DMA((regions // PAIR,)),
         ],
-        compiler_params=pltpu.CompilerParams(vmem_limit_bytes=48 * 2**20),
+        compiler_params=pltpu.CompilerParams(vmem_limit_bytes=24 * 2**20),
         name="analyse",
-    )(odd, halo, state, gram, own, near, far, total)
+    )(flags, *halos, state, gram, *likes, *totals)
 
 
 def on_device(state, obs_index, obs_value, obs_var):
-    lon_dev = state.shape[0]
     count = lax.axis_size("lon")
-    odd = lax.axis_index("lon") % 2
+    place = lax.axis_index("lon")
+
+    def send(value, pairs):
+        return lax.ppermute(value, "lon", pairs)
+
     near_pairs = [(i, i ^ 1) for i in range(count)]
     far_pairs = [(i, (i + 1 if i % 2 else i - 1) % count) for i in range(count)]
-    for_far = lax.dynamic_slice_in_dim(state, odd * (lon_dev - HALO), HALO, axis=0)
-    for_near = lax.dynamic_slice_in_dim(state, (1 - odd) * (lon_dev - HALO), HALO, axis=0)
-    far = lax.ppermute(for_far, "lon", far_pairs)
-    near = lax.ppermute(for_near, "lon", near_pairs)
-    odd = odd.astype(jnp.int32).reshape(1)
-    own_like, near_like, far_like = observe(odd, state, obs_index, obs_value, obs_var)
+    close_pairs = [(i, j) for i, j in far_pairs if (i ^ i >> 1) & 1]
+    wide_pairs = [(i, j) for i, j in far_pairs if not (i ^ i >> 1) & 1]
+    flags = jnp.stack([place & 1, (place ^ place >> 1) & 1]).astype(jnp.int32)
+    own_like, near_like, far_like, for_near, for_far = observe(
+        flags, state, obs_index, obs_value, obs_var
+    )
     blocks = own_like.shape[0]
-    got_near = lax.ppermute(near_like, "lon", near_pairs)
-    total = near_like[blocks:] + got_near[blocks:]
+    close = send(for_far, close_pairs)
+    near = send(for_near, near_pairs)
+    got_near = send(near_like, near_pairs)
+    line = near_like[blocks:] + got_near[blocks:]
+    close, line = lax.optimization_barrier((close, line))
     hop = 4
     while hop < count:
-        total = total + lax.ppermute(total, "lon", [(i, i ^ hop) for i in range(count)])
+        line = line + send(line, [(i, i ^ hop) for i, _ in wide_pairs])
         hop *= 2
-    got_far = lax.ppermute(jnp.concatenate([far_like, total], axis=0), "lon", far_pairs)
-    gram = own_gram(odd, state, near)
+    for_far, near, far_like, line = lax.optimization_barrier((for_far, near, far_like, line))
+    wide = send(for_far, wide_pairs)
+    handed = send(line, [(i, i ^ 1) for i, _ in wide_pairs])
+    got_close = send(jnp.concatenate([far_like, handed], axis=0), close_pairs)
+    got_wide = send(far_like, wide_pairs)
+    total = handed + got_close[blocks:]
+    back = send(total, [(i, i ^ 1) for i, _ in close_pairs])
+    if count % 4 or count & (count - 1):
+        total = lax.psum(near_like[blocks:], "lon")
+        back = jnp.zeros_like(total)
+    gram = own_gram(flags, state, near)
     nobs = float(obs_index.shape[0] * count)
-    return analyse(odd, far, state, gram, own_like, got_near, got_far, total, nobs)
+    likes = own_like, got_near, got_close, got_wide
+    return analyse(flags, (close, wide), state, gram, likes, (total, back), nobs)
 
 
 def solution(mesh):

time: 41.2 us -> 56 us (1.36)
  the two profiles are of different devices: /device:TPU:0 before, /device:TPU:1 now
where the time goes in v5:
time: 56 us; the launch traced here: 55.7 us
  Pallas kernels  21.4 us (38%)
  waiting for transfers between devices  18.9 us (34%)
  starting transfers between devices  14 us (25%)
  local copies, waits for them, and re-layouts  1.22 us (2%)
    ppermute x10, waiting for transfers between devices, send(): return lax.ppermute(value, 'lon', pairs)  18.9 us
    pallas_call x1, Pallas kernels, analyse(): pl.pallas_call(functools.partial(analysis_kernel, count, scale), in_specs...  16.7 us
    ppermute x10, starting transfers between devices, send(): return lax.ppermute(value, 'lon', pairs)  14 us
    pallas_call x1, Pallas kernels, observe(): pl.pallas_call(observe_kernel, in_specs=[pl.BlockSpec(memory_space=pltpu....  2.37 us
    pallas_call x1, Pallas kernels, own_gram(): pl.pallas_call(own_gram_kernel, grid=(steps,), in_specs=[pl.BlockSpec(mem...  2.28 us
    unnamed x2, local copies, waits for them, and re-layouts  1.22 us
  transfers between devices with their start and end apart: 10, of which 4 were waited for; matrix products, arithmetic and copies ran while one was open for 0% of the time, Pallas kernels for 4%

profile of v5, /device:TPU:1, one launch (start us, length us, event | category | flops | bytes accessed | tf_op | source)
XLA Modules:
  0.0 55.7 jit_solution(16171376680677316922)
XLA Ops:
  0.0 0.1 pad_add_fusion.refs_0_.odd_ref
  0.1 2.4 %observe.1 = (f32[8,256]{1,0:T(8,128)S(1)}, f32[16,256]{1,0:T(8,128)S(1)}, f32[8,256]{1,0:T(8,128)S(1)}, bf16[4,4,64,256]{3,2,1,0:T(8,128)(2,1)S(1)}, bf16[4,4,64,256]{3,2,1,0:T(8,128)(2,1)S(1)}) custom-call(s32[2]{0:T(128)S(1)} %pad_add_fusion.refs_0_.odd_ref, bf16[8,4,64,256]{3,2,1,0:T(8,128)(2,1)} %refs_3_.1, s32[1,256]{1,0:T(1,128)} %bitcast.5, ...), custom_call_target="tpu_custom_call" | custom-call | tf_op jit(solution)/shard_map/observe/pallas_call | solution.py:97
  2.5 4.5 %collective-permute-start = (bf16[4,4,64,256]{3,2,1,0:T(8,128)(2,1)S(1)}, bf16[4,4,64,256]{3,2,1,0:T(8,128)(2,1)S(1)}, u32[]{:S(2)}, u32[]{:S(2)}) collective-permute-start(bf16[4,4,64,256]{3,2,1,0:T(8,128)(2,1)S(1)} %get-tuple-element.22), channel_id=1, source_target_pairs={{1,2},{2,1},{5,6},{6,5},{9,10},{10,9},{13,14},{14,13},{17,18},{18,... | collective-permute-start | bytes 1572872 | tf_op jit(solution)/shard_map/ppermute | solution.py:464
  7.0 0.1 collective-permute-start.2
  7.1 0.5 collective-permute-start.1
  7.6 1.4 %collective-permute-done.1.refs_6_ = f32[16,256]{1,0:T(8,128)S(1)} collective-permute-done((f32[16,256]{1,0:T(8,128)S(1)}, f32[16,256]{1,0:T(8,128)S(1)}, u32[]{:S(2)}, u32[]{:S(2)}) %collective-permute-start.1) | collective-permute-done | bytes 16416 | tf_op jit(solution)/shard_map/ppermute | solution.py:464
  9.0 4.8 %collective-permute-done.refs_1_ = bf16[4,4,64,256]{3,2,1,0:T(8,128)(2,1)S(1)} collective-permute-done((bf16[4,4,64,256]{3,2,1,0:T(8,128)(2,1)S(1)}, bf16[4,4,64,256]{3,2,1,0:T(8,128)(2,1)S(1)}, u32[]{:S(2)}, u32[]{:S(2)}) %collective-permute-start) | collective-permute-done | bytes 524320 | tf_op jit(solution)/shard_map/ppermute | solution.py:464
  13.9 0.7 %collective-permute-start.3 = (f32[8,256]{1,0:T(8,128)S(1)}, f32[8,256]{1,0:T(8,128)S(1)}, u32[]{:S(2)}, u32[]{:S(2)}) collective-permute-start(f32[8,256]{1,0:T(8,128)S(1)} %slice_add_fusion.1), channel_id=1, source_target_pairs={{0,4},{3,7},{4,0},{7,3},{8,12},{11,15},{12,8},{15,11},{16,20},{19,... | collective-permute-start | bytes 24584 | tf_op jit(solution)/shard_map/ppermute | solution.py:464
  14.5 0.0 collective-permute-done.3
  14.5 0.7 %collective-permute-start.4 = (f32[8,256]{1,0:T(8,128)S(1)}, f32[8,256]{1,0:T(8,128)S(1)}, u32[]{:S(2)}, u32[]{:S(2)}) collective-permute-start(f32[8,256]{1,0:T(8,128)S(1)} %add.13), channel_id=1, source_target_pairs={{0,8},{3,11},{4,12},{7,15},{8,0},{11,3},{12,4},{15,7},{16,24},{19,... | collective-permute-start | bytes 24584 | tf_op jit(solution)/shard_map/ppermute | solution.py:464
  15.2 0.0 collective-permute-done.4
  15.2 0.0 collective-permute-done.2.near_ref
  15.2 0.7 %collective-permute-start.5 = (bf16[4,4,64,256]{3,2,1,0:T(8,128)(2,1)S(1)}, bf16[4,4,64,256]{3,2,1,0:T(8,128)(2,1)S(1)}, u32[]{:S(2)}, u32[]{:S(2)}) collective-permute-start(bf16[4,4,64,256]{3,2,1,0:T(8,128)(2,1)S(1)} %get-tuple-element.22), channel_id=1, source_target_pairs={{0,15},{3,4},{4,3},{7,8},{8,7},{11,12},{12,11},{15,0},{16,31},{19,... | collective-permute-start | bytes 1572872 | tf_op jit(solution)/shard_map/ppermute | solution.py:464
  15.9 1.3 %collective-permute-start.6 = (f32[8,256]{1,0:T(8,128)S(1)}, f32[8,256]{1,0:T(8,128)S(1)}, u32[]{:S(2)}, u32[]{:S(2)}) collective-permute-start(f32[8,256]{1,0:T(8,128)S(1)} %add.14), channel_id=1, source_target_pairs={{0,1},{3,2},{4,5},{7,6},{8,9},{11,10},{12,13},{15,14},{16,17},{19,... | collective-permute-start | bytes 24584 | tf_op jit(solution)/shard_map/ppermute | solution.py:464
  17.2 8.8 %collective-permute-done.6 = f32[8,256]{1,0:T(8,128)S(1)} collective-permute-done((f32[8,256]{1,0:T(8,128)S(1)}, f32[8,256]{1,0:T(8,128)S(1)}, u32[]{:S(2)}, u32[]{:S(2)}) %collective-permute-start.6) | collective-permute-done | bytes 8224 | tf_op jit(solution)/shard_map/ppermute | solution.py:464
  26.0 3.6 %collective-permute-start.7 = (f32[16,256]{1,0:T(8,128)S(1)}, f32[16,256]{1,0:T(8,128)S(1)}, u32[]{:S(2)}, u32[]{:S(2)}) collective-permute-start(f32[16,256]{1,0:T(8,128)S(1)} %pad_maximum_fusion), channel_id=1, source_target_pairs={{1,2},{2,1},{5,6},{6,5},{9,10},{10,9},{13,14},{14,13},{17,18},{18,... | collective-permute-start | bytes 49160 | tf_op jit(solution)/shard_map/ppermute | solution.py:464
  29.6 0.7 %collective-permute-start.8 = (f32[8,256]{1,0:T(8,128)S(1)}, f32[8,256]{1,0:T(8,128)S(1)}, u32[]{:S(2)}, u32[]{:S(2)}) collective-permute-start(f32[8,256]{1,0:T(8,128)S(1)} %get-tuple-element.25), channel_id=1, source_target_pairs={{0,15},{3,4},{4,3},{7,8},{8,7},{11,12},{12,11},{15,0},{16,31},{19,... | collective-permute-start | bytes 24584 | tf_op jit(solution)/shard_map/ppermute | solution.py:464
  30.3 3.8 %collective-permute-done.7.refs_7_ = f32[16,256]{1,0:T(8,128)S(1)} collective-permute-done((f32[16,256]{1,0:T(8,128)S(1)}, f32[16,256]{1,0:T(8,128)S(1)}, u32[]{:S(2)}, u32[]{:S(2)}) %collective-permute-start.7) | collective-permute-done | bytes 16416 | tf_op jit(solution)/shard_map/ppermute | solution.py:464
  34.1 1.3 %collective-permute-start.9 = (f32[8,256]{1,0:T(8,128)S(1)}, f32[8,256]{1,0:T(8,128)S(1)}, u32[]{:S(2)}, u32[]{:S(2)}) collective-permute-start(f32[8,256]{1,0:T(8,128)S(1)} %slice_add_fusion.refs_9_), channel_id=1, source_target_pairs={{1,0},{2,3},{5,4},{6,7},{9,8},{10,11},{13,12},{14,15},{17,16},{18,... | collective-permute-start | bytes 24584 | tf_op jit(solution)/shard_map/ppermute | solution.py:464
  35.4 0.0 copy-start
  35.4 1.2 %copy-done = bf16[8,4,64,256]{3,2,1,0:T(8,128)(2,1)S(1)} copy-done((bf16[8,4,64,256]{3,2,1,0:T(8,128)(2,1)S(1)}, bf16[8,4,64,256]{3,2,1,0:T(8,128)(2,1)}, u32[]{:S(2)}) %copy-start) | copy-done | bytes 1048600
  36.6 2.3 %own_gram.1.refs_4_ = f32[8,256,256]{2,1,0:T(8,128)S(1)} custom-call(s32[2]{0:T(128)S(1)} %pad_add_fusion.refs_0_.odd_ref, bf16[8,4,64,256]{3,2,1,0:T(8,128)(2,1)S(1)} %copy-done, bf16[4,4,64,256]{3,2,1,0:T(8,128)(2,1)S(1)} %collective-permute-done.2.near_ref), custom_call_target="tpu_custom_call" | custom-call | flops 805306368 | bytes 3670016 | tf_op jit(solution)/shard_map/own_gram/pallas_call | solution.py:179
  38.9 0.0 collective-permute-done.8.refs_8_
  38.9 0.0 collective-permute-done.9.refs_10_
  38.9 0.0 collective-permute-done.5.refs_2_
  39.0 16.7 %analyse.1 = bf16[8,4,64,256]{3,2,1,0:T(8,128)(2,1)} custom-call(s32[2]{0:T(128)S(1)} %pad_add_fusion.refs_0_.odd_ref, bf16[4,4,64,256]{3,2,1,0:T(8,128)(2,1)S(1)} %collective-permute-done.refs_1_, bf16[4,4,64,256]{3,2,1,0:T(8,128)(2,1)S(1)} %collective-permute-done.5.refs_2_, bf16[8,4,64,256]{3,2,1,0:T(8,128)(2,1)S(1)} %copy-done, ...), custom_call_target="tpu_custom_call" | custom-call | tf_op jit(solution)/shard_map/analyse/pallas_call | solution.py:440
  (5 shorter events, 0.0 us)
Async XLA Ops:
  2.5 11.4 %collective-permute-start = (bf16[4,4,64,256]{3,2,1,0:T(8,128)(2,1)S(1)}, bf16[4,4,64,256]{3,2,1,0:T(8,128)(2,1)S(1)}, u32[]{:S(2)}, u32[]{:S(2)}) collective-permute-start(bf16[4,4,64,256]{3,2,1,0:T(8,128)(2,1)S(1)} %get-tuple-element.22), channel_id=1, source_target_pairs={{1,2},{2,1},{5,6},{6,5},{9,10},{10,9},{13,14},{14,13},{17,18},{18,... | collective-permute-start | bytes 1572872 | tf_op jit(solution)/shard_map/ppermute | solution.py:464
  7.0 8.2 %collective-permute-start.2 = (bf16[4,4,64,256]{3,2,1,0:T(8,128)(2,1)S(1)}, bf16[4,4,64,256]{3,2,1,0:T(8,128)(2,1)S(1)}, u32[]{:S(2)}, u32[]{:S(2)}) collective-permute-start(bf16[4,4,64,256]{3,2,1,0:T(8,128)(2,1)S(1)} %get-tuple-element.19), channel_id=1, source_target_pairs={{0,1},{1,0},{2,3},{3,2},{4,5},{5,4},{6,7},{7,6},{8,9},{9,8},{10,11... | collective-permute-start | bytes 1572872 | tf_op jit(solution)/shard_map/ppermute | solution.py:464
  7.1 1.9 %collective-permute-start.1 = (f32[16,256]{1,0:T(8,128)S(1)}, f32[16,256]{1,0:T(8,128)S(1)}, u32[]{:S(2)}, u32[]{:S(2)}) collective-permute-start(f32[16,256]{1,0:T(8,128)S(1)} %get-tuple-element.17), channel_id=1, source_target_pairs={{0,1},{1,0},{2,3},{3,2},{4,5},{5,4},{6,7},{7,6},{8,9},{9,8},{10,11... | collective-permute-start | bytes 49160 | tf_op jit(solution)/shard_map/ppermute | solution.py:464
  13.9 0.7 %collective-permute-start.3 = (f32[8,256]{1,0:T(8,128)S(1)}, f32[8,256]{1,0:T(8,128)S(1)}, u32[]{:S(2)}, u32[]{:S(2)}) collective-permute-start(f32[8,256]{1,0:T(8,128)S(1)} %slice_add_fusion.1), channel_id=1, source_target_pairs={{0,4},{3,7},{4,0},{7,3},{8,12},{11,15},{12,8},{15,11},{16,20},{19,... | collective-permute-start | bytes 24584 | tf_op jit(solution)/shard_map/ppermute | solution.py:464
  14.5 0.7 %collective-permute-start.4 = (f32[8,256]{1,0:T(8,128)S(1)}, f32[8,256]{1,0:T(8,128)S(1)}, u32[]{:S(2)}, u32[]{:S(2)}) collective-permute-start(f32[8,256]{1,0:T(8,128)S(1)} %add.13), channel_id=1, source_target_pairs={{0,8},{3,11},{4,12},{7,15},{8,0},{11,3},{12,4},{15,7},{16,24},{19,... | collective-permute-start | bytes 24584 | tf_op jit(solution)/shard_map/ppermute | solution.py:464
  15.2 23.7 %collective-permute-start.5 = (bf16[4,4,64,256]{3,2,1,0:T(8,128)(2,1)S(1)}, bf16[4,4,64,256]{3,2,1,0:T(8,128)(2,1)S(1)}, u32[]{:S(2)}, u32[]{:S(2)}) collective-permute-start(bf16[4,4,64,256]{3,2,1,0:T(8,128)(2,1)S(1)} %get-tuple-element.22), channel_id=1, source_target_pairs={{0,15},{3,4},{4,3},{7,8},{8,7},{11,12},{12,11},{15,0},{16,31},{19,... | collective-permute-start | bytes 1572872 | tf_op jit(solution)/shard_map/ppermute | solution.py:464
  15.9 10.1 %collective-permute-start.6 = (f32[8,256]{1,0:T(8,128)S(1)}, f32[8,256]{1,0:T(8,128)S(1)}, u32[]{:S(2)}, u32[]{:S(2)}) collective-permute-start(f32[8,256]{1,0:T(8,128)S(1)} %add.14), channel_id=1, source_target_pairs={{0,1},{3,2},{4,5},{7,6},{8,9},{11,10},{12,13},{15,14},{16,17},{19,... | collective-permute-start | bytes 24584 | tf_op jit(solution)/shard_map/ppermute | solution.py:464
  26.0 8.1 %collective-permute-start.7 = (f32[16,256]{1,0:T(8,128)S(1)}, f32[16,256]{1,0:T(8,128)S(1)}, u32[]{:S(2)}, u32[]{:S(2)}) collective-permute-start(f32[16,256]{1,0:T(8,128)S(1)} %pad_maximum_fusion), channel_id=1, source_target_pairs={{1,2},{2,1},{5,6},{6,5},{9,10},{10,9},{13,14},{14,13},{17,18},{18,... | collective-permute-start | bytes 49160 | tf_op jit(solution)/shard_map/ppermute | solution.py:464
  29.6 9.3 %collective-permute-start.8 = (f32[8,256]{1,0:T(8,128)S(1)}, f32[8,256]{1,0:T(8,128)S(1)}, u32[]{:S(2)}, u32[]{:S(2)}) collective-permute-start(f32[8,256]{1,0:T(8,128)S(1)} %get-tuple-element.25), channel_id=1, source_target_pairs={{0,15},{3,4},{4,3},{7,8},{8,7},{11,12},{12,11},{15,0},{16,31},{19,... | collective-permute-start | bytes 24584 | tf_op jit(solution)/shard_map/ppermute | solution.py:464
  34.1 4.8 %collective-permute-start.9 = (f32[8,256]{1,0:T(8,128)S(1)}, f32[8,256]{1,0:T(8,128)S(1)}, u32[]{:S(2)}, u32[]{:S(2)}) collective-permute-start(f32[8,256]{1,0:T(8,128)S(1)} %slice_add_fusion.refs_9_), channel_id=1, source_target_pairs={{1,0},{2,3},{5,4},{6,7},{9,8},{10,11},{13,12},{14,15},{17,16},{18,... | collective-permute-start | bytes 24584 | tf_op jit(solution)/shard_map/ppermute | solution.py:464
  35.4 1.2 %copy-start = (bf16[8,4,64,256]{3,2,1,0:T(8,128)(2,1)S(1)}, bf16[8,4,64,256]{3,2,1,0:T(8,128)(2,1)}, u32[]{:S(2)}) copy-start(bf16[8,4,64,256]{3,2,1,0:T(8,128)(2,1)} %refs_3_.1) | copy-start | bytes 3145732

commit v6 on v3

--- a/solution.py
+++ b/solution.py
@@ -28,7 +28,7 @@
     return jnp.where(inside, 1.0 - dist / (HALO + 1), 0.0)
 
 
-def obs_kernel(odd_ref, cells_ref, index_ref, value_ref, var_ref, own_ref, near_ref, far_ref):
+def obs_kernel(odd_ref, cells_ref, index_ref, value_ref, var_ref, own_ref, near_ref, far_ref, part_ref):
     lon_dev, _, lat, members = cells_ref.shape
     nobs = index_ref.shape[1]
     rows = cells_ref[:, 0].reshape(lon_dev * lat, members)
@@ -49,8 +49,7 @@
     spread = jnp.sum((seen - centre) ** 2, axis=1, keepdims=True) * (1.0 / (members - 1))
     innovation = (value - centre) ** 2 / (var + spread)
     blocks, members = own_ref.shape
-    part = jnp.broadcast_to(jnp.sum(innovation, axis=0, keepdims=True), (TILE, members))
-    near_ref[blocks:, :] = part
+    part_ref[...] = jnp.broadcast_to(jnp.sum(innovation, axis=0, keepdims=True), part_ref.shape)
     terms = (value - seen) ** 2 * (1.0 / var)
     lon = (index // lat).astype(jnp.float32)
     along = index.astype(jnp.float32) - lon * lat
@@ -62,19 +61,19 @@
         jnp.concatenate(weights, axis=0), terms, precision=HIGH, preferred_element_type=jnp.float32
     )
     own_ref[...] = like[:blocks]
-    near_ref[:blocks, :] = like[blocks : 2 * blocks]
+    near_ref[...] = like[blocks : 2 * blocks]
     far_ref[...] = like[2 * blocks :]
 
 
-def observe(odd, state, obs_index, obs_value, obs_var):
+def observe(odd, state, obs_index, obs_value, obs_var, parts):
     lon_dev, _, lat, members = state.shape
     nobs = obs_index.shape[0]
     blocks = lat // REGION
     row = pl.BlockSpec((1, nobs), lambda i: (0, 0))
     like = jax.ShapeDtypeStruct((blocks, members), jnp.float32)
     like_spec = pl.BlockSpec((blocks, members), lambda i: (0, 0))
-    more = jax.ShapeDtypeStruct((blocks + TILE, members), jnp.float32)
-    more_spec = pl.BlockSpec((blocks + TILE, members), lambda i: (0, 0))
+    part = jax.ShapeDtypeStruct((parts * TILE, 128), jnp.float32)
+    part_spec = pl.BlockSpec((parts * TILE, 128), lambda i: (0, 0))
     return pl.pallas_call(
         obs_kernel,
         grid=(1,),
@@ -85,8 +84,8 @@
             row,
             row,
         ],
-        out_specs=[like_spec, more_spec, like_spec],
-        out_shape=[like, more, like],
+        out_specs=[like_spec] * 3 + [part_spec],
+        out_shape=[like] * 3 + [part],
         compiler_params=pltpu.CompilerParams(vmem_limit_bytes=32 * 2**20),
         name="observe",
     )(odd, state, obs_index[None], obs_value[None], obs_var[None])
@@ -329,8 +328,8 @@
     pairs = regions // PAIR
     size = PAIR * TILE
 
-    total = sum_ref[0:1, 0:1] + far_ref[regions : regions + 1, 0:1]
-    like = own_ref[...] + near_ref[:regions, :] + far_ref[:regions, :]
+    total = jnp.sum(sum_ref[...], axis=0, keepdims=True)[:, 0:1] * (1.0 / TILE)
+    like = own_ref[...] + near_ref[...] + far_ref[...]
     like = -0.5 * (count / total) * like
     like = like - jnp.max(like, axis=1, keepdims=True)
     logw = (like - jnp.log(jnp.sum(jnp.exp(like), axis=1, keepdims=True))) * LOG2E
@@ -438,18 +437,15 @@
     far = lax.ppermute(for_far, "lon", far_pairs)
     near = lax.ppermute(for_near, "lon", near_pairs)
     odd = odd.astype(jnp.int32).reshape(1)
-    own_like, near_like, far_like = observe(odd, state, obs_index, obs_value, obs_var)
-    blocks = own_like.shape[0]
+    own_like, near_like, far_like, part = observe(
+        odd, state, obs_index, obs_value, obs_var, count
+    )
+    got_far = lax.ppermute(far_like, "lon", far_pairs)
     got_near = lax.ppermute(near_like, "lon", near_pairs)
-    total = near_like[blocks:] + got_near[blocks:]
-    hop = 4
-    while hop < count:
-        total = total + lax.ppermute(total, "lon", [(i, i ^ hop) for i in range(count)])
-        hop *= 2
-    got_far = lax.ppermute(jnp.concatenate([far_like, total], axis=0), "lon", far_pairs)
+    parts = lax.all_to_all(part, "lon", 0, 0, tiled=True)
     gram = own_gram(odd, state, near)
     nobs = float(obs_index.shape[0] * count)
-    return analyse(odd, far, state, gram, own_like, got_near, got_far, total, nobs)
+    return analyse(odd, far, state, gram, own_like, got_near, got_far, parts, nobs)
 
 
 def solution(mesh):

time: 41.2 us -> 39 us (0.947)
  waiting for transfers between devices: 13.1 us -> 0.01 us
  starting transfers between devices: 7.95 us -> 14.3 us
  local copies, waits for them, and re-layouts: 1.4 us -> 4.04 us
  Pallas kernels: 18.5 us -> 20.2 us
    ppermute x3 -> x1, waiting for transfers between devices: 12 us -> 0.01 us  [on_device(): got_far = lax.ppermute(far_like, 'lon', far_pairs)]
    all_to_all x0 -> x1, starting transfers between devices: none -> 3.49 us  [on_device(): parts = lax.all_to_all(part, 'lon', 0, 0, tiled=True)]
    ppermute x3 -> x1, starting transfers between devices: 1.71 us -> 4.42 us  [on_device(): got_far = lax.ppermute(far_like, 'lon', far_pairs)]
    unnamed x8 -> x12, local copies, waits for them, and re-layouts: 0.01 us -> 1.85 us
    ppermute x1, waiting for transfers between devices: 1.17 us -> 0.01 us  [on_device(): got_near = lax.ppermute(near_like, 'lon', near_pairs)]
    pallas_call x1, Pallas kernels: 16 us -> 17.1 us  [analyse(): pl.pallas_call(functools.partial(analysis_kernel, count, scale), in_specs...]
    dynamic_slice x1, local copies, waits for them, and re-layouts: 1.39 us -> 2.19 us  [on_device(): lax.dynamic_slice_in_dim(state, (1 - odd) * (lon_dev - HALO), HALO, axis=0)]
    pallas_call x1, Pallas kernels: 0.78 us -> 1.42 us  [observe(): pl.pallas_call(obs_kernel, grid=(1,), in_specs=[pl.BlockSpec(memory_space...]
  transfers between devices with their start and end apart: 6 -> 5, of which waited for: 4 -> 0; matrix products, arithmetic and copies ran while one was open for 0% -> 0% of each run, Pallas kernels for 6% -> 8%
where the time goes in v6:
time: 39 us; the launch traced here: 38.7 us
  Pallas kernels  20.2 us (52%)
  starting transfers between devices  14.3 us (37%)
  local copies, waits for them, and re-layouts  4.04 us (10%)
    pallas_call x1, Pallas kernels, analyse(): pl.pallas_call(functools.partial(analysis_kernel, count, scale), in_specs...  17.1 us
    ppermute x1, starting transfers between devices, on_device(): far = lax.ppermute(for_far, 'lon', far_pairs)  5.67 us
    ppermute x1, starting transfers between devices, on_device(): got_far = lax.ppermute(far_like, 'lon', far_pairs)  4.42 us
    all_to_all x1, starting transfers between devices, on_device(): parts = lax.all_to_all(part, 'lon', 0, 0, tiled=True)  3.49 us
    dynamic_slice x1, local copies, waits for them, and re-layouts, on_device(): lax.dynamic_slice_in_dim(state, (1 - odd) * (lon_dev - HALO), HALO, axis=0)  2.19 us
    unnamed x12, local copies, waits for them, and re-layouts  1.85 us
    pallas_call x1, Pallas kernels, own_gram(): pl.pallas_call(own_gram_kernel, grid=(steps,), in_specs=[pl.BlockSpec(mem...  1.72 us
    pallas_call x1, Pallas kernels, observe(): pl.pallas_call(obs_kernel, grid=(1,), in_specs=[pl.BlockSpec(memory_space...  1.42 us
  transfers between devices with their start and end apart: 5, of which 0 were waited for; matrix products, arithmetic and copies ran while one was open for 0% of the time, Pallas kernels for 8%

profile of v6, /device:TPU:0, one launch (start us, length us, event | category | flops | bytes accessed | tf_op | source)
XLA Modules:
  0.0 38.7 jit_solution(15127925717201546401)
XLA Ops:
  0.0 0.0 copy-start
  0.0 0.0 copy-start.5
  0.0 0.0 copy-start.4
  0.0 0.0 copy-start.3
  0.0 2.2 %constant_dynamic-slice_fusion = (bf16[4,4,64,256]{3,2,1,0:T(8,128)(2,1)S(1)}, bf16[4,4,64,256]{3,2,1,0:T(8,128)(2,1)}) fusion(bf16[8,4,64,256]{3,2,1,0:T(8,128)(2,1)} %refs_2_.1, s32[]{:T(128)S(6)} %select_n.15, s32[]{:T(128)S(6)} %select_n.14), kind=kLoop, calls=%fused_computation | loop fusion | bytes 2097160 | tf_op jit(solution)/shard_map/dynamic_slice | solution.py:436
  2.2 0.5 %collective-permute-start.1 = (bf16[4,4,64,256]{3,2,1,0:T(8,128)(2,1)S(1)}, bf16[4,4,64,256]{3,2,1,0:T(8,128)(2,1)S(1)}, u32[]{:S(2)}, u32[]{:S(2)}) collective-permute-start(bf16[4,4,64,256]{3,2,1,0:T(8,128)(2,1)S(1)} %get-tuple-element.13), channel_id=1, source_target_pairs={{0,1},{1,0},{2,3},{3,2},{4,5},{5,4},{6,7},{7,6},{8,9},{9,8},{10,11... | collective-permute-start | bytes 1572872 | tf_op jit(solution)/shard_map/ppermute | solution.py:438
  2.7 5.7 %collective-permute-start = (bf16[4,4,64,256]{3,2,1,0:T(8,128)(2,1)}, bf16[4,4,64,256]{3,2,1,0:T(8,128)(2,1)}, u32[]{:S(2)}, u32[]{:S(2)}) collective-permute-start(bf16[4,4,64,256]{3,2,1,0:T(8,128)(2,1)} %get-tuple-element.14), channel_id=1, source_target_pairs={{0,15},{1,2},{2,1},{3,4},{4,3},{5,6},{6,5},{7,8},{8,7},{9,10},{10,... | collective-permute-start | bytes 1572872 | tf_op jit(solution)/shard_map/ppermute | solution.py:437
  8.3 0.0 copy-done
  8.4 0.0 copy-done.5
  8.4 0.0 copy-done.4
  8.4 0.0 copy-done.3
  8.4 1.4 %observe.1 = (f32[8,256]{1,0:T(8,128)S(1)}, f32[8,256]{1,0:T(8,128)S(1)}, f32[8,256]{1,0:T(8,128)S(1)}, f32[128,128]{1,0:T(8,128)}) custom-call(s32[1]{0:T(128)} %bitcast.odd_ref.refs_0_, bf16[8,4,64,256]{3,2,1,0:T(8,128)(2,1)S(1)} %copy-done, s32[1,256]{1,0:T(1,128)S(1)} %bitcast.7, f32[1,256]{1,0:T(1,128)S(1)} %bitcast.8, f32[1,256]{1,0:T(1,128)S(1)} %bitcast.9), custom_call_target="tpu_custom_call" | custom-call | tf_op jit(solution)/shard_map/observe/pallas_call | solution.py:77
  9.8 3.5 %all-to-all-start = ((f32[16,8,128]{2,1,0:T(8,128)}), f32[16,8,128]{2,1,0:T(8,128)S(1)}, u32[]{:S(2)}, u32[]{:S(2)}) async-start(f32[16,8,128]{2,1,0:T(8,128)} %bitcast.4), calls=%async_computation | async-start | bytes 131072 | tf_op jit(solution)/shard_map/all_to_all | solution.py:445
  13.3 0.3 collective-permute-start.2
  13.6 4.4 %collective-permute-start.3 = (f32[8,256]{1,0:T(8,128)S(1)}, f32[8,256]{1,0:T(8,128)S(1)}, u32[]{:S(2)}, u32[]{:S(2)}) collective-permute-start(f32[8,256]{1,0:T(8,128)S(1)} %get-tuple-element.11), channel_id=1, source_target_pairs={{0,15},{1,2},{2,1},{3,4},{4,3},{5,6},{6,5},{7,8},{8,7},{9,10},{10,... | collective-permute-start | bytes 24584 | tf_op jit(solution)/shard_map/ppermute | solution.py:443
  18.0 0.0 collective-permute-done.1.near_ref
  18.0 0.0 copy-start.1
  18.0 0.8 %copy-done.1 = bf16[4,4,64,256]{3,2,1,0:T(8,128)(2,1)} copy-done((bf16[4,4,64,256]{3,2,1,0:T(8,128)(2,1)}, bf16[4,4,64,256]{3,2,1,0:T(8,128)(2,1)S(1)}, u32[]{:S(2)}) %copy-start.1) | copy-done | bytes 524312
  18.8 0.0 copy-start.2
  18.8 1.0 %copy-done.2 = bf16[4,4,64,256]{3,2,1,0:T(8,128)(2,1)S(1)} copy-done((bf16[4,4,64,256]{3,2,1,0:T(8,128)(2,1)S(1)}, bf16[4,4,64,256]{3,2,1,0:T(8,128)(2,1)}, u32[]{:S(2)}) %copy-start.2) | copy-done | bytes 524312
  19.8 1.7 %own_gram.1.refs_3_ = f32[8,256,256]{2,1,0:T(8,128)S(1)} custom-call(s32[1]{0:T(128)} %bitcast.odd_ref.refs_0_, bf16[8,4,64,256]{3,2,1,0:T(8,128)(2,1)S(1)} %copy-done, bf16[4,4,64,256]{3,2,1,0:T(8,128)(2,1)S(1)} %copy-done.2), custom_call_target="tpu_custom_call" | custom-call | tf_op jit(solution)/shard_map/own_gram/pallas_call | solution.py:156
  21.6 0.0 collective-permute-done.2.refs_5_
  21.6 0.0 collective-permute-done.3.refs_6_
  21.6 0.0 all-to-all-done
  21.6 0.0 collective-permute-done.refs_1_
  21.6 17.1 %analyse.1 = bf16[8,4,64,256]{3,2,1,0:T(8,128)(2,1)} custom-call(s32[1]{0:T(128)} %bitcast.odd_ref.refs_0_, bf16[4,4,64,256]{3,2,1,0:T(8,128)(2,1)} %collective-permute-done.refs_1_, bf16[8,4,64,256]{3,2,1,0:T(8,128)(2,1)S(1)} %copy-done, f32[8,256,256]{2,1,0:T(8,128)S(1)} %own_gram.1.refs_3_, f32[8,256]{1,0:T(8,128)S(1)} %get-tuple-element.9.refs_4_, ...), custom_call_target="tpu_custom_call" | custom-call | tf_op jit(solution)/shard_map/analyse/pallas_call | solution.py:410
Async XLA Ops:
  0.0 8.4 %copy-start = (bf16[8,4,64,256]{3,2,1,0:T(8,128)(2,1)S(1)}, bf16[8,4,64,256]{3,2,1,0:T(8,128)(2,1)}, u32[]{:S(2)}) copy-start(bf16[8,4,64,256]{3,2,1,0:T(8,128)(2,1)} %refs_2_.1) | copy-start | bytes 3145732
  0.0 8.4 %copy-start.5 = (f32[256]{0:T(256)S(1)}, f32[256]{0:T(256)}, u32[]{:S(2)}) copy-start(f32[256]{0:T(256)} %param.7) | copy-start | bytes 3076
  0.0 8.4 %copy-start.4 = (f32[256]{0:T(256)S(1)}, f32[256]{0:T(256)}, u32[]{:S(2)}) copy-start(f32[256]{0:T(256)} %param.6) | copy-start | bytes 3076
  0.0 8.4 %copy-start.3 = (s32[256]{0:T(256)S(1)}, s32[256]{0:T(256)}, u32[]{:S(2)}) copy-start(s32[256]{0:T(256)} %param.5) | copy-start | bytes 3076
  2.2 15.8 %collective-permute-start.1 = (bf16[4,4,64,256]{3,2,1,0:T(8,128)(2,1)S(1)}, bf16[4,4,64,256]{3,2,1,0:T(8,128)(2,1)S(1)}, u32[]{:S(2)}, u32[]{:S(2)}) collective-permute-start(bf16[4,4,64,256]{3,2,1,0:T(8,128)(2,1)S(1)} %get-tuple-element.13), channel_id=1, source_target_pairs={{0,1},{1,0},{2,3},{3,2},{4,5},{5,4},{6,7},{7,6},{8,9},{9,8},{10,11... | collective-permute-start | bytes 1572872 | tf_op jit(solution)/shard_map/ppermute | solution.py:438
  2.7 18.9 %collective-permute-start = (bf16[4,4,64,256]{3,2,1,0:T(8,128)(2,1)}, bf16[4,4,64,256]{3,2,1,0:T(8,128)(2,1)}, u32[]{:S(2)}, u32[]{:S(2)}) collective-permute-start(bf16[4,4,64,256]{3,2,1,0:T(8,128)(2,1)} %get-tuple-element.14), channel_id=1, source_target_pairs={{0,15},{1,2},{2,1},{3,4},{4,3},{5,6},{6,5},{7,8},{8,7},{9,10},{10,... | collective-permute-start | bytes 1572872 | tf_op jit(solution)/shard_map/ppermute | solution.py:437
  9.8 11.8 %all-to-all-start = ((f32[16,8,128]{2,1,0:T(8,128)}), f32[16,8,128]{2,1,0:T(8,128)S(1)}, u32[]{:S(2)}, u32[]{:S(2)}) async-start(f32[16,8,128]{2,1,0:T(8,128)} %bitcast.4), calls=%async_computation | async-start | bytes 131072 | tf_op jit(solution)/shard_map/all_to_all | solution.py:445
  13.3 8.3 %collective-permute-start.2 = (f32[8,256]{1,0:T(8,128)S(1)}, f32[8,256]{1,0:T(8,128)S(1)}, u32[]{:S(2)}, u32[]{:S(2)}) collective-permute-start(f32[8,256]{1,0:T(8,128)S(1)} %get-tuple-element.10), channel_id=1, source_target_pairs={{0,1},{1,0},{2,3},{3,2},{4,5},{5,4},{6,7},{7,6},{8,9},{9,8},{10,11... | collective-permute-start | bytes 24584 | tf_op jit(solution)/shard_map/ppermute | solution.py:444
  13.6 8.0 %collective-permute-start.3 = (f32[8,256]{1,0:T(8,128)S(1)}, f32[8,256]{1,0:T(8,128)S(1)}, u32[]{:S(2)}, u32[]{:S(2)}) collective-permute-start(f32[8,256]{1,0:T(8,128)S(1)} %get-tuple-element.11), channel_id=1, source_target_pairs={{0,15},{1,2},{2,1},{3,4},{4,3},{5,6},{6,5},{7,8},{8,7},{9,10},{10,... | collective-permute-start | bytes 24584 | tf_op jit(solution)/shard_map/ppermute | solution.py:443
  18.0 0.8 %copy-start.1 = (bf16[4,4,64,256]{3,2,1,0:T(8,128)(2,1)}, bf16[4,4,64,256]{3,2,1,0:T(8,128)(2,1)S(1)}, u32[]{:S(2)}) copy-start(bf16[4,4,64,256]{3,2,1,0:T(8,128)(2,1)S(1)} %collective-permute-done.1.near_ref) | copy-start | bytes 1572868
  18.8 1.0 %copy-start.2 = (bf16[4,4,64,256]{3,2,1,0:T(8,128)(2,1)S(1)}, bf16[4,4,64,256]{3,2,1,0:T(8,128)(2,1)}, u32[]{:S(2)}) copy-start(bf16[4,4,64,256]{3,2,1,0:T(8,128)(2,1)} %copy-done.1) | copy-start | bytes 1572868

commit v7 on v6

--- a/solution.py
+++ b/solution.py
@@ -28,10 +28,44 @@
     return jnp.where(inside, 1.0 - dist / (HALO + 1), 0.0)
 
 
-def obs_kernel(odd_ref, cells_ref, index_ref, value_ref, var_ref, own_ref, near_ref, far_ref, part_ref):
-    lon_dev, _, lat, members = cells_ref.shape
+def in_parts(values):
+    high = values.astype(jnp.bfloat16).astype(jnp.float32)
+    middle = (values - high).astype(jnp.bfloat16).astype(jnp.float32)
+    low = values - high - middle
+    return jnp.concatenate([high, middle, low, jnp.zeros_like(low)], axis=0).astype(jnp.bfloat16)
+
+
+def from_parts(ref, start):
+    rows = ref[start : start + 4 * TILE, :].astype(jnp.float32)
+    return rows[:TILE] + rows[TILE : 2 * TILE] + rows[2 * TILE : 3 * TILE]
+
+
+def observe_kernel(*refs):
+    odd_ref, state_ref, rows_ref = refs[:3]
+    own_ref, near_ref, far_ref, part_ref = refs[6:10]
+    cells_ref, index_ref, value_ref, var_ref, sems = refs[10:]
+    lon_dev, lat, members = cells_ref.shape
     nobs = index_ref.shape[1]
-    rows = cells_ref[:, 0].reshape(lon_dev * lat, members)
+    edge = rows_ref.shape[0] // lon_dev * HALO
+    last = rows_ref.shape[0] - edge
+    far_at = pl.multiple_of(odd_ref[0] * last, 16)
+    near_at = pl.multiple_of(last - far_at, 16)
+    fetches = [
+        (refs[3], index_ref),
+        (refs[4], value_ref),
+        (refs[5], var_ref),
+        (state_ref.at[:, 0], cells_ref),
+        (rows_ref.at[pl.ds(far_at, edge), :], far_ref.at[pl.ds(0, edge), :]),
+        (rows_ref.at[pl.ds(near_at, edge), :], near_ref.at[pl.ds(0, edge), :]),
+    ]
+    copies = [
+        pltpu.make_async_copy(src, dst, sems.at[i]) for i, (src, dst) in enumerate(fetches)
+    ]
+    for copy in copies:
+        copy.start()
+    for copy in copies[:4]:
+        copy.wait()
+    rows = cells_ref[...].reshape(lon_dev * lat, members)
     index = index_ref[...]
     sub = lax.broadcasted_iota(jnp.int32, (TILE, nobs), 0)
     table = jnp.where(
@@ -48,11 +82,11 @@
     centre = jnp.sum(seen, axis=1, keepdims=True) * (1.0 / members)
     spread = jnp.sum((seen - centre) ** 2, axis=1, keepdims=True) * (1.0 / (members - 1))
     innovation = (value - centre) ** 2 / (var + spread)
-    blocks, members = own_ref.shape
     part_ref[...] = jnp.broadcast_to(jnp.sum(innovation, axis=0, keepdims=True), part_ref.shape)
     terms = (value - seen) ** 2 * (1.0 / var)
     lon = (index // lat).astype(jnp.float32)
     along = index.astype(jnp.float32) - lon * lat
+    blocks = own_ref.shape[0]
     block = lax.broadcasted_iota(jnp.int32, (blocks, nobs), 0).astype(jnp.float32)
     across = line_weight(along - REGION * block + HALO)
     side = jnp.where(odd_ref[0] == 1, float(REGION), float(-REGION))
@@ -61,41 +95,50 @@
         jnp.concatenate(weights, axis=0), terms, precision=HIGH, preferred_element_type=jnp.float32
     )
     own_ref[...] = like[:blocks]
-    near_ref[...] = like[blocks : 2 * blocks]
-    far_ref[...] = like[2 * blocks :]
+    near_ref[edge:, :] = in_parts(like[blocks : 2 * blocks])
+    far_ref[edge:, :] = in_parts(like[2 * blocks :])
+    for copy in copies[4:]:
+        copy.wait()
 
 
 def observe(odd, state, obs_index, obs_value, obs_var, parts):
-    lon_dev, _, lat, members = state.shape
-    nobs = obs_index.shape[0]
-    blocks = lat // REGION
-    row = pl.BlockSpec((1, nobs), lambda i: (0, 0))
-    like = jax.ShapeDtypeStruct((blocks, members), jnp.float32)
-    like_spec = pl.BlockSpec((blocks, members), lambda i: (0, 0))
+    lon_dev, nvar, lat, members = state.shape
+    nobs = obs_index.size
+    assert lat // REGION == TILE
+    like = jax.ShapeDtypeStruct((lat // REGION, members), jnp.float32)
+    payload = jax.ShapeDtypeStruct((HALO * nvar * lat + 4 * TILE, members), state.dtype)
     part = jax.ShapeDtypeStruct((parts * TILE, 128), jnp.float32)
-    part_spec = pl.BlockSpec((parts * TILE, 128), lambda i: (0, 0))
+    arrays = state, state.reshape(-1, members), obs_index[None], obs_value[None], obs_var[None]
     return pl.pallas_call(
-        obs_kernel,
-        grid=(1,),
-        in_specs=[
-            pl.BlockSpec(memory_space=pltpu.SMEM),
-            pl.BlockSpec((lon_dev, 1, lat, members), lambda i: (0, 0, 0, 0)),
-            row,
-            row,
-            row,
+        observe_kernel,
+        in_specs=[pl.BlockSpec(memory_space=pltpu.SMEM)]
+        + [pl.BlockSpec(memory_space=pltpu.HBM)] * len(arrays),
+        out_specs=[pl.BlockSpec(memory_space=pltpu.VMEM)] * 4,
+        out_shape=[like, payload, payload, part],
+        scratch_shapes=[
+            pltpu.VMEM((lon_dev, lat, members), state.dtype),
+            pltpu.VMEM((1, nobs), jnp.int32),
+            pltpu.VMEM((1, nobs), jnp.float32),
+            pltpu.VMEM((1, nobs), jnp.float32),
+            pltpu.SemaphoreType.DMA((6,)),
         ],
-        out_specs=[like_spec] * 3 + [part_spec],
-        out_shape=[like] * 3 + [part],
-        compiler_params=pltpu.CompilerParams(vmem_limit_bytes=32 * 2**20),
+        compiler_params=pltpu.CompilerParams(vmem_limit_bytes=16 * 2**20),
         name="observe",
-    )(odd, state, obs_index[None], obs_value[None], obs_var[None])
+    )(odd, *[pltpu.with_memory_space_constraint(x, pltpu.HBM) for x in arrays])
 
 
 def pair_tiles(ref, step, steps):
     size = PAIR * TILE
+    lat = steps * size
 
     def load(at):
-        return ref[:, :, pl.ds(pl.multiple_of(at * size, size), size), :].astype(jnp.float32)
+        at = pl.multiple_of(at * size, size)
+        if len(ref.shape) == 4:
+            return ref[:, :, pl.ds(at, size), :].astype(jnp.float32)
+        planes = ref.shape[0] // lat
+        rows = [ref[pl.ds(i * lat + at, size), :] for i in range(planes)]
+        rows = jnp.stack(rows).astype(jnp.float32)
+        return rows.reshape(HALO, planes // HALO, size, rows.shape[-1])
 
     here = load(step)
     before = load(jnp.maximum(step - 1, 0))[:, :, TILE:]
@@ -159,11 +202,11 @@
         in_specs=[
             pl.BlockSpec(memory_space=pltpu.SMEM),
             pl.BlockSpec(state.shape, lambda i: (0, 0, 0, 0)),
-            pl.BlockSpec(near.shape, lambda i: (0, 0, 0, 0)),
+            pl.BlockSpec(near.shape, lambda i: (0, 0)),
         ],
         out_specs=pl.BlockSpec((PAIR, members, members), lambda i: (i, 0, 0)),
         out_shape=jax.ShapeDtypeStruct((steps * PAIR, members, members), jnp.float32),
-        compiler_params=pltpu.CompilerParams(vmem_limit_bytes=48 * 2**20),
+        compiler_params=pltpu.CompilerParams(vmem_limit_bytes=24 * 2**20),
         name="own_gram",
     )(odd, state, near)
 
@@ -322,14 +365,15 @@
 
 def analysis_kernel(count, scale, *refs):
     odd_ref, halo_ref, state_ref, gram_in_ref = refs[0:4]
-    own_ref, near_ref, far_ref, sum_ref, out_ref = refs[4:9]
-    gram_ref, kernel_ref, ratio_ref, weight_ref, logw_ref, result_ref, sems = refs[9:]
+    own_ref, near_ref, sum_ref, out_ref = refs[4:8]
+    gram_ref, kernel_ref, ratio_ref, weight_ref, logw_ref, result_ref, sems = refs[8:]
     regions, members = gram_in_ref.shape[0], gram_in_ref.shape[-1]
     pairs = regions // PAIR
     size = PAIR * TILE
 
     total = jnp.sum(sum_ref[...], axis=0, keepdims=True)[:, 0:1] * (1.0 / TILE)
-    like = own_ref[...] + near_ref[...] + far_ref[...]
+    halo = halo_ref.shape[0] - 4 * TILE
+    like = own_ref[...] + from_parts(near_ref, 0) + from_parts(halo_ref, halo)
     like = -0.5 * (count / total) * like
     like = like - jnp.max(like, axis=1, keepdims=True)
     logw = (like - jnp.log(jnp.sum(jnp.exp(like), axis=1, keepdims=True))) * LOG2E
@@ -400,7 +444,7 @@
         lax.fori_loop(0, pairs, again, 0)
 
 
-def analyse(odd, halo, state, gram, own, near, far, total, count):
+def analyse(odd, halo, state, gram, own, near, total, count):
     lon_dev, nvar, lat, members = state.shape
     regions = lat // REGION
     offsets = range(REGION + 2 * HALO)
@@ -409,7 +453,7 @@
     vmem = pl.BlockSpec(memory_space=pltpu.VMEM)
     return pl.pallas_call(
         functools.partial(analysis_kernel, count, scale),
-        in_specs=[pl.BlockSpec(memory_space=pltpu.SMEM)] + [vmem] * 7,
+        in_specs=[pl.BlockSpec(memory_space=pltpu.SMEM)] + [vmem] * 6,
         out_specs=pl.BlockSpec(memory_space=pl.ANY),
         out_shape=jax.ShapeDtypeStruct(state.shape, state.dtype),
         scratch_shapes=[
@@ -421,31 +465,25 @@
             pltpu.VMEM((regions // PAIR, lon_dev, nvar, PAIR * TILE, members), jnp.bfloat16),
             pltpu.SemaphoreType.DMA((regions // PAIR,)),
         ],
-        compiler_params=pltpu.CompilerParams(vmem_limit_bytes=48 * 2**20),
+        compiler_params=pltpu.CompilerParams(vmem_limit_bytes=24 * 2**20),
         name="analyse",
-    )(odd, halo, state, gram, own, near, far, total)
+    )(odd, halo, state, gram, own, near, total)
 
 
 def on_device(state, obs_index, obs_value, obs_var):
-    lon_dev = state.shape[0]
     count = lax.axis_size("lon")
     odd = lax.axis_index("lon") % 2
     near_pairs = [(i, i ^ 1) for i in range(count)]
     far_pairs = [(i, (i + 1 if i % 2 else i - 1) % count) for i in range(count)]
-    for_far = lax.dynamic_slice_in_dim(state, odd * (lon_dev - HALO), HALO, axis=0)
-    for_near = lax.dynamic_slice_in_dim(state, (1 - odd) * (lon_dev - HALO), HALO, axis=0)
+    odd = odd.astype(jnp.int32).reshape(1)
+    own_like, for_near, for_far, part = observe(odd, state, obs_index, obs_value, obs_var, count)
     far = lax.ppermute(for_far, "lon", far_pairs)
     near = lax.ppermute(for_near, "lon", near_pairs)
-    odd = odd.astype(jnp.int32).reshape(1)
-    own_like, near_like, far_like, part = observe(
-        odd, state, obs_index, obs_value, obs_var, count
-    )
-    got_far = lax.ppermute(far_like, "lon", far_pairs)
-    got_near = lax.ppermute(near_like, "lon", near_pairs)
     parts = lax.all_to_all(part, "lon", 0, 0, tiled=True)
+    near_like = near[near.shape[0] - 4 * TILE :]
     gram = own_gram(odd, state, near)
     nobs = float(obs_index.shape[0] * count)
-    return analyse(odd, far, state, gram, own_like, got_near, got_far, parts, nobs)
+    return analyse(odd, far, state, gram, own_like, near_like, parts, nobs)
 
 
 def solution(mesh):

time: 39 us -> 37.3 us (0.956)
  the two profiles are of different devices: /device:TPU:0 before, /device:TPU:1 now
where the time goes in v7:
time: 37.3 us; the launch traced here: 36.7 us
  Pallas kernels  21.6 us (58%)
  starting transfers between devices  9.51 us (25%)
  waiting for transfers between devices  3.65 us (10%)
  local copies, waits for them, and re-layouts  1.85 us (5%)
    pallas_call x1, Pallas kernels, analyse(): pl.pallas_call(functools.partial(analysis_kernel, count, scale), in_specs...  17.2 us
    all_to_all x1, starting transfers between devices, on_device(): parts = lax.all_to_all(part, 'lon', 0, 0, tiled=True)  6.74 us
    all_to_all x1, waiting for transfers between devices, on_device(): parts = lax.all_to_all(part, 'lon', 0, 0, tiled=True)  3.64 us
    pallas_call x1, Pallas kernels, observe(): pl.pallas_call(observe_kernel, in_specs=[pl.BlockSpec(memory_space=pltpu....  2.72 us
    ppermute x1, starting transfers between devices, on_device(): far = lax.ppermute(for_far, 'lon', far_pairs)  2.65 us
    unnamed x6, local copies, waits for them, and re-layouts  1.84 us
    pallas_call x1, Pallas kernels, own_gram(): pl.pallas_call(own_gram_kernel, grid=(steps,), in_specs=[pl.BlockSpec(mem...  1.74 us
  transfers between devices with their start and end apart: 3, of which 1 were waited for; matrix products, arithmetic and copies ran while one was open for 0% of the time, Pallas kernels for 5%

profile of v7, /device:TPU:1, one launch (start us, length us, event | category | flops | bytes accessed | tf_op | source)
XLA Modules:
  0.0 36.7 jit_solution(10151668210942368098)
XLA Ops:
  0.0 0.0 copy-start
  0.0 2.7 %observe.1 = (f32[8,256]{1,0:T(8,128)S(1)}, bf16[1056,256]{1,0:T(8,128)(2,1)S(1)}, bf16[1056,256]{1,0:T(8,128)(2,1)}, f32[128,128]{1,0:T(8,128)}) custom-call(s32[1]{0:T(128)} %bitcast.refs_0_.odd_ref, bf16[8,4,64,256]{3,2,1,0:T(8,128)(2,1)} %refs_2_.1, bf16[2048,256]{1,0:T(8,128)(2,1)} %bitcast.7, s32[1,256]{1,0:T(1,128)} %bitcast.9, f32[1,256]{1,0:T(1,128)} %bitcast.10, ...), custom_call_target="tpu_custom_call" | custom-call | tf_op jit(solution)/shard_map/observe/pallas_call | solution.py:112
  2.7 0.1 collective-permute-start.1
  2.9 2.7 %collective-permute-start = (bf16[1056,256]{1,0:T(8,128)(2,1)}, bf16[1056,256]{1,0:T(8,128)(2,1)}, u32[]{:S(2)}, u32[]{:S(2)}) collective-permute-start(bf16[1056,256]{1,0:T(8,128)(2,1)} %get-tuple-element.9), channel_id=1, source_target_pairs={{0,15},{1,2},{2,1},{3,4},{4,3},{5,6},{6,5},{7,8},{8,7},{9,10},{10,... | collective-permute-start | bytes 1622024 | tf_op jit(solution)/shard_map/ppermute | solution.py:480
  5.5 6.7 %all-to-all-start = ((f32[16,8,128]{2,1,0:T(8,128)}), f32[16,8,128]{2,1,0:T(8,128)S(1)}, u32[]{:S(2)}, u32[]{:S(2)}) async-start(f32[16,8,128]{2,1,0:T(8,128)} %bitcast.5), calls=%async_computation | async-start | bytes 131072 | tf_op jit(solution)/shard_map/all_to_all | solution.py:482
  12.3 0.0 collective-permute-done.1.near_ref
  12.3 0.0 copy-start.1
  12.3 0.8 %copy-done.1 = bf16[1056,256]{1,0:T(8,128)(2,1)} copy-done((bf16[1056,256]{1,0:T(8,128)(2,1)}, bf16[1056,256]{1,0:T(8,128)(2,1)S(1)}, u32[]{:S(2)}) %copy-start.1) | copy-done | bytes 540696
  13.1 0.0 copy-done
  13.1 0.0 copy-start.2
  13.1 1.0 %copy-done.2 = bf16[1056,256]{1,0:T(8,128)(2,1)S(1)} copy-done((bf16[1056,256]{1,0:T(8,128)(2,1)S(1)}, bf16[1056,256]{1,0:T(8,128)(2,1)}, u32[]{:S(2)}) %copy-start.2) | copy-done | bytes 540696
  14.1 1.7 %own_gram.1.refs_3_ = f32[8,256,256]{2,1,0:T(8,128)S(1)} custom-call(s32[1]{0:T(128)} %bitcast.refs_0_.odd_ref, bf16[8,4,64,256]{3,2,1,0:T(8,128)(2,1)S(1)} %copy-done, bf16[1056,256]{1,0:T(8,128)(2,1)S(1)} %copy-done.2), custom_call_target="tpu_custom_call" | custom-call | tf_op jit(solution)/shard_map/own_gram/pallas_call | solution.py:199
  15.9 3.6 %all-to-all-done = f32[16,8,128]{2,1,0:T(8,128)S(1)} async-done(((f32[16,8,128]{2,1,0:T(8,128)}), f32[16,8,128]{2,1,0:T(8,128)S(1)}, u32[]{:S(2)}, u32[]{:S(2)}) %all-to-all-start) | async-done | bytes 65568 | tf_op jit(solution)/shard_map/all_to_all | solution.py:482
  19.5 0.0 collective-permute-done.refs_1_
  19.5 17.2 %analyse.1 = bf16[8,4,64,256]{3,2,1,0:T(8,128)(2,1)} custom-call(s32[1]{0:T(128)} %bitcast.refs_0_.odd_ref, bf16[1056,256]{1,0:T(8,128)(2,1)} %collective-permute-done.refs_1_, bf16[8,4,64,256]{3,2,1,0:T(8,128)(2,1)S(1)} %copy-done, f32[8,256,256]{2,1,0:T(8,128)S(1)} %own_gram.1.refs_3_, f32[8,256]{1,0:T(8,128)S(1)} %get-tuple-element.11.refs_4_, ...), custom_call_target="tpu_custom_call" | custom-call | tf_op jit(solution)/shard_map/analyse/pallas_call | solution.py:454
  (1 shorter events, 0.0 us)
Async XLA Ops:
  0.0 13.1 %copy-start = (bf16[8,4,64,256]{3,2,1,0:T(8,128)(2,1)S(1)}, bf16[8,4,64,256]{3,2,1,0:T(8,128)(2,1)}, u32[]{:S(2)}) copy-start(bf16[8,4,64,256]{3,2,1,0:T(8,128)(2,1)} %refs_2_.1) | copy-start | bytes 3145732
  2.7 9.5 %collective-permute-start.1 = (bf16[1056,256]{1,0:T(8,128)(2,1)S(1)}, bf16[1056,256]{1,0:T(8,128)(2,1)S(1)}, u32[]{:S(2)}, u32[]{:S(2)}) collective-permute-start(bf16[1056,256]{1,0:T(8,128)(2,1)S(1)} %get-tuple-element.10), channel_id=1, source_target_pairs={{0,1},{1,0},{2,3},{3,2},{4,5},{5,4},{6,7},{7,6},{8,9},{9,8},{10,11... | collective-permute-start | bytes 1622024 | tf_op jit(solution)/shard_map/ppermute | solution.py:481
  2.9 16.7 %collective-permute-start = (bf16[1056,256]{1,0:T(8,128)(2,1)}, bf16[1056,256]{1,0:T(8,128)(2,1)}, u32[]{:S(2)}, u32[]{:S(2)}) collective-permute-start(bf16[1056,256]{1,0:T(8,128)(2,1)} %get-tuple-element.9), channel_id=1, source_target_pairs={{0,15},{1,2},{2,1},{3,4},{4,3},{5,6},{6,5},{7,8},{8,7},{9,10},{10,... | collective-permute-start | bytes 1622024 | tf_op jit(solution)/shard_map/ppermute | solution.py:480
  5.5 14.0 %all-to-all-start = ((f32[16,8,128]{2,1,0:T(8,128)}), f32[16,8,128]{2,1,0:T(8,128)S(1)}, u32[]{:S(2)}, u32[]{:S(2)}) async-start(f32[16,8,128]{2,1,0:T(8,128)} %bitcast.5), calls=%async_computation | async-start | bytes 131072 | tf_op jit(solution)/shard_map/all_to_all | solution.py:482
  12.3 0.8 %copy-start.1 = (bf16[1056,256]{1,0:T(8,128)(2,1)}, bf16[1056,256]{1,0:T(8,128)(2,1)S(1)}, u32[]{:S(2)}) copy-start(bf16[1056,256]{1,0:T(8,128)(2,1)S(1)} %collective-permute-done.1.near_ref) | copy-start | bytes 1622020
  13.1 1.0 %copy-start.2 = (bf16[1056,256]{1,0:T(8,128)(2,1)S(1)}, bf16[1056,256]{1,0:T(8,128)(2,1)}, u32[]{:S(2)}) copy-start(bf16[1056,256]{1,0:T(8,128)(2,1)} %copy-done.1) | copy-start | bytes 1622020

commit v8 on v6

--- a/solution.py
+++ b/solution.py
@@ -28,10 +28,47 @@
     return jnp.where(inside, 1.0 - dist / (HALO + 1), 0.0)
 
 
-def obs_kernel(odd_ref, cells_ref, index_ref, value_ref, var_ref, own_ref, near_ref, far_ref, part_ref):
-    lon_dev, _, lat, members = cells_ref.shape
+def fetch_kernel(*refs):
+    odd_ref, state_ref = refs[:2]
+    far_ref, near_ref, cells_ref = refs[5:8]
+    sems = refs[-1]
+    last = state_ref.shape[0] - HALO
+    far = odd_ref[0] * last
+    pieces = [
+        (state_ref.at[pl.ds(far, HALO)], far_ref),
+        (state_ref.at[pl.ds(last - far, HALO)], near_ref),
+        (state_ref.at[:, 0], cells_ref),
+    ] + list(zip(refs[2:5], refs[8:11]))
+    copies = [pltpu.make_async_copy(src, dst, sems.at[i]) for i, (src, dst) in enumerate(pieces)]
+    for copy in copies:
+        copy.start()
+    for copy in copies:
+        copy.wait()
+
+
+def fetch(odd, state, obs_index, obs_value, obs_var):
+    lon_dev, nvar, lat, members = state.shape
+    arrays = state, obs_index[None], obs_value[None], obs_var[None]
+    edge = jax.ShapeDtypeStruct((HALO, nvar, lat, members), state.dtype)
+    cells = jax.ShapeDtypeStruct((lon_dev, lat, members), state.dtype)
+    shapes = [edge, edge, cells] + [jax.ShapeDtypeStruct(x.shape, x.dtype) for x in arrays[1:]]
+    return pl.pallas_call(
+        fetch_kernel,
+        in_specs=[pl.BlockSpec(memory_space=pltpu.SMEM)]
+        + [pl.BlockSpec(memory_space=pltpu.HBM)] * len(arrays),
+        out_specs=[pl.BlockSpec(memory_space=pltpu.VMEM)] * len(shapes),
+        out_shape=shapes,
+        scratch_shapes=[pltpu.SemaphoreType.DMA((len(shapes),))],
+        compiler_params=pltpu.CompilerParams(vmem_limit_bytes=8 * 2**20),
+        name="fetch",
+    )(odd, *[pltpu.with_memory_space_constraint(x, pltpu.HBM) for x in arrays])
+
+
+def observe_kernel(place_ref, cells_ref, index_ref, value_ref, var_ref, own_ref, slots_ref):
+    lon_dev, lat, members = cells_ref.shape
     nobs = index_ref.shape[1]
-    rows = cells_ref[:, 0].reshape(lon_dev * lat, members)
+    odd = place_ref[0]
+    rows = cells_ref[...].reshape(lon_dev * lat, members)
     index = index_ref[...]
     sub = lax.broadcasted_iota(jnp.int32, (TILE, nobs), 0)
     table = jnp.where(
@@ -48,47 +85,57 @@
     centre = jnp.sum(seen, axis=1, keepdims=True) * (1.0 / members)
     spread = jnp.sum((seen - centre) ** 2, axis=1, keepdims=True) * (1.0 / (members - 1))
     innovation = (value - centre) ** 2 / (var + spread)
-    blocks, members = own_ref.shape
-    part_ref[...] = jnp.broadcast_to(jnp.sum(innovation, axis=0, keepdims=True), part_ref.shape)
+    part = jnp.sum(innovation, axis=0, keepdims=True)
     terms = (value - seen) ** 2 * (1.0 / var)
     lon = (index // lat).astype(jnp.float32)
     along = index.astype(jnp.float32) - lon * lat
+    blocks = own_ref.shape[0]
     block = lax.broadcasted_iota(jnp.int32, (blocks, nobs), 0).astype(jnp.float32)
     across = line_weight(along - REGION * block + HALO)
-    side = jnp.where(odd_ref[0] == 1, float(REGION), float(-REGION))
+    side = jnp.where(odd == 1, float(REGION), float(-REGION))
     weights = [line_weight(lon + (HALO + shift)) * across for shift in (0.0, side, -side)]
     like = jnp.dot(
         jnp.concatenate(weights, axis=0), terms, precision=HIGH, preferred_element_type=jnp.float32
     )
     own_ref[...] = like[:blocks]
-    near_ref[...] = like[blocks : 2 * blocks]
-    far_ref[...] = like[2 * blocks :]
-
-
-def observe(odd, state, obs_index, obs_value, obs_var, parts):
-    lon_dev, _, lat, members = state.shape
-    nobs = obs_index.shape[0]
+    like = like - like[:, 0:1]
+    slots_ref[...] = jnp.broadcast_to(part, slots_ref.shape)
+    first = lax.broadcasted_iota(jnp.int32, (blocks, 128), 1) == 0
+    for at, device in ((1, place_ref[1]), (2, place_ref[2])):
+        start = device * (members // 128 * blocks)
+        for lane in range(members // 128):
+            rows = like[at * blocks : (at + 1) * blocks, lane * 128 : (lane + 1) * 128]
+            if lane == 0:
+                rows = jnp.where(first, part, rows)
+            slots_ref[pl.ds(pl.multiple_of(start + lane * blocks, TILE), blocks), :] = rows
+
+
+def like_of(slots_ref, device, blocks, members):
+    start = device * (members // 128 * blocks)
+    rows = [
+        slots_ref[pl.ds(pl.multiple_of(start + lane * blocks, TILE), blocks), :]
+        for lane in range(members // 128)
+    ]
+    rows[0] = jnp.where(lax.broadcasted_iota(jnp.int32, (blocks, 128), 1) == 0, 0.0, rows[0])
+    return jnp.concatenate(rows, axis=1)
+
+
+def observe(place, cells, obs_index, obs_value, obs_var, devices):
+    lon_dev, lat, members = cells.shape
     blocks = lat // REGION
-    row = pl.BlockSpec((1, nobs), lambda i: (0, 0))
-    like = jax.ShapeDtypeStruct((blocks, members), jnp.float32)
-    like_spec = pl.BlockSpec((blocks, members), lambda i: (0, 0))
-    part = jax.ShapeDtypeStruct((parts * TILE, 128), jnp.float32)
-    part_spec = pl.BlockSpec((parts * TILE, 128), lambda i: (0, 0))
+    assert blocks % TILE == 0 and members % 128 == 0
+    vmem = pl.BlockSpec(memory_space=pltpu.VMEM)
     return pl.pallas_call(
-        obs_kernel,
-        grid=(1,),
-        in_specs=[
-            pl.BlockSpec(memory_space=pltpu.SMEM),
-            pl.BlockSpec((lon_dev, 1, lat, members), lambda i: (0, 0, 0, 0)),
-            row,
-            row,
-            row,
+        observe_kernel,
+        in_specs=[pl.BlockSpec(memory_space=pltpu.SMEM)] + [vmem] * 4,
+        out_specs=[vmem] * 2,
+        out_shape=[
+            jax.ShapeDtypeStruct((blocks, members), jnp.float32),
+            jax.ShapeDtypeStruct((devices * members // 128 * blocks, 128), jnp.float32),
         ],
-        out_specs=[like_spec] * 3 + [part_spec],
-        out_shape=[like] * 3 + [part],
-        compiler_params=pltpu.CompilerParams(vmem_limit_bytes=32 * 2**20),
+        compiler_params=pltpu.CompilerParams(vmem_limit_bytes=16 * 2**20),
         name="observe",
-    )(odd, state, obs_index[None], obs_value[None], obs_var[None])
+    )(place, cells, obs_index, obs_value, obs_var)
 
 
 def pair_tiles(ref, step, steps):
@@ -141,31 +188,40 @@
     return grams
 
 
-def own_gram_kernel(odd_ref, state_ref, near_ref, gram_ref):
-    step, steps = pl.program_id(0), pl.num_programs(0)
-    tiles = zip(pair_tiles(state_ref, step, steps), pair_tiles(near_ref, step, steps))
-    tiles = [jnp.concatenate([x, y], axis=0) for x, y in tiles]
-    grams = gram_of(tiles, [None] * state_ref.shape[0] + halo_weights(odd_ref[0] == 1))
-    for region in range(PAIR):
-        gram_ref[region] = grams[region]
+def own_gram_kernel(odd_ref, state_hbm_ref, near_ref, gram_ref, state_ref, sem):
+    regions = gram_ref.shape[0]
+    copy = pltpu.make_async_copy(state_hbm_ref, state_ref, sem)
+    copy.start()
+    copy.wait()
+
+    def pair(at, carry):
+        steps = regions // PAIR
+        tiles = zip(pair_tiles(state_ref, at, steps), pair_tiles(near_ref, at, steps))
+        tiles = [jnp.concatenate([x, y], axis=0) for x, y in tiles]
+        grams = gram_of(tiles, [None] * state_ref.shape[0] + halo_weights(odd_ref[0] == 1))
+        for region in range(PAIR):
+            gram_ref[at * PAIR + region] = grams[region]
+        return carry
+
+    lax.fori_loop(0, regions // PAIR, pair, 0)
 
 
 def own_gram(odd, state, near):
-    lon_dev, nvar, lat, members = state.shape
-    steps = lat // (PAIR * TILE)
+    _, _, lat, members = state.shape
+    vmem = pl.BlockSpec(memory_space=pltpu.VMEM)
     return pl.pallas_call(
         own_gram_kernel,
-        grid=(steps,),
         in_specs=[
             pl.BlockSpec(memory_space=pltpu.SMEM),
-            pl.BlockSpec(state.shape, lambda i: (0, 0, 0, 0)),
-            pl.BlockSpec(near.shape, lambda i: (0, 0, 0, 0)),
+            pl.BlockSpec(memory_space=pltpu.HBM),
+            vmem,
         ],
-        out_specs=pl.BlockSpec((PAIR, members, members), lambda i: (i, 0, 0)),
-        out_shape=jax.ShapeDtypeStruct((steps * PAIR, members, members), jnp.float32),
-        compiler_params=pltpu.CompilerParams(vmem_limit_bytes=48 * 2**20),
+        out_specs=vmem,
+        out_shape=jax.ShapeDtypeStruct((lat // REGION, members, members), jnp.float32),
+        scratch_shapes=[pltpu.VMEM(state.shape, state.dtype), pltpu.SemaphoreType.DMA],
+        compiler_params=pltpu.CompilerParams(vmem_limit_bytes=24 * 2**20),
         name="own_gram",
-    )(odd, state, near)
+    )(odd, pltpu.with_memory_space_constraint(state, pltpu.HBM), near)
 
 
 def halves(ref, region, rows):
@@ -321,15 +377,22 @@
 
 
 def analysis_kernel(count, scale, *refs):
-    odd_ref, halo_ref, state_ref, gram_in_ref = refs[0:4]
-    own_ref, near_ref, far_ref, sum_ref, out_ref = refs[4:9]
-    gram_ref, kernel_ref, ratio_ref, weight_ref, logw_ref, result_ref, sems = refs[9:]
+    place_ref, halo_ref, state_hbm_ref, gram_in_ref, own_ref, slots_ref, out_ref = refs[:7]
+    gram_ref, kernel_ref, ratio_ref, weight_ref, logw_ref, result_ref, state_ref = refs[7:14]
+    state_sem, sems = refs[14:]
     regions, members = gram_in_ref.shape[0], gram_in_ref.shape[-1]
     pairs = regions // PAIR
     size = PAIR * TILE
 
-    total = jnp.sum(sum_ref[...], axis=0, keepdims=True)[:, 0:1] * (1.0 / TILE)
-    like = own_ref[...] + near_ref[...] + far_ref[...]
+    fetch_state = pltpu.make_async_copy(state_hbm_ref, state_ref, state_sem)
+    fetch_state.start()
+    slot = members // 128 * regions
+    total = slots_ref[0:1, 0:1]
+    for device in range(1, slots_ref.shape[0] // slot):
+        total = total + slots_ref[device * slot : device * slot + 1, 0:1]
+    like = own_ref[...]
+    for neighbour in (1, 2):
+        like = like + like_of(slots_ref, place_ref[neighbour], regions, members)
     like = -0.5 * (count / total) * like
     like = like - jnp.max(like, axis=1, keepdims=True)
     logw = (like - jnp.log(jnp.sum(jnp.exp(like), axis=1, keepdims=True))) * LOG2E
@@ -343,13 +406,14 @@
         return pltpu.make_async_copy(result_ref.at[pair], out_ref.at[:, :, at, :], sems.at[pair])
 
     def halo_grams(pair, carry):
-        grams = gram_of(pair_tiles(halo_ref, pair, pairs), halo_weights(odd_ref[0] == 0))
+        grams = gram_of(pair_tiles(halo_ref, pair, pairs), halo_weights(place_ref[0] == 0))
         for at in range(PAIR):
             region = pair * PAIR + at
             gram_ref[region] = gram_in_ref[region] + grams[at]
         return carry
 
     lax.fori_loop(0, pairs, halo_grams, 0)
+    fetch_state.wait()
 
     def group(at, carry):
         least_row, least_col, most_row = carry
@@ -400,7 +464,7 @@
         lax.fori_loop(0, pairs, again, 0)
 
 
-def analyse(odd, halo, state, gram, own, near, far, total, count):
+def analyse(place, halo, state, gram, own, slots, count):
     lon_dev, nvar, lat, members = state.shape
     regions = lat // REGION
     offsets = range(REGION + 2 * HALO)
@@ -409,7 +473,14 @@
     vmem = pl.BlockSpec(memory_space=pltpu.VMEM)
     return pl.pallas_call(
         functools.partial(analysis_kernel, count, scale),
-        in_specs=[pl.BlockSpec(memory_space=pltpu.SMEM)] + [vmem] * 7,
+        in_specs=[
+            pl.BlockSpec(memory_space=pltpu.SMEM),
+            vmem,
+            pl.BlockSpec(memory_space=pltpu.HBM),
+            vmem,
+            vmem,
+            vmem,
+        ],
         out_specs=pl.BlockSpec(memory_space=pl.ANY),
         out_shape=jax.ShapeDtypeStruct(state.shape, state.dtype),
         scratch_shapes=[
@@ -419,33 +490,32 @@
             pltpu.VMEM((regions, members, 128), jnp.float32),
             pltpu.VMEM((regions, members), jnp.float32),
             pltpu.VMEM((regions // PAIR, lon_dev, nvar, PAIR * TILE, members), jnp.bfloat16),
+            pltpu.VMEM(state.shape, state.dtype),
+            pltpu.SemaphoreType.DMA,
             pltpu.SemaphoreType.DMA((regions // PAIR,)),
         ],
-        compiler_params=pltpu.CompilerParams(vmem_limit_bytes=48 * 2**20),
+        compiler_params=pltpu.CompilerParams(vmem_limit_bytes=24 * 2**20),
         name="analyse",
-    )(odd, halo, state, gram, own, near, far, total)
+    )(place, halo, pltpu.with_memory_space_constraint(state, pltpu.HBM), gram, own, slots)
 
 
 def on_device(state, obs_index, obs_value, obs_var):
-    lon_dev = state.shape[0]
     count = lax.axis_size("lon")
-    odd = lax.axis_index("lon") % 2
+    me = lax.axis_index("lon").astype(jnp.int32)
+    odd = me & 1
     near_pairs = [(i, i ^ 1) for i in range(count)]
     far_pairs = [(i, (i + 1 if i % 2 else i - 1) % count) for i in range(count)]
-    for_far = lax.dynamic_slice_in_dim(state, odd * (lon_dev - HALO), HALO, axis=0)
-    for_near = lax.dynamic_slice_in_dim(state, (1 - odd) * (lon_dev - HALO), HALO, axis=0)
+    far_place = me + 2 * odd - 1
+    far_place = jnp.where(far_place < 0, count - 1, jnp.where(far_place == count, 0, far_place))
+    place = jnp.stack([odd, me ^ 1, far_place])
+    for_far, for_near, cells, *obs = fetch(place, state, obs_index, obs_value, obs_var)
     far = lax.ppermute(for_far, "lon", far_pairs)
     near = lax.ppermute(for_near, "lon", near_pairs)
-    odd = odd.astype(jnp.int32).reshape(1)
-    own_like, near_like, far_like, part = observe(
-        odd, state, obs_index, obs_value, obs_var, count
-    )
-    got_far = lax.ppermute(far_like, "lon", far_pairs)
-    got_near = lax.ppermute(near_like, "lon", near_pairs)
-    parts = lax.all_to_all(part, "lon", 0, 0, tiled=True)
-    gram = own_gram(odd, state, near)
+    own_like, slots = observe(place, cells, *obs, count)
+    slots = lax.all_to_all(slots, "lon", 0, 0, tiled=True)
+    gram = own_gram(place, state, near)
     nobs = float(obs_index.shape[0] * count)
-    return analyse(odd, far, state, gram, own_like, got_near, got_far, parts, nobs)
+    return analyse(place, far, state, gram, own_like, slots, nobs)
 
 
 def solution(mesh):

time: 39 us -> 39.2 us (level)
  starting transfers between devices: 14.3 us -> 9.69 us
  Pallas kernels: 20.2 us -> 24.8 us
  waiting for transfers between devices: 0.01 us -> 4.37 us
  local copies, waits for them, and re-layouts: 4.04 us -> 0 us
    pallas_call x2 -> x3, Pallas kernels: 3.14 us -> 8.19 us  [the longest x1 3.52 us: own_gram(): pl.pallas_call(own_gram_kernel, in_specs=[pl.BlockSpec(memory_space=pltpu...]
    ppermute x2 -> x0, starting transfers between devices: 4.71 us -> none  [the longest x1 4.42 us: on_device(): got_far = lax.ppermute(far_like, 'lon', far_pairs)]
    all_to_all x1, waiting for transfers between devices: 0.01 us -> 4.36 us  [on_device(): slots = lax.all_to_all(slots, 'lon', 0, 0, tiled=True)]
    dynamic_slice x1 -> x0, local copies, waits for them, and re-layouts: 2.19 us -> none  [on_device(): lax.dynamic_slice_in_dim(state, (1 - odd) * (lon_dev - HALO), HALO, axis=0)]
    unnamed x12 -> x0, local copies, waits for them, and re-layouts: 1.85 us -> none
    pallas_call x1, Pallas kernels: 17.1 us -> 16.6 us  [analyse(): pl.pallas_call(functools.partial(analysis_kernel, count, scale), in_specs...]
  transfers between devices with their start and end apart: 5 -> 3, of which waited for: 0 -> 1; matrix products, arithmetic and copies ran while one was open for 0% -> 0% of each run, Pallas kernels for 8% -> 14%
where the time goes in v8:
time: 39.2 us; the launch traced here: 39 us
  Pallas kernels  24.8 us (63%)
  starting transfers between devices  9.69 us (25%)
  waiting for transfers between devices  4.37 us (11%)
    pallas_call x1, Pallas kernels, analyse(): pl.pallas_call(functools.partial(analysis_kernel, count, scale), in_specs...  16.6 us
    ppermute x1, starting transfers between devices, on_device(): far = lax.ppermute(for_far, 'lon', far_pairs)  5.67 us
    all_to_all x1, waiting for transfers between devices, on_device(): slots = lax.all_to_all(slots, 'lon', 0, 0, tiled=True)  4.36 us
    pallas_call x1, Pallas kernels, own_gram(): pl.pallas_call(own_gram_kernel, in_specs=[pl.BlockSpec(memory_space=pltpu...  3.52 us
    all_to_all x1, starting transfers between devices, on_device(): slots = lax.all_to_all(slots, 'lon', 0, 0, tiled=True)  3.51 us
    pallas_call x1, Pallas kernels, fetch(): pl.pallas_call(fetch_kernel, in_specs=[pl.BlockSpec(memory_space=pltpu.SM...  2.66 us
    pallas_call x1, Pallas kernels, observe(): pl.pallas_call(observe_kernel, in_specs=[pl.BlockSpec(memory_space=pltpu....  2.01 us
  transfers between devices with their start and end apart: 3, of which 1 were waited for; matrix products, arithmetic and copies ran while one was open for 0% of the time, Pallas kernels for 14%

profile of v8, /device:TPU:0, one launch (start us, length us, event | category | flops | bytes accessed | tf_op | source)
XLA Modules:
  0.0 39.0 jit_solution(4213285607347068942)
XLA Ops:
  0.0 0.1 pad_add_fusion.refs_0_.odd_ref.place_ref
  0.1 2.7 %fetch.1 = (bf16[4,4,64,256]{3,2,1,0:T(8,128)(2,1)}, bf16[4,4,64,256]{3,2,1,0:T(8,128)(2,1)S(1)}, bf16[8,64,256]{2,1,0:T(8,128)(2,1)S(1)}, s32[1,256]{1,0:T(1,12...) custom-call(s32[3]{0:T(128)S(1)} %pad_add_fusion.refs_0_.odd_ref.place_ref, bf16[8,4,64,256]{3,2,1,0:T(8,128)(2,1)} %refs_2_.1, ...), custom_call_target="tpu_custom_call" | custom-call | tf_op jit(solution)/shard_map/fetch/pallas_call | solution.py:55
  2.7 0.5 %collective-permute-start.1 = (bf16[4,4,64,256]{3,2,1,0:T(8,128)(2,1)S(1)}, bf16[4,4,64,256]{3,2,1,0:T(8,128)(2,1)S(1)}, u32[]{:S(2)}, u32[]{:S(2)}) collective-permute-start(bf16[4,4,64,256]{3,2,1,0:T(8,128)(2,1)S(1)} %get-tuple-element.14), channel_id=1, source_target_pairs={{0,1},{1,0},{2,3},{3,2},{4,5},{5,4},{6,7},{7,6},{8,9},{9,8},{10,11... | collective-permute-start | bytes 1572872 | tf_op jit(solution)/shard_map/ppermute | solution.py:513
  3.3 5.7 %collective-permute-start = (bf16[4,4,64,256]{3,2,1,0:T(8,128)(2,1)}, bf16[4,4,64,256]{3,2,1,0:T(8,128)(2,1)S(1)}, u32[]{:S(2)}, u32[]{:S(2)}) collective-permute-start(bf16[4,4,64,256]{3,2,1,0:T(8,128)(2,1)} %get-tuple-element.13), channel_id=1, source_target_pairs={{0,15},{1,2},{2,1},{3,4},{4,3},{5,6},{6,5},{7,8},{8,7},{9,10},{10,... | collective-permute-start | bytes 1572872 | tf_op jit(solution)/shard_map/ppermute | solution.py:512
  8.9 2.0 %observe.1 = (f32[8,256]{1,0:T(8,128)S(1)}, f32[256,128]{1,0:T(8,128)}) custom-call(s32[3]{0:T(128)S(1)} %pad_add_fusion.refs_0_.odd_ref.place_ref, bf16[8,64,256]{2,1,0:T(8,128)(2,1)S(1)} %get-tuple-element.15.cells_ref, s32[1,256]{1,0:T(1,128)S(1)} %get-tuple-element.16.index_ref, f32[1,256]{1,0:T(1,128)S(1)} %get-tuple-element.17.value_ref, ...), custom_call_target="tpu_custom_call" | custom-call | tf_op jit(solution)/shard_map/observe/pallas_call | solution.py:128
  10.9 3.5 %all-to-all-start = ((f32[16,16,128]{2,1,0:T(8,128)}), f32[16,16,128]{2,1,0:T(8,128)S(1)}, u32[]{:S(2)}, u32[]{:S(2)}) async-start(f32[16,16,128]{2,1,0:T(8,128)} %bitcast.6), calls=%async_computation | async-start | bytes 262144 | tf_op jit(solution)/shard_map/all_to_all | solution.py:515
  14.5 0.0 collective-permute-done.1.near_ref
  14.5 3.5 %own_gram.1.refs_3_ = f32[8,256,256]{2,1,0:T(8,128)S(1)} custom-call(s32[3]{0:T(128)S(1)} %pad_add_fusion.refs_0_.odd_ref.place_ref, bf16[8,4,64,256]{3,2,1,0:T(8,128)(2,1)} %refs_2_.1, bf16[4,4,64,256]{3,2,1,0:T(8,128)(2,1)S(1)} %collective-permute-done.1.near_ref), custom_call_target="tpu_custom_call" | custom-call | tf_op jit(solution)/shard_map/own_gram/pallas_call | solution.py:212
  18.0 4.4 %all-to-all-done = f32[16,16,128]{2,1,0:T(8,128)S(1)} async-done(((f32[16,16,128]{2,1,0:T(8,128)}), f32[16,16,128]{2,1,0:T(8,128)S(1)}, u32[]{:S(2)}, u32[]{:S(2)}) %all-to-all-start) | async-done | bytes 131104 | tf_op jit(solution)/shard_map/all_to_all | solution.py:515
  22.4 0.0 collective-permute-done.refs_1_
  22.4 16.6 %analyse.1 = bf16[8,4,64,256]{3,2,1,0:T(8,128)(2,1)} custom-call(s32[3]{0:T(128)S(1)} %pad_add_fusion.refs_0_.odd_ref.place_ref, bf16[4,4,64,256]{3,2,1,0:T(8,128)(2,1)S(1)} %collective-permute-done.refs_1_, bf16[8,4,64,256]{3,2,1,0:T(8,128)(2,1)} %refs_2_.1, f32[8,256,256]{2,1,0:T(8,128)S(1)} %own_gram.1.refs_3_, f32[8,256]{1,0:T(8,128)S(1)} %get-tuple-element.19.refs_4_, ...), custom_call_target="tpu_custom_call" | custom-call | tf_op jit(solution)/shard_map/analyse/pallas_call | solution.py:474
Async XLA Ops:
  2.7 11.7 %collective-permute-start.1 = (bf16[4,4,64,256]{3,2,1,0:T(8,128)(2,1)S(1)}, bf16[4,4,64,256]{3,2,1,0:T(8,128)(2,1)S(1)}, u32[]{:S(2)}, u32[]{:S(2)}) collective-permute-start(bf16[4,4,64,256]{3,2,1,0:T(8,128)(2,1)S(1)} %get-tuple-element.14), channel_id=1, source_target_pairs={{0,1},{1,0},{2,3},{3,2},{4,5},{5,4},{6,7},{7,6},{8,9},{9,8},{10,11... | collective-permute-start | bytes 1572872 | tf_op jit(solution)/shard_map/ppermute | solution.py:513
  3.3 19.1 %collective-permute-start = (bf16[4,4,64,256]{3,2,1,0:T(8,128)(2,1)}, bf16[4,4,64,256]{3,2,1,0:T(8,128)(2,1)S(1)}, u32[]{:S(2)}, u32[]{:S(2)}) collective-permute-start(bf16[4,4,64,256]{3,2,1,0:T(8,128)(2,1)} %get-tuple-element.13), channel_id=1, source_target_pairs={{0,15},{1,2},{2,1},{3,4},{4,3},{5,6},{6,5},{7,8},{8,7},{9,10},{10,... | collective-permute-start | bytes 1572872 | tf_op jit(solution)/shard_map/ppermute | solution.py:512
  10.9 11.4 %all-to-all-start = ((f32[16,16,128]{2,1,0:T(8,128)}), f32[16,16,128]{2,1,0:T(8,128)S(1)}, u32[]{:S(2)}, u32[]{:S(2)}) async-start(f32[16,16,128]{2,1,0:T(8,128)} %bitcast.6), calls=%async_computation | async-start | bytes 262144 | tf_op jit(solution)/shard_map/all_to_all | solution.py:515

commit v9 on v7

--- a/solution.py
+++ b/solution.py
@@ -28,15 +28,21 @@
     return jnp.where(inside, 1.0 - dist / (HALO + 1), 0.0)
 
 
-def in_parts(values):
+def in_parts(values, extra):
+    below = lax.broadcasted_iota(jnp.int32, values.shape, 0)
+    extra_high = extra.astype(jnp.bfloat16).astype(jnp.float32)
+    extra_middle = (extra - extra_high).astype(jnp.bfloat16).astype(jnp.float32)
+    extra_low = extra - extra_high - extra_middle
+    last = jnp.where(below == 0, extra_high, jnp.where(below == 1, extra_middle, extra_low))
+    last = jnp.where(below < 3, last, 0.0)
     high = values.astype(jnp.bfloat16).astype(jnp.float32)
     middle = (values - high).astype(jnp.bfloat16).astype(jnp.float32)
     low = values - high - middle
-    return jnp.concatenate([high, middle, low, jnp.zeros_like(low)], axis=0).astype(jnp.bfloat16)
-
-
-def from_parts(ref, start):
-    rows = ref[start : start + 4 * TILE, :].astype(jnp.float32)
+    return jnp.concatenate([high, middle, low, last], axis=0).astype(jnp.bfloat16)
+
+
+def from_parts(ref):
+    rows = ref[ref.shape[0] - 4 * TILE :, :].astype(jnp.float32)
     return rows[:TILE] + rows[TILE : 2 * TILE] + rows[2 * TILE : 3 * TILE]
 
 
@@ -82,7 +88,8 @@
     centre = jnp.sum(seen, axis=1, keepdims=True) * (1.0 / members)
     spread = jnp.sum((seen - centre) ** 2, axis=1, keepdims=True) * (1.0 / (members - 1))
     innovation = (value - centre) ** 2 / (var + spread)
-    part_ref[...] = jnp.broadcast_to(jnp.sum(innovation, axis=0, keepdims=True), part_ref.shape)
+    part = jnp.sum(innovation, axis=0, keepdims=True)
+    part_ref[...] = jnp.broadcast_to(part, part_ref.shape)
     terms = (value - seen) ** 2 * (1.0 / var)
     lon = (index // lat).astype(jnp.float32)
     along = index.astype(jnp.float32) - lon * lat
@@ -95,19 +102,19 @@
         jnp.concatenate(weights, axis=0), terms, precision=HIGH, preferred_element_type=jnp.float32
     )
     own_ref[...] = like[:blocks]
-    near_ref[edge:, :] = in_parts(like[blocks : 2 * blocks])
-    far_ref[edge:, :] = in_parts(like[2 * blocks :])
+    near_ref[edge:, :] = in_parts(like[blocks : 2 * blocks], part)
+    far_ref[edge:, :] = in_parts(like[2 * blocks :], jnp.zeros_like(part))
     for copy in copies[4:]:
         copy.wait()
 
 
-def observe(odd, state, obs_index, obs_value, obs_var, parts):
+def observe(odd, state, obs_index, obs_value, obs_var):
     lon_dev, nvar, lat, members = state.shape
     nobs = obs_index.size
     assert lat // REGION == TILE
     like = jax.ShapeDtypeStruct((lat // REGION, members), jnp.float32)
-    payload = jax.ShapeDtypeStruct((HALO * nvar * lat + 4 * TILE, members), state.dtype)
-    part = jax.ShapeDtypeStruct((parts * TILE, 128), jnp.float32)
+    payload = pltpu.VMEM((HALO * nvar * lat + 4 * TILE, members), state.dtype)
+    part = jax.ShapeDtypeStruct((TILE, 128), jnp.float32)
     arrays = state, state.reshape(-1, members), obs_index[None], obs_value[None], obs_var[None]
     return pl.pallas_call(
         observe_kernel,
@@ -184,31 +191,56 @@
     return grams
 
 
-def own_gram_kernel(odd_ref, state_ref, near_ref, gram_ref):
-    step, steps = pl.program_id(0), pl.num_programs(0)
-    tiles = zip(pair_tiles(state_ref, step, steps), pair_tiles(near_ref, step, steps))
-    tiles = [jnp.concatenate([x, y], axis=0) for x, y in tiles]
-    grams = gram_of(tiles, [None] * state_ref.shape[0] + halo_weights(odd_ref[0] == 1))
-    for region in range(PAIR):
-        gram_ref[region] = grams[region]
-
-
-def own_gram(odd, state, near):
-    lon_dev, nvar, lat, members = state.shape
-    steps = lat // (PAIR * TILE)
+def slab_copies(src_ref, dst_ref, sems):
+    size = PAIR * TILE
+    return [
+        pltpu.make_async_copy(
+            src_ref.at[:, :, pl.ds(i * size, size), :], dst_ref.at[:, :, pl.ds(i * size, size), :], sems.at[i]
+        )
+        for i in range(src_ref.shape[2] // size)
+    ]
+
+
+def own_gram_kernel(odd_ref, state_hbm_ref, near_ref, own_ref, gram_ref, like_ref, state_ref, sems):
+    steps = gram_ref.shape[0] // PAIR
+    copies = slab_copies(state_hbm_ref, state_ref, sems)
+    for copy in copies:
+        copy.start()
+    like_ref[...] = own_ref[...] + from_parts(near_ref)
+    copies[0].wait()
+    for step in range(steps):
+        if step + 1 < steps:
+            copies[step + 1].wait()
+        tiles = zip(pair_tiles(state_ref, step, steps), pair_tiles(near_ref, step, steps))
+        tiles = [jnp.concatenate([x, y], axis=0) for x, y in tiles]
+        grams = gram_of(tiles, [None] * state_ref.shape[0] + halo_weights(odd_ref[0] == 1))
+        for region in range(PAIR):
+            gram_ref[step * PAIR + region] = grams[region]
+
+
+def own_gram(odd, state, near, own):
+    _, _, lat, members = state.shape
+    vmem = pl.BlockSpec(memory_space=pltpu.VMEM)
     return pl.pallas_call(
         own_gram_kernel,
-        grid=(steps,),
         in_specs=[
             pl.BlockSpec(memory_space=pltpu.SMEM),
-            pl.BlockSpec(state.shape, lambda i: (0, 0, 0, 0)),
-            pl.BlockSpec(near.shape, lambda i: (0, 0)),
-        ],
-        out_specs=pl.BlockSpec((PAIR, members, members), lambda i: (i, 0, 0)),
-        out_shape=jax.ShapeDtypeStruct((steps * PAIR, members, members), jnp.float32),
-        compiler_params=pltpu.CompilerParams(vmem_limit_bytes=24 * 2**20),
+            pl.BlockSpec(memory_space=pltpu.HBM),
+            vmem,
+            vmem,
+        ],
+        out_specs=[vmem, vmem],
+        out_shape=[
+            jax.ShapeDtypeStruct((lat // REGION, members, members), jnp.float32),
+            jax.ShapeDtypeStruct(own.shape, jnp.float32),
+        ],
+        scratch_shapes=[
+            pltpu.VMEM(state.shape, state.dtype),
+            pltpu.SemaphoreType.DMA((lat // (PAIR * TILE),)),
+        ],
+        compiler_params=pltpu.CompilerParams(vmem_limit_bytes=16 * 2**20),
         name="own_gram",
-    )(odd, state, near)
+    )(odd, pltpu.with_memory_space_constraint(state, pltpu.HBM), near, own)
 
 
 def halves(ref, region, rows):
@@ -232,15 +264,66 @@
     return [jnp.sum(x, axis=0, keepdims=True) for x in across], down
 
 
-def sweep_rows(parts, weight, totals):
-    scaled, mass = parts
-    mass = jnp.broadcast_to(jnp.sum(mass, axis=1, keepdims=True), weight.shape)
-    near = pl.reciprocal(mass, approx=True)
-    ratio = weight * (near * (2.0 - mass * near))
-    for lane, part in enumerate(scaled):
-        part = jnp.sum((part * ratio).reshape(ROWS // TILE, TILE, 128), axis=0)
-        totals[lane] = part if totals[lane] is None else totals[lane] + part
-    return mass, ratio
+def prepare_kernel(scale, *refs):
+    odd_ref, halo_ref, gram_in_ref, like_in_ref = refs[:4]
+    gram_hbm_ref, kernel_ref, most_ref, like_ref, gram_ref, sems = refs[4:]
+    regions, members, _ = gram_ref.shape
+    steps = regions // PAIR
+    like_ref[...] = like_in_ref[...] + from_parts(halo_ref)
+
+    def keep(step):
+        part = pl.ds(step * PAIR, PAIR)
+        return pltpu.make_async_copy(gram_ref.at[part], gram_hbm_ref.at[part], sems.at[step])
+
+    def pair(step, most):
+        grams = gram_of(pair_tiles(halo_ref, step, steps), halo_weights(odd_ref[0] == 0))
+        for at in range(PAIR):
+            region = step * PAIR + at
+            gram_ref[region] = gram_in_ref[region] + grams[at]
+        keep(step).start()
+        for at in range(PAIR):
+            region = step * PAIR + at
+            across, down = diagonal(gram_ref, region)
+            across = [0.5 * LIFT - x * scale for x in across]
+            for i, start in enumerate(range(0, members, ROWS)):
+                rows = pl.ds(start, ROWS)
+                base = 0.5 * LIFT - down[i] * scale
+                for lane, (gram, x) in enumerate(zip(halves(gram_ref, region, rows), across)):
+                    part = jnp.exp2(gram * (2.0 * scale) + base + x)
+                    kernel_ref[region, rows, lane * 128 : lane * 128 + 128] = part
+                    most = jnp.maximum(most, part)
+        return most
+
+    most = lax.fori_loop(0, steps, pair, jnp.zeros((ROWS, 128), jnp.float32))
+    most_ref[...] = jnp.max(most.reshape(ROWS // TILE, TILE, 128), axis=0)
+
+    def drain(step, carry):
+        keep(step).wait()
+        return carry
+
+    lax.fori_loop(0, steps, drain, 0)
+
+
+def prepare(odd, halo, gram, like, scale):
+    regions = gram.shape[0]
+    vmem = pl.BlockSpec(memory_space=pltpu.VMEM)
+    return pl.pallas_call(
+        functools.partial(prepare_kernel, scale),
+        in_specs=[pl.BlockSpec(memory_space=pltpu.SMEM)] + [vmem] * 3,
+        out_specs=[pl.BlockSpec(memory_space=pltpu.HBM)] + [vmem] * 3,
+        out_shape=[
+            pltpu.HBM(gram.shape, jnp.float32),
+            jax.ShapeDtypeStruct(gram.shape, jnp.float32),
+            jax.ShapeDtypeStruct((TILE, 128), jnp.float32),
+            jax.ShapeDtypeStruct(like.shape, jnp.float32),
+        ],
+        scratch_shapes=[
+            pltpu.VMEM(gram.shape, jnp.float32),
+            pltpu.SemaphoreType.DMA((regions // PAIR,)),
+        ],
+        compiler_params=pltpu.CompilerParams(vmem_limit_bytes=16 * 2**20),
+        name="prepare",
+    )(odd, halo, gram, like)
 
 
 def fold(values, op):
@@ -250,71 +333,42 @@
     return out
 
 
-def sweeps_scaled(regions, gram_ref, kernel_ref, ratio_ref, weight_ref, scale):
-    members = gram_ref.shape[-1]
+def sweeps_scaled(regions, kernel_ref, ratio_ref, weight_ref):
+    members = kernel_ref.shape[-1]
     starts = range(0, members, ROWS)
     lanes = range(members // 128)
-    least_row, most_row, least_col, cols = [], [], [], []
     share = 2.0**MASS / members
 
-    def settle(totals):
-        totals = [jnp.sum(x, axis=0, keepdims=True) for x in totals]
-        return totals, fold(totals, jnp.minimum)
-
-    for region in regions:
-        across, down = diagonal(gram_ref, region)
-        across = [0.5 * LIFT - x * scale for x in across]
-        totals = [None] * len(lanes)
-        masses = []
-        for at, start in enumerate(starts):
-            rows = pl.ds(start, ROWS)
-            base = 0.5 * LIFT - down[at] * scale
-            kernel = [
-                jnp.exp2(g * (2.0 * scale) + base + x)
-                for g, x in zip(halves(gram_ref, region, rows), across)
-            ]
-            for lane, part in enumerate(kernel):
-                kernel_ref[region, rows, lane * 128 : lane * 128 + 128] = part
-            mass, _ = sweep_rows(
-                (kernel, fold(kernel, jnp.add) * 2.0**START), weight_ref[region, rows, :], totals
-            )
-            masses.append(mass)
-        least_row.append(fold(masses, jnp.minimum))
-        most_row.append(fold(masses, jnp.maximum))
-        totals, least = settle(totals)
-        least_col.append(least)
-        cols.append(totals)
-
     def sweep(last, carry):
-        least_row, least_col, cols = carry
-        rows_out, least_out, cols_out = [], [], []
-        for region, lrow, lcol, col in zip(regions, least_row, least_col, cols):
-            factor = [share / x for x in col]
-            totals = [None] * len(lanes)
+        least_row, least_col, factors = carry
+        rows_out, least_out, factors_out = [], [], []
+        for region, lrow, lcol, factor in zip(regions, least_row, least_col, factors):
+            totals = [None for _ in lanes]
             for start in starts:
                 rows = pl.ds(start, ROWS)
                 kernel = halves(kernel_ref, region, rows)
                 mass = fold([k * f for k, f in zip(kernel, factor)], jnp.add)
-                mass, ratio = sweep_rows((kernel, mass), weight_ref[region, rows, :], totals)
+                mass = jnp.broadcast_to(jnp.sum(mass, axis=1, keepdims=True), (ROWS, 128))
+                near = pl.reciprocal(mass, approx=True)
+                ratio = weight_ref[region, rows, :] * (near * (2.0 - mass * near))
+                for lane, part in enumerate(kernel):
+                    part = jnp.sum((part * ratio).reshape(ROWS // TILE, TILE, 128), axis=0)
+                    totals[lane] = part if totals[lane] is None else totals[lane] + part
                 if last:
                     ratio_ref[region, rows, :] = ratio
                 lrow = jnp.minimum(lrow, mass)
-            totals, least = settle(totals)
+            totals = [jnp.sum(x, axis=0, keepdims=True) for x in totals]
             rows_out.append(lrow)
-            least_out.append(jnp.minimum(lcol, least))
-            cols_out.append(totals)
-        return rows_out, least_out, cols_out
-
-    carry = least_row, least_col, cols
-    carry = lax.fori_loop(0, SWEEPS - 2, lambda i, c: sweep(False, c), carry)
-    least_row, least_col, cols = sweep(True, carry)
-    factors = [[1.0 / x for x in col] for col in cols]
-    return (
-        factors,
-        fold(least_row, jnp.minimum),
-        fold(least_col, jnp.minimum),
-        fold(most_row, jnp.maximum),
-    )
+            least_out.append(jnp.minimum(lcol, fold(totals, jnp.minimum)))
+            factors_out.append([(1.0 if last else share) / x for x in totals])
+        return rows_out, least_out, factors_out
+
+    high = jnp.full((ROWS, 128), 1e30, jnp.float32)
+    first = jnp.full((1, 128), 2.0**START, jnp.float32)
+    carry = [high for _ in regions], [high[:1] for _ in regions], [[first] * len(lanes) for _ in regions]
+    carry = lax.fori_loop(0, SWEEPS - 1, lambda i, c: sweep(False, c), carry)
+    least_row, least_col, factors = sweep(True, carry)
+    return factors, fold(least_row, jnp.minimum), fold(least_col, jnp.minimum)
 
 
 def transport_scaled(region, factor, kernel_ref, ratio_ref):
@@ -363,18 +417,19 @@
     return jnp.concatenate(parts, axis=2).astype(jnp.bfloat16)
 
 
-def analysis_kernel(count, scale, *refs):
-    odd_ref, halo_ref, state_ref, gram_in_ref = refs[0:4]
-    own_ref, near_ref, sum_ref, out_ref = refs[4:8]
-    gram_ref, kernel_ref, ratio_ref, weight_ref, logw_ref, result_ref, sems = refs[8:]
-    regions, members = gram_in_ref.shape[0], gram_in_ref.shape[-1]
+def finish_kernel(count, scale, *refs):
+    state_hbm_ref, gram_hbm_ref, kernel_ref, most_ref, like_ref, sums_ref, out_ref = refs[:7]
+    ratio_ref, weight_ref, logw_ref, result_ref, state_ref, gram_ref = refs[7:13]
+    sems, state_sems = refs[13:]
+    regions, members = kernel_ref.shape[0], kernel_ref.shape[-1]
     pairs = regions // PAIR
     size = PAIR * TILE
-
-    total = jnp.sum(sum_ref[...], axis=0, keepdims=True)[:, 0:1] * (1.0 / TILE)
-    halo = halo_ref.shape[0] - 4 * TILE
-    like = own_ref[...] + from_parts(near_ref, 0) + from_parts(halo_ref, halo)
-    like = -0.5 * (count / total) * like
+    fetches = slab_copies(state_hbm_ref, state_ref, state_sems)
+    for copy in fetches:
+        copy.start()
+
+    total = jnp.sum(sums_ref[...], axis=0, keepdims=True)[:, 0:1] * (1.0 / TILE)
+    like = -0.5 * (count / total) * like_ref[...]
     like = like - jnp.max(like, axis=1, keepdims=True)
     logw = (like - jnp.log(jnp.sum(jnp.exp(like), axis=1, keepdims=True))) * LOG2E
     logw_ref[...] = logw
@@ -386,20 +441,13 @@
         at = pl.ds(pl.multiple_of(pair * size, size), size)
         return pltpu.make_async_copy(result_ref.at[pair], out_ref.at[:, :, at, :], sems.at[pair])
 
-    def halo_grams(pair, carry):
-        grams = gram_of(pair_tiles(halo_ref, pair, pairs), halo_weights(odd_ref[0] == 0))
-        for at in range(PAIR):
-            region = pair * PAIR + at
-            gram_ref[region] = gram_in_ref[region] + grams[at]
-        return carry
-
-    lax.fori_loop(0, pairs, halo_grams, 0)
+    for copy in fetches:
+        copy.wait()
 
     def group(at, carry):
-        least_row, least_col, most_row = carry
         first = at * GROUP
-        factors, row, col, most = sweeps_scaled(
-            [first + r for r in range(GROUP)], gram_ref, kernel_ref, ratio_ref, weight_ref, scale
+        factors, row, col = sweeps_scaled(
+            [first + r for r in range(GROUP)], kernel_ref, ratio_ref, weight_ref
         )
         for pair in range(GROUP // PAIR):
             moves = [
@@ -409,24 +457,18 @@
             where = at * (GROUP // PAIR) + pair
             result_ref[where] = transform(state_ref, where, moves)
             send(where).start()
-        return (
-            jnp.minimum(least_row, row),
-            jnp.minimum(least_col, col),
-            jnp.maximum(most_row, most),
-        )
+        return jnp.minimum(carry[0], row), jnp.minimum(carry[1], col)
 
     high = jnp.full((ROWS, 128), 1e30, jnp.float32)
-    least_row, least_col, most_row = lax.fori_loop(
-        0, regions // GROUP, group, (high, high[:1], jnp.zeros((ROWS, 128), jnp.float32))
-    )
+    least_row, least_col = lax.fori_loop(0, regions // GROUP, group, (high, high[:1]))
 
     def drain(pair, carry):
         send(pair).wait()
         return carry
 
     lax.fori_loop(0, pairs, drain, 0)
-    row, col, most = jnp.min(least_row), jnp.min(least_col), jnp.max(most_row)
-    sound = (row >= 2.0**-24) & (col >= 2.0**-30) & (most <= 2.0**20) & (row * col >= 2.0**-34)
+    row, col, most = jnp.min(least_row), jnp.min(least_col), jnp.max(most_ref[...])
+    sound = (row >= 2.0**-24) & (col >= 2.0**-30) & (most <= 2.0**30) & (row * col >= 2.0**-34)
 
     @pl.when(jnp.logical_not(sound))
     def _():
@@ -434,7 +476,11 @@
             moves = []
             for at in range(PAIR):
                 region = pair * PAIR + at
-                moves.append(transport_logs(region, gram_ref, logw_ref[pl.ds(region, 1), :], scale))
+                copy = pltpu.make_async_copy(gram_hbm_ref.at[region], gram_ref.at[at], state_sems.at[0])
+                copy.start()
+                copy.wait()
+                logw = logw_ref[pl.ds(region, 1), :]
+                moves.append(transport_logs(at, gram_ref, logw, scale))
             result_ref[pair] = transform(state_ref, pair, moves)
             copy = send(pair)
             copy.start()
@@ -444,46 +490,57 @@
         lax.fori_loop(0, pairs, again, 0)
 
 
-def analyse(odd, halo, state, gram, own, near, total, count):
+def finish(state, gram, kernel, most, like, sums, count, scale):
     lon_dev, nvar, lat, members = state.shape
     regions = lat // REGION
-    offsets = range(REGION + 2 * HALO)
-    line = [1.0 - max(0, HALO - p, p - (HALO + REGION - 1)) / (HALO + 1) for p in offsets]
-    scale = LOG2E / EPS / (nvar * sum(line) ** 2)
     vmem = pl.BlockSpec(memory_space=pltpu.VMEM)
+    hbm = pl.BlockSpec(memory_space=pltpu.HBM)
     return pl.pallas_call(
-        functools.partial(analysis_kernel, count, scale),
-        in_specs=[pl.BlockSpec(memory_space=pltpu.SMEM)] + [vmem] * 6,
+        functools.partial(finish_kernel, count, scale),
+        in_specs=[hbm, hbm] + [vmem] * 4,
         out_specs=pl.BlockSpec(memory_space=pl.ANY),
         out_shape=jax.ShapeDtypeStruct(state.shape, state.dtype),
         scratch_shapes=[
-            pltpu.VMEM((regions, members, members), jnp.float32),
-            pltpu.VMEM((regions, members, members), jnp.float32),
             pltpu.VMEM((regions, members, 128), jnp.float32),
             pltpu.VMEM((regions, members, 128), jnp.float32),
             pltpu.VMEM((regions, members), jnp.float32),
             pltpu.VMEM((regions // PAIR, lon_dev, nvar, PAIR * TILE, members), jnp.bfloat16),
+            pltpu.VMEM(state.shape, state.dtype),
+            pltpu.VMEM((PAIR, members, members), jnp.float32),
             pltpu.SemaphoreType.DMA((regions // PAIR,)),
+            pltpu.SemaphoreType.DMA((regions // PAIR,)),
         ],
         compiler_params=pltpu.CompilerParams(vmem_limit_bytes=24 * 2**20),
-        name="analyse",
-    )(odd, halo, state, gram, own, near, total)
+        name="finish",
+    )(*[pltpu.with_memory_space_constraint(x, pltpu.HBM) for x in (state, gram)], kernel, most, like, sums)
 
 
 def on_device(state, obs_index, obs_value, obs_var):
+    nvar = state.shape[1]
     count = lax.axis_size("lon")
-    odd = lax.axis_index("lon") % 2
+    odd = (lax.axis_index("lon") & 1).astype(jnp.int32).reshape(1)
     near_pairs = [(i, i ^ 1) for i in range(count)]
     far_pairs = [(i, (i + 1 if i % 2 else i - 1) % count) for i in range(count)]
-    odd = odd.astype(jnp.int32).reshape(1)
-    own_like, for_near, for_far, part = observe(odd, state, obs_index, obs_value, obs_var, count)
+    own_like, for_near, for_far, part = observe(odd, state, obs_index, obs_value, obs_var)
     far = lax.ppermute(for_far, "lon", far_pairs)
     near = lax.ppermute(for_near, "lon", near_pairs)
-    parts = lax.all_to_all(part, "lon", 0, 0, tiled=True)
-    near_like = near[near.shape[0] - 4 * TILE :]
-    gram = own_gram(odd, state, near)
+    start = near.shape[0] - TILE
+    part = part[0] + jnp.sum(near[start : start + 3, :128].astype(jnp.float32), axis=0)
+    sums = lax.all_to_all(
+        jnp.broadcast_to(part, (count // 2 * TILE, 128)),
+        "lon",
+        0,
+        0,
+        axis_index_groups=[list(range(core, count, 2)) for core in range(2)],
+        tiled=True,
+    )
+    offsets = range(REGION + 2 * HALO)
+    line = [1.0 - max(0, HALO - p, p - (HALO + REGION - 1)) / (HALO + 1) for p in offsets]
+    scale = LOG2E / EPS / (nvar * sum(line) ** 2)
+    gram, like = own_gram(odd, state, near, own_like)
+    gram, kernel, most, like = prepare(odd, far, gram, like, scale)
     nobs = float(obs_index.shape[0] * count)
-    return analyse(odd, far, state, gram, own_like, near_like, parts, nobs)
+    return finish(state, gram, kernel, most, like, sums, nobs, scale)
 
 
 def solution(mesh):

time: 37.3 us -> 42.8 us (1.15)
  Pallas kernels: 21.6 us -> 28.8 us
  local copies, waits for them, and re-layouts: 1.85 us -> 0.62 us
  starting transfers between devices: 9.51 us -> 8.68 us
  waiting for transfers between devices: 3.65 us -> 4.28 us
    pallas_call x2 -> x3, Pallas kernels: 18.9 us -> 27 us  [the longest x1 22.1 us: finish(): pl.pallas_call(functools.partial(finish_kernel, count, scale), in_specs=[...]
    ppermute x1, waiting for transfers between devices: 0.01 us -> 4.27 us  [on_device(): far = lax.ppermute(for_far, 'lon', far_pairs)]
    all_to_all x1, waiting for transfers between devices: 3.64 us -> 0.01 us  [on_device(): lax.all_to_all(jnp.broadcast_to(part, (count // 2 * TILE, 128)), 'lon', 0...]
    unnamed x6 -> x0, local copies, waits for them, and re-layouts: 1.84 us -> none
    pallas_call x1, Pallas kernels: 2.72 us -> 1.84 us  [observe(): pl.pallas_call(observe_kernel, in_specs=[pl.BlockSpec(memory_space=pltpu....]
    all_to_all x1, starting transfers between devices: 6.74 us -> 5.91 us  [on_device(): lax.all_to_all(jnp.broadcast_to(part, (count // 2 * TILE, 128)), 'lon', 0...]
    broadcast_in_dim x0 -> x1, local copies, waits for them, and re-layouts: none -> 0.62 us  [on_device(): jnp.broadcast_to(part, (count // 2 * TILE, 128))]
  transfers between devices with their start and end apart: 3 -> 3, of which waited for: 1 -> 1; matrix products, arithmetic and copies ran while one was open for 0% -> 2% of each run, Pallas kernels for 5% -> 12%
where the time goes in v9:
time: 42.8 us; the launch traced here: 42.5 us
  Pallas kernels  28.8 us (67%)
  starting transfers between devices  8.68 us (20%)
  waiting for transfers between devices  4.28 us (10%)
  local copies, waits for them, and re-layouts  0.62 us (1%)
    pallas_call x1, Pallas kernels, finish(): pl.pallas_call(functools.partial(finish_kernel, count, scale), in_specs=[...  22.1 us
    all_to_all x1, starting transfers between devices, on_device(): lax.all_to_all(jnp.broadcast_to(part, (count // 2 * TILE, 128)), 'lon', 0...  5.91 us
    ppermute x1, waiting for transfers between devices, on_device(): far = lax.ppermute(for_far, 'lon', far_pairs)  4.27 us
    ppermute x1, starting transfers between devices, on_device(): far = lax.ppermute(for_far, 'lon', far_pairs)  2.65 us
    pallas_call x1, Pallas kernels, own_gram(): pl.pallas_call(own_gram_kernel, in_specs=[pl.BlockSpec(memory_space=pltpu...  2.55 us
    pallas_call x1, Pallas kernels, prepare(): pl.pallas_call(functools.partial(prepare_kernel, scale), in_specs=[pl.Blo...  2.34 us
    pallas_call x1, Pallas kernels, observe(): pl.pallas_call(observe_kernel, in_specs=[pl.BlockSpec(memory_space=pltpu....  1.84 us
  transfers between devices with their start and end apart: 3, of which 1 were waited for; matrix products, arithmetic and copies ran while one was open for 2% of the time, Pallas kernels for 12%

profile of v9, /device:TPU:1, one launch (start us, length us, event | category | flops | bytes accessed | tf_op | source)
XLA Modules:
  0.0 42.5 jit_solution(253973348846488243)
XLA Ops:
  0.0 1.8 %observe.1 = (f32[8,256]{1,0:T(8,128)S(1)}, bf16[1056,256]{1,0:T(8,128)(2,1)S(1)}, bf16[1056,256]{1,0:T(8,128)(2,1)S(1)}, f32[8,128]{1,0:T(8,128)S(1)}) custom-call(s32[1]{0:T(128)} %bitcast.refs_0_.odd_ref, bf16[8,4,64,256]{3,2,1,0:T(8,128)(2,1)} %refs_0_.1, bf16[2048,256]{1,0:T(8,128)(2,1)} %bitcast.9, s32[1,256]{1,0:T(1,128)} %bitcast.10, ...), custom_call_target="tpu_custom_call" | custom-call | tf_op jit(solution)/shard_map/observe/pallas_call | solution.py:119
  1.9 0.1 collective-permute-start.1
  2.0 2.7 %collective-permute-start = (bf16[1056,256]{1,0:T(8,128)(2,1)S(1)}, bf16[1056,256]{1,0:T(8,128)(2,1)S(1)}, u32[]{:S(2)}, u32[]{:S(2)}) collective-permute-start(bf16[1056,256]{1,0:T(8,128)(2,1)S(1)} %get-tuple-element.15), channel_id=1, source_target_pairs={{0,15},{1,2},{2,1},{3,4},{4,3},{5,6},{6,5},{7,8},{8,7},{9,10},{10,... | collective-permute-start | bytes 1622024 | tf_op jit(solution)/shard_map/ppermute | solution.py:525
  4.6 0.0 collective-permute-done.1.near_ref
  4.7 0.6 %broadcast_in_dim.15 = f32[8,8,128]{2,1,0:T(8,128)} broadcast(f32[128]{0:T(128)S(1)} %bitcast_add_fusion), dimensions={2} | broadcast | bytes 33280 | tf_op jit(solution)/shard_map/broadcast_in_dim | solution.py:530
  5.3 5.9 %all-to-all-start = ((f32[8,8,128]{2,1,0:T(8,128)}), f32[8,8,128]{2,1,0:T(8,128)S(1)}, u32[]{:S(2)}, u32[]{:S(2)}) async-start(f32[8,8,128]{2,1,0:T(8,128)} %broadcast_in_dim.15), calls=%async_computation | async-start | bytes 65536 | tf_op jit(solution)/shard_map/all_to_all | solution.py:529
  11.2 2.6 %own_gram.1 = (f32[8,256,256]{2,1,0:T(8,128)S(1)}, f32[8,256]{1,0:T(8,128)S(1)}) custom-call(s32[1]{0:T(128)} %bitcast.refs_0_.odd_ref, bf16[8,4,64,256]{3,2,1,0:T(8,128)(2,1)} %refs_0_.1, bf16[1056,256]{1,0:T(8,128)(2,1)S(1)} %collective-permute-done.1.near_ref, f32[8,256]{1,0:T(8,128)S(1)} %get-tuple-element.17.own_ref), custom_call_target="tpu_custom_call" | custom-call | tf_op jit(solution)/shard_map/own_gram/pallas_call | solution.py:224
  13.7 4.3 %collective-permute-done.refs_1_ = bf16[1056,256]{1,0:T(8,128)(2,1)S(1)} collective-permute-done((bf16[1056,256]{1,0:T(8,128)(2,1)S(1)}, bf16[1056,256]{1,0:T(8,128)(2,1)S(1)}, u32[]{:S(2)}, u32[]{:S(2)}) %collective-permute-start) | collective-permute-done | bytes 540704 | tf_op jit(solution)/shard_map/ppermute | solution.py:525
  18.0 2.3 %prepare.1 = (f32[8,256,256]{2,1,0:T(8,128)}, f32[8,256,256]{2,1,0:T(8,128)S(1)}, f32[8,128]{1,0:T(8,128)S(1)}, f32[8,256]{1,0:T(8,128)S(1)}) custom-call(s32[1]{0:T(128)} %bitcast.refs_0_.odd_ref, bf16[1056,256]{1,0:T(8,128)(2,1)S(1)} %collective-permute-done.refs_1_, f32[8,256,256]{2,1,0:T(8,128)S(1)} %get-tuple-element.18.refs_2_, ...), custom_call_target="tpu_custom_call" | custom-call | tf_op jit(solution)/shard_map/prepare/pallas_call | solution.py:310
  20.4 0.0 all-to-all-done
  20.4 22.1 %finish.1 = bf16[8,4,64,256]{3,2,1,0:T(8,128)(2,1)} custom-call(bf16[8,4,64,256]{3,2,1,0:T(8,128)(2,1)} %refs_0_.1, f32[8,256,256]{2,1,0:T(8,128)} %get-tuple-element.20.refs_1_, f32[8,256,256]{2,1,0:T(8,128)S(1)} %get-tuple-element.21.refs_2_, f32[8,128]{1,0:T(8,128)S(1)} %get-tuple-element.22.refs_3_, f32[8,256]{1,0:T(8,128)S(1)} %get-tuple-element.23.refs_4_, ...), custom_call_target="tpu_custom_call" | custom-call | tf_op jit(solution)/shard_map/finish/pallas_call | solution.py:498
  (2 shorter events, 0.0 us)
Async XLA Ops:
  1.9 2.8 %collective-permute-start.1 = (bf16[1056,256]{1,0:T(8,128)(2,1)S(1)}, bf16[1056,256]{1,0:T(8,128)(2,1)S(1)}, u32[]{:S(2)}, u32[]{:S(2)}) collective-permute-start(bf16[1056,256]{1,0:T(8,128)(2,1)S(1)} %get-tuple-element.16), channel_id=1, source_target_pairs={{0,1},{1,0},{2,3},{3,2},{4,5},{5,4},{6,7},{7,6},{8,9},{9,8},{10,11... | collective-permute-start | bytes 1622024 | tf_op jit(solution)/shard_map/ppermute | solution.py:526
  2.0 16.0 %collective-permute-start = (bf16[1056,256]{1,0:T(8,128)(2,1)S(1)}, bf16[1056,256]{1,0:T(8,128)(2,1)S(1)}, u32[]{:S(2)}, u32[]{:S(2)}) collective-permute-start(bf16[1056,256]{1,0:T(8,128)(2,1)S(1)} %get-tuple-element.15), channel_id=1, source_target_pairs={{0,15},{1,2},{2,1},{3,4},{4,3},{5,6},{6,5},{7,8},{8,7},{9,10},{10,... | collective-permute-start | bytes 1622024 | tf_op jit(solution)/shard_map/ppermute | solution.py:525
  5.3 15.1 %all-to-all-start = ((f32[8,8,128]{2,1,0:T(8,128)}), f32[8,8,128]{2,1,0:T(8,128)S(1)}, u32[]{:S(2)}, u32[]{:S(2)}) async-start(f32[8,8,128]{2,1,0:T(8,128)} %broadcast_in_dim.15), calls=%async_computation | async-start | bytes 65536 | tf_op jit(solution)/shard_map/all_to_all | solution.py:529

commit v10 on v9

--- a/solution.py
+++ b/solution.py
@@ -160,34 +160,42 @@
     return [jnp.where(to_left, x, y) for x, y in zip(steps, steps[::-1])]
 
 
-def gram_of(tiles, weights):
+def turn_tiles(low, high, turned_ref, step):
+    for at, tile in enumerate((low, high)):
+        flat = tile.reshape(-1, tile.shape[-1]).astype(jnp.bfloat16)
+        turned_ref[step * PAIR + at] = flat.T
+
+
+def gram_of(tiles, turned_ref, weights, step, steps):
     before, low, high, after = tiles
     columns, nvar, _, members = low.shape
+    depth = columns * nvar * TILE
     row = lax.broadcasted_iota(jnp.int32, (1, TILE, members), 1)
     upper = row < HALO
     rowf = row.astype(jnp.float32)
     edge = line_weight(jnp.where(upper, rowf + (HALO + REGION), rowf - HALO))
+    lane = lax.broadcasted_iota(jnp.int32, (1, depth), 1) & (TILE - 1)
     grams = []
-    for own, following, preceding in ((low, high, before), (high, after, low)):
+    for at, (own, following, preceding) in enumerate(((low, high, before), (high, after, low))):
+        region = step * PAIR + at
         margin = jnp.where(upper, following, preceding)
-        win = jnp.concatenate([own, margin], axis=2)
-        weighted = []
+        main_rows, margin_rows = [], []
         for column, weight in enumerate(weights):
-            if weight is None:
-                parts = [own[column], margin[column] * edge]
-            else:
-                parts = [own[column] * weight, margin[column] * (edge * weight)]
-            weighted.append(jnp.concatenate(parts, axis=1))
-        weighted = jnp.stack(weighted)
-        shape = (columns * nvar * 2 * TILE, members)
-        grams.append(
-            lax.dot_general(
-                weighted.astype(jnp.bfloat16).reshape(shape),
-                win.astype(jnp.bfloat16).reshape(shape),
-                (((0,), (0,)), ((), ())),
-                preferred_element_type=jnp.float32,
-            )
+            main_rows.append(own[column] if weight is None else own[column] * weight)
+            scale = edge if weight is None else edge * weight
+            margin_rows.append(margin[column] * scale)
+        weighted = jnp.concatenate([jnp.stack(main_rows), jnp.stack(margin_rows)], axis=0)
+        weighted = weighted.reshape(2 * depth, members).astype(jnp.bfloat16)
+        has_next = jnp.where(region + 1 < steps * PAIR, 1.0, 0.0)
+        has_prev = jnp.where(region > 0, 1.0, 0.0)
+        take_next = jnp.where(lane < HALO, has_next, 0.0).astype(jnp.bfloat16)
+        take_prev = jnp.where(lane < HALO, 0.0, has_prev).astype(jnp.bfloat16)
+        turned = (
+            turned_ref[jnp.minimum(region + 1, steps * PAIR - 1)] * take_next
+            + turned_ref[jnp.maximum(region - 1, 0)] * take_prev
         )
+        turned = jnp.concatenate([turned_ref[region], turned], axis=1)
+        grams.append(jnp.dot(turned, weighted, preferred_element_type=jnp.float32))
     return grams
 
 
@@ -201,25 +209,30 @@
     ]
 
 
-def own_gram_kernel(odd_ref, state_hbm_ref, near_ref, own_ref, gram_ref, like_ref, state_ref, sems):
+def own_gram_kernel(odd_ref, state_hbm_ref, near_ref, own_ref, gram_ref, like_ref, *scratch):
+    state_ref, turned_ref, sems = scratch
     steps = gram_ref.shape[0] // PAIR
     copies = slab_copies(state_hbm_ref, state_ref, sems)
     for copy in copies:
         copy.start()
     like_ref[...] = own_ref[...] + from_parts(near_ref)
-    copies[0].wait()
+    pairs = []
     for step in range(steps):
-        if step + 1 < steps:
-            copies[step + 1].wait()
+        copies[step].wait()
+    for step in range(steps):
         tiles = zip(pair_tiles(state_ref, step, steps), pair_tiles(near_ref, step, steps))
-        tiles = [jnp.concatenate([x, y], axis=0) for x, y in tiles]
-        grams = gram_of(tiles, [None] * state_ref.shape[0] + halo_weights(odd_ref[0] == 1))
-        for region in range(PAIR):
-            gram_ref[step * PAIR + region] = grams[region]
+        pairs.append([jnp.concatenate([x, y], axis=0) for x, y in tiles])
+        turn_tiles(pairs[-1][1], pairs[-1][2], turned_ref, step)
+    weights = [None] * state_ref.shape[0] + halo_weights(odd_ref[0] == 1)
+    for step in range(steps):
+        grams = gram_of(pairs[step], turned_ref, weights, step, steps)
+        for at in range(PAIR):
+            gram_ref[step * PAIR + at] = grams[at]
 
 
 def own_gram(odd, state, near, own):
-    _, _, lat, members = state.shape
+    lon_dev, nvar, lat, members = state.shape
+    depth = (lon_dev + HALO) * nvar * TILE
     vmem = pl.BlockSpec(memory_space=pltpu.VMEM)
     return pl.pallas_call(
         own_gram_kernel,
@@ -236,6 +249,7 @@
         ],
         scratch_shapes=[
             pltpu.VMEM(state.shape, state.dtype),
+            pltpu.VMEM((lat // TILE, members, depth), state.dtype),
             pltpu.SemaphoreType.DMA((lat // (PAIR * TILE),)),
         ],
         compiler_params=pltpu.CompilerParams(vmem_limit_bytes=16 * 2**20),
@@ -266,7 +280,7 @@
 
 def prepare_kernel(scale, *refs):
     odd_ref, halo_ref, gram_in_ref, like_in_ref = refs[:4]
-    gram_hbm_ref, kernel_ref, most_ref, like_ref, gram_ref, sems = refs[4:]
+    gram_hbm_ref, kernel_ref, mass_ref, most_ref, like_ref, gram_ref, turned_ref, sems = refs[4:]
     regions, members, _ = gram_ref.shape
     steps = regions // PAIR
     like_ref[...] = like_in_ref[...] + from_parts(halo_ref)
@@ -275,8 +289,16 @@
         part = pl.ds(step * PAIR, PAIR)
         return pltpu.make_async_copy(gram_ref.at[part], gram_hbm_ref.at[part], sems.at[step])
 
+    def turn(step, carry):
+        tiles = pair_tiles(halo_ref, step, steps)
+        turn_tiles(tiles[1], tiles[2], turned_ref, step)
+        return carry
+
+    lax.fori_loop(0, steps, turn, 0)
+
     def pair(step, most):
-        grams = gram_of(pair_tiles(halo_ref, step, steps), halo_weights(odd_ref[0] == 0))
+        weights = halo_weights(odd_ref[0] == 0)
+        grams = gram_of(pair_tiles(halo_ref, step, steps), turned_ref, weights, step, steps)
         for at in range(PAIR):
             region = step * PAIR + at
             gram_ref[region] = gram_in_ref[region] + grams[at]
@@ -285,6 +307,7 @@
             region = step * PAIR + at
             across, down = diagonal(gram_ref, region)
             across = [0.5 * LIFT - x * scale for x in across]
+            masses = [0.0 for _ in across]
             for i, start in enumerate(range(0, members, ROWS)):
                 rows = pl.ds(start, ROWS)
                 base = 0.5 * LIFT - down[i] * scale
@@ -292,6 +315,10 @@
                     part = jnp.exp2(gram * (2.0 * scale) + base + x)
                     kernel_ref[region, rows, lane * 128 : lane * 128 + 128] = part
                     most = jnp.maximum(most, part)
+                    part = jnp.sum(part.reshape(ROWS // TILE, TILE, 128), axis=0)
+                    masses[lane] = masses[lane] + part
+            masses = [jnp.sum(x, axis=0, keepdims=True) for x in masses]
+            mass_ref[region] = jnp.concatenate(masses, axis=1)
         return most
 
     most = lax.fori_loop(0, steps, pair, jnp.zeros((ROWS, 128), jnp.float32))
@@ -306,19 +333,22 @@
 
 def prepare(odd, halo, gram, like, scale):
     regions = gram.shape[0]
+    halo_depth = (halo.shape[0] - 4 * TILE) // regions
     vmem = pl.BlockSpec(memory_space=pltpu.VMEM)
     return pl.pallas_call(
         functools.partial(prepare_kernel, scale),
         in_specs=[pl.BlockSpec(memory_space=pltpu.SMEM)] + [vmem] * 3,
-        out_specs=[pl.BlockSpec(memory_space=pltpu.HBM)] + [vmem] * 3,
+        out_specs=[pl.BlockSpec(memory_space=pltpu.HBM)] + [vmem] * 4,
         out_shape=[
             pltpu.HBM(gram.shape, jnp.float32),
             jax.ShapeDtypeStruct(gram.shape, jnp.float32),
+            jax.ShapeDtypeStruct((regions, 1, like.shape[1]), jnp.float32),
             jax.ShapeDtypeStruct((TILE, 128), jnp.float32),
             jax.ShapeDtypeStruct(like.shape, jnp.float32),
         ],
         scratch_shapes=[
             pltpu.VMEM(gram.shape, jnp.float32),
+            pltpu.VMEM((regions, gram.shape[1], halo_depth), halo.dtype),
             pltpu.SemaphoreType.DMA((regions // PAIR,)),
         ],
         compiler_params=pltpu.CompilerParams(vmem_limit_bytes=16 * 2**20),
@@ -333,74 +363,79 @@
     return out
 
 
-def sweeps_scaled(regions, kernel_ref, ratio_ref, weight_ref):
+def transports_scaled(regions, kernel_ref, weight_ref, mass_ref):
     members = kernel_ref.shape[-1]
     starts = range(0, members, ROWS)
     lanes = range(members // 128)
     share = 2.0**MASS / members
 
-    def sweep(last, carry):
-        least_row, least_col, factors = carry
-        rows_out, least_out, factors_out = [], [], []
-        for region, lrow, lcol, factor in zip(regions, least_row, least_col, factors):
+    def lane_parts(ref, region):
+        row = ref[region]
+        return [row[:, lane * 128 : lane * 128 + 128] for lane in lanes]
+
+    def settle(totals, region):
+        return [w / x for w, x in zip(lane_parts(weight_ref, region), totals)]
+
+    def masses_of(region, rows, factor):
+        parts = [k * f for k, f in zip(halves(kernel_ref, region, rows), factor)]
+        mass = jnp.sum(fold(parts, jnp.add), axis=1, keepdims=True)
+        mass = jnp.broadcast_to(mass, (ROWS, 128))
+        near = pl.reciprocal(mass, approx=True)
+        return parts, mass, near * (2.0 - mass * near)
+
+    def sweep(_, carry):
+        least_i, least_j, factors = carry
+        next_i, next_j, next_factors = [], [], []
+        for region, low_i, low_j, factor in zip(regions, least_i, least_j, factors):
             totals = [None for _ in lanes]
             for start in starts:
                 rows = pl.ds(start, ROWS)
-                kernel = halves(kernel_ref, region, rows)
-                mass = fold([k * f for k, f in zip(kernel, factor)], jnp.add)
-                mass = jnp.broadcast_to(jnp.sum(mass, axis=1, keepdims=True), (ROWS, 128))
-                near = pl.reciprocal(mass, approx=True)
-                ratio = weight_ref[region, rows, :] * (near * (2.0 - mass * near))
-                for lane, part in enumerate(kernel):
-                    part = jnp.sum((part * ratio).reshape(ROWS // TILE, TILE, 128), axis=0)
+                _, mass, ratio = masses_of(region, rows, factor)
+                low_j = jnp.minimum(low_j, mass)
+                for lane, kernel in enumerate(halves(kernel_ref, region, rows)):
+                    part = jnp.sum((kernel * ratio).reshape(ROWS // TILE, TILE, 128), axis=0)
                     totals[lane] = part if totals[lane] is None else totals[lane] + part
-                if last:
-                    ratio_ref[region, rows, :] = ratio
-                lrow = jnp.minimum(lrow, mass)
-            totals = [jnp.sum(x, axis=0, keepdims=True) for x in totals]
-            rows_out.append(lrow)
-            least_out.append(jnp.minimum(lcol, fold(totals, jnp.minimum)))
-            factors_out.append([(1.0 if last else share) / x for x in totals])
-        return rows_out, least_out, factors_out
-
-    high = jnp.full((ROWS, 128), 1e30, jnp.float32)
-    first = jnp.full((1, 128), 2.0**START, jnp.float32)
-    carry = [high for _ in regions], [high[:1] for _ in regions], [[first] * len(lanes) for _ in regions]
-    carry = lax.fori_loop(0, SWEEPS - 1, lambda i, c: sweep(False, c), carry)
-    least_row, least_col, factors = sweep(True, carry)
-    return factors, fold(least_row, jnp.minimum), fold(least_col, jnp.minimum)
-
-
-def transport_scaled(region, factor, kernel_ref, ratio_ref):
-    members = kernel_ref.shape[-1]
-    parts = []
-    for start in range(0, members, ROWS):
-        rows = pl.ds(start, ROWS)
-        ratio = ratio_ref[region, rows, :]
-        row = [k * ratio * f for k, f in zip(halves(kernel_ref, region, rows), factor)]
-        parts.append(jnp.concatenate(row, axis=1).astype(jnp.bfloat16))
-    return jnp.concatenate(parts, axis=0)
-
-
-def transport_logs(region, gram_ref, logw, scale):
-    members = gram_ref.shape[-1]
-    gram = gram_ref[region]
-    i = lax.broadcasted_iota(jnp.int32, gram.shape, 0)
-    j = lax.broadcasted_iota(jnp.int32, gram.shape, 1)
+            totals = [jnp.sum(x, axis=0, keepdims=True) * share for x in totals]
+            next_i.append(jnp.minimum(low_i, fold(totals, jnp.minimum)))
+            next_j.append(low_j)
+            next_factors.append(settle(totals, region))
+        return next_i, next_j, next_factors
+
+    totals = [[x * 2.0**START for x in lane_parts(mass_ref, region)] for region in regions]
+    least_i = [fold(x, jnp.minimum) for x in totals]
+    least_j = [jnp.full((ROWS, 128), 1e30, jnp.float32) for _ in regions]
+    factors = [settle(x, region) for x, region in zip(totals, regions)]
+    carry = lax.fori_loop(0, SWEEPS - 1, sweep, (least_i, least_j, factors))
+    least_i, least_j, factors = carry
+    moves, last_j = [], []
+    for region, low_j, factor in zip(regions, least_j, factors):
+        blocks = []
+        for start in starts:
+            parts, mass, ratio = masses_of(region, pl.ds(start, ROWS), factor)
+            low_j = jnp.minimum(low_j, mass)
+            blocks.append(jnp.concatenate([x * ratio for x in parts], axis=1).astype(jnp.bfloat16))
+        moves.append(jnp.concatenate(blocks, axis=0))
+        last_j.append(low_j)
+    return moves, fold(least_i, jnp.minimum), fold(last_j, jnp.minimum)
+
+
+def transport_logs(gram, logw, scale):
+    members = gram.shape[-1]
+    j = lax.broadcasted_iota(jnp.int32, gram.shape, 0)
+    i = lax.broadcasted_iota(jnp.int32, gram.shape, 1)
     kept = jnp.where(i == j, gram, 0.0)
     down = jnp.sum(kept, axis=1, keepdims=True)
     across = jnp.sum(kept, axis=0, keepdims=True)
     cost = (down + across - 2.0 * gram) * scale
-    logw = jnp.sum(jnp.where(i == j, logw, 0.0), axis=1, keepdims=True)
-    pot_g = jnp.zeros((1, members), jnp.float32)
+    pot_g = jnp.zeros((members, 1), jnp.float32)
     for sweep in range(SWEEPS):
         term = pot_g - cost
+        top = jnp.max(term, axis=0, keepdims=True)
+        pot_f = logw - top - jnp.log(jnp.sum(jnp.exp2(term - top), axis=0, keepdims=True)) * LOG2E
+        term = pot_f - cost
         top = jnp.max(term, axis=1, keepdims=True)
-        pot_f = logw - top - jnp.log(jnp.sum(jnp.exp2(term - top), axis=1, keepdims=True)) * LOG2E
-        term = pot_f - cost
-        top = jnp.max(term, axis=0, keepdims=True)
         pot_g = -math.log2(members) - top
-        pot_g = pot_g - jnp.log(jnp.sum(jnp.exp2(term - top), axis=0, keepdims=True)) * LOG2E
+        pot_g = pot_g - jnp.log(jnp.sum(jnp.exp2(term - top), axis=1, keepdims=True)) * LOG2E
     return (members * jnp.exp2(pot_f + pot_g - cost)).astype(jnp.bfloat16)
 
 
@@ -412,15 +447,16 @@
     for region, move in enumerate(moves):
         cells = own[:, :, region * TILE : (region + 1) * TILE].astype(jnp.bfloat16)
         cells = cells.reshape(lon_dev * nvar * TILE, members)
-        moved = jnp.dot(cells, move, preferred_element_type=jnp.float32)
+        moved = lax.dot_general(
+            cells, move, (((1,), (1,)), ((), ())), preferred_element_type=jnp.float32
+        )
         parts.append(moved.reshape(lon_dev, nvar, TILE, members))
     return jnp.concatenate(parts, axis=2).astype(jnp.bfloat16)
 
 
 def finish_kernel(count, scale, *refs):
-    state_hbm_ref, gram_hbm_ref, kernel_ref, most_ref, like_ref, sums_ref, out_ref = refs[:7]
-    ratio_ref, weight_ref, logw_ref, result_ref, state_ref, gram_ref = refs[7:13]
-    sems, state_sems = refs[13:]
+    state_hbm_ref, gram_hbm_ref, kernel_ref, mass_ref, most_ref, like_ref, sums_ref = refs[:7]
+    out_ref, weight_ref, logw_ref, result_ref, state_ref, gram_ref, sems, state_sems = refs[7:]
     regions, members = kernel_ref.shape[0], kernel_ref.shape[-1]
     pairs = regions // PAIR
     size = PAIR * TILE
@@ -432,10 +468,10 @@
     like = -0.5 * (count / total) * like_ref[...]
     like = like - jnp.max(like, axis=1, keepdims=True)
     logw = (like - jnp.log(jnp.sum(jnp.exp(like), axis=1, keepdims=True))) * LOG2E
-    logw_ref[...] = logw
-    weight = jnp.exp2(logw + MASS).T
+    weight = jnp.exp2(logw + MASS)
     for region in range(regions):
-        weight_ref[region] = jnp.broadcast_to(weight[:, region : region + 1], (members, 128))
+        weight_ref[region] = weight[region : region + 1]
+        logw_ref[region] = logw[region : region + 1]
 
     def send(pair):
         at = pl.ds(pl.multiple_of(pair * size, size), size)
@@ -446,28 +482,24 @@
 
     def group(at, carry):
         first = at * GROUP
-        factors, row, col = sweeps_scaled(
-            [first + r for r in range(GROUP)], kernel_ref, ratio_ref, weight_ref
+        moves, least_i, least_j = transports_scaled(
+            [first + r for r in range(GROUP)], kernel_ref, weight_ref, mass_ref
         )
         for pair in range(GROUP // PAIR):
-            moves = [
-                transport_scaled(first + r, factors[r], kernel_ref, ratio_ref)
-                for r in range(pair * PAIR, (pair + 1) * PAIR)
-            ]
             where = at * (GROUP // PAIR) + pair
-            result_ref[where] = transform(state_ref, where, moves)
+            result_ref[where] = transform(state_ref, where, moves[pair * PAIR : (pair + 1) * PAIR])
             send(where).start()
-        return jnp.minimum(carry[0], row), jnp.minimum(carry[1], col)
+        return jnp.minimum(carry[0], least_i), jnp.minimum(carry[1], least_j)
 
     high = jnp.full((ROWS, 128), 1e30, jnp.float32)
-    least_row, least_col = lax.fori_loop(0, regions // GROUP, group, (high, high[:1]))
+    least_i, least_j = lax.fori_loop(0, regions // GROUP, group, (high[:1], high))
 
     def drain(pair, carry):
         send(pair).wait()
         return carry
 
     lax.fori_loop(0, pairs, drain, 0)
-    row, col, most = jnp.min(least_row), jnp.min(least_col), jnp.max(most_ref[...])
+    row, col, most = jnp.min(least_i), jnp.min(least_j), jnp.max(most_ref[...])
     sound = (row >= 2.0**-24) & (col >= 2.0**-30) & (most <= 2.0**30) & (row * col >= 2.0**-34)
 
     @pl.when(jnp.logical_not(sound))
@@ -479,8 +511,7 @@
                 copy = pltpu.make_async_copy(gram_hbm_ref.at[region], gram_ref.at[at], state_sems.at[0])
                 copy.start()
                 copy.wait()
-                logw = logw_ref[pl.ds(region, 1), :]
-                moves.append(transport_logs(at, gram_ref, logw, scale))
+                moves.append(transport_logs(gram_ref[at], logw_ref[region], scale))
             result_ref[pair] = transform(state_ref, pair, moves)
             copy = send(pair)
             copy.start()
@@ -490,20 +521,19 @@
         lax.fori_loop(0, pairs, again, 0)
 
 
-def finish(state, gram, kernel, most, like, sums, count, scale):
+def finish(state, gram, kernel, mass, most, like, sums, count, scale):
     lon_dev, nvar, lat, members = state.shape
     regions = lat // REGION
     vmem = pl.BlockSpec(memory_space=pltpu.VMEM)
     hbm = pl.BlockSpec(memory_space=pltpu.HBM)
     return pl.pallas_call(
         functools.partial(finish_kernel, count, scale),
-        in_specs=[hbm, hbm] + [vmem] * 4,
+        in_specs=[hbm, hbm] + [vmem] * 5,
         out_specs=pl.BlockSpec(memory_space=pl.ANY),
         out_shape=jax.ShapeDtypeStruct(state.shape, state.dtype),
         scratch_shapes=[
-            pltpu.VMEM((regions, members, 128), jnp.float32),
-            pltpu.VMEM((regions, members, 128), jnp.float32),
-            pltpu.VMEM((regions, members), jnp.float32),
+            pltpu.VMEM((regions, 1, members), jnp.float32),
+            pltpu.VMEM((regions, 1, members), jnp.float32),
             pltpu.VMEM((regions // PAIR, lon_dev, nvar, PAIR * TILE, members), jnp.bfloat16),
             pltpu.VMEM(state.shape, state.dtype),
             pltpu.VMEM((PAIR, members, members), jnp.float32),
@@ -512,7 +542,14 @@
         ],
         compiler_params=pltpu.CompilerParams(vmem_limit_bytes=24 * 2**20),
         name="finish",
-    )(*[pltpu.with_memory_space_constraint(x, pltpu.HBM) for x in (state, gram)], kernel, most, like, sums)
+    )(
+        *[pltpu.with_memory_space_constraint(x, pltpu.HBM) for x in (state, gram)],
+        kernel,
+        mass,
+        most,
+        like,
+        sums,
+    )
 
 
 def on_device(state, obs_index, obs_value, obs_var):
@@ -538,9 +575,9 @@
     line = [1.0 - max(0, HALO - p, p - (HALO + REGION - 1)) / (HALO + 1) for p in offsets]
     scale = LOG2E / EPS / (nvar * sum(line) ** 2)
     gram, like = own_gram(odd, state, near, own_like)
-    gram, kernel, most, like = prepare(odd, far, gram, like, scale)
+    gram, kernel, mass, most, like = prepare(odd, far, gram, like, scale)
     nobs = float(obs_index.shape[0] * count)
-    return finish(state, gram, kernel, most, like, sums, nobs, scale)
+    return finish(state, gram, kernel, mass, most, like, sums, nobs, scale)
 
 
 def solution(mesh):

time: 42.8 us -> 43.4 us (1.014)
  Pallas kernels: 28.8 us -> 29.3 us
where the time goes in v10:
time: 43.4 us; the launch traced here: 43 us
  Pallas kernels  29.3 us (68%)
  starting transfers between devices  8.68 us (20%)
  waiting for transfers between devices  4.28 us (10%)
  local copies, waits for them, and re-layouts  0.62 us (1%)
    pallas_call x1, Pallas kernels, finish(): pl.pallas_call(functools.partial(finish_kernel, count, scale), in_specs=[...  22.2 us
    all_to_all x1, starting transfers between devices, on_device(): lax.all_to_all(jnp.broadcast_to(part, (count // 2 * TILE, 128)), 'lon', 0...  5.91 us
    ppermute x1, waiting for transfers between devices, on_device(): far = lax.ppermute(for_far, 'lon', far_pairs)  4.28 us
    pallas_call x1, Pallas kernels, prepare(): pl.pallas_call(functools.partial(prepare_kernel, scale), in_specs=[pl.Blo...  2.76 us
    ppermute x1, starting transfers between devices, on_device(): far = lax.ppermute(for_far, 'lon', far_pairs)  2.65 us
    pallas_call x1, Pallas kernels, own_gram(): pl.pallas_call(own_gram_kernel, in_specs=[pl.BlockSpec(memory_space=pltpu...  2.55 us
    pallas_call x1, Pallas kernels, observe(): pl.pallas_call(observe_kernel, in_specs=[pl.BlockSpec(memory_space=pltpu....  1.84 us
  transfers between devices with their start and end apart: 3, of which 1 were waited for; matrix products, arithmetic and copies ran while one was open for 2% of the time, Pallas kernels for 12%

profile of v10, /device:TPU:1, one launch (start us, length us, event | category | flops | bytes accessed | tf_op | source)
XLA Modules:
  0.0 43.0 jit_solution(7360169765364047585)
XLA Ops:
  0.0 1.8 %observe.1 = (f32[8,256]{1,0:T(8,128)S(1)}, bf16[1056,256]{1,0:T(8,128)(2,1)S(1)}, bf16[1056,256]{1,0:T(8,128)(2,1)S(1)}, f32[8,128]{1,0:T(8,128)S(1)}) custom-call(s32[1]{0:T(128)} %bitcast.refs_0_.odd_ref, bf16[8,4,64,256]{3,2,1,0:T(8,128)(2,1)} %refs_0_.1, bf16[2048,256]{1,0:T(8,128)(2,1)} %bitcast.9, s32[1,256]{1,0:T(1,128)} %bitcast.10, ...), custom_call_target="tpu_custom_call" | custom-call | tf_op jit(solution)/shard_map/observe/pallas_call | solution.py:119
  1.9 0.1 collective-permute-start.1
  2.0 2.7 %collective-permute-start = (bf16[1056,256]{1,0:T(8,128)(2,1)S(1)}, bf16[1056,256]{1,0:T(8,128)(2,1)S(1)}, u32[]{:S(2)}, u32[]{:S(2)}) collective-permute-start(bf16[1056,256]{1,0:T(8,128)(2,1)S(1)} %get-tuple-element.16), channel_id=1, source_target_pairs={{0,15},{1,2},{2,1},{3,4},{4,3},{5,6},{6,5},{7,8},{8,7},{9,10},{10,... | collective-permute-start | bytes 1622024 | tf_op jit(solution)/shard_map/ppermute | solution.py:562
  4.6 0.0 collective-permute-done.1.near_ref
  4.7 0.6 %broadcast_in_dim.15 = f32[8,8,128]{2,1,0:T(8,128)} broadcast(f32[128]{0:T(128)S(1)} %bitcast_add_fusion), dimensions={2} | broadcast | bytes 33280 | tf_op jit(solution)/shard_map/broadcast_in_dim | solution.py:567
  5.3 5.9 %all-to-all-start = ((f32[8,8,128]{2,1,0:T(8,128)}), f32[8,8,128]{2,1,0:T(8,128)S(1)}, u32[]{:S(2)}, u32[]{:S(2)}) async-start(f32[8,8,128]{2,1,0:T(8,128)} %broadcast_in_dim.15), calls=%async_computation | async-start | bytes 65536 | tf_op jit(solution)/shard_map/all_to_all | solution.py:566
  11.2 2.5 %own_gram.1 = (f32[8,256,256]{2,1,0:T(8,128)S(1)}, f32[8,256]{1,0:T(8,128)S(1)}) custom-call(s32[1]{0:T(128)} %bitcast.refs_0_.odd_ref, bf16[8,4,64,256]{3,2,1,0:T(8,128)(2,1)} %refs_0_.1, bf16[1056,256]{1,0:T(8,128)(2,1)S(1)} %collective-permute-done.1.near_ref, f32[8,256]{1,0:T(8,128)S(1)} %get-tuple-element.18.own_ref), custom_call_target="tpu_custom_call" | custom-call | tf_op jit(solution)/shard_map/own_gram/pallas_call | solution.py:237
  13.7 4.3 %collective-permute-done.refs_1_ = bf16[1056,256]{1,0:T(8,128)(2,1)S(1)} collective-permute-done((bf16[1056,256]{1,0:T(8,128)(2,1)S(1)}, bf16[1056,256]{1,0:T(8,128)(2,1)S(1)}, u32[]{:S(2)}, u32[]{:S(2)}) %collective-permute-start) | collective-permute-done | bytes 540704 | tf_op jit(solution)/shard_map/ppermute | solution.py:562
  18.0 2.8 %prepare.1 = (f32[8,256,256]{2,1,0:T(8,128)}, f32[8,256,256]{2,1,0:T(8,128)S(1)}, f32[8,1,256]{2,1,0:T(1,128)S(1)}, f32[8,128]{1,0:T(8,128)S(1)}, f32[8,256]{1,0:T(8,128)S(1)}) custom-call(s32[1]{0:T(128)} %bitcast.refs_0_.odd_ref, bf16[1056,256]{1,0:T(8,128)(2,1)S(1)} %collective-permute-done.refs_1_, f32[8,256,256]{2,1,0:T(8,128)S(1)} %get-tuple-element.19.refs_2_, ...), custom_call_target="tpu_custom_call" | custom-call | tf_op jit(solution)/shard_map/prepare/pallas_call | solution.py:338
  20.8 0.0 all-to-all-done
  20.8 22.2 %finish.1 = bf16[8,4,64,256]{3,2,1,0:T(8,128)(2,1)} custom-call(bf16[8,4,64,256]{3,2,1,0:T(8,128)(2,1)} %refs_0_.1, f32[8,256,256]{2,1,0:T(8,128)} %get-tuple-element.21.refs_1_, f32[8,256,256]{2,1,0:T(8,128)S(1)} %get-tuple-element.22.refs_2_, f32[8,1,256]{2,1,0:T(1,128)S(1)} %get-tuple-element.23.refs_3_, f32[8,128]{1,0:T(8,128)S(1)} %get-tuple-element.24.refs_4_, ...), custom_call_target="tpu_custom_call" | custom-call | tf_op jit(solution)/shard_map/finish/pallas_call | solution.py:529
  (2 shorter events, 0.0 us)
Async XLA Ops:
  1.9 2.8 %collective-permute-start.1 = (bf16[1056,256]{1,0:T(8,128)(2,1)S(1)}, bf16[1056,256]{1,0:T(8,128)(2,1)S(1)}, u32[]{:S(2)}, u32[]{:S(2)}) collective-permute-start(bf16[1056,256]{1,0:T(8,128)(2,1)S(1)} %get-tuple-element.17), channel_id=1, source_target_pairs={{0,1},{1,0},{2,3},{3,2},{4,5},{5,4},{6,7},{7,6},{8,9},{9,8},{10,11... | collective-permute-start | bytes 1622024 | tf_op jit(solution)/shard_map/ppermute | solution.py:563
  2.0 16.0 %collective-permute-start = (bf16[1056,256]{1,0:T(8,128)(2,1)S(1)}, bf16[1056,256]{1,0:T(8,128)(2,1)S(1)}, u32[]{:S(2)}, u32[]{:S(2)}) collective-permute-start(bf16[1056,256]{1,0:T(8,128)(2,1)S(1)} %get-tuple-element.16), channel_id=1, source_target_pairs={{0,15},{1,2},{2,1},{3,4},{4,3},{5,6},{6,5},{7,8},{8,7},{9,10},{10,... | collective-permute-start | bytes 1622024 | tf_op jit(solution)/shard_map/ppermute | solution.py:562
  5.3 15.5 %all-to-all-start = ((f32[8,8,128]{2,1,0:T(8,128)}), f32[8,8,128]{2,1,0:T(8,128)S(1)}, u32[]{:S(2)}, u32[]{:S(2)}) async-start(f32[8,8,128]{2,1,0:T(8,128)} %broadcast_in_dim.15), calls=%async_computation | async-start | bytes 65536 | tf_op jit(solution)/shard_map/all_to_all | solution.py:566

commit v11 on v10

--- a/solution.py
+++ b/solution.py
@@ -199,40 +199,51 @@
     return grams
 
 
-def slab_copies(src_ref, dst_ref, sems):
+def slab_copies(src_ref, dst_ref, sems, only=None):
     size = PAIR * TILE
-    return [
-        pltpu.make_async_copy(
-            src_ref.at[:, :, pl.ds(i * size, size), :], dst_ref.at[:, :, pl.ds(i * size, size), :], sems.at[i]
+
+    def slab(at):
+        rows = pl.ds(pl.multiple_of(at * size, size), size)
+        return pltpu.make_async_copy(
+            src_ref.at[:, :, rows, :], dst_ref.at[:, :, rows, :], sems.at[at]
         )
-        for i in range(src_ref.shape[2] // size)
-    ]
+
+    return slab(only) if only is not None else [slab(i) for i in range(src_ref.shape[2] // size)]
 
 
 def own_gram_kernel(odd_ref, state_hbm_ref, near_ref, own_ref, gram_ref, like_ref, *scratch):
-    state_ref, turned_ref, sems = scratch
+    state_ref, near_turned_ref, turned_ref, sems = scratch
     steps = gram_ref.shape[0] // PAIR
     copies = slab_copies(state_hbm_ref, state_ref, sems)
     for copy in copies:
         copy.start()
     like_ref[...] = own_ref[...] + from_parts(near_ref)
-    pairs = []
-    for step in range(steps):
-        copies[step].wait()
-    for step in range(steps):
-        tiles = zip(pair_tiles(state_ref, step, steps), pair_tiles(near_ref, step, steps))
-        pairs.append([jnp.concatenate([x, y], axis=0) for x, y in tiles])
-        turn_tiles(pairs[-1][1], pairs[-1][2], turned_ref, step)
-    weights = [None] * state_ref.shape[0] + halo_weights(odd_ref[0] == 1)
-    for step in range(steps):
-        grams = gram_of(pairs[step], turned_ref, weights, step, steps)
-        for at in range(PAIR):
-            gram_ref[step * PAIR + at] = grams[at]
+
+    def add_strip(ref, turned_ref, weights, first):
+        def turn(step, carry):
+            tiles = pair_tiles(ref, step, steps)
+            turn_tiles(tiles[1], tiles[2], turned_ref, step)
+            return carry
+
+        def pair(step, carry):
+            grams = gram_of(pair_tiles(ref, step, steps), turned_ref, weights, step, steps)
+            for at in range(PAIR):
+                region = step * PAIR + at
+                gram_ref[region] = grams[at] if first else gram_ref[region] + grams[at]
+            return carry
+
+        lax.fori_loop(0, steps, turn, 0)
+        lax.fori_loop(0, steps, pair, 0)
+
+    add_strip(near_ref, near_turned_ref, halo_weights(odd_ref[0] == 1), True)
+    for copy in copies:
+        copy.wait()
+    add_strip(state_ref, turned_ref, [None] * state_ref.shape[0], False)
 
 
 def own_gram(odd, state, near, own):
     lon_dev, nvar, lat, members = state.shape
-    depth = (lon_dev + HALO) * nvar * TILE
+    tiles = lat // TILE
     vmem = pl.BlockSpec(memory_space=pltpu.VMEM)
     return pl.pallas_call(
         own_gram_kernel,
@@ -249,7 +260,8 @@
         ],
         scratch_shapes=[
             pltpu.VMEM(state.shape, state.dtype),
-            pltpu.VMEM((lat // TILE, members, depth), state.dtype),
+            pltpu.VMEM((tiles, members, HALO * nvar * TILE), state.dtype),
+            pltpu.VMEM((tiles, members, lon_dev * nvar * TILE), state.dtype),
             pltpu.SemaphoreType.DMA((lat // (PAIR * TILE),)),
         ],
         compiler_params=pltpu.CompilerParams(vmem_limit_bytes=16 * 2**20),
@@ -296,13 +308,18 @@
 
     lax.fori_loop(0, steps, turn, 0)
 
-    def pair(step, most):
+    def pair(step, carry):
         weights = halo_weights(odd_ref[0] == 0)
         grams = gram_of(pair_tiles(halo_ref, step, steps), turned_ref, weights, step, steps)
         for at in range(PAIR):
             region = step * PAIR + at
             gram_ref[region] = gram_in_ref[region] + grams[at]
         keep(step).start()
+        return carry
+
+    lax.fori_loop(0, steps, pair, 0)
+
+    def exponentials(step, most):
         for at in range(PAIR):
             region = step * PAIR + at
             across, down = diagonal(gram_ref, region)
@@ -321,7 +338,7 @@
             mass_ref[region] = jnp.concatenate(masses, axis=1)
         return most
 
-    most = lax.fori_loop(0, steps, pair, jnp.zeros((ROWS, 128), jnp.float32))
+    most = lax.fori_loop(0, steps, exponentials, jnp.zeros((ROWS, 128), jnp.float32))
     most_ref[...] = jnp.max(most.reshape(ROWS // TILE, TILE, 128), axis=0)
 
     def drain(step, carry):
@@ -477,9 +494,6 @@
         at = pl.ds(pl.multiple_of(pair * size, size), size)
         return pltpu.make_async_copy(result_ref.at[pair], out_ref.at[:, :, at, :], sems.at[pair])
 
-    for copy in fetches:
-        copy.wait()
-
     def group(at, carry):
         first = at * GROUP
         moves, least_i, least_j = transports_scaled(
@@ -487,6 +501,7 @@
         )
         for pair in range(GROUP // PAIR):
             where = at * (GROUP // PAIR) + pair
+            slab_copies(state_hbm_ref, state_ref, state_sems, where).wait()
             result_ref[where] = transform(state_ref, where, moves[pair * PAIR : (pair + 1) * PAIR])
             send(where).start()
         return jnp.minimum(carry[0], least_i), jnp.minimum(carry[1], least_j)

time: 43.4 us -> 42.6 us (0.982)
  waiting for transfers between devices: 4.28 us -> 3.47 us
    pallas_call x1, Pallas kernels: 2.55 us -> 3.36 us  [own_gram(): pl.pallas_call(own_gram_kernel, in_specs=[pl.BlockSpec(memory_space=pltpu...]
    ppermute x1, waiting for transfers between devices: 4.28 us -> 3.46 us  [on_device(): far = lax.ppermute(for_far, 'lon', far_pairs)]
  transfers between devices with their start and end apart: 3 -> 3, of which waited for: 1 -> 1; matrix products, arithmetic and copies ran while one was open for 2% -> 2% of each run, Pallas kernels for 12% -> 14%
where the time goes in v11:
time: 42.6 us; the launch traced here: 42.3 us
  Pallas kernels  29.5 us (69%)
  starting transfers between devices  8.68 us (20%)
  waiting for transfers between devices  3.47 us (8%)
  local copies, waits for them, and re-layouts  0.62 us (1%)
    pallas_call x1, Pallas kernels, finish(): pl.pallas_call(functools.partial(finish_kernel, count, scale), in_specs=[...  21.9 us
    all_to_all x1, starting transfers between devices, on_device(): lax.all_to_all(jnp.broadcast_to(part, (count // 2 * TILE, 128)), 'lon', 0...  5.91 us
    ppermute x1, waiting for transfers between devices, on_device(): far = lax.ppermute(for_far, 'lon', far_pairs)  3.46 us
    pallas_call x1, Pallas kernels, own_gram(): pl.pallas_call(own_gram_kernel, in_specs=[pl.BlockSpec(memory_space=pltpu...  3.36 us
    ppermute x1, starting transfers between devices, on_device(): far = lax.ppermute(for_far, 'lon', far_pairs)  2.65 us
    pallas_call x1, Pallas kernels, prepare(): pl.pallas_call(functools.partial(prepare_kernel, scale), in_specs=[pl.Blo...  2.39 us
    pallas_call x1, Pallas kernels, observe(): pl.pallas_call(observe_kernel, in_specs=[pl.BlockSpec(memory_space=pltpu....  1.84 us
  transfers between devices with their start and end apart: 3, of which 1 were waited for; matrix products, arithmetic and copies ran while one was open for 2% of the time, Pallas kernels for 14%

profile of v11, /device:TPU:1, one launch (start us, length us, event | category | flops | bytes accessed | tf_op | source)
XLA Modules:
  0.0 42.3 jit_solution(4460137891422783503)
XLA Ops:
  0.0 1.8 %observe.1 = (f32[8,256]{1,0:T(8,128)S(1)}, bf16[1056,256]{1,0:T(8,128)(2,1)S(1)}, bf16[1056,256]{1,0:T(8,128)(2,1)S(1)}, f32[8,128]{1,0:T(8,128)S(1)}) custom-call(s32[1]{0:T(128)} %bitcast.refs_0_.odd_ref, bf16[8,4,64,256]{3,2,1,0:T(8,128)(2,1)} %refs_0_.1, bf16[2048,256]{1,0:T(8,128)(2,1)} %bitcast.9, s32[1,256]{1,0:T(1,128)} %bitcast.10, ...), custom_call_target="tpu_custom_call" | custom-call | tf_op jit(solution)/shard_map/observe/pallas_call | solution.py:119
  1.9 0.1 collective-permute-start.1
  2.0 2.7 %collective-permute-start = (bf16[1056,256]{1,0:T(8,128)(2,1)S(1)}, bf16[1056,256]{1,0:T(8,128)(2,1)S(1)}, u32[]{:S(2)}, u32[]{:S(2)}) collective-permute-start(bf16[1056,256]{1,0:T(8,128)(2,1)S(1)} %get-tuple-element.16), channel_id=1, source_target_pairs={{0,15},{1,2},{2,1},{3,4},{4,3},{5,6},{6,5},{7,8},{8,7},{9,10},{10,... | collective-permute-start | bytes 1622024 | tf_op jit(solution)/shard_map/ppermute | solution.py:577
  4.6 0.0 collective-permute-done.1.near_ref
  4.7 0.6 %broadcast_in_dim.15 = f32[8,8,128]{2,1,0:T(8,128)} broadcast(f32[128]{0:T(128)S(1)} %bitcast_add_fusion), dimensions={2} | broadcast | bytes 33280 | tf_op jit(solution)/shard_map/broadcast_in_dim | solution.py:582
  5.3 5.9 %all-to-all-start = ((f32[8,8,128]{2,1,0:T(8,128)}), f32[8,8,128]{2,1,0:T(8,128)S(1)}, u32[]{:S(2)}, u32[]{:S(2)}) async-start(f32[8,8,128]{2,1,0:T(8,128)} %broadcast_in_dim.15), calls=%async_computation | async-start | bytes 65536 | tf_op jit(solution)/shard_map/all_to_all | solution.py:581
  11.2 3.4 %own_gram.1 = (f32[8,256,256]{2,1,0:T(8,128)S(1)}, f32[8,256]{1,0:T(8,128)S(1)}) custom-call(s32[1]{0:T(128)} %bitcast.refs_0_.odd_ref, bf16[8,4,64,256]{3,2,1,0:T(8,128)(2,1)} %refs_0_.1, bf16[1056,256]{1,0:T(8,128)(2,1)S(1)} %collective-permute-done.1.near_ref, f32[8,256]{1,0:T(8,128)S(1)} %get-tuple-element.18.own_ref), custom_call_target="tpu_custom_call" | custom-call | tf_op jit(solution)/shard_map/own_gram/pallas_call | solution.py:248
  14.6 3.5 %collective-permute-done.refs_1_ = bf16[1056,256]{1,0:T(8,128)(2,1)S(1)} collective-permute-done((bf16[1056,256]{1,0:T(8,128)(2,1)S(1)}, bf16[1056,256]{1,0:T(8,128)(2,1)S(1)}, u32[]{:S(2)}, u32[]{:S(2)}) %collective-permute-start) | collective-permute-done | bytes 540704 | tf_op jit(solution)/shard_map/ppermute | solution.py:577
  18.0 2.4 %prepare.1 = (f32[8,256,256]{2,1,0:T(8,128)}, f32[8,256,256]{2,1,0:T(8,128)S(1)}, f32[8,1,256]{2,1,0:T(1,128)S(1)}, f32[8,128]{1,0:T(8,128)S(1)}, f32[8,256]{1,0:T(8,128)S(1)}) custom-call(s32[1]{0:T(128)} %bitcast.refs_0_.odd_ref, bf16[1056,256]{1,0:T(8,128)(2,1)S(1)} %collective-permute-done.refs_1_, f32[8,256,256]{2,1,0:T(8,128)S(1)} %get-tuple-element.19.refs_2_, ...), custom_call_target="tpu_custom_call" | custom-call | tf_op jit(solution)/shard_map/prepare/pallas_call | solution.py:355
  20.4 0.0 all-to-all-done
  20.4 21.9 %finish.1 = bf16[8,4,64,256]{3,2,1,0:T(8,128)(2,1)} custom-call(bf16[8,4,64,256]{3,2,1,0:T(8,128)(2,1)} %refs_0_.1, f32[8,256,256]{2,1,0:T(8,128)} %get-tuple-element.21.refs_1_, f32[8,256,256]{2,1,0:T(8,128)S(1)} %get-tuple-element.22.refs_2_, f32[8,1,256]{2,1,0:T(1,128)S(1)} %get-tuple-element.23.refs_3_, f32[8,128]{1,0:T(8,128)S(1)} %get-tuple-element.24.refs_4_, ...), custom_call_target="tpu_custom_call" | custom-call | tf_op jit(solution)/shard_map/finish/pallas_call | solution.py:544
  (2 shorter events, 0.0 us)
Async XLA Ops:
  1.9 2.8 %collective-permute-start.1 = (bf16[1056,256]{1,0:T(8,128)(2,1)S(1)}, bf16[1056,256]{1,0:T(8,128)(2,1)S(1)}, u32[]{:S(2)}, u32[]{:S(2)}) collective-permute-start(bf16[1056,256]{1,0:T(8,128)(2,1)S(1)} %get-tuple-element.17), channel_id=1, source_target_pairs={{0,1},{1,0},{2,3},{3,2},{4,5},{5,4},{6,7},{7,6},{8,9},{9,8},{10,11... | collective-permute-start | bytes 1622024 | tf_op jit(solution)/shard_map/ppermute | solution.py:578
  2.0 16.0 %collective-permute-start = (bf16[1056,256]{1,0:T(8,128)(2,1)S(1)}, bf16[1056,256]{1,0:T(8,128)(2,1)S(1)}, u32[]{:S(2)}, u32[]{:S(2)}) collective-permute-start(bf16[1056,256]{1,0:T(8,128)(2,1)S(1)} %get-tuple-element.16), channel_id=1, source_target_pairs={{0,15},{1,2},{2,1},{3,4},{4,3},{5,6},{6,5},{7,8},{8,7},{9,10},{10,... | collective-permute-start | bytes 1622024 | tf_op jit(solution)/shard_map/ppermute | solution.py:577
  5.3 15.1 %all-to-all-start = ((f32[8,8,128]{2,1,0:T(8,128)}), f32[8,8,128]{2,1,0:T(8,128)S(1)}, u32[]{:S(2)}, u32[]{:S(2)}) async-start(f32[8,8,128]{2,1,0:T(8,128)} %broadcast_in_dim.15), calls=%async_computation | async-start | bytes 65536 | tf_op jit(solution)/shard_map/all_to_all | solution.py:581

commit v12 on v11

v12 whole, which is shorter than its diff:
```python
import functools
import math

import jax
import jax.numpy as jnp
from jax import lax
from jax.experimental import pallas as pl
from jax.experimental.pallas import tpu as pltpu
from jax.sharding import PartitionSpec as P

REGION = 8
HALO = 4
SWEEPS = 4
EPS = 0.05
TILE = 8
PAIR = 2
LOG2E = 1.4426950408889634
ROWS = 32
FIRST = 3
LIFT, START, MASS = 20, -10, 60

HIGH = lax.Precision.HIGHEST


def line_weight(place):
    dist = jnp.maximum(0.0, jnp.maximum(HALO - place, place - (HALO + REGION - 1)))
    inside = (place >= 0) & (place < REGION + 2 * HALO)
    return jnp.where(inside, 1.0 - dist / (HALO + 1), 0.0)


def like_rows(rows):
    rows = rows.astype(jnp.float32)
    return rows[:TILE] + rows[TILE : 2 * TILE] + rows[2 * TILE : 3 * TILE]


def in_parts(values, extra):
    below = lax.broadcasted_iota(jnp.int32, values.shape, 0)
    extra_high = extra.astype(jnp.bfloat16).astype(jnp.float32)
    extra_middle = (extra - extra_high).astype(jnp.bfloat16).astype(jnp.float32)
    extra_low = extra - extra_high - extra_middle
    last = jnp.where(below == 0, extra_high, jnp.where(below == 1, extra_middle, extra_low))
    last = jnp.where(below < 3, last, 0.0)
    high = values.astype(jnp.bfloat16).astype(jnp.float32)
    middle = (values - high).astype(jnp.bfloat16).astype(jnp.float32)
    low = values - high - middle
    return jnp.concatenate([high, middle, low, last], axis=0).astype(jnp.bfloat16)


def observe_kernel(*refs):
    odd_ref, state_ref, planes_ref = refs[:3]
    own_ref, near_ref, far_ref, far_last_ref, part_ref = refs[6:11]
    cells_ref, index_ref, value_ref, var_ref, sems = refs[11:]
    lon_dev, lat, members = cells_ref.shape
    nobs = index_ref.shape[1]
    edge = planes_ref.shape[0] // lon_dev * HALO
    last = planes_ref.shape[0] - edge
    far_at = odd_ref[0] * last
    cut = far_ref.shape[1]
    far_planes = planes_ref.at[pl.ds(far_at, edge)]
    fetches = [
        (refs[3], index_ref),
        (refs[4], value_ref),
        (refs[5], var_ref),
        (state_ref.at[:, 0], cells_ref),
        (far_planes.at[:, pl.ds(0, cut), :], far_ref.at[pl.ds(0, edge)]),
        (planes_ref.at[pl.ds(last - far_at, edge)], near_ref.at[pl.ds(0, edge)]),
        (far_planes.at[:, pl.ds(cut, lat - cut), :], far_last_ref),
    ]
    copies = [
        pltpu.make_async_copy(src, dst, sems.at[i]) for i, (src, dst) in enumerate(fetches)
    ]
    for copy in copies:
        copy.start()
    for copy in copies[:4]:
        copy.wait()
    rows = cells_ref[...].reshape(lon_dev * lat, members)
    index = index_ref[...]
    sub = lax.broadcasted_iota(jnp.int32, (TILE, nobs), 0)
    table = jnp.where(
        sub == 0,
        index.astype(jnp.float32),
        jnp.where(sub == 1, value_ref[...], var_ref[...]),
    ).T
    index_col = table[:, 0:1].astype(jnp.int32)
    value = table[:, 1:2]
    var = table[:, 2:3]
    pick = index_col == lax.broadcasted_iota(jnp.int32, (nobs, lon_dev * lat), 1)
    pick = jnp.where(pick, 1.0, 0.0).astype(jnp.bfloat16)
    seen = jnp.dot(pick, rows, preferred_element_type=jnp.float32)
    centre = jnp.sum(seen, axis=1, keepdims=True) * (1.0 / members)
    spread = jnp.sum((seen - centre) ** 2, axis=1, keepdims=True) * (1.0 / (members - 1))
    innovation = (value - centre) ** 2 / (var + spread)
    part = jnp.sum(innovation, axis=0, keepdims=True)
    part_ref[...] = jnp.broadcast_to(part, part_ref.shape)
    terms = (value - seen) ** 2 * (1.0 / var)
    lon = (index // lat).astype(jnp.float32)
    along = index.astype(jnp.float32) - lon * lat
    blocks = own_ref.shape[0]
    block = lax.broadcasted_iota(jnp.int32, (blocks, nobs), 0).astype(jnp.float32)
    across = line_weight(along - REGION * block + HALO)
    side = jnp.where(odd_ref[0] == 1, float(REGION), float(-REGION))
    weights = [line_weight(lon + (HALO + shift)) * across for shift in (0.0, side, -side)]
    like = jnp.dot(
        jnp.concatenate(weights, axis=0), terms, precision=HIGH, preferred_element_type=jnp.float32
    )
    own_ref[...] = like[:blocks]
    near_ref[edge, : 4 * TILE, :] = in_parts(like[blocks : 2 * blocks], part)
    far_ref[edge, : 4 * TILE, :] = in_parts(like[2 * blocks :], jnp.zeros_like(part))
    for copy in copies[4:]:
        copy.wait()


def observe(odd, state, obs_index, obs_value, obs_var):
    lon_dev, nvar, lat, members = state.shape
    nobs = obs_index.size
    assert lat // REGION == TILE
    like = jax.ShapeDtypeStruct((lat // REGION, members), jnp.float32)
    planes = HALO * nvar
    cut = FIRST * PAIR * TILE
    near = pltpu.VMEM((planes + 1, lat, members), state.dtype)
    far = pltpu.VMEM((planes + 1, cut, members), state.dtype)
    far_last = pltpu.VMEM((planes, lat - cut, members), state.dtype)
    part = jax.ShapeDtypeStruct((TILE, 128), jnp.float32)
    arrays = state, state.reshape(-1, lat, members), obs_index[None], obs_value[None], obs_var[None]
    return pl.pallas_call(
        observe_kernel,
        in_specs=[pl.BlockSpec(memory_space=pltpu.SMEM)]
        + [pl.BlockSpec(memory_space=pltpu.HBM)] * len(arrays),
        out_specs=[pl.BlockSpec(memory_space=pltpu.VMEM)] * 5,
        out_shape=[like, near, far, far_last, part],
        scratch_shapes=[
            pltpu.VMEM((lon_dev, lat, members), state.dtype),
            pltpu.VMEM((1, nobs), jnp.int32),
            pltpu.VMEM((1, nobs), jnp.float32),
            pltpu.VMEM((1, nobs), jnp.float32),
            pltpu.SemaphoreType.DMA((7,)),
        ],
        compiler_params=pltpu.CompilerParams(vmem_limit_bytes=16 * 2**20),
        name="observe",
    )(odd, *[pltpu.with_memory_space_constraint(x, pltpu.HBM) for x in arrays])


def slab_of(refs, planes, at):
    size = PAIR * TILE
    for ref in refs:
        if at * size < ref.shape[1]:
            return ref[:planes, at * size : (at + 1) * size, :].astype(jnp.float32)
        at -= ref.shape[1] // size


def pair_tiles(load, step, steps):
    here = load(step)
    none = jnp.zeros_like(here[:, :TILE])
    before = load(step - 1)[:, TILE:] if step else none
    after = load(step + 1)[:, :TILE] if step + 1 < steps else none
    return before, here[:, :TILE], here[:, TILE:], after


def halo_weights(to_left):
    steps = [jnp.float32(1.0) - jnp.float32(d) / jnp.float32(HALO + 1) for d in range(HALO, 0, -1)]
    return [jnp.where(to_left, x, y) for x, y in zip(steps, steps[::-1])]


def turn(tile):
    return tile.reshape(-1, tile.shape[-1]).astype(jnp.bfloat16).T


def gram_of(tiles, turned, weights):
    planes, _, members = tiles[0].shape
    depth = planes * TILE
    row = lax.broadcasted_iota(jnp.int32, (TILE, members), 0)
    upper = row < HALO
    rowf = row.astype(jnp.float32)
    edge = line_weight(jnp.where(upper, rowf + (HALO + REGION), rowf - HALO))
    lane = lax.broadcasted_iota(jnp.int32, (1, depth), 1) & (TILE - 1)
    take_next = jnp.where(lane < HALO, 1.0, 0.0).astype(jnp.bfloat16)
    take_prev = jnp.where(lane < HALO, 0.0, 1.0).astype(jnp.bfloat16)
    grams = []
    for at in (1, 2):
        margin = jnp.where(upper, tiles[at + 1], tiles[at - 1])
        main_rows, margin_rows = [], []
        for plane, weight in enumerate(weights):
            own = tiles[at][plane]
            main_rows.append(own if weight is None else own * weight)
            margin_rows.append(margin[plane] * (edge if weight is None else edge * weight))
        weighted = jnp.stack(main_rows + margin_rows)
        weighted = weighted.reshape(2 * depth, members).astype(jnp.bfloat16)
        margin = turned[at + 1] * take_next + turned[at - 1] * take_prev
        both = jnp.concatenate([turned[at], margin], axis=1)
        grams.append(jnp.dot(both, weighted, preferred_element_type=jnp.float32))
    return grams


def slab_copies(src_ref, dst_ref, sems, only=None):
    size = PAIR * TILE

    def slab(at):
        rows = pl.ds(pl.multiple_of(at * size, size), size)
        return pltpu.make_async_copy(
            src_ref.at[:, :, rows, :], dst_ref.at[:, :, rows, :], sems.at[at]
        )

    return slab(only) if only is not None else [slab(i) for i in range(src_ref.shape[2] // size)]


def own_gram_kernel(odd_ref, state_hbm_ref, near_ref, own_ref, *refs):
    gram_refs, like_ref, state_ref, sems = refs[:-3], refs[-3], refs[-2], refs[-1]
    near_planes = near_ref.shape[0] - 1
    nvar = near_planes // HALO
    lon_dev = state_ref.shape[0]
    steps = state_ref.shape[2] // (PAIR * TILE)
    copies = slab_copies(state_hbm_ref, state_ref, sems)
    for copy in copies:
        copy.start()
    like_ref[...] = own_ref[...] + like_rows(near_ref[near_planes, : 4 * TILE, :])
    size = PAIR * TILE

    def load(step):
        own = state_ref[:, :, step * size : (step + 1) * size, :].astype(jnp.float32)
        own = own.reshape(lon_dev * nvar, size, own.shape[-1])
        return jnp.concatenate([own, slab_of([near_ref], near_planes, step)], axis=0)

    weights = [None] * (lon_dev * nvar)
    weights += [w for w in halo_weights(odd_ref[0] == 1) for _ in range(nvar)]
    for copy in copies:
        copy.wait()
    slabs = [load(step) for step in range(steps)]
    add_grams(slabs, weights, range(steps), None, gram_refs)


def add_grams(slabs, weights, pairs, old_refs, new_refs):
    steps = len(slabs)
    none = jnp.zeros_like(slabs[pairs[0]][:, :TILE])
    turned_none = jnp.zeros((none.shape[-1], none.shape[0] * TILE), jnp.bfloat16)
    tiles, turned = {}, {}
    for at in range(pairs[0] * PAIR - 1, pairs[-1] * PAIR + PAIR + 1):
        if 0 <= at < steps * PAIR:
            half = at % PAIR
            tiles[at] = slabs[at // PAIR][:, half * TILE : (half + 1) * TILE]
            turned[at] = turn(tiles[at])
        else:
            tiles[at], turned[at] = none, turned_none
    for index, pair in enumerate(pairs):
        window = range(pair * PAIR - 1, pair * PAIR + PAIR + 1)
        grams = gram_of([tiles[i] for i in window], [turned[i] for i in window], weights)
        for half in range(PAIR):
            per = new_refs[0].shape[0]
            ref, region = divmod(index * PAIR + half, per)
            gram = grams[half]
            new_refs[ref][region] = gram if old_refs is None else old_refs[ref][region] + gram


def own_gram(odd, state, near, own):
    _, _, lat, members = state.shape
    vmem = pl.BlockSpec(memory_space=pltpu.VMEM)
    half = jax.ShapeDtypeStruct((lat // REGION // 2, members, members), jnp.float32)
    return pl.pallas_call(
        own_gram_kernel,
        in_specs=[
            pl.BlockSpec(memory_space=pltpu.SMEM),
            pl.BlockSpec(memory_space=pltpu.HBM),
            vmem,
            vmem,
        ],
        out_specs=[vmem] * 3,
        out_shape=[half, half, jax.ShapeDtypeStruct(own.shape, jnp.float32)],
        scratch_shapes=[
            pltpu.VMEM(state.shape, state.dtype),
            pltpu.SemaphoreType.DMA((lat // (PAIR * TILE),)),
        ],
        compiler_params=pltpu.CompilerParams(vmem_limit_bytes=24 * 2**20),
        name="own_gram",
    )(odd, pltpu.with_memory_space_constraint(state, pltpu.HBM), near, own)


def halves(ref, region, rows):
    members = ref.shape[-1]
    return [ref[region, rows, at : at + 128] for at in range(0, members, 128)]


def diagonal(gram_ref, region):
    members = gram_ref.shape[-1]
    across = [None] * (members // 128)
    down = []
    for start in range(0, members, ROWS):
        lane = start // 128
        gram = gram_ref[region, pl.ds(start, ROWS), lane * 128 : lane * 128 + 128]
        i = lax.broadcasted_iota(jnp.int32, gram.shape, 0) + start
        j = lax.broadcasted_iota(jnp.int32, gram.shape, 1) + lane * 128
        kept = jnp.where(i == j, gram, 0.0)
        down.append(jnp.broadcast_to(jnp.sum(kept, axis=1, keepdims=True), gram.shape))
        part = jnp.sum(kept.reshape(ROWS // TILE, TILE, 128), axis=0)
        across[lane] = part if across[lane] is None else across[lane] + part
    return [jnp.sum(x, axis=0, keepdims=True) for x in across], down


def kernel_matrices(gram_ref, kernel_ref, mass_ref, scale):
    members = gram_ref.shape[-1]
    most = None
    for region in range(gram_ref.shape[0]):
        across, down = diagonal(gram_ref, region)
        across = [0.5 * LIFT - x * scale for x in across]
        masses = [0.0 for _ in across]
        for i, start in enumerate(range(0, members, ROWS)):
            rows = pl.ds(start, ROWS)
            base = 0.5 * LIFT - down[i] * scale
            for lane, (gram, x) in enumerate(zip(halves(gram_ref, region, rows), across)):
                part = jnp.exp2(gram * (2.0 * scale) + base + x)
                kernel_ref[region, rows, lane * 128 : lane * 128 + 128] = part
                most = part if most is None else jnp.maximum(most, part)
                part = jnp.sum(part.reshape(ROWS // TILE, TILE, 128), axis=0)
                masses[lane] = masses[lane] + part
        masses = [jnp.sum(x, axis=0, keepdims=True) for x in masses]
        mass_ref[region] = jnp.concatenate(masses, axis=1)
    return jnp.max(most.reshape(ROWS // TILE, TILE, 128), axis=0)


def far_grams(odd_ref, halo_refs, lat, pairs, old_ref, new_ref):
    planes = halo_refs[0].shape[0] - 1
    slabs = [None] * (lat // (PAIR * TILE))
    for at in range(max(pairs[0] - 1, 0), min(pairs[-1] + 2, len(slabs))):
        slabs[at] = slab_of(halo_refs, planes, at)
    weights = [w for w in halo_weights(odd_ref[0] == 0) for _ in range(planes // HALO)]
    add_grams(slabs, weights, pairs, [old_ref], [new_ref])


def prepare_kernel(scale, lat, *refs):
    odd_ref, halo_ref, old_ref, like_in_ref = refs[:4]
    gram_hbm_ref, kernel_ref, mass_ref, most_ref, like_ref, gram_ref, sem = refs[4:]
    like_ref[...] = like_in_ref[...] + like_rows(halo_ref[halo_ref.shape[0] - 1, : 4 * TILE, :])
    far_grams(odd_ref, [halo_ref], lat, range(gram_ref.shape[0] // PAIR), old_ref, gram_ref)
    keep = pltpu.make_async_copy(gram_ref, gram_hbm_ref, sem)
    keep.start()
    most_ref[...] = kernel_matrices(gram_ref, kernel_ref, mass_ref, scale)
    keep.wait()


def prepare(odd, halo, gram, like, lat, scale):
    vmem = pl.BlockSpec(memory_space=pltpu.VMEM)
    return pl.pallas_call(
        functools.partial(prepare_kernel, scale, lat),
        in_specs=[pl.BlockSpec(memory_space=pltpu.SMEM)] + [vmem] * 3,
        out_specs=[pl.BlockSpec(memory_space=pltpu.HBM)] + [vmem] * 4,
        out_shape=[
            pltpu.HBM(gram.shape, jnp.float32),
            jax.ShapeDtypeStruct(gram.shape, jnp.float32),
            jax.ShapeDtypeStruct((gram.shape[0], 1, like.shape[1]), jnp.float32),
            jax.ShapeDtypeStruct((TILE, 128), jnp.float32),
            jax.ShapeDtypeStruct(like.shape, jnp.float32),
        ],
        scratch_shapes=[pltpu.VMEM(gram.shape, jnp.float32), pltpu.SemaphoreType.DMA],
        compiler_params=pltpu.CompilerParams(vmem_limit_bytes=24 * 2**20),
        name="prepare",
    )(odd, halo, gram, like)


def fold(values, op):
    out = values[0]
    for value in values[1:]:
        out = op(out, value)
    return out


def transports_scaled(kernel_ref, weights, mass_ref):
    regions = range(kernel_ref.shape[0])
    members = kernel_ref.shape[-1]
    starts = range(0, members, ROWS)
    lanes = range(members // 128)
    share = 2.0**MASS / members

    def lane_parts(row):
        return [row[:, lane * 128 : lane * 128 + 128] for lane in lanes]

    def settle(totals, region):
        return [w / x for w, x in zip(lane_parts(weights[region : region + 1]), totals)]

    def masses_of(region, rows, factor):
        parts = [k * f for k, f in zip(halves(kernel_ref, region, rows), factor)]
        mass = jnp.sum(fold(parts, jnp.add), axis=1, keepdims=True)
        mass = jnp.broadcast_to(mass, (ROWS, 128))
        near = pl.reciprocal(mass, approx=True)
        return parts, mass, near * (2.0 - mass * near)

    def sweep(_, carry):
        least_i, least_j, factors = carry
        next_i, next_j, next_factors = [], [], []
        for region, low_i, low_j, factor in zip(regions, least_i, least_j, factors):
            totals = [None for _ in lanes]
            for start in starts:
                rows = pl.ds(start, ROWS)
                _, mass, ratio = masses_of(region, rows, factor)
                low_j = jnp.minimum(low_j, mass)
                for lane, kernel in enumerate(halves(kernel_ref, region, rows)):
                    part = jnp.sum((kernel * ratio).reshape(ROWS // TILE, TILE, 128), axis=0)
                    totals[lane] = part if totals[lane] is None else totals[lane] + part
            totals = [jnp.sum(x, axis=0, keepdims=True) * share for x in totals]
            next_i.append(jnp.minimum(low_i, fold(totals, jnp.minimum)))
            next_j.append(low_j)
            next_factors.append(settle(totals, region))
        return next_i, next_j, next_factors

    totals = [[x * 2.0**START for x in lane_parts(mass_ref[region])] for region in regions]
    least_i = [fold(x, jnp.minimum) for x in totals]
    least_j = [jnp.full((ROWS, 128), 1e30, jnp.float32) for _ in regions]
    factors = [settle(x, region) for x, region in zip(totals, regions)]
    carry = lax.fori_loop(0, SWEEPS - 1, sweep, (least_i, least_j, factors))
    least_i, least_j, factors = carry
    moves, last_j = [], []
    for region, low_j, factor in zip(regions, least_j, factors):
        blocks = []
        for start in starts:
            parts, mass, ratio = masses_of(region, pl.ds(start, ROWS), factor)
            low_j = jnp.minimum(low_j, mass)
            blocks.append(jnp.concatenate([x * ratio for x in parts], axis=1).astype(jnp.bfloat16))
        moves.append(jnp.concatenate(blocks, axis=0))
        last_j.append(low_j)
    return moves, fold(least_i, jnp.minimum), fold(last_j, jnp.minimum)


def transport_logs(gram, logw, scale):
    members = gram.shape[-1]
    j = lax.broadcasted_iota(jnp.int32, gram.shape, 0)
    i = lax.broadcasted_iota(jnp.int32, gram.shape, 1)
    kept = jnp.where(i == j, gram, 0.0)
    down = jnp.sum(kept, axis=1, keepdims=True)
    across = jnp.sum(kept, axis=0, keepdims=True)
    cost = (down + across - 2.0 * gram) * scale
    pot_g = jnp.zeros((members, 1), jnp.float32)
    for sweep in range(SWEEPS):
        term = pot_g - cost
        top = jnp.max(term, axis=0, keepdims=True)
        pot_f = logw - top - jnp.log(jnp.sum(jnp.exp2(term - top), axis=0, keepdims=True)) * LOG2E
        term = pot_f - cost
        top = jnp.max(term, axis=1, keepdims=True)
        pot_g = -math.log2(members) - top
        pot_g = pot_g - jnp.log(jnp.sum(jnp.exp2(term - top), axis=1, keepdims=True)) * LOG2E
    return (members * jnp.exp2(pot_f + pot_g - cost)).astype(jnp.bfloat16)


def transform(state_ref, pair, moves):
    lon_dev, nvar, _, members = state_ref.shape
    size = PAIR * TILE
    own = state_ref[:, :, pair * size : (pair + 1) * size, :].astype(jnp.float32)
    parts = []
    for region, move in enumerate(moves):
        cells = own[:, :, region * TILE : (region + 1) * TILE].astype(jnp.bfloat16)
        cells = cells.reshape(lon_dev * nvar * TILE, members)
        moved = lax.dot_general(
            cells, move, (((1,), (1,)), ((), ())), preferred_element_type=jnp.float32
        )
        parts.append(moved.reshape(lon_dev, nvar, TILE, members))
    return jnp.concatenate(parts, axis=2).astype(jnp.bfloat16)


def analyse_half(half, count, scale, like_ref, sums_ref, kernel_ref, mass_ref, most, gram, state, out):
    regions = kernel_ref.shape[0]
    pairs = regions // PAIR
    size = PAIR * TILE
    state_hbm_ref, state_ref, state_sems = state
    out_ref, result_ref, out_sems = out
    first = half * pairs

    def fetch(pair):
        rows = pl.ds((first + pair) * size, size)
        return pltpu.make_async_copy(
            state_hbm_ref.at[:, :, rows, :],
            state_ref.at[:, :, pl.ds(pair * size, size), :],
            state_sems.at[pair],
        )

    def send(pair):
        rows = pl.ds((first + pair) * size, size)
        return pltpu.make_async_copy(
            result_ref.at[pair], out_ref.at[:, :, rows, :], out_sems.at[pair]
        )

    total = jnp.sum(sums_ref[...], axis=0, keepdims=True)[:, 0:1] * (1.0 / TILE)
    like = like_ref[half * regions : (half + 1) * regions, :]
    like = -0.5 * (count / total) * like
    like = like - jnp.max(like, axis=1, keepdims=True)
    logw = (like - jnp.log(jnp.sum(jnp.exp(like), axis=1, keepdims=True))) * LOG2E
    moves, least_i, least_j = transports_scaled(kernel_ref, jnp.exp2(logw + MASS), mass_ref)
    for pair in range(pairs):
        fetch(pair).wait()
        result_ref[pair] = transform(state_ref, pair, moves[pair * PAIR : (pair + 1) * PAIR])
        send(pair).start()
    row, col, most = jnp.min(least_i), jnp.min(least_j), jnp.max(most)
    sound = (row >= 2.0**-24) & (col >= 2.0**-30) & (most <= 2.0**30) & (row * col >= 2.0**-34)
    for pair in range(pairs):
        send(pair).wait()

    @pl.when(jnp.logical_not(sound))
    def _():
        for pair in range(pairs):
            again = [
                transport_logs(gram(region), logw[region : region + 1], scale)
                for region in range(pair * PAIR, (pair + 1) * PAIR)
            ]
            result_ref[pair] = transform(state_ref, pair, again)
            send(pair).start()
            send(pair).wait()


def start_fetches(half, pairs, state):
    state_hbm_ref, state_ref, state_sems = state
    size = PAIR * TILE
    for pair in range(pairs):
        rows = pl.ds((half * pairs + pair) * size, size)
        pltpu.make_async_copy(
            state_hbm_ref.at[:, :, rows, :],
            state_ref.at[:, :, pl.ds(pair * size, size), :],
            state_sems.at[pair],
        ).start()


def first_kernel(count, scale, *refs):
    state_hbm_ref, gram_hbm_ref, kernel_ref, mass_ref, most_ref, like_ref, sums_ref = refs[:7]
    out_ref, result_ref, state_ref, gram_ref, out_sems, state_sems, sem = refs[7:]
    state = state_hbm_ref, state_ref, state_sems
    start_fetches(0, kernel_ref.shape[0] // PAIR, state)

    def gram(region):
        copy = pltpu.make_async_copy(gram_hbm_ref.at[region], gram_ref, sem)
        copy.start()
        copy.wait()
        return gram_ref[...]

    out = out_ref, result_ref, out_sems
    analyse_half(
        0, count, scale, like_ref, sums_ref, kernel_ref, mass_ref, most_ref[...], gram, state, out
    )


def last_kernel(count, scale, *refs):
    odd_ref, halo_ref, halo_last_ref, old_ref, state_hbm_ref, like_ref, sums_ref = refs[:7]
    out_ref, result_ref, state_ref, gram_ref, kernel_ref, mass_ref, out_sems, state_sems = refs[8:]
    state = state_hbm_ref, state_ref, state_sems
    pairs = gram_ref.shape[0] // PAIR
    start_fetches(1, pairs, state)
    halos = [halo_ref, halo_last_ref]
    far_grams(odd_ref, halos, 2 * pairs * PAIR * TILE, range(pairs, 2 * pairs), old_ref, gram_ref)
    most = kernel_matrices(gram_ref, kernel_ref, mass_ref, scale)
    out = out_ref, result_ref, out_sems
    analyse_half(
        1,
        count,
        scale,
        like_ref,
        sums_ref,
        kernel_ref,
        mass_ref,
        most,
        lambda region: gram_ref[region],
        state,
        out,
    )


def half_buffers(state):
    lon_dev, nvar, lat, members = state.shape
    pairs = lat // (PAIR * TILE) // 2
    return [
        pltpu.VMEM((pairs, lon_dev, nvar, PAIR * TILE, members), state.dtype),
        pltpu.VMEM((lon_dev, nvar, lat // 2, members), state.dtype),
    ], [pltpu.SemaphoreType.DMA((pairs,)), pltpu.SemaphoreType.DMA((pairs,))]


def analyse_first(state, gram, kernel, mass, most, like, sums, count, scale):
    members = state.shape[-1]
    vmem = pl.BlockSpec(memory_space=pltpu.VMEM)
    hbm = pl.BlockSpec(memory_space=pltpu.HBM)
    buffers, sems = half_buffers(state)
    return pl.pallas_call(
        functools.partial(first_kernel, count, scale),
        in_specs=[hbm, hbm] + [vmem] * 5,
        out_specs=pl.BlockSpec(memory_space=pl.ANY),
        out_shape=jax.ShapeDtypeStruct(state.shape, state.dtype),
        scratch_shapes=buffers
        + [pltpu.VMEM((members, members), jnp.float32)]
        + sems
        + [pltpu.SemaphoreType.DMA],
        compiler_params=pltpu.CompilerParams(vmem_limit_bytes=24 * 2**20),
        name="analyse_first",
    )(
        *[pltpu.with_memory_space_constraint(x, pltpu.HBM) for x in (state, gram)],
        kernel,
        mass,
        most,
        like,
        sums,
    )


def analyse_last(odd, halo, halo_last, gram, state, like, sums, out, count, scale):
    vmem = pl.BlockSpec(memory_space=pltpu.VMEM)
    hbm = pl.BlockSpec(memory_space=pltpu.HBM)
    buffers, sems = half_buffers(state)
    return pl.pallas_call(
        functools.partial(last_kernel, count, scale),
        in_specs=[pl.BlockSpec(memory_space=pltpu.SMEM)]
        + [vmem] * 3
        + [hbm, vmem, vmem, pl.BlockSpec(memory_space=pl.ANY)],
        out_specs=pl.BlockSpec(memory_space=pl.ANY),
        out_shape=jax.ShapeDtypeStruct(state.shape, state.dtype),
        input_output_aliases={7: 0},
        scratch_shapes=buffers
        + [pltpu.VMEM(gram.shape, jnp.float32)] * 2
        + [pltpu.VMEM((gram.shape[0], 1, gram.shape[2]), jnp.float32)]
        + sems,
        compiler_params=pltpu.CompilerParams(vmem_limit_bytes=24 * 2**20),
        name="analyse_last",
    )(
        odd,
        halo,
        halo_last,
        gram,
        pltpu.with_memory_space_constraint(state, pltpu.HBM),
        like,
        sums,
        out,
    )


def on_device(state, obs_index, obs_value, obs_var):
    nvar = state.shape[1]
    count = lax.axis_size("lon")
    odd = (lax.axis_index("lon") & 1).astype(jnp.int32).reshape(1)
    near_pairs = [(i, i ^ 1) for i in range(count)]
    far_pairs = [(i, (i + 1 if i % 2 else i - 1) % count) for i in range(count)]
    own_like, for_near, for_far, for_far_last, part = observe(
        odd, state, obs_index, obs_value, obs_var
    )
    far = lax.ppermute(for_far, "lon", far_pairs)
    near = lax.ppermute(for_near, "lon", near_pairs)
    sums = near[HALO * nvar, 3 * TILE : 3 * TILE + 3, :128].astype(jnp.float32)
    sums = jnp.broadcast_to(part[0] + jnp.sum(sums, axis=0), (count // 2 * TILE, 128))
    sums, for_far_last = lax.optimization_barrier((sums, for_far_last))
    sums = lax.all_to_all(
        sums,
        "lon",
        0,
        0,
        axis_index_groups=[list(range(core, count, 2)) for core in range(2)],
        tiled=True,
    )
    far_last = lax.ppermute(for_far_last, "lon", far_pairs)
    offsets = range(REGION + 2 * HALO)
    line = [1.0 - max(0, HALO - p, p - (HALO + REGION - 1)) / (HALO + 1) for p in offsets]
    scale = LOG2E / EPS / (nvar * sum(line) ** 2)
    gram_first, gram_last, like = own_gram(odd, state, near, own_like)
    gram, kernel, mass, most, like = prepare(odd, far, gram_first, like, state.shape[2], scale)
    nobs = float(obs_index.shape[0] * count)
    out = analyse_first(state, gram, kernel, mass, most, like, sums, nobs, scale)
    return analyse_last(odd, far, far_last, gram_last, state, like, sums, out, nobs, scale)


def solution(mesh):
    return jax.shard_map(
        on_device,
        mesh=mesh,
        in_specs=(
            P(("ens", "lon"), None, None, None),
            P(("ens", "lon")),
            P(("ens", "lon")),
            P(("ens", "lon")),
        ),
        out_specs=P(("ens", "lon"), None, None, None),
        check_vma=False,
    )
```

time: 42.6 us -> 40.1 us (0.941)
  Pallas kernels: 29.5 us -> 24.9 us
  starting transfers between devices: 8.68 us -> 11.6 us
  waiting for transfers between devices: 3.47 us -> 2.15 us
    pallas_call x2 -> x3, Pallas kernels: 24.3 us -> 20.6 us  [the longest x1 11.3 us: analyse_first(): pl.pallas_call(functools.partial(first_kernel, count, scale), in_specs=[h...]
    ppermute x1, waiting for transfers between devices: 3.46 us -> 0.01 us  [on_device(): far = lax.ppermute(for_far, 'lon', far_pairs)]
    all_to_all x1, waiting for transfers between devices: 0.01 us -> 2.15 us  [on_device(): lax.all_to_all(sums, 'lon', 0, 0, axis_index_groups=[list(range(core, cou...]
    ppermute x0 -> x1, starting transfers between devices: none -> 1.87 us  [on_device(): far_last = lax.ppermute(for_far_last, 'lon', far_pairs)]
    all_to_all x1, starting transfers between devices: 5.91 us -> 6.92 us  [on_device(): lax.all_to_all(sums, 'lon', 0, 0, axis_index_groups=[list(range(core, cou...]
    pallas_call x1, Pallas kernels: 3.36 us -> 2.47 us  [own_gram(): pl.pallas_call(own_gram_kernel, in_specs=[pl.BlockSpec(memory_space=pltpu...]
  transfers between devices with their start and end apart: 3 -> 4, of which waited for: 1 -> 1; matrix products, arithmetic and copies ran while one was open for 2% -> 2% of each run, Pallas kernels for 14% -> 38%
where the time goes in v12:
time: 40.1 us; the launch traced here: 39.5 us
  Pallas kernels  24.9 us (62%)
  starting transfers between devices  11.6 us (29%)
  waiting for transfers between devices  2.15 us (5%)
  local copies, waits for them, and re-layouts  0.62 us (2%)
    pallas_call x1, Pallas kernels, analyse_first(): pl.pallas_call(functools.partial(first_kernel, count, scale), in_specs=[h...  11.3 us
    pallas_call x1, Pallas kernels, analyse_last(): pl.pallas_call(functools.partial(last_kernel, count, scale), in_specs=[pl...  7.86 us
    all_to_all x1, starting transfers between devices, on_device(): lax.all_to_all(sums, 'lon', 0, 0, axis_index_groups=[list(range(core, cou...  6.92 us
    ppermute x1, starting transfers between devices, on_device(): far = lax.ppermute(for_far, 'lon', far_pairs)  2.65 us
    pallas_call x1, Pallas kernels, own_gram(): pl.pallas_call(own_gram_kernel, in_specs=[pl.BlockSpec(memory_space=pltpu...  2.47 us
    all_to_all x1, waiting for transfers between devices, on_device(): lax.all_to_all(sums, 'lon', 0, 0, axis_index_groups=[list(range(core, cou...  2.15 us
    ppermute x1, starting transfers between devices, on_device(): far_last = lax.ppermute(for_far_last, 'lon', far_pairs)  1.87 us
    pallas_call x1, Pallas kernels, observe(): pl.pallas_call(observe_kernel, in_specs=[pl.BlockSpec(memory_space=pltpu....  1.85 us
  transfers between devices with their start and end apart: 4, of which 1 were waited for; matrix products, arithmetic and copies ran while one was open for 2% of the time, Pallas kernels for 38%

profile of v12, /device:TPU:1, one launch (start us, length us, event | category | flops | bytes accessed | tf_op | source)
XLA Modules:
  0.0 39.5 jit_solution(15698380464817361064)
XLA Ops:
  0.0 1.9 %observe.1 = (f32[8,256]{1,0:T(8,128)S(1)}, bf16[17,64,256]{2,1,0:T(8,128)(2,1)S(1)}, bf16[17,48,256]{2,1,0:T(8,128)(2,1)S(1)}, bf16[16,16,256]{2,1,0:T(8,128)(2,1)S(1)}, f32[8,128]{1,0:T(8,128)S(1)}) custom-call(s32[1]{0:T(128)} %bitcast.refs_0_.odd_ref, bf16[8,4,64,256]{3,2,1,0:T(8,128)(2,1)} %refs_4_.1, bf16[32,64,256]{2,1,0:T(8,128)(2,1)} %bitcast.11, ...), custom_call_target="tpu_custom_call" | custom-call | tf_op jit(solution)/shard_map/observe/pallas_call | solution.py:125
  1.9 0.1 collective-permute-start.1
  2.0 2.7 %collective-permute-start = (bf16[17,48,256]{2,1,0:T(8,128)(2,1)S(1)}, bf16[17,48,256]{2,1,0:T(8,128)(2,1)S(1)}, u32[]{:S(2)}, u32[]{:S(2)}) collective-permute-start(bf16[17,48,256]{2,1,0:T(8,128)(2,1)S(1)} %get-tuple-element.20), channel_id=1, source_target_pairs={{0,15},{1,2},{2,1},{3,4},{4,3},{5,6},{6,5},{7,8},{8,7},{9,10},{10,... | collective-permute-start | bytes 1253384 | tf_op jit(solution)/shard_map/ppermute | solution.py:633
  4.6 0.0 collective-permute-done.1.near_ref
  4.7 0.6 %broadcast_in_dim.15 = f32[64,128]{1,0:T(8,128)} broadcast(f32[128]{0:T(128)S(1)} %bitcast_add_fusion), dimensions={1} | broadcast | bytes 33280 | tf_op jit(solution)/shard_map/broadcast_in_dim | solution.py:636
  5.3 1.9 %collective-permute-start.2 = (bf16[16,16,256]{2,1,0:T(8,128)(2,1)S(1)}, bf16[16,16,256]{2,1,0:T(8,128)(2,1)S(1)}, u32[]{:S(2)}, u32[]{:S(2)}) collective-permute-start(bf16[16,16,256]{2,1,0:T(8,128)(2,1)S(1)} %get-tuple-element.24), channel_id=1, source_target_pairs={{0,15},{1,2},{2,1},{3,4},{4,3},{5,6},{6,5},{7,8},{8,7},{9,10},{10,... | collective-permute-start | bytes 393224 | tf_op jit(solution)/shard_map/ppermute | solution.py:646
  7.2 6.9 %all-to-all-start = ((f32[8,8,128]{2,1,0:T(8,128)}), f32[8,8,128]{2,1,0:T(8,128)S(1)}, u32[]{:S(2)}, u32[]{:S(2)}) async-start(f32[8,8,128]{2,1,0:T(8,128)} %bitcast.6), calls=%async_computation | async-start | bytes 65536 | tf_op jit(solution)/shard_map/all_to_all | solution.py:638
  14.1 2.5 %own_gram.1 = (f32[4,256,256]{2,1,0:T(8,128)S(1)}, f32[4,256,256]{2,1,0:T(8,128)S(1)}, f32[8,256]{1,0:T(8,128)S(1)}) custom-call(s32[1]{0:T(128)} %bitcast.refs_0_.odd_ref, bf16[8,4,64,256]{3,2,1,0:T(8,128)(2,1)} %refs_4_.1, bf16[17,64,256]{2,1,0:T(8,128)(2,1)S(1)} %collective-permute-done.1.near_ref, f32[8,256]{1,0:T(8,128)S(1)} %get-tuple-element.25.own_ref), custom_call_target="tpu_custom_call" | custom-call | tf_op jit(solution)/shard_map/own_gram/pallas_call | solution.py:257
  16.6 0.0 collective-permute-done.refs_1_
  16.6 1.4 %prepare.1 = (f32[4,256,256]{2,1,0:T(8,128)}, f32[4,256,256]{2,1,0:T(8,128)S(1)}, f32[4,1,256]{2,1,0:T(1,128)S(1)}, f32[8,128]{1,0:T(8,128)S(1)}, f32[8,256]{1,0:T(8,128)S(1)}) custom-call(s32[1]{0:T(128)} %bitcast.refs_0_.odd_ref, bf16[17,48,256]{2,1,0:T(8,128)(2,1)S(1)} %collective-permute-done.refs_1_, f32[4,256,256]{2,1,0:T(8,128)S(1)} %get-tuple-element.27.refs_2_, ...), custom_call_target="tpu_custom_call" | custom-call | tf_op jit(solution)/shard_map/prepare/pallas_call | solution.py:340
  18.0 2.1 %all-to-all-done = f32[8,8,128]{2,1,0:T(8,128)S(1)} async-done(((f32[8,8,128]{2,1,0:T(8,128)}), f32[8,8,128]{2,1,0:T(8,128)S(1)}, u32[]{:S(2)}, u32[]{:S(2)}) %all-to-all-start) | async-done | bytes 32800 | tf_op jit(solution)/shard_map/all_to_all | solution.py:638
  20.1 11.3 %analyse_first.1.refs_7_ = bf16[8,4,64,256]{3,2,1,0:T(8,128)(2,1)} custom-call(bf16[8,4,64,256]{3,2,1,0:T(8,128)(2,1)} %refs_4_.1, f32[4,256,256]{2,1,0:T(8,128)} %get-tuple-element.31.refs_1_, f32[4,256,256]{2,1,0:T(8,128)S(1)} %get-tuple-element.32.refs_2_, f32[4,1,256]{2,1,0:T(1,128)S(1)} %get-tuple-element.33.refs_3_, ...), custom_call_target="tpu_custom_call" | custom-call | tf_op jit(solution)/shard_map/analyse_first/pallas_call | solution.py:573
  31.5 0.0 collective-permute-done.2.refs_2_
  31.5 7.9 %analyse_last.1 = bf16[8,4,64,256]{3,2,1,0:T(8,128)(2,1)} custom-call(s32[1]{0:T(128)} %bitcast.refs_0_.odd_ref, bf16[17,48,256]{2,1,0:T(8,128)(2,1)S(1)} %collective-permute-done.refs_1_, bf16[16,16,256]{2,1,0:T(8,128)(2,1)S(1)} %collective-permute-done.2.refs_2_, f32[4,256,256]{2,1,0:T(8,128)S(1)} %get-tuple-element.26.refs_3_, ...), custom_call_target="tpu_custom_call", output_to_operand_aliasing={{}: (7, {})} | custom-call | tf_op jit(solution)/shard_map/analyse_last/pallas_call | solution.py:598
  (2 shorter events, 0.0 us)
Async XLA Ops:
  1.9 2.8 %collective-permute-start.1 = (bf16[17,64,256]{2,1,0:T(8,128)(2,1)S(1)}, bf16[17,64,256]{2,1,0:T(8,128)(2,1)S(1)}, u32[]{:S(2)}, u32[]{:S(2)}) collective-permute-start(bf16[17,64,256]{2,1,0:T(8,128)(2,1)S(1)} %get-tuple-element.22), channel_id=1, source_target_pairs={{0,1},{1,0},{2,3},{3,2},{4,5},{5,4},{6,7},{7,6},{8,9},{9,8},{10,11... | collective-permute-start | bytes 1671176 | tf_op jit(solution)/shard_map/ppermute | solution.py:634
  2.0 14.6 %collective-permute-start = (bf16[17,48,256]{2,1,0:T(8,128)(2,1)S(1)}, bf16[17,48,256]{2,1,0:T(8,128)(2,1)S(1)}, u32[]{:S(2)}, u32[]{:S(2)}) collective-permute-start(bf16[17,48,256]{2,1,0:T(8,128)(2,1)S(1)} %get-tuple-element.20), channel_id=1, source_target_pairs={{0,15},{1,2},{2,1},{3,4},{4,3},{5,6},{6,5},{7,8},{8,7},{9,10},{10,... | collective-permute-start | bytes 1253384 | tf_op jit(solution)/shard_map/ppermute | solution.py:633
  5.3 26.2 %collective-permute-start.2 = (bf16[16,16,256]{2,1,0:T(8,128)(2,1)S(1)}, bf16[16,16,256]{2,1,0:T(8,128)(2,1)S(1)}, u32[]{:S(2)}, u32[]{:S(2)}) collective-permute-start(bf16[16,16,256]{2,1,0:T(8,128)(2,1)S(1)} %get-tuple-element.24), channel_id=1, source_target_pairs={{0,15},{1,2},{2,1},{3,4},{4,3},{5,6},{6,5},{7,8},{8,7},{9,10},{10,... | collective-permute-start | bytes 393224 | tf_op jit(solution)/shard_map/ppermute | solution.py:646
  7.2 13.0 %all-to-all-start = ((f32[8,8,128]{2,1,0:T(8,128)}), f32[8,8,128]{2,1,0:T(8,128)S(1)}, u32[]{:S(2)}, u32[]{:S(2)}) async-start(f32[8,8,128]{2,1,0:T(8,128)} %bitcast.6), calls=%async_computation | async-start | bytes 65536 | tf_op jit(solution)/shard_map/all_to_all | solution.py:638

commit v13 on v12

--- a/solution.py
+++ b/solution.py
@@ -16,7 +16,6 @@
 PAIR = 2
 LOG2E = 1.4426950408889634
 ROWS = 32
-FIRST = 3
 LIFT, START, MASS = 20, -10, 60
 
 HIGH = lax.Precision.HIGHEST
@@ -47,24 +46,22 @@
 
 
 def observe_kernel(*refs):
-    odd_ref, state_ref, planes_ref = refs[:3]
-    own_ref, near_ref, far_ref, far_last_ref, part_ref = refs[6:11]
-    cells_ref, index_ref, value_ref, var_ref, sems = refs[11:]
+    odd_ref, state_ref, rows_ref = refs[:3]
+    own_ref, near_ref, far_ref, part_ref = refs[6:10]
+    cells_ref, index_ref, value_ref, var_ref, sems = refs[10:]
     lon_dev, lat, members = cells_ref.shape
     nobs = index_ref.shape[1]
-    edge = planes_ref.shape[0] // lon_dev * HALO
-    last = planes_ref.shape[0] - edge
-    far_at = odd_ref[0] * last
-    cut = far_ref.shape[1]
-    far_planes = planes_ref.at[pl.ds(far_at, edge)]
+    edge = rows_ref.shape[0] // lon_dev * HALO
+    last = rows_ref.shape[0] - edge
+    far_at = pl.multiple_of(odd_ref[0] * last, 16)
+    near_at = pl.multiple_of(last - far_at, 16)
     fetches = [
         (refs[3], index_ref),
         (refs[4], value_ref),
         (refs[5], var_ref),
         (state_ref.at[:, 0], cells_ref),
-        (far_planes.at[:, pl.ds(0, cut), :], far_ref.at[pl.ds(0, edge)]),
-        (planes_ref.at[pl.ds(last - far_at, edge)], near_ref.at[pl.ds(0, edge)]),
-        (far_planes.at[:, pl.ds(cut, lat - cut), :], far_last_ref),
+        (rows_ref.at[pl.ds(far_at, edge), :], far_ref.at[pl.ds(0, edge), :]),
+        (rows_ref.at[pl.ds(near_at, edge), :], near_ref.at[pl.ds(0, edge), :]),
     ]
     copies = [
         pltpu.make_async_copy(src, dst, sems.at[i]) for i, (src, dst) in enumerate(fetches)
@@ -104,8 +101,8 @@
         jnp.concatenate(weights, axis=0), terms, precision=HIGH, preferred_element_type=jnp.float32
     )
     own_ref[...] = like[:blocks]
-    near_ref[edge, : 4 * TILE, :] = in_parts(like[blocks : 2 * blocks], part)
-    far_ref[edge, : 4 * TILE, :] = in_parts(like[2 * blocks :], jnp.zeros_like(part))
+    near_ref[edge:, :] = in_parts(like[blocks : 2 * blocks], part)
+    far_ref[edge:, :] = in_parts(like[2 * blocks :], jnp.zeros_like(part))
     for copy in copies[4:]:
         copy.wait()
 
@@ -115,37 +112,32 @@
     nobs = obs_index.size
     assert lat // REGION == TILE
     like = jax.ShapeDtypeStruct((lat // REGION, members), jnp.float32)
-    planes = HALO * nvar
-    cut = FIRST * PAIR * TILE
-    near = pltpu.VMEM((planes + 1, lat, members), state.dtype)
-    far = pltpu.VMEM((planes + 1, cut, members), state.dtype)
-    far_last = pltpu.VMEM((planes, lat - cut, members), state.dtype)
+    payload = pltpu.VMEM((HALO * nvar * lat + 4 * TILE, members), state.dtype)
     part = jax.ShapeDtypeStruct((TILE, 128), jnp.float32)
-    arrays = state, state.reshape(-1, lat, members), obs_index[None], obs_value[None], obs_var[None]
+    arrays = state, state.reshape(-1, members), obs_index[None], obs_value[None], obs_var[None]
     return pl.pallas_call(
         observe_kernel,
         in_specs=[pl.BlockSpec(memory_space=pltpu.SMEM)]
         + [pl.BlockSpec(memory_space=pltpu.HBM)] * len(arrays),
-        out_specs=[pl.BlockSpec(memory_space=pltpu.VMEM)] * 5,
-        out_shape=[like, near, far, far_last, part],
+        out_specs=[pl.BlockSpec(memory_space=pltpu.VMEM)] * 4,
+        out_shape=[like, payload, payload, part],
         scratch_shapes=[
             pltpu.VMEM((lon_dev, lat, members), state.dtype),
             pltpu.VMEM((1, nobs), jnp.int32),
             pltpu.VMEM((1, nobs), jnp.float32),
             pltpu.VMEM((1, nobs), jnp.float32),
-            pltpu.SemaphoreType.DMA((7,)),
+            pltpu.SemaphoreType.DMA((6,)),
         ],
         compiler_params=pltpu.CompilerParams(vmem_limit_bytes=16 * 2**20),
         name="observe",
     )(odd, *[pltpu.with_memory_space_constraint(x, pltpu.HBM) for x in arrays])
 
 
-def slab_of(refs, planes, at):
+def slab_of(ref, lat, at):
     size = PAIR * TILE
-    for ref in refs:
-        if at * size < ref.shape[1]:
-            return ref[:planes, at * size : (at + 1) * size, :].astype(jnp.float32)
-        at -= ref.shape[1] // size
+    planes = ref.shape[0] // lat
+    rows = [ref[i * lat + at * size : i * lat + (at + 1) * size, :] for i in range(planes)]
+    return jnp.stack(rows).astype(jnp.float32)
 
 
 def pair_tiles(load, step, steps):
@@ -204,56 +196,47 @@
 
 
 def own_gram_kernel(odd_ref, state_hbm_ref, near_ref, own_ref, *refs):
-    gram_refs, like_ref, state_ref, sems = refs[:-3], refs[-3], refs[-2], refs[-1]
-    near_planes = near_ref.shape[0] - 1
-    nvar = near_planes // HALO
-    lon_dev = state_ref.shape[0]
-    steps = state_ref.shape[2] // (PAIR * TILE)
+    gram_ref, like_ref, state_ref, sems = refs
+    lon_dev, nvar, lat, members = state_ref.shape
+    steps = lat // (PAIR * TILE)
     copies = slab_copies(state_hbm_ref, state_ref, sems)
     for copy in copies:
         copy.start()
-    like_ref[...] = own_ref[...] + like_rows(near_ref[near_planes, : 4 * TILE, :])
+    like_ref[...] = own_ref[...] + like_rows(near_ref[near_ref.shape[0] - 4 * TILE :, :])
     size = PAIR * TILE
 
     def load(step):
         own = state_ref[:, :, step * size : (step + 1) * size, :].astype(jnp.float32)
-        own = own.reshape(lon_dev * nvar, size, own.shape[-1])
-        return jnp.concatenate([own, slab_of([near_ref], near_planes, step)], axis=0)
+        own = own.reshape(lon_dev * nvar, size, members)
+        return jnp.concatenate([own, slab_of(near_ref, lat, step)], axis=0)
 
     weights = [None] * (lon_dev * nvar)
     weights += [w for w in halo_weights(odd_ref[0] == 1) for _ in range(nvar)]
     for copy in copies:
         copy.wait()
     slabs = [load(step) for step in range(steps)]
-    add_grams(slabs, weights, range(steps), None, gram_refs)
-
-
-def add_grams(slabs, weights, pairs, old_refs, new_refs):
-    steps = len(slabs)
-    none = jnp.zeros_like(slabs[pairs[0]][:, :TILE])
-    turned_none = jnp.zeros((none.shape[-1], none.shape[0] * TILE), jnp.bfloat16)
-    tiles, turned = {}, {}
-    for at in range(pairs[0] * PAIR - 1, pairs[-1] * PAIR + PAIR + 1):
-        if 0 <= at < steps * PAIR:
-            half = at % PAIR
-            tiles[at] = slabs[at // PAIR][:, half * TILE : (half + 1) * TILE]
-            turned[at] = turn(tiles[at])
-        else:
-            tiles[at], turned[at] = none, turned_none
-    for index, pair in enumerate(pairs):
-        window = range(pair * PAIR - 1, pair * PAIR + PAIR + 1)
-        grams = gram_of([tiles[i] for i in window], [turned[i] for i in window], weights)
-        for half in range(PAIR):
-            per = new_refs[0].shape[0]
-            ref, region = divmod(index * PAIR + half, per)
-            gram = grams[half]
-            new_refs[ref][region] = gram if old_refs is None else old_refs[ref][region] + gram
+    add_grams(slabs, weights, None, gram_ref)
+
+
+def add_grams(slabs, weights, old_ref, new_ref):
+    none = jnp.zeros_like(slabs[0][:, :TILE])
+    tiles = [none]
+    for slab in slabs:
+        tiles += [slab[:, :TILE], slab[:, TILE:]]
+    tiles.append(none)
+    turned = [turn(tile) for tile in tiles[1:-1]]
+    turned = [jnp.zeros_like(turned[0])] + turned + [jnp.zeros_like(turned[0])]
+    for pair in range(len(slabs)):
+        window = slice(pair * PAIR, pair * PAIR + PAIR + 2)
+        grams = gram_of(tiles[window], turned[window], weights)
+        for at, gram in enumerate(grams):
+            region = pair * PAIR + at
+            new_ref[region] = gram if old_ref is None else old_ref[region] + gram
 
 
 def own_gram(odd, state, near, own):
     _, _, lat, members = state.shape
     vmem = pl.BlockSpec(memory_space=pltpu.VMEM)
-    half = jax.ShapeDtypeStruct((lat // REGION // 2, members, members), jnp.float32)
     return pl.pallas_call(
         own_gram_kernel,
         in_specs=[
@@ -262,8 +245,11 @@
             vmem,
             vmem,
         ],
-        out_specs=[vmem] * 3,
-        out_shape=[half, half, jax.ShapeDtypeStruct(own.shape, jnp.float32)],
+        out_specs=[vmem] * 2,
+        out_shape=[
+            jax.ShapeDtypeStruct((lat // REGION, members, members), jnp.float32),
+            jax.ShapeDtypeStruct(own.shape, jnp.float32),
+        ],
         scratch_shapes=[
             pltpu.VMEM(state.shape, state.dtype),
             pltpu.SemaphoreType.DMA((lat // (PAIR * TILE),)),
@@ -315,30 +301,25 @@
     return jnp.max(most.reshape(ROWS // TILE, TILE, 128), axis=0)
 
 
-def far_grams(odd_ref, halo_refs, lat, pairs, old_ref, new_ref):
-    planes = halo_refs[0].shape[0] - 1
-    slabs = [None] * (lat // (PAIR * TILE))
-    for at in range(max(pairs[0] - 1, 0), min(pairs[-1] + 2, len(slabs))):
-        slabs[at] = slab_of(halo_refs, planes, at)
-    weights = [w for w in halo_weights(odd_ref[0] == 0) for _ in range(planes // HALO)]
-    add_grams(slabs, weights, pairs, [old_ref], [new_ref])
-
-
-def prepare_kernel(scale, lat, *refs):
+def prepare_kernel(scale, *refs):
     odd_ref, halo_ref, old_ref, like_in_ref = refs[:4]
     gram_hbm_ref, kernel_ref, mass_ref, most_ref, like_ref, gram_ref, sem = refs[4:]
-    like_ref[...] = like_in_ref[...] + like_rows(halo_ref[halo_ref.shape[0] - 1, : 4 * TILE, :])
-    far_grams(odd_ref, [halo_ref], lat, range(gram_ref.shape[0] // PAIR), old_ref, gram_ref)
+    like_ref[...] = like_in_ref[...] + like_rows(halo_ref[halo_ref.shape[0] - 4 * TILE :, :])
+    lat = gram_ref.shape[0] * REGION
+    planes = halo_ref.shape[0] // lat
+    weights = [w for w in halo_weights(odd_ref[0] == 0) for _ in range(planes // HALO)]
+    slabs = [slab_of(halo_ref, lat, at) for at in range(lat // (PAIR * TILE))]
+    add_grams(slabs, weights, old_ref, gram_ref)
     keep = pltpu.make_async_copy(gram_ref, gram_hbm_ref, sem)
     keep.start()
     most_ref[...] = kernel_matrices(gram_ref, kernel_ref, mass_ref, scale)
     keep.wait()
 
 
-def prepare(odd, halo, gram, like, lat, scale):
+def prepare(odd, halo, gram, like, scale):
     vmem = pl.BlockSpec(memory_space=pltpu.VMEM)
     return pl.pallas_call(
-        functools.partial(prepare_kernel, scale, lat),
+        functools.partial(prepare_kernel, scale),
         in_specs=[pl.BlockSpec(memory_space=pltpu.SMEM)] + [vmem] * 3,
         out_specs=[pl.BlockSpec(memory_space=pltpu.HBM)] + [vmem] * 4,
         out_shape=[
@@ -452,39 +433,31 @@
     return jnp.concatenate(parts, axis=2).astype(jnp.bfloat16)
 
 
-def analyse_half(half, count, scale, like_ref, sums_ref, kernel_ref, mass_ref, most, gram, state, out):
-    regions = kernel_ref.shape[0]
-    pairs = regions // PAIR
+def finish_kernel(count, scale, *refs):
+    state_hbm_ref, gram_hbm_ref, kernel_ref, mass_ref, most_ref, like_ref, sums_ref = refs[:7]
+    out_ref, result_ref, state_ref, gram_ref, out_sems, state_sems, sem = refs[7:]
+    pairs = kernel_ref.shape[0] // PAIR
     size = PAIR * TILE
-    state_hbm_ref, state_ref, state_sems = state
-    out_ref, result_ref, out_sems = out
-    first = half * pairs
-
-    def fetch(pair):
-        rows = pl.ds((first + pair) * size, size)
-        return pltpu.make_async_copy(
-            state_hbm_ref.at[:, :, rows, :],
-            state_ref.at[:, :, pl.ds(pair * size, size), :],
-            state_sems.at[pair],
-        )
+    fetches = slab_copies(state_hbm_ref, state_ref, state_sems)
+    for copy in fetches:
+        copy.start()
 
     def send(pair):
-        rows = pl.ds((first + pair) * size, size)
+        rows = pl.ds(pair * size, size)
         return pltpu.make_async_copy(
             result_ref.at[pair], out_ref.at[:, :, rows, :], out_sems.at[pair]
         )
 
     total = jnp.sum(sums_ref[...], axis=0, keepdims=True)[:, 0:1] * (1.0 / TILE)
-    like = like_ref[half * regions : (half + 1) * regions, :]
-    like = -0.5 * (count / total) * like
+    like = -0.5 * (count / total) * like_ref[...]
     like = like - jnp.max(like, axis=1, keepdims=True)
     logw = (like - jnp.log(jnp.sum(jnp.exp(like), axis=1, keepdims=True))) * LOG2E
     moves, least_i, least_j = transports_scaled(kernel_ref, jnp.exp2(logw + MASS), mass_ref)
     for pair in range(pairs):
-        fetch(pair).wait()
+        fetches[pair].wait()
         result_ref[pair] = transform(state_ref, pair, moves[pair * PAIR : (pair + 1) * PAIR])
         send(pair).start()
-    row, col, most = jnp.min(least_i), jnp.min(least_j), jnp.max(most)
+    row, col, most = jnp.min(least_i), jnp.min(least_j), jnp.max(most_ref[...])
     sound = (row >= 2.0**-24) & (col >= 2.0**-30) & (most <= 2.0**30) & (row * col >= 2.0**-34)
     for pair in range(pairs):
         send(pair).wait()
@@ -492,95 +465,37 @@
     @pl.when(jnp.logical_not(sound))
     def _():
         for pair in range(pairs):
-            again = [
-                transport_logs(gram(region), logw[region : region + 1], scale)
-                for region in range(pair * PAIR, (pair + 1) * PAIR)
-            ]
+            again = []
+            for region in range(pair * PAIR, (pair + 1) * PAIR):
+                copy = pltpu.make_async_copy(gram_hbm_ref.at[region], gram_ref, sem)
+                copy.start()
+                copy.wait()
+                again.append(transport_logs(gram_ref[...], logw[region : region + 1], scale))
             result_ref[pair] = transform(state_ref, pair, again)
             send(pair).start()
             send(pair).wait()
 
 
-def start_fetches(half, pairs, state):
-    state_hbm_ref, state_ref, state_sems = state
-    size = PAIR * TILE
-    for pair in range(pairs):
-        rows = pl.ds((half * pairs + pair) * size, size)
-        pltpu.make_async_copy(
-            state_hbm_ref.at[:, :, rows, :],
-            state_ref.at[:, :, pl.ds(pair * size, size), :],
-            state_sems.at[pair],
-        ).start()
-
-
-def first_kernel(count, scale, *refs):
-    state_hbm_ref, gram_hbm_ref, kernel_ref, mass_ref, most_ref, like_ref, sums_ref = refs[:7]
-    out_ref, result_ref, state_ref, gram_ref, out_sems, state_sems, sem = refs[7:]
-    state = state_hbm_ref, state_ref, state_sems
-    start_fetches(0, kernel_ref.shape[0] // PAIR, state)
-
-    def gram(region):
-        copy = pltpu.make_async_copy(gram_hbm_ref.at[region], gram_ref, sem)
-        copy.start()
-        copy.wait()
-        return gram_ref[...]
-
-    out = out_ref, result_ref, out_sems
-    analyse_half(
-        0, count, scale, like_ref, sums_ref, kernel_ref, mass_ref, most_ref[...], gram, state, out
-    )
-
-
-def last_kernel(count, scale, *refs):
-    odd_ref, halo_ref, halo_last_ref, old_ref, state_hbm_ref, like_ref, sums_ref = refs[:7]
-    out_ref, result_ref, state_ref, gram_ref, kernel_ref, mass_ref, out_sems, state_sems = refs[8:]
-    state = state_hbm_ref, state_ref, state_sems
-    pairs = gram_ref.shape[0] // PAIR
-    start_fetches(1, pairs, state)
-    halos = [halo_ref, halo_last_ref]
-    far_grams(odd_ref, halos, 2 * pairs * PAIR * TILE, range(pairs, 2 * pairs), old_ref, gram_ref)
-    most = kernel_matrices(gram_ref, kernel_ref, mass_ref, scale)
-    out = out_ref, result_ref, out_sems
-    analyse_half(
-        1,
-        count,
-        scale,
-        like_ref,
-        sums_ref,
-        kernel_ref,
-        mass_ref,
-        most,
-        lambda region: gram_ref[region],
-        state,
-        out,
-    )
-
-
-def half_buffers(state):
+def finish(state, gram, kernel, mass, most, like, sums, count, scale):
     lon_dev, nvar, lat, members = state.shape
-    pairs = lat // (PAIR * TILE) // 2
-    return [
-        pltpu.VMEM((pairs, lon_dev, nvar, PAIR * TILE, members), state.dtype),
-        pltpu.VMEM((lon_dev, nvar, lat // 2, members), state.dtype),
-    ], [pltpu.SemaphoreType.DMA((pairs,)), pltpu.SemaphoreType.DMA((pairs,))]
-
-
-def analyse_first(state, gram, kernel, mass, most, like, sums, count, scale):
-    members = state.shape[-1]
+    pairs = lat // (PAIR * TILE)
     vmem = pl.BlockSpec(memory_space=pltpu.VMEM)
     hbm = pl.BlockSpec(memory_space=pltpu.HBM)
-    buffers, sems = half_buffers(state)
     return pl.pallas_call(
-        functools.partial(first_kernel, count, scale),
+        functools.partial(finish_kernel, count, scale),
         in_specs=[hbm, hbm] + [vmem] * 5,
         out_specs=pl.BlockSpec(memory_space=pl.ANY),
         out_shape=jax.ShapeDtypeStruct(state.shape, state.dtype),
-        scratch_shapes=buffers
-        + [pltpu.VMEM((members, members), jnp.float32)]
-        + sems
-        + [pltpu.SemaphoreType.DMA],
+        scratch_shapes=[
+            pltpu.VMEM((pairs, lon_dev, nvar, PAIR * TILE, members), state.dtype),
+            pltpu.VMEM(state.shape, state.dtype),
+            pltpu.VMEM((members, members), jnp.float32),
+            pltpu.SemaphoreType.DMA((pairs,)),
+            pltpu.SemaphoreType.DMA((pairs,)),
+            pltpu.SemaphoreType.DMA,
+        ],
         compiler_params=pltpu.CompilerParams(vmem_limit_bytes=24 * 2**20),
-        name="analyse_first",
+        name="finish",
     )(
         *[pltpu.with_memory_space_constraint(x, pltpu.HBM) for x in (state, gram)],
         kernel,
@@ -591,67 +506,32 @@
     )
 
 
-def analyse_last(odd, halo, halo_last, gram, state, like, sums, out, count, scale):
-    vmem = pl.BlockSpec(memory_space=pltpu.VMEM)
-    hbm = pl.BlockSpec(memory_space=pltpu.HBM)
-    buffers, sems = half_buffers(state)
-    return pl.pallas_call(
-        functools.partial(last_kernel, count, scale),
-        in_specs=[pl.BlockSpec(memory_space=pltpu.SMEM)]
-        + [vmem] * 3
-        + [hbm, vmem, vmem, pl.BlockSpec(memory_space=pl.ANY)],
-        out_specs=pl.BlockSpec(memory_space=pl.ANY),
-        out_shape=jax.ShapeDtypeStruct(state.shape, state.dtype),
-        input_output_aliases={7: 0},
-        scratch_shapes=buffers
-        + [pltpu.VMEM(gram.shape, jnp.float32)] * 2
-        + [pltpu.VMEM((gram.shape[0], 1, gram.shape[2]), jnp.float32)]
-        + sems,
-        compiler_params=pltpu.CompilerParams(vmem_limit_bytes=24 * 2**20),
-        name="analyse_last",
-    )(
-        odd,
-        halo,
-        halo_last,
-        gram,
-        pltpu.with_memory_space_constraint(state, pltpu.HBM),
-        like,
-        sums,
-        out,
-    )
-
-
 def on_device(state, obs_index, obs_value, obs_var):
     nvar = state.shape[1]
     count = lax.axis_size("lon")
     odd = (lax.axis_index("lon") & 1).astype(jnp.int32).reshape(1)
     near_pairs = [(i, i ^ 1) for i in range(count)]
     far_pairs = [(i, (i + 1 if i % 2 else i - 1) % count) for i in range(count)]
-    own_like, for_near, for_far, for_far_last, part = observe(
-        odd, state, obs_index, obs_value, obs_var
-    )
+    own_like, for_near, for_far, part = observe(odd, state, obs_index, obs_value, obs_var)
     far = lax.ppermute(for_far, "lon", far_pairs)
     near = lax.ppermute(for_near, "lon", near_pairs)
-    sums = near[HALO * nvar, 3 * TILE : 3 * TILE + 3, :128].astype(jnp.float32)
-    sums = jnp.broadcast_to(part[0] + jnp.sum(sums, axis=0), (count // 2 * TILE, 128))
-    sums, for_far_last = lax.optimization_barrier((sums, for_far_last))
+    start = near.shape[0] - TILE
+    part = part[0] + jnp.sum(near[start : start + 3, :128].astype(jnp.float32), axis=0)
     sums = lax.all_to_all(
-        sums,
+        jnp.broadcast_to(part, (count // 2 * TILE, 128)),
         "lon",
         0,
         0,
         axis_index_groups=[list(range(core, count, 2)) for core in range(2)],
         tiled=True,
     )
-    far_last = lax.ppermute(for_far_last, "lon", far_pairs)
     offsets = range(REGION + 2 * HALO)
     line = [1.0 - max(0, HALO - p, p - (HALO + REGION - 1)) / (HALO + 1) for p in offsets]
     scale = LOG2E / EPS / (nvar * sum(line) ** 2)
-    gram_first, gram_last, like = own_gram(odd, state, near, own_like)
-    gram, kernel, mass, most, like = prepare(odd, far, gram_first, like, state.shape[2], scale)
+    gram, like = own_gram(odd, state, near, own_like)
+    gram, kernel, mass, most, like = prepare(odd, far, gram, like, scale)
     nobs = float(obs_index.shape[0] * count)
-    out = analyse_first(state, gram, kernel, mass, most, like, sums, nobs, scale)
-    return analyse_last(odd, far, far_last, gram_last, state, like, sums, out, nobs, scale)
+    return finish(state, gram, kernel, mass, most, like, sums, nobs, scale)
 
 
 def solution(mesh):

time: 40.1 us -> 42.2 us (1.052)
  Pallas kernels: 24.9 us -> 27.9 us
  starting transfers between devices: 11.6 us -> 8.68 us
  waiting for transfers between devices: 2.15 us -> 4.39 us
    ppermute x1, waiting for transfers between devices: 0.01 us -> 4.39 us  [on_device(): far = lax.ppermute(for_far, 'lon', far_pairs)]
    pallas_call x3 -> x2, Pallas kernels: 20.6 us -> 23.6 us  [the longest x1 21.4 us: finish(): pl.pallas_call(functools.partial(finish_kernel, count, scale), in_specs=[...]
    all_to_all x1, waiting for transfers between devices: 2.15 us -> 0.01 us  [on_device(): lax.all_to_all(jnp.broadcast_to(part, (count // 2 * TILE, 128)), 'lon', 0...]
    ppermute x1 -> x0, starting transfers between devices: 1.87 us -> none  [on_device(): far_last = lax.ppermute(for_far_last, 'lon', far_pairs)]
    all_to_all x1, starting transfers between devices: 6.92 us -> 5.91 us  [on_device(): lax.all_to_all(jnp.broadcast_to(part, (count // 2 * TILE, 128)), 'lon', 0...]
  transfers between devices with their start and end apart: 4 -> 3, of which waited for: 1 -> 1; matrix products, arithmetic and copies ran while one was open for 2% -> 2% of each run, Pallas kernels for 38% -> 11%
where the time goes in v13:
time: 42.2 us; the launch traced here: 41.8 us
  Pallas kernels  27.9 us (66%)
  starting transfers between devices  8.68 us (21%)
  waiting for transfers between devices  4.39 us (10%)
  local copies, waits for them, and re-layouts  0.62 us (1%)
    pallas_call x1, Pallas kernels, finish(): pl.pallas_call(functools.partial(finish_kernel, count, scale), in_specs=[...  21.4 us
    all_to_all x1, starting transfers between devices, on_device(): lax.all_to_all(jnp.broadcast_to(part, (count // 2 * TILE, 128)), 'lon', 0...  5.91 us
    ppermute x1, waiting for transfers between devices, on_device(): far = lax.ppermute(for_far, 'lon', far_pairs)  4.39 us
    ppermute x1, starting transfers between devices, on_device(): far = lax.ppermute(for_far, 'lon', far_pairs)  2.65 us
    pallas_call x1, Pallas kernels, own_gram(): pl.pallas_call(own_gram_kernel, in_specs=[pl.BlockSpec(memory_space=pltpu...  2.44 us
    pallas_call x1, Pallas kernels, prepare(): pl.pallas_call(functools.partial(prepare_kernel, scale), in_specs=[pl.Blo...  2.17 us
    pallas_call x1, Pallas kernels, observe(): pl.pallas_call(observe_kernel, in_specs=[pl.BlockSpec(memory_space=pltpu....  1.84 us
  transfers between devices with their start and end apart: 3, of which 1 were waited for; matrix products, arithmetic and copies ran while one was open for 2% of the time, Pallas kernels for 11%

profile of v13, /device:TPU:1, one launch (start us, length us, event | category | flops | bytes accessed | tf_op | source)
XLA Modules:
  0.0 41.8 jit_solution(18169045018223802338)
XLA Ops:
  0.0 1.8 %observe.1 = (f32[8,256]{1,0:T(8,128)S(1)}, bf16[1056,256]{1,0:T(8,128)(2,1)S(1)}, bf16[1056,256]{1,0:T(8,128)(2,1)S(1)}, f32[8,128]{1,0:T(8,128)S(1)}) custom-call(s32[1]{0:T(128)} %bitcast.refs_0_.odd_ref, bf16[8,4,64,256]{3,2,1,0:T(8,128)(2,1)} %refs_0_.1, bf16[2048,256]{1,0:T(8,128)(2,1)} %bitcast.9, s32[1,256]{1,0:T(1,128)} %bitcast.10, ...), custom_call_target="tpu_custom_call" | custom-call | tf_op jit(solution)/shard_map/observe/pallas_call | solution.py:118
  1.9 0.1 collective-permute-start.1
  2.0 2.7 %collective-permute-start = (bf16[1056,256]{1,0:T(8,128)(2,1)S(1)}, bf16[1056,256]{1,0:T(8,128)(2,1)S(1)}, u32[]{:S(2)}, u32[]{:S(2)}) collective-permute-start(bf16[1056,256]{1,0:T(8,128)(2,1)S(1)} %get-tuple-element.16), channel_id=1, source_target_pairs={{0,15},{1,2},{2,1},{3,4},{4,3},{5,6},{6,5},{7,8},{8,7},{9,10},{10,... | collective-permute-start | bytes 1622024 | tf_op jit(solution)/shard_map/ppermute | solution.py:516
  4.6 0.0 collective-permute-done.1.near_ref
  4.7 0.6 %broadcast_in_dim.15 = f32[8,8,128]{2,1,0:T(8,128)} broadcast(f32[128]{0:T(128)S(1)} %bitcast_add_fusion), dimensions={2} | broadcast | bytes 33280 | tf_op jit(solution)/shard_map/broadcast_in_dim | solution.py:521
  5.3 5.9 %all-to-all-start = ((f32[8,8,128]{2,1,0:T(8,128)}), f32[8,8,128]{2,1,0:T(8,128)S(1)}, u32[]{:S(2)}, u32[]{:S(2)}) async-start(f32[8,8,128]{2,1,0:T(8,128)} %broadcast_in_dim.15), calls=%async_computation | async-start | bytes 65536 | tf_op jit(solution)/shard_map/all_to_all | solution.py:520
  11.2 2.4 %own_gram.1 = (f32[8,256,256]{2,1,0:T(8,128)S(1)}, f32[8,256]{1,0:T(8,128)S(1)}) custom-call(s32[1]{0:T(128)} %bitcast.refs_0_.odd_ref, bf16[8,4,64,256]{3,2,1,0:T(8,128)(2,1)} %refs_0_.1, bf16[1056,256]{1,0:T(8,128)(2,1)S(1)} %collective-permute-done.1.near_ref, f32[8,256]{1,0:T(8,128)S(1)} %get-tuple-element.18.own_ref), custom_call_target="tpu_custom_call" | custom-call | tf_op jit(solution)/shard_map/own_gram/pallas_call | solution.py:240
  13.6 4.4 %collective-permute-done.refs_1_ = bf16[1056,256]{1,0:T(8,128)(2,1)S(1)} collective-permute-done((bf16[1056,256]{1,0:T(8,128)(2,1)S(1)}, bf16[1056,256]{1,0:T(8,128)(2,1)S(1)}, u32[]{:S(2)}, u32[]{:S(2)}) %collective-permute-start) | collective-permute-done | bytes 540704 | tf_op jit(solution)/shard_map/ppermute | solution.py:516
  18.0 2.2 %prepare.1 = (f32[8,256,256]{2,1,0:T(8,128)}, f32[8,256,256]{2,1,0:T(8,128)S(1)}, f32[8,1,256]{2,1,0:T(1,128)S(1)}, f32[8,128]{1,0:T(8,128)S(1)}, f32[8,256]{1,0:T(8,128)S(1)}) custom-call(s32[1]{0:T(128)} %bitcast.refs_0_.odd_ref, bf16[1056,256]{1,0:T(8,128)(2,1)S(1)} %collective-permute-done.refs_1_, f32[8,256,256]{2,1,0:T(8,128)S(1)} %get-tuple-element.19.refs_2_, ...), custom_call_target="tpu_custom_call" | custom-call | tf_op jit(solution)/shard_map/prepare/pallas_call | solution.py:321
  20.2 0.0 all-to-all-done
  20.2 21.4 %finish.1 = bf16[8,4,64,256]{3,2,1,0:T(8,128)(2,1)} custom-call(bf16[8,4,64,256]{3,2,1,0:T(8,128)(2,1)} %refs_0_.1, f32[8,256,256]{2,1,0:T(8,128)} %get-tuple-element.21.refs_1_, f32[8,256,256]{2,1,0:T(8,128)S(1)} %get-tuple-element.22.refs_2_, f32[8,1,256]{2,1,0:T(1,128)S(1)} %get-tuple-element.23.refs_3_, f32[8,128]{1,0:T(8,128)S(1)} %get-tuple-element.24.refs_4_, ...), custom_call_target="tpu_custom_call" | custom-call | tf_op jit(solution)/shard_map/finish/pallas_call | solution.py:484
  (2 shorter events, 0.0 us)
Async XLA Ops:
  1.9 2.8 %collective-permute-start.1 = (bf16[1056,256]{1,0:T(8,128)(2,1)S(1)}, bf16[1056,256]{1,0:T(8,128)(2,1)S(1)}, u32[]{:S(2)}, u32[]{:S(2)}) collective-permute-start(bf16[1056,256]{1,0:T(8,128)(2,1)S(1)} %get-tuple-element.17), channel_id=1, source_target_pairs={{0,1},{1,0},{2,3},{3,2},{4,5},{5,4},{6,7},{7,6},{8,9},{9,8},{10,11... | collective-permute-start | bytes 1622024 | tf_op jit(solution)/shard_map/ppermute | solution.py:517
  2.0 16.0 %collective-permute-start = (bf16[1056,256]{1,0:T(8,128)(2,1)S(1)}, bf16[1056,256]{1,0:T(8,128)(2,1)S(1)}, u32[]{:S(2)}, u32[]{:S(2)}) collective-permute-start(bf16[1056,256]{1,0:T(8,128)(2,1)S(1)} %get-tuple-element.16), channel_id=1, source_target_pairs={{0,15},{1,2},{2,1},{3,4},{4,3},{5,6},{6,5},{7,8},{8,7},{9,10},{10,... | collective-permute-start | bytes 1622024 | tf_op jit(solution)/shard_map/ppermute | solution.py:516
  5.3 14.9 %all-to-all-start = ((f32[8,8,128]{2,1,0:T(8,128)}), f32[8,8,128]{2,1,0:T(8,128)S(1)}, u32[]{:S(2)}, u32[]{:S(2)}) async-start(f32[8,8,128]{2,1,0:T(8,128)} %broadcast_in_dim.15), calls=%async_computation | async-start | bytes 65536 | tf_op jit(solution)/shard_map/all_to_all | solution.py:520

commit v14 on v13

--- a/solution.py
+++ b/solution.py
@@ -68,9 +68,8 @@
     ]
     for copy in copies:
         copy.start()
-    for copy in copies[:4]:
+    for copy in copies[:3]:
         copy.wait()
-    rows = cells_ref[...].reshape(lon_dev * lat, members)
     index = index_ref[...]
     sub = lax.broadcasted_iota(jnp.int32, (TILE, nobs), 0)
     table = jnp.where(
@@ -83,13 +82,6 @@
     var = table[:, 2:3]
     pick = index_col == lax.broadcasted_iota(jnp.int32, (nobs, lon_dev * lat), 1)
     pick = jnp.where(pick, 1.0, 0.0).astype(jnp.bfloat16)
-    seen = jnp.dot(pick, rows, preferred_element_type=jnp.float32)
-    centre = jnp.sum(seen, axis=1, keepdims=True) * (1.0 / members)
-    spread = jnp.sum((seen - centre) ** 2, axis=1, keepdims=True) * (1.0 / (members - 1))
-    innovation = (value - centre) ** 2 / (var + spread)
-    part = jnp.sum(innovation, axis=0, keepdims=True)
-    part_ref[...] = jnp.broadcast_to(part, part_ref.shape)
-    terms = (value - seen) ** 2 * (1.0 / var)
     lon = (index // lat).astype(jnp.float32)
     along = index.astype(jnp.float32) - lon * lat
     blocks = own_ref.shape[0]
@@ -97,9 +89,18 @@
     across = line_weight(along - REGION * block + HALO)
     side = jnp.where(odd_ref[0] == 1, float(REGION), float(-REGION))
     weights = [line_weight(lon + (HALO + shift)) * across for shift in (0.0, side, -side)]
-    like = jnp.dot(
-        jnp.concatenate(weights, axis=0), terms, precision=HIGH, preferred_element_type=jnp.float32
-    )
+    weights = jnp.concatenate(weights, axis=0)
+    inverse = 1.0 / var
+    copies[3].wait()
+    rows = cells_ref[...].reshape(lon_dev * lat, members)
+    seen = jnp.dot(pick, rows, preferred_element_type=jnp.float32)
+    terms = (value - seen) ** 2 * inverse
+    like = jnp.dot(weights, terms, precision=HIGH, preferred_element_type=jnp.float32)
+    centre = jnp.sum(seen, axis=1, keepdims=True) * (1.0 / members)
+    spread = jnp.sum((seen - centre) ** 2, axis=1, keepdims=True) * (1.0 / (members - 1))
+    innovation = (value - centre) ** 2 / (var + spread)
+    part = jnp.sum(innovation, axis=0, keepdims=True)
+    part_ref[...] = jnp.broadcast_to(part, part_ref.shape)
     own_ref[...] = like[:blocks]
     near_ref[edge:, :] = in_parts(like[blocks : 2 * blocks], part)
     far_ref[edge:, :] = in_parts(like[2 * blocks :], jnp.zeros_like(part))
@@ -218,7 +219,7 @@
     add_grams(slabs, weights, None, gram_ref)
 
 
-def add_grams(slabs, weights, old_ref, new_ref):
+def add_grams(slabs, weights, old_ref, new_ref, done=None):
     none = jnp.zeros_like(slabs[0][:, :TILE])
     tiles = [none]
     for slab in slabs:
@@ -232,6 +233,8 @@
         for at, gram in enumerate(grams):
             region = pair * PAIR + at
             new_ref[region] = gram if old_ref is None else old_ref[region] + gram
+        if done is not None:
+            done(pair)
 
 
 def own_gram(odd, state, near, own):
@@ -282,7 +285,6 @@
 
 def kernel_matrices(gram_ref, kernel_ref, mass_ref, scale):
     members = gram_ref.shape[-1]
-    most = None
     for region in range(gram_ref.shape[0]):
         across, down = diagonal(gram_ref, region)
         across = [0.5 * LIFT - x * scale for x in across]
@@ -293,27 +295,29 @@
             for lane, (gram, x) in enumerate(zip(halves(gram_ref, region, rows), across)):
                 part = jnp.exp2(gram * (2.0 * scale) + base + x)
                 kernel_ref[region, rows, lane * 128 : lane * 128 + 128] = part
-                most = part if most is None else jnp.maximum(most, part)
                 part = jnp.sum(part.reshape(ROWS // TILE, TILE, 128), axis=0)
                 masses[lane] = masses[lane] + part
         masses = [jnp.sum(x, axis=0, keepdims=True) for x in masses]
         mass_ref[region] = jnp.concatenate(masses, axis=1)
-    return jnp.max(most.reshape(ROWS // TILE, TILE, 128), axis=0)
 
 
 def prepare_kernel(scale, *refs):
     odd_ref, halo_ref, old_ref, like_in_ref = refs[:4]
-    gram_hbm_ref, kernel_ref, mass_ref, most_ref, like_ref, gram_ref, sem = refs[4:]
+    gram_hbm_ref, kernel_ref, mass_ref, like_ref, gram_ref, sems = refs[4:]
     like_ref[...] = like_in_ref[...] + like_rows(halo_ref[halo_ref.shape[0] - 4 * TILE :, :])
     lat = gram_ref.shape[0] * REGION
     planes = halo_ref.shape[0] // lat
     weights = [w for w in halo_weights(odd_ref[0] == 0) for _ in range(planes // HALO)]
     slabs = [slab_of(halo_ref, lat, at) for at in range(lat // (PAIR * TILE))]
-    add_grams(slabs, weights, old_ref, gram_ref)
-    keep = pltpu.make_async_copy(gram_ref, gram_hbm_ref, sem)
-    keep.start()
-    most_ref[...] = kernel_matrices(gram_ref, kernel_ref, mass_ref, scale)
-    keep.wait()
+
+    def keep(pair):
+        part = pl.ds(pair * PAIR, PAIR)
+        return pltpu.make_async_copy(gram_ref.at[part], gram_hbm_ref.at[part], sems.at[pair])
+
+    add_grams(slabs, weights, old_ref, gram_ref, lambda pair: keep(pair).start())
+    kernel_matrices(gram_ref, kernel_ref, mass_ref, scale)
+    for pair in range(len(slabs)):
+        keep(pair).wait()
 
 
 def prepare(odd, halo, gram, like, scale):
@@ -321,15 +325,17 @@
     return pl.pallas_call(
         functools.partial(prepare_kernel, scale),
         in_specs=[pl.BlockSpec(memory_space=pltpu.SMEM)] + [vmem] * 3,
-        out_specs=[pl.BlockSpec(memory_space=pltpu.HBM)] + [vmem] * 4,
+        out_specs=[pl.BlockSpec(memory_space=pltpu.HBM)] + [vmem] * 3,
         out_shape=[
             pltpu.HBM(gram.shape, jnp.float32),
             jax.ShapeDtypeStruct(gram.shape, jnp.float32),
             jax.ShapeDtypeStruct((gram.shape[0], 1, like.shape[1]), jnp.float32),
-            jax.ShapeDtypeStruct((TILE, 128), jnp.float32),
             jax.ShapeDtypeStruct(like.shape, jnp.float32),
         ],
-        scratch_shapes=[pltpu.VMEM(gram.shape, jnp.float32), pltpu.SemaphoreType.DMA],
+        scratch_shapes=[
+            pltpu.VMEM(gram.shape, jnp.float32),
+            pltpu.SemaphoreType.DMA((gram.shape[0] // PAIR,)),
+        ],
         compiler_params=pltpu.CompilerParams(vmem_limit_bytes=24 * 2**20),
         name="prepare",
     )(odd, halo, gram, like)
@@ -342,7 +348,7 @@
     return out
 
 
-def transports_scaled(kernel_ref, weights, mass_ref):
+def transports_scaled(kernel_ref, weights, mass_ref, use):
     regions = range(kernel_ref.shape[0])
     members = kernel_ref.shape[-1]
     starts = range(0, members, ROWS)
@@ -359,8 +365,7 @@
         parts = [k * f for k, f in zip(halves(kernel_ref, region, rows), factor)]
         mass = jnp.sum(fold(parts, jnp.add), axis=1, keepdims=True)
         mass = jnp.broadcast_to(mass, (ROWS, 128))
-        near = pl.reciprocal(mass, approx=True)
-        return parts, mass, near * (2.0 - mass * near)
+        return parts, mass, pl.reciprocal(mass, approx=True)
 
     def sweep(_, carry):
         least_i, least_j, factors = carry
@@ -380,7 +385,9 @@
             next_factors.append(settle(totals, region))
         return next_i, next_j, next_factors
 
-    totals = [[x * 2.0**START for x in lane_parts(mass_ref[region])] for region in regions]
+    masses = [lane_parts(mass_ref[region]) for region in regions]
+    most = fold([fold(x, jnp.maximum) for x in masses], jnp.maximum)
+    totals = [[x * 2.0**START for x in mass] for mass in masses]
     least_i = [fold(x, jnp.minimum) for x in totals]
     least_j = [jnp.full((ROWS, 128), 1e30, jnp.float32) for _ in regions]
     factors = [settle(x, region) for x, region in zip(totals, regions)]
@@ -395,7 +402,11 @@
             blocks.append(jnp.concatenate([x * ratio for x in parts], axis=1).astype(jnp.bfloat16))
         moves.append(jnp.concatenate(blocks, axis=0))
         last_j.append(low_j)
-    return moves, fold(least_i, jnp.minimum), fold(last_j, jnp.minimum)
+        if len(moves) == PAIR:
+            use(region // PAIR, moves)
+            moves = []
+    least_i = fold(least_i, jnp.minimum)
+    return jnp.min(least_i), jnp.min(fold(last_j, jnp.minimum)), jnp.max(most)
 
 
 def transport_logs(gram, logw, scale):
@@ -434,8 +445,8 @@
 
 
 def finish_kernel(count, scale, *refs):
-    state_hbm_ref, gram_hbm_ref, kernel_ref, mass_ref, most_ref, like_ref, sums_ref = refs[:7]
-    out_ref, result_ref, state_ref, gram_ref, out_sems, state_sems, sem = refs[7:]
+    state_hbm_ref, gram_hbm_ref, kernel_ref, mass_ref, like_ref, sums_ref = refs[:6]
+    out_ref, result_ref, state_ref, gram_ref, out_sems, state_sems, sem = refs[6:]
     pairs = kernel_ref.shape[0] // PAIR
     size = PAIR * TILE
     fetches = slab_copies(state_hbm_ref, state_ref, state_sems)
@@ -452,12 +463,14 @@
     like = -0.5 * (count / total) * like_ref[...]
     like = like - jnp.max(like, axis=1, keepdims=True)
     logw = (like - jnp.log(jnp.sum(jnp.exp(like), axis=1, keepdims=True))) * LOG2E
-    moves, least_i, least_j = transports_scaled(kernel_ref, jnp.exp2(logw + MASS), mass_ref)
-    for pair in range(pairs):
+
+    def use(pair, moves):
         fetches[pair].wait()
-        result_ref[pair] = transform(state_ref, pair, moves[pair * PAIR : (pair + 1) * PAIR])
+        result_ref[pair] = transform(state_ref, pair, moves)
         send(pair).start()
-    row, col, most = jnp.min(least_i), jnp.min(least_j), jnp.max(most_ref[...])
+
+    weights = jnp.exp2(logw + MASS)
+    row, col, most = transports_scaled(kernel_ref, weights, mass_ref, use)
     sound = (row >= 2.0**-24) & (col >= 2.0**-30) & (most <= 2.0**30) & (row * col >= 2.0**-34)
     for pair in range(pairs):
         send(pair).wait()
@@ -476,14 +489,14 @@
             send(pair).wait()
 
 
-def finish(state, gram, kernel, mass, most, like, sums, count, scale):
+def finish(state, gram, kernel, mass, like, sums, count, scale):
     lon_dev, nvar, lat, members = state.shape
     pairs = lat // (PAIR * TILE)
     vmem = pl.BlockSpec(memory_space=pltpu.VMEM)
     hbm = pl.BlockSpec(memory_space=pltpu.HBM)
     return pl.pallas_call(
         functools.partial(finish_kernel, count, scale),
-        in_specs=[hbm, hbm] + [vmem] * 5,
+        in_specs=[hbm, hbm] + [vmem] * 4,
         out_specs=pl.BlockSpec(memory_space=pl.ANY),
         out_shape=jax.ShapeDtypeStruct(state.shape, state.dtype),
         scratch_shapes=[
@@ -500,7 +513,6 @@
         *[pltpu.with_memory_space_constraint(x, pltpu.HBM) for x in (state, gram)],
         kernel,
         mass,
-        most,
         like,
         sums,
     )
@@ -529,9 +541,9 @@
     line = [1.0 - max(0, HALO - p, p - (HALO + REGION - 1)) / (HALO + 1) for p in offsets]
     scale = LOG2E / EPS / (nvar * sum(line) ** 2)
     gram, like = own_gram(odd, state, near, own_like)
-    gram, kernel, mass, most, like = prepare(odd, far, gram, like, scale)
+    gram, kernel, mass, like = prepare(odd, far, gram, like, scale)
     nobs = float(obs_index.shape[0] * count)
-    return finish(state, gram, kernel, mass, most, like, sums, nobs, scale)
+    return finish(state, gram, kernel, mass, like, sums, nobs, scale)
 
 
 def solution(mesh):

time: 42.2 us -> 41.1 us (0.974)
  Pallas kernels: 27.9 us -> 26.8 us
    pallas_call x1, Pallas kernels: 21.4 us -> 21 us  [finish(): pl.pallas_call(functools.partial(finish_kernel, count, scale), in_specs=[...]
  transfers between devices with their start and end apart: 3 -> 3, of which waited for: 1 -> 1; matrix products, arithmetic and copies ran while one was open for 2% -> 2% of each run, Pallas kernels for 11% -> 10%
where the time goes in v14:
time: 41.1 us; the launch traced here: 40.7 us
  Pallas kernels  26.8 us (65%)
  starting transfers between devices  8.68 us (21%)
  waiting for transfers between devices  4.39 us (11%)
  local copies, waits for them, and re-layouts  0.62 us (2%)
    pallas_call x1, Pallas kernels, finish(): pl.pallas_call(functools.partial(finish_kernel, count, scale), in_specs=[...  21 us
    all_to_all x1, starting transfers between devices, on_device(): lax.all_to_all(jnp.broadcast_to(part, (count // 2 * TILE, 128)), 'lon', 0...  5.91 us
    ppermute x1, waiting for transfers between devices, on_device(): far = lax.ppermute(for_far, 'lon', far_pairs)  4.39 us
    ppermute x1, starting transfers between devices, on_device(): far = lax.ppermute(for_far, 'lon', far_pairs)  2.65 us
    pallas_call x1, Pallas kernels, own_gram(): pl.pallas_call(own_gram_kernel, in_specs=[pl.BlockSpec(memory_space=pltpu...  2.44 us
    pallas_call x1, Pallas kernels, prepare(): pl.pallas_call(functools.partial(prepare_kernel, scale), in_specs=[pl.Blo...  1.75 us
    pallas_call x1, Pallas kernels, observe(): pl.pallas_call(observe_kernel, in_specs=[pl.BlockSpec(memory_space=pltpu....  1.67 us
  transfers between devices with their start and end apart: 3, of which 1 were waited for; matrix products, arithmetic and copies ran while one was open for 2% of the time, Pallas kernels for 10%

profile of v14, /device:TPU:1, one launch (start us, length us, event | category | flops | bytes accessed | tf_op | source)
XLA Modules:
  0.0 40.7 jit_solution(7595851366569155827)
XLA Ops:
  0.0 1.7 %observe.1 = (f32[8,256]{1,0:T(8,128)S(1)}, bf16[1056,256]{1,0:T(8,128)(2,1)S(1)}, bf16[1056,256]{1,0:T(8,128)(2,1)S(1)}, f32[8,128]{1,0:T(8,128)S(1)}) custom-call(s32[1]{0:T(128)} %bitcast.refs_0_.odd_ref, bf16[8,4,64,256]{3,2,1,0:T(8,128)(2,1)} %refs_0_.1, bf16[2048,256]{1,0:T(8,128)(2,1)} %bitcast.9, s32[1,256]{1,0:T(1,128)} %bitcast.10, ...), custom_call_target="tpu_custom_call" | custom-call | tf_op jit(solution)/shard_map/observe/pallas_call | solution.py:119
  1.7 0.1 collective-permute-start.1
  1.8 2.7 %collective-permute-start = (bf16[1056,256]{1,0:T(8,128)(2,1)S(1)}, bf16[1056,256]{1,0:T(8,128)(2,1)S(1)}, u32[]{:S(2)}, u32[]{:S(2)}) collective-permute-start(bf16[1056,256]{1,0:T(8,128)(2,1)S(1)} %get-tuple-element.15), channel_id=1, source_target_pairs={{0,15},{1,2},{2,1},{3,4},{4,3},{5,6},{6,5},{7,8},{8,7},{9,10},{10,... | collective-permute-start | bytes 1622024 | tf_op jit(solution)/shard_map/ppermute | solution.py:528
  4.5 0.0 collective-permute-done.1.near_ref
  4.5 0.6 %broadcast_in_dim.15 = f32[8,8,128]{2,1,0:T(8,128)} broadcast(f32[128]{0:T(128)S(1)} %bitcast_add_fusion), dimensions={2} | broadcast | bytes 33280 | tf_op jit(solution)/shard_map/broadcast_in_dim | solution.py:533
  5.1 5.9 %all-to-all-start = ((f32[8,8,128]{2,1,0:T(8,128)}), f32[8,8,128]{2,1,0:T(8,128)S(1)}, u32[]{:S(2)}, u32[]{:S(2)}) async-start(f32[8,8,128]{2,1,0:T(8,128)} %broadcast_in_dim.15), calls=%async_computation | async-start | bytes 65536 | tf_op jit(solution)/shard_map/all_to_all | solution.py:532
  11.0 2.4 %own_gram.1 = (f32[8,256,256]{2,1,0:T(8,128)S(1)}, f32[8,256]{1,0:T(8,128)S(1)}) custom-call(s32[1]{0:T(128)} %bitcast.refs_0_.odd_ref, bf16[8,4,64,256]{3,2,1,0:T(8,128)(2,1)} %refs_0_.1, bf16[1056,256]{1,0:T(8,128)(2,1)S(1)} %collective-permute-done.1.near_ref, f32[8,256]{1,0:T(8,128)S(1)} %get-tuple-element.17.own_ref), custom_call_target="tpu_custom_call" | custom-call | tf_op jit(solution)/shard_map/own_gram/pallas_call | solution.py:243
  13.5 4.4 %collective-permute-done.refs_1_ = bf16[1056,256]{1,0:T(8,128)(2,1)S(1)} collective-permute-done((bf16[1056,256]{1,0:T(8,128)(2,1)S(1)}, bf16[1056,256]{1,0:T(8,128)(2,1)S(1)}, u32[]{:S(2)}, u32[]{:S(2)}) %collective-permute-start) | collective-permute-done | bytes 540704 | tf_op jit(solution)/shard_map/ppermute | solution.py:528
  17.8 1.7 %prepare.1 = (f32[8,256,256]{2,1,0:T(8,128)}, f32[8,256,256]{2,1,0:T(8,128)S(1)}, f32[8,1,256]{2,1,0:T(1,128)S(1)}, f32[8,256]{1,0:T(8,128)S(1)}) custom-call(s32[1]{0:T(128)} %bitcast.refs_0_.odd_ref, bf16[1056,256]{1,0:T(8,128)(2,1)S(1)} %collective-permute-done.refs_1_, f32[8,256,256]{2,1,0:T(8,128)S(1)} %get-tuple-element.18.refs_2_, ...), custom_call_target="tpu_custom_call" | custom-call | tf_op jit(solution)/shard_map/prepare/pallas_call | solution.py:325
  19.6 0.0 all-to-all-done
  19.6 21.0 %finish.1 = bf16[8,4,64,256]{3,2,1,0:T(8,128)(2,1)} custom-call(bf16[8,4,64,256]{3,2,1,0:T(8,128)(2,1)} %refs_0_.1, f32[8,256,256]{2,1,0:T(8,128)} %get-tuple-element.20.refs_1_, f32[8,256,256]{2,1,0:T(8,128)S(1)} %get-tuple-element.21.refs_2_, f32[8,1,256]{2,1,0:T(1,128)S(1)} %get-tuple-element.22.refs_3_, f32[8,256]{1,0:T(8,128)S(1)} %get-tuple-element.23.refs_4_, ...), custom_call_target="tpu_custom_call" | custom-call | tf_op jit(solution)/shard_map/finish/pallas_call | solution.py:497
  (2 shorter events, 0.0 us)
Async XLA Ops:
  1.7 2.8 %collective-permute-start.1 = (bf16[1056,256]{1,0:T(8,128)(2,1)S(1)}, bf16[1056,256]{1,0:T(8,128)(2,1)S(1)}, u32[]{:S(2)}, u32[]{:S(2)}) collective-permute-start(bf16[1056,256]{1,0:T(8,128)(2,1)S(1)} %get-tuple-element.16), channel_id=1, source_target_pairs={{0,1},{1,0},{2,3},{3,2},{4,5},{5,4},{6,7},{7,6},{8,9},{9,8},{10,11... | collective-permute-start | bytes 1622024 | tf_op jit(solution)/shard_map/ppermute | solution.py:529
  1.8 16.0 %collective-permute-start = (bf16[1056,256]{1,0:T(8,128)(2,1)S(1)}, bf16[1056,256]{1,0:T(8,128)(2,1)S(1)}, u32[]{:S(2)}, u32[]{:S(2)}) collective-permute-start(bf16[1056,256]{1,0:T(8,128)(2,1)S(1)} %get-tuple-element.15), channel_id=1, source_target_pairs={{0,15},{1,2},{2,1},{3,4},{4,3},{5,6},{6,5},{7,8},{8,7},{9,10},{10,... | collective-permute-start | bytes 1622024 | tf_op jit(solution)/shard_map/ppermute | solution.py:528
  5.1 14.5 %all-to-all-start = ((f32[8,8,128]{2,1,0:T(8,128)}), f32[8,8,128]{2,1,0:T(8,128)S(1)}, u32[]{:S(2)}, u32[]{:S(2)}) async-start(f32[8,8,128]{2,1,0:T(8,128)} %broadcast_in_dim.15), calls=%async_computation | async-start | bytes 65536 | tf_op jit(solution)/shard_map/all_to_all | solution.py:532

commit v15 on v14

--- a/solution.py
+++ b/solution.py
@@ -459,7 +459,7 @@
             result_ref.at[pair], out_ref.at[:, :, rows, :], out_sems.at[pair]
         )
 
-    total = jnp.sum(sums_ref[...], axis=0, keepdims=True)[:, 0:1] * (1.0 / TILE)
+    total = jnp.sum(sums_ref[...], axis=0, keepdims=True)[:, 0:1]
     like = -0.5 * (count / total) * like_ref[...]
     like = like - jnp.max(like, axis=1, keepdims=True)
     logw = (like - jnp.log(jnp.sum(jnp.exp(like), axis=1, keepdims=True))) * LOG2E
@@ -530,11 +530,11 @@
     start = near.shape[0] - TILE
     part = part[0] + jnp.sum(near[start : start + 3, :128].astype(jnp.float32), axis=0)
     sums = lax.all_to_all(
-        jnp.broadcast_to(part, (count // 2 * TILE, 128)),
+        jnp.broadcast_to(part, (count // 2, 128)),
         "lon",
         0,
         0,
-        axis_index_groups=[list(range(core, count, 2)) for core in range(2)],
+        axis_index_groups=[[i for i in range(count) if (i ^ i >> 1) & 1 == kind] for kind in range(2)],
         tiled=True,
     )
     offsets = range(REGION + 2 * HALO)

time: 41.1 us -> 40.5 us (0.985)
  waiting for transfers between devices: 4.39 us -> 3.64 us
    ppermute x1, waiting for transfers between devices: 4.39 us -> 3.63 us  [on_device(): far = lax.ppermute(for_far, 'lon', far_pairs)]
where the time goes in v15:
time: 40.5 us; the launch traced here: 40.2 us
  Pallas kernels  26.8 us (66%)
  starting transfers between devices  8.94 us (22%)
  waiting for transfers between devices  3.64 us (9%)
  local copies, waits for them, and re-layouts  0.6 us (1%)
    pallas_call x1, Pallas kernels, finish(): pl.pallas_call(functools.partial(finish_kernel, count, scale), in_specs=[...  21 us
    all_to_all x1, starting transfers between devices, on_device(): lax.all_to_all(jnp.broadcast_to(part, (count // 2, 128)), 'lon', 0, 0, ax...  6.17 us
    ppermute x1, waiting for transfers between devices, on_device(): far = lax.ppermute(for_far, 'lon', far_pairs)  3.63 us
    ppermute x1, starting transfers between devices, on_device(): far = lax.ppermute(for_far, 'lon', far_pairs)  2.65 us
    pallas_call x1, Pallas kernels, own_gram(): pl.pallas_call(own_gram_kernel, in_specs=[pl.BlockSpec(memory_space=pltpu...  2.44 us
    pallas_call x1, Pallas kernels, prepare(): pl.pallas_call(functools.partial(prepare_kernel, scale), in_specs=[pl.Blo...  1.75 us
    pallas_call x1, Pallas kernels, observe(): pl.pallas_call(observe_kernel, in_specs=[pl.BlockSpec(memory_space=pltpu....  1.67 us
  transfers between devices with their start and end apart: 3, of which 1 were waited for; matrix products, arithmetic and copies ran while one was open for 2% of the time, Pallas kernels for 10%

profile of v15, /device:TPU:1, one launch (start us, length us, event | category | flops | bytes accessed | tf_op | source)
XLA Modules:
  0.0 40.2 jit_solution(12829268601820070925)
XLA Ops:
  0.0 1.7 %observe.1 = (f32[8,256]{1,0:T(8,128)S(1)}, bf16[1056,256]{1,0:T(8,128)(2,1)S(1)}, bf16[1056,256]{1,0:T(8,128)(2,1)S(1)}, f32[8,128]{1,0:T(8,128)S(1)}) custom-call(s32[1]{0:T(128)} %bitcast.refs_0_.odd_ref, bf16[8,4,64,256]{3,2,1,0:T(8,128)(2,1)} %refs_0_.1, bf16[2048,256]{1,0:T(8,128)(2,1)} %bitcast.9, s32[1,256]{1,0:T(1,128)} %bitcast.10, ...), custom_call_target="tpu_custom_call" | custom-call | tf_op jit(solution)/shard_map/observe/pallas_call | solution.py:119
  1.7 0.1 collective-permute-start.1
  1.8 2.7 %collective-permute-start = (bf16[1056,256]{1,0:T(8,128)(2,1)S(1)}, bf16[1056,256]{1,0:T(8,128)(2,1)S(1)}, u32[]{:S(2)}, u32[]{:S(2)}) collective-permute-start(bf16[1056,256]{1,0:T(8,128)(2,1)S(1)} %get-tuple-element.15), channel_id=1, source_target_pairs={{0,15},{1,2},{2,1},{3,4},{4,3},{5,6},{6,5},{7,8},{8,7},{9,10},{10,... | collective-permute-start | bytes 1622024 | tf_op jit(solution)/shard_map/ppermute | solution.py:528
  4.5 0.0 collective-permute-done.1.near_ref
  4.5 0.6 %broadcast_in_dim.15 = f32[8,1,128]{2,1,0:T(1,128)} broadcast(f32[128]{0:T(128)S(1)} %bitcast_add_fusion), dimensions={2} | broadcast | bytes 4608 | tf_op jit(solution)/shard_map/broadcast_in_dim | solution.py:533
  5.1 6.2 %all-to-all-start = ((f32[8,1,128]{2,1,0:T(1,128)}), f32[8,1,128]{2,1,0:T(1,128)S(1)}, u32[]{:S(2)}, u32[]{:S(2)}) async-start(f32[8,1,128]{2,1,0:T(1,128)} %broadcast_in_dim.15), calls=%async_computation | async-start | bytes 8192 | tf_op jit(solution)/shard_map/all_to_all | solution.py:532
  11.2 2.4 %own_gram.1 = (f32[8,256,256]{2,1,0:T(8,128)S(1)}, f32[8,256]{1,0:T(8,128)S(1)}) custom-call(s32[1]{0:T(128)} %bitcast.refs_0_.odd_ref, bf16[8,4,64,256]{3,2,1,0:T(8,128)(2,1)} %refs_0_.1, bf16[1056,256]{1,0:T(8,128)(2,1)S(1)} %collective-permute-done.1.near_ref, f32[8,256]{1,0:T(8,128)S(1)} %get-tuple-element.17.own_ref), custom_call_target="tpu_custom_call" | custom-call | tf_op jit(solution)/shard_map/own_gram/pallas_call | solution.py:243
  13.7 3.6 %collective-permute-done.refs_1_ = bf16[1056,256]{1,0:T(8,128)(2,1)S(1)} collective-permute-done((bf16[1056,256]{1,0:T(8,128)(2,1)S(1)}, bf16[1056,256]{1,0:T(8,128)(2,1)S(1)}, u32[]{:S(2)}, u32[]{:S(2)}) %collective-permute-start) | collective-permute-done | bytes 540704 | tf_op jit(solution)/shard_map/ppermute | solution.py:528
  17.3 1.7 %prepare.1 = (f32[8,256,256]{2,1,0:T(8,128)}, f32[8,256,256]{2,1,0:T(8,128)S(1)}, f32[8,1,256]{2,1,0:T(1,128)S(1)}, f32[8,256]{1,0:T(8,128)S(1)}) custom-call(s32[1]{0:T(128)} %bitcast.refs_0_.odd_ref, bf16[1056,256]{1,0:T(8,128)(2,1)S(1)} %collective-permute-done.refs_1_, f32[8,256,256]{2,1,0:T(8,128)S(1)} %get-tuple-element.18.refs_2_, ...), custom_call_target="tpu_custom_call" | custom-call | tf_op jit(solution)/shard_map/prepare/pallas_call | solution.py:325
  19.1 0.0 all-to-all-done
  19.1 21.0 %finish.1 = bf16[8,4,64,256]{3,2,1,0:T(8,128)(2,1)} custom-call(bf16[8,4,64,256]{3,2,1,0:T(8,128)(2,1)} %refs_0_.1, f32[8,256,256]{2,1,0:T(8,128)} %get-tuple-element.20.refs_1_, f32[8,256,256]{2,1,0:T(8,128)S(1)} %get-tuple-element.21.refs_2_, f32[8,1,256]{2,1,0:T(1,128)S(1)} %get-tuple-element.22.refs_3_, f32[8,256]{1,0:T(8,128)S(1)} %get-tuple-element.23.refs_4_, ...), custom_call_target="tpu_custom_call" | custom-call | tf_op jit(solution)/shard_map/finish/pallas_call | solution.py:497
  (2 shorter events, 0.0 us)
Async XLA Ops:
  1.7 2.8 %collective-permute-start.1 = (bf16[1056,256]{1,0:T(8,128)(2,1)S(1)}, bf16[1056,256]{1,0:T(8,128)(2,1)S(1)}, u32[]{:S(2)}, u32[]{:S(2)}) collective-permute-start(bf16[1056,256]{1,0:T(8,128)(2,1)S(1)} %get-tuple-element.16), channel_id=1, source_target_pairs={{0,1},{1,0},{2,3},{3,2},{4,5},{5,4},{6,7},{7,6},{8,9},{9,8},{10,11... | collective-permute-start | bytes 1622024 | tf_op jit(solution)/shard_map/ppermute | solution.py:529
  1.8 15.5 %collective-permute-start = (bf16[1056,256]{1,0:T(8,128)(2,1)S(1)}, bf16[1056,256]{1,0:T(8,128)(2,1)S(1)}, u32[]{:S(2)}, u32[]{:S(2)}) collective-permute-start(bf16[1056,256]{1,0:T(8,128)(2,1)S(1)} %get-tuple-element.15), channel_id=1, source_target_pairs={{0,15},{1,2},{2,1},{3,4},{4,3},{5,6},{6,5},{7,8},{8,7},{9,10},{10,... | collective-permute-start | bytes 1622024 | tf_op jit(solution)/shard_map/ppermute | solution.py:528
  5.1 14.0 %all-to-all-start = ((f32[8,1,128]{2,1,0:T(1,128)}), f32[8,1,128]{2,1,0:T(1,128)S(1)}, u32[]{:S(2)}, u32[]{:S(2)}) async-start(f32[8,1,128]{2,1,0:T(1,128)} %broadcast_in_dim.15), calls=%async_computation | async-start | bytes 8192 | tf_op jit(solution)/shard_map/all_to_all | solution.py:532

commit v16 on v15

--- a/solution.py
+++ b/solution.py
@@ -18,7 +18,12 @@
 ROWS = 32
 LIFT, START, MASS = 20, -10, 60
 
-HIGH = lax.Precision.HIGHEST
+
+def fold(values, op):
+    out = values[0]
+    for value in values[1:]:
+        out = op(out, value)
+    return out
 
 
 def line_weight(place):
@@ -43,6 +48,12 @@
     middle = (values - high).astype(jnp.bfloat16).astype(jnp.float32)
     low = values - high - middle
     return jnp.concatenate([high, middle, low, last], axis=0).astype(jnp.bfloat16)
+
+
+def steps_inside(place):
+    dist = jnp.maximum(0.0, jnp.maximum(HALO - place, place - (HALO + REGION - 1)))
+    inside = (place >= 0) & (place < REGION + 2 * HALO)
+    return jnp.where(inside, HALO + 1 - dist, 0.0)
 
 
 def observe_kernel(*refs):
@@ -86,16 +97,21 @@
     along = index.astype(jnp.float32) - lon * lat
     blocks = own_ref.shape[0]
     block = lax.broadcasted_iota(jnp.int32, (blocks, nobs), 0).astype(jnp.float32)
-    across = line_weight(along - REGION * block + HALO)
+    across = steps_inside(along - REGION * block + HALO)
     side = jnp.where(odd_ref[0] == 1, float(REGION), float(-REGION))
-    weights = [line_weight(lon + (HALO + shift)) * across for shift in (0.0, side, -side)]
-    weights = jnp.concatenate(weights, axis=0)
+    weights = [steps_inside(lon + (HALO + shift)) * across for shift in (0.0, side, -side)]
+    weights = jnp.concatenate(weights, axis=0).astype(jnp.bfloat16)
     inverse = 1.0 / var
     copies[3].wait()
     rows = cells_ref[...].reshape(lon_dev * lat, members)
     seen = jnp.dot(pick, rows, preferred_element_type=jnp.float32)
     terms = (value - seen) ** 2 * inverse
-    like = jnp.dot(weights, terms, precision=HIGH, preferred_element_type=jnp.float32)
+    high = terms.astype(jnp.bfloat16)
+    rest = terms - high.astype(jnp.float32)
+    middle = rest.astype(jnp.bfloat16)
+    low = (rest - middle.astype(jnp.float32)).astype(jnp.bfloat16)
+    sums = [jnp.dot(weights, x, preferred_element_type=jnp.float32) for x in (low, middle, high)]
+    like = fold(sums, jnp.add) * (1.0 / (HALO + 1) ** 2)
     centre = jnp.sum(seen, axis=1, keepdims=True) * (1.0 / members)
     spread = jnp.sum((seen - centre) ** 2, axis=1, keepdims=True) * (1.0 / (members - 1))
     innovation = (value - centre) ** 2 / (var + spread)
@@ -304,7 +320,8 @@
 def prepare_kernel(scale, *refs):
     odd_ref, halo_ref, old_ref, like_in_ref = refs[:4]
     gram_hbm_ref, kernel_ref, mass_ref, like_ref, gram_ref, sems = refs[4:]
-    like_ref[...] = like_in_ref[...] + like_rows(halo_ref[halo_ref.shape[0] - 4 * TILE :, :])
+    like = like_in_ref[...] + like_rows(halo_ref[halo_ref.shape[0] - 4 * TILE :, :])
+    like_ref[...] = like - jnp.min(like, axis=1, keepdims=True)
     lat = gram_ref.shape[0] * REGION
     planes = halo_ref.shape[0] // lat
     weights = [w for w in halo_weights(odd_ref[0] == 0) for _ in range(planes // HALO)]
@@ -341,13 +358,6 @@
     )(odd, halo, gram, like)
 
 
-def fold(values, op):
-    out = values[0]
-    for value in values[1:]:
-        out = op(out, value)
-    return out
-
-
 def transports_scaled(kernel_ref, weights, mass_ref, use):
     regions = range(kernel_ref.shape[0])
     members = kernel_ref.shape[-1]
@@ -367,8 +377,7 @@
         mass = jnp.broadcast_to(mass, (ROWS, 128))
         return parts, mass, pl.reciprocal(mass, approx=True)
 
-    def sweep(_, carry):
-        least_i, least_j, factors = carry
+    def sweep(least_i, least_j, factors):
         next_i, next_j, next_factors = [], [], []
         for region, low_i, low_j, factor in zip(regions, least_i, least_j, factors):
             totals = [None for _ in lanes]
@@ -391,8 +400,8 @@
     least_i = [fold(x, jnp.minimum) for x in totals]
     least_j = [jnp.full((ROWS, 128), 1e30, jnp.float32) for _ in regions]
     factors = [settle(x, region) for x, region in zip(totals, regions)]
-    carry = lax.fori_loop(0, SWEEPS - 1, sweep, (least_i, least_j, factors))
-    least_i, least_j, factors = carry
+    for _ in range(SWEEPS - 1):
+        least_i, least_j, factors = sweep(least_i, least_j, factors)
     moves, last_j = [], []
     for region, low_j, factor in zip(regions, least_j, factors):
         blocks = []
@@ -461,7 +470,6 @@
 
     total = jnp.sum(sums_ref[...], axis=0, keepdims=True)[:, 0:1]
     like = -0.5 * (count / total) * like_ref[...]
-    like = like - jnp.max(like, axis=1, keepdims=True)
     logw = (like - jnp.log(jnp.sum(jnp.exp(like), axis=1, keepdims=True))) * LOG2E
 
     def use(pair, moves):

time: 40.5 us -> 40.2 us (level)
  no operation moved by 1% of the time
where the time goes in v16:
time: 40.2 us; the launch traced here: 39.8 us
  Pallas kernels  26.4 us (66%)
  starting transfers between devices  8.94 us (22%)
  waiting for transfers between devices  3.64 us (9%)
  local copies, waits for them, and re-layouts  0.6 us (1%)
    pallas_call x1, Pallas kernels, finish(): pl.pallas_call(functools.partial(finish_kernel, count, scale), in_specs=[...  20.6 us
    all_to_all x1, starting transfers between devices, on_device(): lax.all_to_all(jnp.broadcast_to(part, (count // 2, 128)), 'lon', 0, 0, ax...  6.17 us
    ppermute x1, waiting for transfers between devices, on_device(): far = lax.ppermute(for_far, 'lon', far_pairs)  3.63 us
    ppermute x1, starting transfers between devices, on_device(): far = lax.ppermute(for_far, 'lon', far_pairs)  2.65 us
    pallas_call x1, Pallas kernels, own_gram(): pl.pallas_call(own_gram_kernel, in_specs=[pl.BlockSpec(memory_space=pltpu...  2.44 us
    pallas_call x1, Pallas kernels, prepare(): pl.pallas_call(functools.partial(prepare_kernel, scale), in_specs=[pl.Blo...  1.74 us
    pallas_call x1, Pallas kernels, observe(): pl.pallas_call(observe_kernel, in_specs=[pl.BlockSpec(memory_space=pltpu....  1.65 us
  transfers between devices with their start and end apart: 3, of which 1 were waited for; matrix products, arithmetic and copies ran while one was open for 2% of the time, Pallas kernels for 10%

profile of v16, /device:TPU:1, one launch (start us, length us, event | category | flops | bytes accessed | tf_op | source)
XLA Modules:
  0.0 39.8 jit_solution(9286389046946302700)
XLA Ops:
  0.0 1.7 %observe.1 = (f32[8,256]{1,0:T(8,128)S(1)}, bf16[1056,256]{1,0:T(8,128)(2,1)S(1)}, bf16[1056,256]{1,0:T(8,128)(2,1)S(1)}, f32[8,128]{1,0:T(8,128)S(1)}) custom-call(s32[1]{0:T(128)} %bitcast.refs_0_.odd_ref, bf16[8,4,64,256]{3,2,1,0:T(8,128)(2,1)} %refs_0_.1, bf16[2048,256]{1,0:T(8,128)(2,1)} %bitcast.9, s32[1,256]{1,0:T(1,128)} %bitcast.10, ...), custom_call_target="tpu_custom_call" | custom-call | tf_op jit(solution)/shard_map/observe/pallas_call | solution.py:135
  1.7 0.1 collective-permute-start.1
  1.8 2.7 %collective-permute-start = (bf16[1056,256]{1,0:T(8,128)(2,1)S(1)}, bf16[1056,256]{1,0:T(8,128)(2,1)S(1)}, u32[]{:S(2)}, u32[]{:S(2)}) collective-permute-start(bf16[1056,256]{1,0:T(8,128)(2,1)S(1)} %get-tuple-element.15), channel_id=1, source_target_pairs={{0,15},{1,2},{2,1},{3,4},{4,3},{5,6},{6,5},{7,8},{8,7},{9,10},{10,... | collective-permute-start | bytes 1622024 | tf_op jit(solution)/shard_map/ppermute | solution.py:536
  4.4 0.0 collective-permute-done.1.near_ref
  4.5 0.6 %broadcast_in_dim.15 = f32[8,1,128]{2,1,0:T(1,128)} broadcast(f32[128]{0:T(128)S(1)} %bitcast_add_fusion), dimensions={2} | broadcast | bytes 4608 | tf_op jit(solution)/shard_map/broadcast_in_dim | solution.py:541
  5.1 6.2 %all-to-all-start = ((f32[8,1,128]{2,1,0:T(1,128)}), f32[8,1,128]{2,1,0:T(1,128)S(1)}, u32[]{:S(2)}, u32[]{:S(2)}) async-start(f32[8,1,128]{2,1,0:T(1,128)} %broadcast_in_dim.15), calls=%async_computation | async-start | bytes 8192 | tf_op jit(solution)/shard_map/all_to_all | solution.py:540
  11.2 2.4 %own_gram.1 = (f32[8,256,256]{2,1,0:T(8,128)S(1)}, f32[8,256]{1,0:T(8,128)S(1)}) custom-call(s32[1]{0:T(128)} %bitcast.refs_0_.odd_ref, bf16[8,4,64,256]{3,2,1,0:T(8,128)(2,1)} %refs_0_.1, bf16[1056,256]{1,0:T(8,128)(2,1)S(1)} %collective-permute-done.1.near_ref, f32[8,256]{1,0:T(8,128)S(1)} %get-tuple-element.17.own_ref), custom_call_target="tpu_custom_call" | custom-call | tf_op jit(solution)/shard_map/own_gram/pallas_call | solution.py:259
  13.7 3.6 %collective-permute-done.refs_1_ = bf16[1056,256]{1,0:T(8,128)(2,1)S(1)} collective-permute-done((bf16[1056,256]{1,0:T(8,128)(2,1)S(1)}, bf16[1056,256]{1,0:T(8,128)(2,1)S(1)}, u32[]{:S(2)}, u32[]{:S(2)}) %collective-permute-start) | collective-permute-done | bytes 540704 | tf_op jit(solution)/shard_map/ppermute | solution.py:536
  17.3 1.7 %prepare.1 = (f32[8,256,256]{2,1,0:T(8,128)}, f32[8,256,256]{2,1,0:T(8,128)S(1)}, f32[8,1,256]{2,1,0:T(1,128)S(1)}, f32[8,256]{1,0:T(8,128)S(1)}) custom-call(s32[1]{0:T(128)} %bitcast.refs_0_.odd_ref, bf16[1056,256]{1,0:T(8,128)(2,1)S(1)} %collective-permute-done.refs_1_, f32[8,256,256]{2,1,0:T(8,128)S(1)} %get-tuple-element.18.refs_2_, ...), custom_call_target="tpu_custom_call" | custom-call | tf_op jit(solution)/shard_map/prepare/pallas_call | solution.py:342
  19.1 0.0 all-to-all-done
  19.1 20.6 %finish.1 = bf16[8,4,64,256]{3,2,1,0:T(8,128)(2,1)} custom-call(bf16[8,4,64,256]{3,2,1,0:T(8,128)(2,1)} %refs_0_.1, f32[8,256,256]{2,1,0:T(8,128)} %get-tuple-element.20.refs_1_, f32[8,256,256]{2,1,0:T(8,128)S(1)} %get-tuple-element.21.refs_2_, f32[8,1,256]{2,1,0:T(1,128)S(1)} %get-tuple-element.22.refs_3_, f32[8,256]{1,0:T(8,128)S(1)} %get-tuple-element.23.refs_4_, ...), custom_call_target="tpu_custom_call" | custom-call | tf_op jit(solution)/shard_map/finish/pallas_call | solution.py:505
  (2 shorter events, 0.0 us)
Async XLA Ops:
  1.7 2.8 %collective-permute-start.1 = (bf16[1056,256]{1,0:T(8,128)(2,1)S(1)}, bf16[1056,256]{1,0:T(8,128)(2,1)S(1)}, u32[]{:S(2)}, u32[]{:S(2)}) collective-permute-start(bf16[1056,256]{1,0:T(8,128)(2,1)S(1)} %get-tuple-element.16), channel_id=1, source_target_pairs={{0,1},{1,0},{2,3},{3,2},{4,5},{5,4},{6,7},{7,6},{8,9},{9,8},{10,11... | collective-permute-start | bytes 1622024 | tf_op jit(solution)/shard_map/ppermute | solution.py:537
  1.8 15.5 %collective-permute-start = (bf16[1056,256]{1,0:T(8,128)(2,1)S(1)}, bf16[1056,256]{1,0:T(8,128)(2,1)S(1)}, u32[]{:S(2)}, u32[]{:S(2)}) collective-permute-start(bf16[1056,256]{1,0:T(8,128)(2,1)S(1)} %get-tuple-element.15), channel_id=1, source_target_pairs={{0,15},{1,2},{2,1},{3,4},{4,3},{5,6},{6,5},{7,8},{8,7},{9,10},{10,... | collective-permute-start | bytes 1622024 | tf_op jit(solution)/shard_map/ppermute | solution.py:536
  5.1 14.0 %all-to-all-start = ((f32[8,1,128]{2,1,0:T(1,128)}), f32[8,1,128]{2,1,0:T(1,128)S(1)}, u32[]{:S(2)}, u32[]{:S(2)}) async-start(f32[8,1,128]{2,1,0:T(1,128)} %broadcast_in_dim.15), calls=%async_computation | async-start | bytes 8192 | tf_op jit(solution)/shard_map/all_to_all | solution.py:540

commit v17 on v16

--- a/solution.py
+++ b/solution.py
@@ -235,7 +235,7 @@
     add_grams(slabs, weights, None, gram_ref)
 
 
-def add_grams(slabs, weights, old_ref, new_ref, done=None):
+def add_grams(slabs, weights, old_ref, new_ref):
     none = jnp.zeros_like(slabs[0][:, :TILE])
     tiles = [none]
     for slab in slabs:
@@ -249,8 +249,6 @@
         for at, gram in enumerate(grams):
             region = pair * PAIR + at
             new_ref[region] = gram if old_ref is None else old_ref[region] + gram
-        if done is not None:
-            done(pair)
 
 
 def own_gram(odd, state, near, own):
@@ -317,47 +315,6 @@
         mass_ref[region] = jnp.concatenate(masses, axis=1)
 
 
-def prepare_kernel(scale, *refs):
-    odd_ref, halo_ref, old_ref, like_in_ref = refs[:4]
-    gram_hbm_ref, kernel_ref, mass_ref, like_ref, gram_ref, sems = refs[4:]
-    like = like_in_ref[...] + like_rows(halo_ref[halo_ref.shape[0] - 4 * TILE :, :])
-    like_ref[...] = like - jnp.min(like, axis=1, keepdims=True)
-    lat = gram_ref.shape[0] * REGION
-    planes = halo_ref.shape[0] // lat
-    weights = [w for w in halo_weights(odd_ref[0] == 0) for _ in range(planes // HALO)]
-    slabs = [slab_of(halo_ref, lat, at) for at in range(lat // (PAIR * TILE))]
-
-    def keep(pair):
-        part = pl.ds(pair * PAIR, PAIR)
-        return pltpu.make_async_copy(gram_ref.at[part], gram_hbm_ref.at[part], sems.at[pair])
-
-    add_grams(slabs, weights, old_ref, gram_ref, lambda pair: keep(pair).start())
-    kernel_matrices(gram_ref, kernel_ref, mass_ref, scale)
-    for pair in range(len(slabs)):
-        keep(pair).wait()
-
-
-def prepare(odd, halo, gram, like, scale):
-    vmem = pl.BlockSpec(memory_space=pltpu.VMEM)
-    return pl.pallas_call(
-        functools.partial(prepare_kernel, scale),
-        in_specs=[pl.BlockSpec(memory_space=pltpu.SMEM)] + [vmem] * 3,
-        out_specs=[pl.BlockSpec(memory_space=pltpu.HBM)] + [vmem] * 3,
-        out_shape=[
-            pltpu.HBM(gram.shape, jnp.float32),
-            jax.ShapeDtypeStruct(gram.shape, jnp.float32),
-            jax.ShapeDtypeStruct((gram.shape[0], 1, like.shape[1]), jnp.float32),
-            jax.ShapeDtypeStruct(like.shape, jnp.float32),
-        ],
-        scratch_shapes=[
-            pltpu.VMEM(gram.shape, jnp.float32),
-            pltpu.SemaphoreType.DMA((gram.shape[0] // PAIR,)),
-        ],
-        compiler_params=pltpu.CompilerParams(vmem_limit_bytes=24 * 2**20),
-        name="prepare",
-    )(odd, halo, gram, like)
-
-
 def transports_scaled(kernel_ref, weights, mass_ref, use):
     regions = range(kernel_ref.shape[0])
     members = kernel_ref.shape[-1]
@@ -453,11 +410,13 @@
     return jnp.concatenate(parts, axis=2).astype(jnp.bfloat16)
 
 
-def finish_kernel(count, scale, *refs):
-    state_hbm_ref, gram_hbm_ref, kernel_ref, mass_ref, like_ref, sums_ref = refs[:6]
-    out_ref, result_ref, state_ref, gram_ref, out_sems, state_sems, sem = refs[6:]
-    pairs = kernel_ref.shape[0] // PAIR
+def analyse_kernel(count, scale, *refs):
+    odd_ref, halo_ref, old_ref, state_hbm_ref, like_ref, sums_ref, out_ref = refs[:7]
+    gram_ref, kernel_ref, mass_ref, result_ref, state_ref, out_sems, state_sems = refs[7:]
+    regions, members, _ = gram_ref.shape
+    pairs = regions // PAIR
     size = PAIR * TILE
+    lat = regions * REGION
     fetches = slab_copies(state_hbm_ref, state_ref, state_sems)
     for copy in fetches:
         copy.start()
@@ -468,16 +427,25 @@
             result_ref.at[pair], out_ref.at[:, :, rows, :], out_sems.at[pair]
         )
 
-    total = jnp.sum(sums_ref[...], axis=0, keepdims=True)[:, 0:1]
-    like = -0.5 * (count / total) * like_ref[...]
-    logw = (like - jnp.log(jnp.sum(jnp.exp(like), axis=1, keepdims=True))) * LOG2E
+    misfit = like_ref[...] + like_rows(halo_ref[halo_ref.shape[0] - 4 * TILE :, :])
+    misfit = misfit - jnp.min(misfit, axis=1, keepdims=True)
+    factor = (-0.5 * LOG2E * count) / jnp.sum(sums_ref[...], axis=0, keepdims=True)
+    like = misfit * jnp.concatenate([factor] * (members // 128), axis=1)
+    weights = jnp.exp2(like + MASS)
+    norm = jnp.sum(weights, axis=1, keepdims=True) * 2.0**-MASS
+    weights = weights / norm
+
+    planes = halo_ref.shape[0] // lat
+    halo = [w for w in halo_weights(odd_ref[0] == 0) for _ in range(planes // HALO)]
+    slabs = [slab_of(halo_ref, lat, at) for at in range(lat // size)]
+    add_grams(slabs, halo, old_ref, gram_ref)
+    kernel_matrices(gram_ref, kernel_ref, mass_ref, scale)
 
     def use(pair, moves):
         fetches[pair].wait()
         result_ref[pair] = transform(state_ref, pair, moves)
         send(pair).start()
 
-    weights = jnp.exp2(logw + MASS)
     row, col, most = transports_scaled(kernel_ref, weights, mass_ref, use)
     sound = (row >= 2.0**-24) & (col >= 2.0**-30) & (most <= 2.0**30) & (row * col >= 2.0**-34)
     for pair in range(pairs):
@@ -485,45 +453,46 @@
 
     @pl.when(jnp.logical_not(sound))
     def _():
+        logw = like - jnp.log(norm) * LOG2E
         for pair in range(pairs):
-            again = []
-            for region in range(pair * PAIR, (pair + 1) * PAIR):
-                copy = pltpu.make_async_copy(gram_hbm_ref.at[region], gram_ref, sem)
-                copy.start()
-                copy.wait()
-                again.append(transport_logs(gram_ref[...], logw[region : region + 1], scale))
+            again = [
+                transport_logs(gram_ref[region], logw[region : region + 1], scale)
+                for region in range(pair * PAIR, (pair + 1) * PAIR)
+            ]
             result_ref[pair] = transform(state_ref, pair, again)
             send(pair).start()
             send(pair).wait()
 
 
-def finish(state, gram, kernel, mass, like, sums, count, scale):
+def analyse(odd, halo, gram, state, like, sums, count, scale):
     lon_dev, nvar, lat, members = state.shape
-    pairs = lat // (PAIR * TILE)
+    regions = lat // REGION
+    pairs = regions // PAIR
     vmem = pl.BlockSpec(memory_space=pltpu.VMEM)
-    hbm = pl.BlockSpec(memory_space=pltpu.HBM)
     return pl.pallas_call(
-        functools.partial(finish_kernel, count, scale),
-        in_specs=[hbm, hbm] + [vmem] * 4,
+        functools.partial(analyse_kernel, count, scale),
+        in_specs=[
+            pl.BlockSpec(memory_space=pltpu.SMEM),
+            vmem,
+            vmem,
+            pl.BlockSpec(memory_space=pltpu.HBM),
+            vmem,
+            vmem,
+        ],
         out_specs=pl.BlockSpec(memory_space=pl.ANY),
         out_shape=jax.ShapeDtypeStruct(state.shape, state.dtype),
         scratch_shapes=[
+            pltpu.VMEM(gram.shape, jnp.float32),
+            pltpu.VMEM(gram.shape, jnp.float32),
+            pltpu.VMEM((regions, 1, members), jnp.float32),
             pltpu.VMEM((pairs, lon_dev, nvar, PAIR * TILE, members), state.dtype),
             pltpu.VMEM(state.shape, state.dtype),
-            pltpu.VMEM((members, members), jnp.float32),
             pltpu.SemaphoreType.DMA((pairs,)),
             pltpu.SemaphoreType.DMA((pairs,)),
-            pltpu.SemaphoreType.DMA,
         ],
         compiler_params=pltpu.CompilerParams(vmem_limit_bytes=24 * 2**20),
-        name="finish",
-    )(
-        *[pltpu.with_memory_space_constraint(x, pltpu.HBM) for x in (state, gram)],
-        kernel,
-        mass,
-        like,
-        sums,
-    )
+        name="analyse",
+    )(odd, halo, gram, pltpu.with_memory_space_constraint(state, pltpu.HBM), like, sums)
 
 
 def on_device(state, obs_index, obs_value, obs_var):
@@ -549,9 +518,8 @@
     line = [1.0 - max(0, HALO - p, p - (HALO + REGION - 1)) / (HALO + 1) for p in offsets]
     scale = LOG2E / EPS / (nvar * sum(line) ** 2)
     gram, like = own_gram(odd, state, near, own_like)
-    gram, kernel, mass, like = prepare(odd, far, gram, like, scale)
     nobs = float(obs_index.shape[0] * count)
-    return finish(state, gram, kernel, mass, like, sums, nobs, scale)
+    return analyse(odd, far, gram, state, like, sums, nobs, scale)
 
 
 def solution(mesh):

time: 40.2 us -> 32.3 us (0.80)
  Pallas kernels: 26.4 us -> 18.6 us
    pallas_call x2 -> x1, Pallas kernels: 22.4 us -> 13.7 us  [analyse(): pl.pallas_call(functools.partial(analyse_kernel, count, scale), in_specs=...]
    pallas_call x1, Pallas kernels: 1.65 us -> 2.45 us  [observe(): pl.pallas_call(observe_kernel, in_specs=[pl.BlockSpec(memory_space=pltpu....]
  transfers between devices with their start and end apart: 3 -> 3, of which waited for: 1 -> 2; matrix products, arithmetic and copies ran while one was open for 2% -> 2% of each run, Pallas kernels for 10% -> 8%
where the time goes in v17:
time: 32.3 us; the launch traced here: 32.1 us
  Pallas kernels  18.6 us (58%)
  starting transfers between devices  8.94 us (28%)
  waiting for transfers between devices  3.91 us (12%)
  local copies, waits for them, and re-layouts  0.6 us (2%)
    pallas_call x1, Pallas kernels, analyse(): pl.pallas_call(functools.partial(analyse_kernel, count, scale), in_specs=...  13.7 us
    all_to_all x1, starting transfers between devices, on_device(): lax.all_to_all(jnp.broadcast_to(part, (count // 2, 128)), 'lon', 0, 0, ax...  6.17 us
    ppermute x1, waiting for transfers between devices, on_device(): far = lax.ppermute(for_far, 'lon', far_pairs)  3.85 us
    ppermute x1, starting transfers between devices, on_device(): far = lax.ppermute(for_far, 'lon', far_pairs)  2.65 us
    pallas_call x1, Pallas kernels, observe(): pl.pallas_call(observe_kernel, in_specs=[pl.BlockSpec(memory_space=pltpu....  2.45 us
    pallas_call x1, Pallas kernels, own_gram(): pl.pallas_call(own_gram_kernel, in_specs=[pl.BlockSpec(memory_space=pltpu...  2.44 us
  transfers between devices with their start and end apart: 3, of which 2 were waited for; matrix products, arithmetic and copies ran while one was open for 2% of the time, Pallas kernels for 8%

profile of v17, /device:TPU:1, one launch (start us, length us, event | category | flops | bytes accessed | tf_op | source)
XLA Modules:
  0.0 32.1 jit_solution(10528940933506979931)
XLA Ops:
  0.0 2.4 %observe.1 = (f32[8,256]{1,0:T(8,128)S(1)}, bf16[1056,256]{1,0:T(8,128)(2,1)S(1)}, bf16[1056,256]{1,0:T(8,128)(2,1)}, f32[8,128]{1,0:T(8,128)S(1)}) custom-call(s32[1]{0:T(128)} %bitcast.refs_0_.odd_ref, bf16[8,4,64,256]{3,2,1,0:T(8,128)(2,1)} %refs_3_.1, bf16[2048,256]{1,0:T(8,128)(2,1)} %bitcast.9, s32[1,256]{1,0:T(1,128)} %bitcast.10, f32[1,256]{1,0:T(1,128)} %bitcast.11, ...), custom_call_target="tpu_custom_call" | custom-call | tf_op jit(solution)/shard_map/observe/pallas_call | solution.py:135
  2.5 0.1 collective-permute-start.1
  2.6 2.7 %collective-permute-start = (bf16[1056,256]{1,0:T(8,128)(2,1)}, bf16[1056,256]{1,0:T(8,128)(2,1)S(1)}, u32[]{:S(2)}, u32[]{:S(2)}) collective-permute-start(bf16[1056,256]{1,0:T(8,128)(2,1)} %get-tuple-element.11), channel_id=1, source_target_pairs={{0,15},{1,2},{2,1},{3,4},{4,3},{5,6},{6,5},{7,8},{8,7},{9,10},{10,... | collective-permute-start | bytes 1622024 | tf_op jit(solution)/shard_map/ppermute | solution.py:505
  5.2 0.0 collective-permute-done.1.near_ref
  5.3 0.6 %broadcast_in_dim.15 = f32[8,1,128]{2,1,0:T(1,128)} broadcast(f32[128]{0:T(128)S(1)} %bitcast_add_fusion), dimensions={2} | broadcast | bytes 4608 | tf_op jit(solution)/shard_map/broadcast_in_dim | solution.py:510
  5.9 6.2 %all-to-all-start = ((f32[8,1,128]{2,1,0:T(1,128)}), f32[8,1,128]{2,1,0:T(1,128)S(1)}, u32[]{:S(2)}, u32[]{:S(2)}) async-start(f32[8,1,128]{2,1,0:T(1,128)} %broadcast_in_dim.15), calls=%async_computation | async-start | bytes 8192 | tf_op jit(solution)/shard_map/all_to_all | solution.py:509
  12.0 2.4 %own_gram.1 = (f32[8,256,256]{2,1,0:T(8,128)S(1)}, f32[8,256]{1,0:T(8,128)S(1)}) custom-call(s32[1]{0:T(128)} %bitcast.refs_0_.odd_ref, bf16[8,4,64,256]{3,2,1,0:T(8,128)(2,1)} %refs_3_.1, bf16[1056,256]{1,0:T(8,128)(2,1)S(1)} %collective-permute-done.1.near_ref, f32[8,256]{1,0:T(8,128)S(1)} %get-tuple-element.13.own_ref), custom_call_target="tpu_custom_call" | custom-call | tf_op jit(solution)/shard_map/own_gram/pallas_call | solution.py:257
  14.5 3.8 %collective-permute-done.refs_1_ = bf16[1056,256]{1,0:T(8,128)(2,1)S(1)} collective-permute-done((bf16[1056,256]{1,0:T(8,128)(2,1)}, bf16[1056,256]{1,0:T(8,128)(2,1)S(1)}, u32[]{:S(2)}, u32[]{:S(2)}) %collective-permute-start) | collective-permute-done | bytes 540704 | tf_op jit(solution)/shard_map/ppermute | solution.py:505
  18.3 0.1 all-to-all-done
  18.4 13.7 %analyse.1 = bf16[8,4,64,256]{3,2,1,0:T(8,128)(2,1)} custom-call(s32[1]{0:T(128)} %bitcast.refs_0_.odd_ref, bf16[1056,256]{1,0:T(8,128)(2,1)S(1)} %collective-permute-done.refs_1_, f32[8,256,256]{2,1,0:T(8,128)S(1)} %get-tuple-element.14.refs_2_, bf16[8,4,64,256]{3,2,1,0:T(8,128)(2,1)} %refs_3_.1, f32[8,256]{1,0:T(8,128)S(1)} %get-tuple-element.15.refs_4_, ...), custom_call_target="tpu_custom_call" | custom-call | tf_op jit(solution)/shard_map/analyse/pallas_call | solution.py:472
  (2 shorter events, 0.0 us)
Async XLA Ops:
  2.5 2.8 %collective-permute-start.1 = (bf16[1056,256]{1,0:T(8,128)(2,1)S(1)}, bf16[1056,256]{1,0:T(8,128)(2,1)S(1)}, u32[]{:S(2)}, u32[]{:S(2)}) collective-permute-start(bf16[1056,256]{1,0:T(8,128)(2,1)S(1)} %get-tuple-element.12), channel_id=1, source_target_pairs={{0,1},{1,0},{2,3},{3,2},{4,5},{5,4},{6,7},{7,6},{8,9},{9,8},{10,11... | collective-permute-start | bytes 1622024 | tf_op jit(solution)/shard_map/ppermute | solution.py:506
  2.6 15.7 %collective-permute-start = (bf16[1056,256]{1,0:T(8,128)(2,1)}, bf16[1056,256]{1,0:T(8,128)(2,1)S(1)}, u32[]{:S(2)}, u32[]{:S(2)}) collective-permute-start(bf16[1056,256]{1,0:T(8,128)(2,1)} %get-tuple-element.11), channel_id=1, source_target_pairs={{0,15},{1,2},{2,1},{3,4},{4,3},{5,6},{6,5},{7,8},{8,7},{9,10},{10,... | collective-permute-start | bytes 1622024 | tf_op jit(solution)/shard_map/ppermute | solution.py:505
  5.9 12.5 %all-to-all-start = ((f32[8,1,128]{2,1,0:T(1,128)}), f32[8,1,128]{2,1,0:T(1,128)S(1)}, u32[]{:S(2)}, u32[]{:S(2)}) async-start(f32[8,1,128]{2,1,0:T(1,128)} %broadcast_in_dim.15), calls=%async_computation | async-start | bytes 8192 | tf_op jit(solution)/shard_map/all_to_all | solution.py:509

commit v18 on v17

--- a/solution.py
+++ b/solution.py
@@ -213,8 +213,9 @@
 
 
 def own_gram_kernel(odd_ref, state_hbm_ref, near_ref, own_ref, *refs):
-    gram_ref, like_ref, state_ref, sems = refs
+    first_ref, last_hbm_ref, like_ref, state_ref, last_ref, sems, last_sems = refs
     lon_dev, nvar, lat, members = state_ref.shape
+    kept = first_ref.shape[0]
     steps = lat // (PAIR * TILE)
     copies = slab_copies(state_hbm_ref, state_ref, sems)
     for copy in copies:
@@ -232,10 +233,23 @@
     for copy in copies:
         copy.wait()
     slabs = [load(step) for step in range(steps)]
-    add_grams(slabs, weights, None, gram_ref)
-
-
-def add_grams(slabs, weights, old_ref, new_ref):
+
+    def put(region, gram):
+        if region < kept:
+            first_ref[region] = gram
+        else:
+            last_ref[region - kept] = gram
+            keep(region - kept).start()
+
+    def keep(at):
+        return pltpu.make_async_copy(last_ref.at[at], last_hbm_ref.at[at], last_sems.at[at])
+
+    add_grams(slabs, weights, put)
+    for at in range(last_ref.shape[0]):
+        keep(at).wait()
+
+
+def add_grams(slabs, weights, put):
     none = jnp.zeros_like(slabs[0][:, :TILE])
     tiles = [none]
     for slab in slabs:
@@ -247,12 +261,12 @@
         window = slice(pair * PAIR, pair * PAIR + PAIR + 2)
         grams = gram_of(tiles[window], turned[window], weights)
         for at, gram in enumerate(grams):
-            region = pair * PAIR + at
-            new_ref[region] = gram if old_ref is None else old_ref[region] + gram
+            put(pair * PAIR + at, gram)
 
 
 def own_gram(odd, state, near, own):
     _, _, lat, members = state.shape
+    half = lat // REGION // 2
     vmem = pl.BlockSpec(memory_space=pltpu.VMEM)
     return pl.pallas_call(
         own_gram_kernel,
@@ -262,14 +276,17 @@
             vmem,
             vmem,
         ],
-        out_specs=[vmem] * 2,
+        out_specs=[vmem, pl.BlockSpec(memory_space=pltpu.HBM), vmem],
         out_shape=[
-            jax.ShapeDtypeStruct((lat // REGION, members, members), jnp.float32),
+            jax.ShapeDtypeStruct((half, members, members), jnp.float32),
+            pltpu.HBM((half, members, members), jnp.float32),
             jax.ShapeDtypeStruct(own.shape, jnp.float32),
         ],
         scratch_shapes=[
             pltpu.VMEM(state.shape, state.dtype),
+            pltpu.VMEM((half, members, members), jnp.float32),
             pltpu.SemaphoreType.DMA((lat // (PAIR * TILE),)),
+            pltpu.SemaphoreType.DMA((half,)),
         ],
         compiler_params=pltpu.CompilerParams(vmem_limit_bytes=24 * 2**20),
         name="own_gram",
@@ -411,8 +428,16 @@
 
 
 def analyse_kernel(count, scale, *refs):
-    odd_ref, halo_ref, old_ref, state_hbm_ref, like_ref, sums_ref, out_ref = refs[:7]
-    gram_ref, kernel_ref, mass_ref, result_ref, state_ref, out_sems, state_sems = refs[7:]
+    odd_ref, halo_ref, first_ref, last_hbm_ref, state_hbm_ref, like_ref, sums_ref = refs[:7]
+    out_ref, gram_ref, kernel_ref, mass_ref, result_ref, state_ref, last_ref = refs[7:14]
+    out_sems, state_sems, last_sems = refs[14:]
+    kept = first_ref.shape[0]
+    olds = [
+        pltpu.make_async_copy(last_hbm_ref.at[at], last_ref.at[at], last_sems.at[at])
+        for at in range(last_ref.shape[0])
+    ]
+    for copy in olds:
+        copy.start()
     regions, members, _ = gram_ref.shape
     pairs = regions // PAIR
     size = PAIR * TILE
@@ -438,7 +463,15 @@
     planes = halo_ref.shape[0] // lat
     halo = [w for w in halo_weights(odd_ref[0] == 0) for _ in range(planes // HALO)]
     slabs = [slab_of(halo_ref, lat, at) for at in range(lat // size)]
-    add_grams(slabs, halo, old_ref, gram_ref)
+
+    def put(region, gram):
+        if region < kept:
+            gram_ref[region] = first_ref[region] + gram
+        else:
+            olds[region - kept].wait()
+            gram_ref[region] = last_ref[region - kept] + gram
+
+    add_grams(slabs, halo, put)
     kernel_matrices(gram_ref, kernel_ref, mass_ref, scale)
 
     def use(pair, moves):
@@ -464,7 +497,7 @@
             send(pair).wait()
 
 
-def analyse(odd, halo, gram, state, like, sums, count, scale):
+def analyse(odd, halo, first, last, state, like, sums, count, scale):
     lon_dev, nvar, lat, members = state.shape
     regions = lat // REGION
     pairs = regions // PAIR
@@ -476,23 +509,33 @@
             vmem,
             vmem,
             pl.BlockSpec(memory_space=pltpu.HBM),
+            pl.BlockSpec(memory_space=pltpu.HBM),
             vmem,
             vmem,
         ],
         out_specs=pl.BlockSpec(memory_space=pl.ANY),
         out_shape=jax.ShapeDtypeStruct(state.shape, state.dtype),
         scratch_shapes=[
-            pltpu.VMEM(gram.shape, jnp.float32),
-            pltpu.VMEM(gram.shape, jnp.float32),
+            pltpu.VMEM((regions, members, members), jnp.float32),
+            pltpu.VMEM((regions, members, members), jnp.float32),
             pltpu.VMEM((regions, 1, members), jnp.float32),
             pltpu.VMEM((pairs, lon_dev, nvar, PAIR * TILE, members), state.dtype),
             pltpu.VMEM(state.shape, state.dtype),
+            pltpu.VMEM(last.shape, jnp.float32),
             pltpu.SemaphoreType.DMA((pairs,)),
             pltpu.SemaphoreType.DMA((pairs,)),
+            pltpu.SemaphoreType.DMA((last.shape[0],)),
         ],
         compiler_params=pltpu.CompilerParams(vmem_limit_bytes=24 * 2**20),
         name="analyse",
-    )(odd, halo, gram, pltpu.with_memory_space_constraint(state, pltpu.HBM), like, sums)
+    )(
+        odd,
+        halo,
+        first,
+        *[pltpu.with_memory_space_constraint(x, pltpu.HBM) for x in (last, state)],
+        like,
+        sums,
+    )
 
 
 def on_device(state, obs_index, obs_value, obs_var):
@@ -517,9 +560,9 @@
     offsets = range(REGION + 2 * HALO)
     line = [1.0 - max(0, HALO - p, p - (HALO + REGION - 1)) / (HALO + 1) for p in offsets]
     scale = LOG2E / EPS / (nvar * sum(line) ** 2)
-    gram, like = own_gram(odd, state, near, own_like)
+    first, last, like = own_gram(odd, state, near, own_like)
     nobs = float(obs_index.shape[0] * count)
-    return analyse(odd, far, gram, state, like, sums, nobs, scale)
+    return analyse(odd, far, first, last, state, like, sums, nobs, scale)
 
 
 def solution(mesh):

time: 32.3 us -> 32.8 us (1.015)
  Pallas kernels: 18.6 us -> 19.8 us
  waiting for transfers between devices: 3.91 us -> 2.96 us
    pallas_call x1, Pallas kernels: 13.7 us -> 15 us  [analyse(): pl.pallas_call(functools.partial(analyse_kernel, count, scale), in_specs=...]
    ppermute x1, waiting for transfers between devices: 3.85 us -> 2.9 us  [on_device(): far = lax.ppermute(for_far, 'lon', far_pairs)]
    pallas_call x1, Pallas kernels: 2.45 us -> 1.65 us  [observe(): pl.pallas_call(observe_kernel, in_specs=[pl.BlockSpec(memory_space=pltpu....]
    pallas_call x1, Pallas kernels: 2.44 us -> 3.17 us  [own_gram(): pl.pallas_call(own_gram_kernel, in_specs=[pl.BlockSpec(memory_space=pltpu...]
  transfers between devices with their start and end apart: 3 -> 3, of which waited for: 2 -> 2; matrix products, arithmetic and copies ran while one was open for 2% -> 2% of each run, Pallas kernels for 8% -> 10%
where the time goes in v18:
time: 32.8 us; the launch traced here: 32.4 us
  Pallas kernels  19.8 us (60%)
  starting transfers between devices  8.94 us (27%)
  waiting for transfers between devices  2.96 us (9%)
  local copies, waits for them, and re-layouts  0.6 us (2%)
    pallas_call x1, Pallas kernels, analyse(): pl.pallas_call(functools.partial(analyse_kernel, count, scale), in_specs=...  15 us
    all_to_all x1, starting transfers between devices, on_device(): lax.all_to_all(jnp.broadcast_to(part, (count // 2, 128)), 'lon', 0, 0, ax...  6.17 us
    pallas_call x1, Pallas kernels, own_gram(): pl.pallas_call(own_gram_kernel, in_specs=[pl.BlockSpec(memory_space=pltpu...  3.17 us
    ppermute x1, waiting for transfers between devices, on_device(): far = lax.ppermute(for_far, 'lon', far_pairs)  2.9 us
    ppermute x1, starting transfers between devices, on_device(): far = lax.ppermute(for_far, 'lon', far_pairs)  2.65 us
    pallas_call x1, Pallas kernels, observe(): pl.pallas_call(observe_kernel, in_specs=[pl.BlockSpec(memory_space=pltpu....  1.65 us
  transfers between devices with their start and end apart: 3, of which 2 were waited for; matrix products, arithmetic and copies ran while one was open for 2% of the time, Pallas kernels for 10%

profile of v18, /device:TPU:1, one launch (start us, length us, event | category | flops | bytes accessed | tf_op | source)
XLA Modules:
  0.0 32.4 jit_solution(13961752398941905642)
XLA Ops:
  0.0 1.7 %observe.1 = (f32[8,256]{1,0:T(8,128)S(1)}, bf16[1056,256]{1,0:T(8,128)(2,1)S(1)}, bf16[1056,256]{1,0:T(8,128)(2,1)S(1)}, f32[8,128]{1,0:T(8,128)S(1)}) custom-call(s32[1]{0:T(128)} %bitcast.refs_0_.odd_ref, bf16[8,4,64,256]{3,2,1,0:T(8,128)(2,1)} %refs_4_.1, bf16[2048,256]{1,0:T(8,128)(2,1)} %bitcast.9, s32[1,256]{1,0:T(1,128)} %bitcast.10, ...), custom_call_target="tpu_custom_call" | custom-call | tf_op jit(solution)/shard_map/observe/pallas_call | solution.py:135
  1.7 0.1 collective-permute-start.1
  1.8 2.7 %collective-permute-start = (bf16[1056,256]{1,0:T(8,128)(2,1)S(1)}, bf16[1056,256]{1,0:T(8,128)(2,1)S(1)}, u32[]{:S(2)}, u32[]{:S(2)}) collective-permute-start(bf16[1056,256]{1,0:T(8,128)(2,1)S(1)} %get-tuple-element.12), channel_id=1, source_target_pairs={{0,15},{1,2},{2,1},{3,4},{4,3},{5,6},{6,5},{7,8},{8,7},{9,10},{10,... | collective-permute-start | bytes 1622024 | tf_op jit(solution)/shard_map/ppermute | solution.py:548
  4.4 0.0 collective-permute-done.1.near_ref
  4.5 0.6 %broadcast_in_dim.15 = f32[8,1,128]{2,1,0:T(1,128)} broadcast(f32[128]{0:T(128)S(1)} %bitcast_add_fusion), dimensions={2} | broadcast | bytes 4608 | tf_op jit(solution)/shard_map/broadcast_in_dim | solution.py:553
  5.1 6.2 %all-to-all-start = ((f32[8,1,128]{2,1,0:T(1,128)}), f32[8,1,128]{2,1,0:T(1,128)S(1)}, u32[]{:S(2)}, u32[]{:S(2)}) async-start(f32[8,1,128]{2,1,0:T(1,128)} %broadcast_in_dim.15), calls=%async_computation | async-start | bytes 8192 | tf_op jit(solution)/shard_map/all_to_all | solution.py:552
  11.2 3.2 %own_gram.1 = (f32[4,256,256]{2,1,0:T(8,128)S(1)}, f32[4,256,256]{2,1,0:T(8,128)}, f32[8,256]{1,0:T(8,128)S(1)}) custom-call(s32[1]{0:T(128)} %bitcast.refs_0_.odd_ref, bf16[8,4,64,256]{3,2,1,0:T(8,128)(2,1)} %refs_4_.1, bf16[1056,256]{1,0:T(8,128)(2,1)S(1)} %collective-permute-done.1.near_ref, f32[8,256]{1,0:T(8,128)S(1)} %get-tuple-element.14.own_ref), custom_call_target="tpu_custom_call" | custom-call | tf_op jit(solution)/shard_map/own_gram/pallas_call | solution.py:271
  14.4 2.9 %collective-permute-done.refs_1_ = bf16[1056,256]{1,0:T(8,128)(2,1)S(1)} collective-permute-done((bf16[1056,256]{1,0:T(8,128)(2,1)S(1)}, bf16[1056,256]{1,0:T(8,128)(2,1)S(1)}, u32[]{:S(2)}, u32[]{:S(2)}) %collective-permute-start) | collective-permute-done | bytes 540704 | tf_op jit(solution)/shard_map/ppermute | solution.py:548
  17.3 0.1 all-to-all-done
  17.4 15.0 %analyse.1 = bf16[8,4,64,256]{3,2,1,0:T(8,128)(2,1)} custom-call(s32[1]{0:T(128)} %bitcast.refs_0_.odd_ref, bf16[1056,256]{1,0:T(8,128)(2,1)S(1)} %collective-permute-done.refs_1_, f32[4,256,256]{2,1,0:T(8,128)S(1)} %get-tuple-element.15.refs_2_, f32[4,256,256]{2,1,0:T(8,128)} %get-tuple-element.16.refs_3_, bf16[8,4,64,256]{3,2,1,0:T(8,128)(2,1)} %refs_4_.1, ...), custom_call_target="tpu_custom_call" | custom-call | tf_op jit(solution)/shard_map/analyse/pallas_call | solution.py:505
  (2 shorter events, 0.0 us)
Async XLA Ops:
  1.7 2.8 %collective-permute-start.1 = (bf16[1056,256]{1,0:T(8,128)(2,1)S(1)}, bf16[1056,256]{1,0:T(8,128)(2,1)S(1)}, u32[]{:S(2)}, u32[]{:S(2)}) collective-permute-start(bf16[1056,256]{1,0:T(8,128)(2,1)S(1)} %get-tuple-element.13), channel_id=1, source_target_pairs={{0,1},{1,0},{2,3},{3,2},{4,5},{5,4},{6,7},{7,6},{8,9},{9,8},{10,11... | collective-permute-start | bytes 1622024 | tf_op jit(solution)/shard_map/ppermute | solution.py:549
  1.8 15.5 %collective-permute-start = (bf16[1056,256]{1,0:T(8,128)(2,1)S(1)}, bf16[1056,256]{1,0:T(8,128)(2,1)S(1)}, u32[]{:S(2)}, u32[]{:S(2)}) collective-permute-start(bf16[1056,256]{1,0:T(8,128)(2,1)S(1)} %get-tuple-element.12), channel_id=1, source_target_pairs={{0,15},{1,2},{2,1},{3,4},{4,3},{5,6},{6,5},{7,8},{8,7},{9,10},{10,... | collective-permute-start | bytes 1622024 | tf_op jit(solution)/shard_map/ppermute | solution.py:548
  5.1 12.3 %all-to-all-start = ((f32[8,1,128]{2,1,0:T(1,128)}), f32[8,1,128]{2,1,0:T(1,128)S(1)}, u32[]{:S(2)}, u32[]{:S(2)}) async-start(f32[8,1,128]{2,1,0:T(1,128)} %broadcast_in_dim.15), calls=%async_computation | async-start | bytes 8192 | tf_op jit(solution)/shard_map/all_to_all | solution.py:552

commit v19 on v18

--- a/solution.py
+++ b/solution.py
@@ -213,7 +213,7 @@
 
 
 def own_gram_kernel(odd_ref, state_hbm_ref, near_ref, own_ref, *refs):
-    first_ref, last_hbm_ref, like_ref, state_ref, last_ref, sems, last_sems = refs
+    first_ref, last_hbm_ref, like_ref, state_ref, last_ref, sems, last_sem = refs
     lon_dev, nvar, lat, members = state_ref.shape
     kept = first_ref.shape[0]
     steps = lat // (PAIR * TILE)
@@ -239,14 +239,11 @@
             first_ref[region] = gram
         else:
             last_ref[region - kept] = gram
-            keep(region - kept).start()
-
-    def keep(at):
-        return pltpu.make_async_copy(last_ref.at[at], last_hbm_ref.at[at], last_sems.at[at])
 
     add_grams(slabs, weights, put)
-    for at in range(last_ref.shape[0]):
-        keep(at).wait()
+    keep = pltpu.make_async_copy(last_ref, last_hbm_ref, last_sem)
+    keep.start()
+    keep.wait()
 
 
 def add_grams(slabs, weights, put):
@@ -266,7 +263,7 @@
 
 def own_gram(odd, state, near, own):
     _, _, lat, members = state.shape
-    half = lat // REGION // 2
+    kept = lat // REGION - PAIR
     vmem = pl.BlockSpec(memory_space=pltpu.VMEM)
     return pl.pallas_call(
         own_gram_kernel,
@@ -278,15 +275,15 @@
         ],
         out_specs=[vmem, pl.BlockSpec(memory_space=pltpu.HBM), vmem],
         out_shape=[
-            jax.ShapeDtypeStruct((half, members, members), jnp.float32),
-            pltpu.HBM((half, members, members), jnp.float32),
+            jax.ShapeDtypeStruct((kept, members, members), jnp.float32),
+            pltpu.HBM((PAIR, members, members), jnp.float32),
             jax.ShapeDtypeStruct(own.shape, jnp.float32),
         ],
         scratch_shapes=[
             pltpu.VMEM(state.shape, state.dtype),
-            pltpu.VMEM((half, members, members), jnp.float32),
+            pltpu.VMEM((PAIR, members, members), jnp.float32),
             pltpu.SemaphoreType.DMA((lat // (PAIR * TILE),)),
-            pltpu.SemaphoreType.DMA((half,)),
+            pltpu.SemaphoreType.DMA,
         ],
         compiler_params=pltpu.CompilerParams(vmem_limit_bytes=24 * 2**20),
         name="own_gram",
@@ -314,9 +311,9 @@
     return [jnp.sum(x, axis=0, keepdims=True) for x in across], down
 
 
-def kernel_matrices(gram_ref, kernel_ref, mass_ref, scale):
+def kernel_matrices(regions, gram_ref, kernel_ref, mass_ref, scale):
     members = gram_ref.shape[-1]
-    for region in range(gram_ref.shape[0]):
+    for region in regions:
         across, down = diagonal(gram_ref, region)
         across = [0.5 * LIFT - x * scale for x in across]
         masses = [0.0 for _ in across]
@@ -430,14 +427,10 @@
 def analyse_kernel(count, scale, *refs):
     odd_ref, halo_ref, first_ref, last_hbm_ref, state_hbm_ref, like_ref, sums_ref = refs[:7]
     out_ref, gram_ref, kernel_ref, mass_ref, result_ref, state_ref, last_ref = refs[7:14]
-    out_sems, state_sems, last_sems = refs[14:]
+    out_sems, state_sems, last_sem = refs[14:]
     kept = first_ref.shape[0]
-    olds = [
-        pltpu.make_async_copy(last_hbm_ref.at[at], last_ref.at[at], last_sems.at[at])
-        for at in range(last_ref.shape[0])
-    ]
-    for copy in olds:
-        copy.start()
+    fetch_last = pltpu.make_async_copy(last_hbm_ref, last_ref, last_sem)
+    fetch_last.start()
     regions, members, _ = gram_ref.shape
     pairs = regions // PAIR
     size = PAIR * TILE
@@ -468,11 +461,13 @@
         if region < kept:
             gram_ref[region] = first_ref[region] + gram
         else:
-            olds[region - kept].wait()
+            if region == kept:
+                kernel_matrices(range(kept), gram_ref, kernel_ref, mass_ref, scale)
+                fetch_last.wait()
             gram_ref[region] = last_ref[region - kept] + gram
 
     add_grams(slabs, halo, put)
-    kernel_matrices(gram_ref, kernel_ref, mass_ref, scale)
+    kernel_matrices(range(kept, regions), gram_ref, kernel_ref, mass_ref, scale)
 
     def use(pair, moves):
         fetches[pair].wait()
@@ -524,7 +519,7 @@
             pltpu.VMEM(last.shape, jnp.float32),
             pltpu.SemaphoreType.DMA((pairs,)),
             pltpu.SemaphoreType.DMA((pairs,)),
-            pltpu.SemaphoreType.DMA((last.shape[0],)),
+            pltpu.SemaphoreType.DMA,
         ],
         compiler_params=pltpu.CompilerParams(vmem_limit_bytes=24 * 2**20),
         name="analyse",

time: 32.8 us -> 31.8 us (0.970)
  Pallas kernels: 19.8 us -> 18.9 us
    pallas_call x1, Pallas kernels: 15 us -> 14 us  [analyse(): pl.pallas_call(functools.partial(analyse_kernel, count, scale), in_specs=...]
where the time goes in v19:
time: 31.8 us; the launch traced here: 31.4 us
  Pallas kernels  18.9 us (59%)
  starting transfers between devices  8.94 us (28%)
  waiting for transfers between devices  2.9 us (9%)
  local copies, waits for them, and re-layouts  0.6 us (2%)
    pallas_call x1, Pallas kernels, analyse(): pl.pallas_call(functools.partial(analyse_kernel, count, scale), in_specs=...  14 us
    all_to_all x1, starting transfers between devices, on_device(): lax.all_to_all(jnp.broadcast_to(part, (count // 2, 128)), 'lon', 0, 0, ax...  6.17 us
    pallas_call x1, Pallas kernels, own_gram(): pl.pallas_call(own_gram_kernel, in_specs=[pl.BlockSpec(memory_space=pltpu...  3.23 us
    ppermute x1, waiting for transfers between devices, on_device(): far = lax.ppermute(for_far, 'lon', far_pairs)  2.83 us
    ppermute x1, starting transfers between devices, on_device(): far = lax.ppermute(for_far, 'lon', far_pairs)  2.65 us
    pallas_call x1, Pallas kernels, observe(): pl.pallas_call(observe_kernel, in_specs=[pl.BlockSpec(memory_space=pltpu....  1.65 us
  transfers between devices with their start and end apart: 3, of which 2 were waited for; matrix products, arithmetic and copies ran while one was open for 2% of the time, Pallas kernels for 10%

profile of v19, /device:TPU:1, one launch (start us, length us, event | category | flops | bytes accessed | tf_op | source)
XLA Modules:
  0.0 31.4 jit_solution(15660014727486634356)
XLA Ops:
  0.0 1.7 %observe.1 = (f32[8,256]{1,0:T(8,128)S(1)}, bf16[1056,256]{1,0:T(8,128)(2,1)S(1)}, bf16[1056,256]{1,0:T(8,128)(2,1)S(1)}, f32[8,128]{1,0:T(8,128)S(1)}) custom-call(s32[1]{0:T(128)} %bitcast.refs_0_.odd_ref, bf16[8,4,64,256]{3,2,1,0:T(8,128)(2,1)} %refs_4_.1, bf16[2048,256]{1,0:T(8,128)(2,1)} %bitcast.9, s32[1,256]{1,0:T(1,128)} %bitcast.10, ...), custom_call_target="tpu_custom_call" | custom-call | tf_op jit(solution)/shard_map/observe/pallas_call | solution.py:135
  1.7 0.1 collective-permute-start.1
  1.8 2.7 %collective-permute-start = (bf16[1056,256]{1,0:T(8,128)(2,1)S(1)}, bf16[1056,256]{1,0:T(8,128)(2,1)S(1)}, u32[]{:S(2)}, u32[]{:S(2)}) collective-permute-start(bf16[1056,256]{1,0:T(8,128)(2,1)S(1)} %get-tuple-element.12), channel_id=1, source_target_pairs={{0,15},{1,2},{2,1},{3,4},{4,3},{5,6},{6,5},{7,8},{8,7},{9,10},{10,... | collective-permute-start | bytes 1622024 | tf_op jit(solution)/shard_map/ppermute | solution.py:543
  4.4 0.0 collective-permute-done.1.near_ref
  4.5 0.6 %broadcast_in_dim.15 = f32[8,1,128]{2,1,0:T(1,128)} broadcast(f32[128]{0:T(128)S(1)} %bitcast_add_fusion), dimensions={2} | broadcast | bytes 4608 | tf_op jit(solution)/shard_map/broadcast_in_dim | solution.py:548
  5.1 6.2 %all-to-all-start = ((f32[8,1,128]{2,1,0:T(1,128)}), f32[8,1,128]{2,1,0:T(1,128)S(1)}, u32[]{:S(2)}, u32[]{:S(2)}) async-start(f32[8,1,128]{2,1,0:T(1,128)} %broadcast_in_dim.15), calls=%async_computation | async-start | bytes 8192 | tf_op jit(solution)/shard_map/all_to_all | solution.py:547
  11.2 3.2 %own_gram.1 = (f32[6,256,256]{2,1,0:T(8,128)S(1)}, f32[2,256,256]{2,1,0:T(8,128)}, f32[8,256]{1,0:T(8,128)S(1)}) custom-call(s32[1]{0:T(128)} %bitcast.refs_0_.odd_ref, bf16[8,4,64,256]{3,2,1,0:T(8,128)(2,1)} %refs_4_.1, bf16[1056,256]{1,0:T(8,128)(2,1)S(1)} %collective-permute-done.1.near_ref, f32[8,256]{1,0:T(8,128)S(1)} %get-tuple-element.14.own_ref), custom_call_target="tpu_custom_call" | custom-call | tf_op jit(solution)/shard_map/own_gram/pallas_call | solution.py:268
  14.5 2.8 %collective-permute-done.refs_1_ = bf16[1056,256]{1,0:T(8,128)(2,1)S(1)} collective-permute-done((bf16[1056,256]{1,0:T(8,128)(2,1)S(1)}, bf16[1056,256]{1,0:T(8,128)(2,1)S(1)}, u32[]{:S(2)}, u32[]{:S(2)}) %collective-permute-start) | collective-permute-done | bytes 540704 | tf_op jit(solution)/shard_map/ppermute | solution.py:543
  17.3 0.1 all-to-all-done
  17.4 14.0 %analyse.1 = bf16[8,4,64,256]{3,2,1,0:T(8,128)(2,1)} custom-call(s32[1]{0:T(128)} %bitcast.refs_0_.odd_ref, bf16[1056,256]{1,0:T(8,128)(2,1)S(1)} %collective-permute-done.refs_1_, f32[6,256,256]{2,1,0:T(8,128)S(1)} %get-tuple-element.15.refs_2_, f32[2,256,256]{2,1,0:T(8,128)} %get-tuple-element.16.refs_3_, bf16[8,4,64,256]{3,2,1,0:T(8,128)(2,1)} %refs_4_.1, ...), custom_call_target="tpu_custom_call" | custom-call | tf_op jit(solution)/shard_map/analyse/pallas_call | solution.py:500
  (2 shorter events, 0.0 us)
Async XLA Ops:
  1.7 2.8 %collective-permute-start.1 = (bf16[1056,256]{1,0:T(8,128)(2,1)S(1)}, bf16[1056,256]{1,0:T(8,128)(2,1)S(1)}, u32[]{:S(2)}, u32[]{:S(2)}) collective-permute-start(bf16[1056,256]{1,0:T(8,128)(2,1)S(1)} %get-tuple-element.13), channel_id=1, source_target_pairs={{0,1},{1,0},{2,3},{3,2},{4,5},{5,4},{6,7},{7,6},{8,9},{9,8},{10,11... | collective-permute-start | bytes 1622024 | tf_op jit(solution)/shard_map/ppermute | solution.py:544
  1.8 15.5 %collective-permute-start = (bf16[1056,256]{1,0:T(8,128)(2,1)S(1)}, bf16[1056,256]{1,0:T(8,128)(2,1)S(1)}, u32[]{:S(2)}, u32[]{:S(2)}) collective-permute-start(bf16[1056,256]{1,0:T(8,128)(2,1)S(1)} %get-tuple-element.12), channel_id=1, source_target_pairs={{0,15},{1,2},{2,1},{3,4},{4,3},{5,6},{6,5},{7,8},{8,7},{9,10},{10,... | collective-permute-start | bytes 1622024 | tf_op jit(solution)/shard_map/ppermute | solution.py:543
  5.1 12.3 %all-to-all-start = ((f32[8,1,128]{2,1,0:T(1,128)}), f32[8,1,128]{2,1,0:T(1,128)S(1)}, u32[]{:S(2)}, u32[]{:S(2)}) async-start(f32[8,1,128]{2,1,0:T(1,128)} %broadcast_in_dim.15), calls=%async_computation | async-start | bytes 8192 | tf_op jit(solution)/shard_map/all_to_all | solution.py:547

commit v20 on v19

--- a/solution.py
+++ b/solution.py
@@ -464,13 +464,14 @@
             if region == kept:
                 kernel_matrices(range(kept), gram_ref, kernel_ref, mass_ref, scale)
                 fetch_last.wait()
+                for copy in fetches:
+                    copy.wait()
             gram_ref[region] = last_ref[region - kept] + gram
 
     add_grams(slabs, halo, put)
     kernel_matrices(range(kept, regions), gram_ref, kernel_ref, mass_ref, scale)
 
     def use(pair, moves):
-        fetches[pair].wait()
         result_ref[pair] = transform(state_ref, pair, moves)
         send(pair).start()
 

time: 31.8 us -> 32 us (level)
  no operation moved by 1% of the time
where the time goes in v20:
time: 32 us; the launch traced here: 31.6 us
  Pallas kernels  19.1 us (60%)
  starting transfers between devices  8.94 us (28%)
  waiting for transfers between devices  2.9 us (9%)
  local copies, waits for them, and re-layouts  0.6 us (2%)
    pallas_call x1, Pallas kernels, analyse(): pl.pallas_call(functools.partial(analyse_kernel, count, scale), in_specs=...  14.2 us
    all_to_all x1, starting transfers between devices, on_device(): lax.all_to_all(jnp.broadcast_to(part, (count // 2, 128)), 'lon', 0, 0, ax...  6.17 us
    pallas_call x1, Pallas kernels, own_gram(): pl.pallas_call(own_gram_kernel, in_specs=[pl.BlockSpec(memory_space=pltpu...  3.23 us
    ppermute x1, waiting for transfers between devices, on_device(): far = lax.ppermute(for_far, 'lon', far_pairs)  2.83 us
    ppermute x1, starting transfers between devices, on_device(): far = lax.ppermute(for_far, 'lon', far_pairs)  2.65 us
    pallas_call x1, Pallas kernels, observe(): pl.pallas_call(observe_kernel, in_specs=[pl.BlockSpec(memory_space=pltpu....  1.65 us
  transfers between devices with their start and end apart: 3, of which 2 were waited for; matrix products, arithmetic and copies ran while one was open for 2% of the time, Pallas kernels for 10%

profile of v20, /device:TPU:1, one launch (start us, length us, event | category | flops | bytes accessed | tf_op | source)
XLA Modules:
  0.0 31.6 jit_solution(6708355501529483180)
XLA Ops:
  0.0 1.7 %observe.1 = (f32[8,256]{1,0:T(8,128)S(1)}, bf16[1056,256]{1,0:T(8,128)(2,1)S(1)}, bf16[1056,256]{1,0:T(8,128)(2,1)S(1)}, f32[8,128]{1,0:T(8,128)S(1)}) custom-call(s32[1]{0:T(128)} %bitcast.refs_0_.odd_ref, bf16[8,4,64,256]{3,2,1,0:T(8,128)(2,1)} %refs_4_.1, bf16[2048,256]{1,0:T(8,128)(2,1)} %bitcast.9, s32[1,256]{1,0:T(1,128)} %bitcast.10, ...), custom_call_target="tpu_custom_call" | custom-call | tf_op jit(solution)/shard_map/observe/pallas_call | solution.py:135
  1.7 0.1 collective-permute-start.1
  1.8 2.7 %collective-permute-start = (bf16[1056,256]{1,0:T(8,128)(2,1)S(1)}, bf16[1056,256]{1,0:T(8,128)(2,1)S(1)}, u32[]{:S(2)}, u32[]{:S(2)}) collective-permute-start(bf16[1056,256]{1,0:T(8,128)(2,1)S(1)} %get-tuple-element.12), channel_id=1, source_target_pairs={{0,15},{1,2},{2,1},{3,4},{4,3},{5,6},{6,5},{7,8},{8,7},{9,10},{10,... | collective-permute-start | bytes 1622024 | tf_op jit(solution)/shard_map/ppermute | solution.py:544
  4.4 0.0 collective-permute-done.1.near_ref
  4.5 0.6 %broadcast_in_dim.15 = f32[8,1,128]{2,1,0:T(1,128)} broadcast(f32[128]{0:T(128)S(1)} %bitcast_add_fusion), dimensions={2} | broadcast | bytes 4608 | tf_op jit(solution)/shard_map/broadcast_in_dim | solution.py:549
  5.1 6.2 %all-to-all-start = ((f32[8,1,128]{2,1,0:T(1,128)}), f32[8,1,128]{2,1,0:T(1,128)S(1)}, u32[]{:S(2)}, u32[]{:S(2)}) async-start(f32[8,1,128]{2,1,0:T(1,128)} %broadcast_in_dim.15), calls=%async_computation | async-start | bytes 8192 | tf_op jit(solution)/shard_map/all_to_all | solution.py:548
  11.2 3.2 %own_gram.1 = (f32[6,256,256]{2,1,0:T(8,128)S(1)}, f32[2,256,256]{2,1,0:T(8,128)}, f32[8,256]{1,0:T(8,128)S(1)}) custom-call(s32[1]{0:T(128)} %bitcast.refs_0_.odd_ref, bf16[8,4,64,256]{3,2,1,0:T(8,128)(2,1)} %refs_4_.1, bf16[1056,256]{1,0:T(8,128)(2,1)S(1)} %collective-permute-done.1.near_ref, f32[8,256]{1,0:T(8,128)S(1)} %get-tuple-element.14.own_ref), custom_call_target="tpu_custom_call" | custom-call | tf_op jit(solution)/shard_map/own_gram/pallas_call | solution.py:268
  14.5 2.8 %collective-permute-done.refs_1_ = bf16[1056,256]{1,0:T(8,128)(2,1)S(1)} collective-permute-done((bf16[1056,256]{1,0:T(8,128)(2,1)S(1)}, bf16[1056,256]{1,0:T(8,128)(2,1)S(1)}, u32[]{:S(2)}, u32[]{:S(2)}) %collective-permute-start) | collective-permute-done | bytes 540704 | tf_op jit(solution)/shard_map/ppermute | solution.py:544
  17.3 0.1 all-to-all-done
  17.4 14.2 %analyse.1 = bf16[8,4,64,256]{3,2,1,0:T(8,128)(2,1)} custom-call(s32[1]{0:T(128)} %bitcast.refs_0_.odd_ref, bf16[1056,256]{1,0:T(8,128)(2,1)S(1)} %collective-permute-done.refs_1_, f32[6,256,256]{2,1,0:T(8,128)S(1)} %get-tuple-element.15.refs_2_, f32[2,256,256]{2,1,0:T(8,128)} %get-tuple-element.16.refs_3_, bf16[8,4,64,256]{3,2,1,0:T(8,128)(2,1)} %refs_4_.1, ...), custom_call_target="tpu_custom_call" | custom-call | tf_op jit(solution)/shard_map/analyse/pallas_call | solution.py:501
  (2 shorter events, 0.0 us)
Async XLA Ops:
  1.7 2.8 %collective-permute-start.1 = (bf16[1056,256]{1,0:T(8,128)(2,1)S(1)}, bf16[1056,256]{1,0:T(8,128)(2,1)S(1)}, u32[]{:S(2)}, u32[]{:S(2)}) collective-permute-start(bf16[1056,256]{1,0:T(8,128)(2,1)S(1)} %get-tuple-element.13), channel_id=1, source_target_pairs={{0,1},{1,0},{2,3},{3,2},{4,5},{5,4},{6,7},{7,6},{8,9},{9,8},{10,11... | collective-permute-start | bytes 1622024 | tf_op jit(solution)/shard_map/ppermute | solution.py:545
  1.8 15.5 %collective-permute-start = (bf16[1056,256]{1,0:T(8,128)(2,1)S(1)}, bf16[1056,256]{1,0:T(8,128)(2,1)S(1)}, u32[]{:S(2)}, u32[]{:S(2)}) collective-permute-start(bf16[1056,256]{1,0:T(8,128)(2,1)S(1)} %get-tuple-element.12), channel_id=1, source_target_pairs={{0,15},{1,2},{2,1},{3,4},{4,3},{5,6},{6,5},{7,8},{8,7},{9,10},{10,... | collective-permute-start | bytes 1622024 | tf_op jit(solution)/shard_map/ppermute | solution.py:544
  5.1 12.3 %all-to-all-start = ((f32[8,1,128]{2,1,0:T(1,128)}), f32[8,1,128]{2,1,0:T(1,128)S(1)}, u32[]{:S(2)}, u32[]{:S(2)}) async-start(f32[8,1,128]{2,1,0:T(1,128)} %broadcast_in_dim.15), calls=%async_computation | async-start | bytes 8192 | tf_op jit(solution)/shard_map/all_to_all | solution.py:548

commit v21 on v19

--- a/solution.py
+++ b/solution.py
@@ -470,7 +470,9 @@
     kernel_matrices(range(kept, regions), gram_ref, kernel_ref, mass_ref, scale)
 
     def use(pair, moves):
-        fetches[pair].wait()
+        if pair == 0:
+            for copy in fetches:
+                copy.wait()
         result_ref[pair] = transform(state_ref, pair, moves)
         send(pair).start()
 

time: 31.8 us -> 31.3 us (0.984)
  Pallas kernels: 18.9 us -> 18.4 us
    pallas_call x1, Pallas kernels: 14 us -> 13.5 us  [analyse(): pl.pallas_call(functools.partial(analyse_kernel, count, scale), in_specs=...]
where the time goes in v21:
time: 31.3 us; the launch traced here: 30.9 us
  Pallas kernels  18.4 us (59%)
  starting transfers between devices  8.94 us (29%)
  waiting for transfers between devices  2.9 us (9%)
  local copies, waits for them, and re-layouts  0.6 us (2%)
    pallas_call x1, Pallas kernels, analyse(): pl.pallas_call(functools.partial(analyse_kernel, count, scale), in_specs=...  13.5 us
    all_to_all x1, starting transfers between devices, on_device(): lax.all_to_all(jnp.broadcast_to(part, (count // 2, 128)), 'lon', 0, 0, ax...  6.17 us
    pallas_call x1, Pallas kernels, own_gram(): pl.pallas_call(own_gram_kernel, in_specs=[pl.BlockSpec(memory_space=pltpu...  3.23 us
    ppermute x1, waiting for transfers between devices, on_device(): far = lax.ppermute(for_far, 'lon', far_pairs)  2.83 us
    ppermute x1, starting transfers between devices, on_device(): far = lax.ppermute(for_far, 'lon', far_pairs)  2.65 us
    pallas_call x1, Pallas kernels, observe(): pl.pallas_call(observe_kernel, in_specs=[pl.BlockSpec(memory_space=pltpu....  1.65 us
  transfers between devices with their start and end apart: 3, of which 2 were waited for; matrix products, arithmetic and copies ran while one was open for 2% of the time, Pallas kernels for 10%

profile of v21, /device:TPU:1, one launch (start us, length us, event | category | flops | bytes accessed | tf_op | source)
XLA Modules:
  0.0 30.9 jit_solution(12753964256415799536)
XLA Ops:
  0.0 1.7 %observe.1 = (f32[8,256]{1,0:T(8,128)S(1)}, bf16[1056,256]{1,0:T(8,128)(2,1)S(1)}, bf16[1056,256]{1,0:T(8,128)(2,1)S(1)}, f32[8,128]{1,0:T(8,128)S(1)}) custom-call(s32[1]{0:T(128)} %bitcast.refs_0_.odd_ref, bf16[8,4,64,256]{3,2,1,0:T(8,128)(2,1)} %refs_4_.1, bf16[2048,256]{1,0:T(8,128)(2,1)} %bitcast.9, s32[1,256]{1,0:T(1,128)} %bitcast.10, ...), custom_call_target="tpu_custom_call" | custom-call | tf_op jit(solution)/shard_map/observe/pallas_call | solution.py:135
  1.7 0.1 collective-permute-start.1
  1.8 2.7 %collective-permute-start = (bf16[1056,256]{1,0:T(8,128)(2,1)S(1)}, bf16[1056,256]{1,0:T(8,128)(2,1)S(1)}, u32[]{:S(2)}, u32[]{:S(2)}) collective-permute-start(bf16[1056,256]{1,0:T(8,128)(2,1)S(1)} %get-tuple-element.12), channel_id=1, source_target_pairs={{0,15},{1,2},{2,1},{3,4},{4,3},{5,6},{6,5},{7,8},{8,7},{9,10},{10,... | collective-permute-start | bytes 1622024 | tf_op jit(solution)/shard_map/ppermute | solution.py:545
  4.4 0.0 collective-permute-done.1.near_ref
  4.5 0.6 %broadcast_in_dim.15 = f32[8,1,128]{2,1,0:T(1,128)} broadcast(f32[128]{0:T(128)S(1)} %bitcast_add_fusion), dimensions={2} | broadcast | bytes 4608 | tf_op jit(solution)/shard_map/broadcast_in_dim | solution.py:550
  5.1 6.2 %all-to-all-start = ((f32[8,1,128]{2,1,0:T(1,128)}), f32[8,1,128]{2,1,0:T(1,128)S(1)}, u32[]{:S(2)}, u32[]{:S(2)}) async-start(f32[8,1,128]{2,1,0:T(1,128)} %broadcast_in_dim.15), calls=%async_computation | async-start | bytes 8192 | tf_op jit(solution)/shard_map/all_to_all | solution.py:549
  11.2 3.2 %own_gram.1 = (f32[6,256,256]{2,1,0:T(8,128)S(1)}, f32[2,256,256]{2,1,0:T(8,128)}, f32[8,256]{1,0:T(8,128)S(1)}) custom-call(s32[1]{0:T(128)} %bitcast.refs_0_.odd_ref, bf16[8,4,64,256]{3,2,1,0:T(8,128)(2,1)} %refs_4_.1, bf16[1056,256]{1,0:T(8,128)(2,1)S(1)} %collective-permute-done.1.near_ref, f32[8,256]{1,0:T(8,128)S(1)} %get-tuple-element.14.own_ref), custom_call_target="tpu_custom_call" | custom-call | tf_op jit(solution)/shard_map/own_gram/pallas_call | solution.py:268
  14.5 2.8 %collective-permute-done.refs_1_ = bf16[1056,256]{1,0:T(8,128)(2,1)S(1)} collective-permute-done((bf16[1056,256]{1,0:T(8,128)(2,1)S(1)}, bf16[1056,256]{1,0:T(8,128)(2,1)S(1)}, u32[]{:S(2)}, u32[]{:S(2)}) %collective-permute-start) | collective-permute-done | bytes 540704 | tf_op jit(solution)/shard_map/ppermute | solution.py:545
  17.3 0.1 all-to-all-done
  17.4 13.5 %analyse.1 = bf16[8,4,64,256]{3,2,1,0:T(8,128)(2,1)} custom-call(s32[1]{0:T(128)} %bitcast.refs_0_.odd_ref, bf16[1056,256]{1,0:T(8,128)(2,1)S(1)} %collective-permute-done.refs_1_, f32[6,256,256]{2,1,0:T(8,128)S(1)} %get-tuple-element.15.refs_2_, f32[2,256,256]{2,1,0:T(8,128)} %get-tuple-element.16.refs_3_, bf16[8,4,64,256]{3,2,1,0:T(8,128)(2,1)} %refs_4_.1, ...), custom_call_target="tpu_custom_call" | custom-call | tf_op jit(solution)/shard_map/analyse/pallas_call | solution.py:502
  (2 shorter events, 0.0 us)
Async XLA Ops:
  1.7 2.8 %collective-permute-start.1 = (bf16[1056,256]{1,0:T(8,128)(2,1)S(1)}, bf16[1056,256]{1,0:T(8,128)(2,1)S(1)}, u32[]{:S(2)}, u32[]{:S(2)}) collective-permute-start(bf16[1056,256]{1,0:T(8,128)(2,1)S(1)} %get-tuple-element.13), channel_id=1, source_target_pairs={{0,1},{1,0},{2,3},{3,2},{4,5},{5,4},{6,7},{7,6},{8,9},{9,8},{10,11... | collective-permute-start | bytes 1622024 | tf_op jit(solution)/shard_map/ppermute | solution.py:546
  1.8 15.5 %collective-permute-start = (bf16[1056,256]{1,0:T(8,128)(2,1)S(1)}, bf16[1056,256]{1,0:T(8,128)(2,1)S(1)}, u32[]{:S(2)}, u32[]{:S(2)}) collective-permute-start(bf16[1056,256]{1,0:T(8,128)(2,1)S(1)} %get-tuple-element.12), channel_id=1, source_target_pairs={{0,15},{1,2},{2,1},{3,4},{4,3},{5,6},{6,5},{7,8},{8,7},{9,10},{10,... | collective-permute-start | bytes 1622024 | tf_op jit(solution)/shard_map/ppermute | solution.py:545
  5.1 12.3 %all-to-all-start = ((f32[8,1,128]{2,1,0:T(1,128)}), f32[8,1,128]{2,1,0:T(1,128)S(1)}, u32[]{:S(2)}, u32[]{:S(2)}) async-start(f32[8,1,128]{2,1,0:T(1,128)} %broadcast_in_dim.15), calls=%async_computation | async-start | bytes 8192 | tf_op jit(solution)/shard_map/all_to_all | solution.py:549

commit v22 on v21

--- a/solution.py
+++ b/solution.py
@@ -474,7 +474,9 @@
             for copy in fetches:
                 copy.wait()
         result_ref[pair] = transform(state_ref, pair, moves)
-        send(pair).start()
+        if pair % 2 or pair == pairs - 1:
+            for at in range(pair - pair % 2, pair + 1):
+                send(at).start()
 
     row, col, most = transports_scaled(kernel_ref, weights, mass_ref, use)
     sound = (row >= 2.0**-24) & (col >= 2.0**-30) & (most <= 2.0**30) & (row * col >= 2.0**-34)

time: 31.3 us -> 31.4 us (level)
  no operation moved by 1% of the time
where the time goes in v22:
time: 31.4 us; the launch traced here: 31 us
  Pallas kernels  18.5 us (59%)
  starting transfers between devices  8.94 us (28%)
  waiting for transfers between devices  2.9 us (9%)
  local copies, waits for them, and re-layouts  0.6 us (2%)
    pallas_call x1, Pallas kernels, analyse(): pl.pallas_call(functools.partial(analyse_kernel, count, scale), in_specs=...  13.6 us
    all_to_all x1, starting transfers between devices, on_device(): lax.all_to_all(jnp.broadcast_to(part, (count // 2, 128)), 'lon', 0, 0, ax...  6.17 us
    pallas_call x1, Pallas kernels, own_gram(): pl.pallas_call(own_gram_kernel, in_specs=[pl.BlockSpec(memory_space=pltpu...  3.23 us
    ppermute x1, waiting for transfers between devices, on_device(): far = lax.ppermute(for_far, 'lon', far_pairs)  2.83 us
    ppermute x1, starting transfers between devices, on_device(): far = lax.ppermute(for_far, 'lon', far_pairs)  2.65 us
    pallas_call x1, Pallas kernels, observe(): pl.pallas_call(observe_kernel, in_specs=[pl.BlockSpec(memory_space=pltpu....  1.65 us
  transfers between devices with their start and end apart: 3, of which 2 were waited for; matrix products, arithmetic and copies ran while one was open for 2% of the time, Pallas kernels for 10%

profile of v22, /device:TPU:1, one launch (start us, length us, event | category | flops | bytes accessed | tf_op | source)
XLA Modules:
  0.0 31.0 jit_solution(10365454444416910891)
XLA Ops:
  0.0 1.7 %observe.1 = (f32[8,256]{1,0:T(8,128)S(1)}, bf16[1056,256]{1,0:T(8,128)(2,1)S(1)}, bf16[1056,256]{1,0:T(8,128)(2,1)S(1)}, f32[8,128]{1,0:T(8,128)S(1)}) custom-call(s32[1]{0:T(128)} %bitcast.refs_0_.odd_ref, bf16[8,4,64,256]{3,2,1,0:T(8,128)(2,1)} %refs_4_.1, bf16[2048,256]{1,0:T(8,128)(2,1)} %bitcast.9, s32[1,256]{1,0:T(1,128)} %bitcast.10, ...), custom_call_target="tpu_custom_call" | custom-call | tf_op jit(solution)/shard_map/observe/pallas_call | solution.py:135
  1.7 0.1 collective-permute-start.1
  1.8 2.7 %collective-permute-start = (bf16[1056,256]{1,0:T(8,128)(2,1)S(1)}, bf16[1056,256]{1,0:T(8,128)(2,1)S(1)}, u32[]{:S(2)}, u32[]{:S(2)}) collective-permute-start(bf16[1056,256]{1,0:T(8,128)(2,1)S(1)} %get-tuple-element.12), channel_id=1, source_target_pairs={{0,15},{1,2},{2,1},{3,4},{4,3},{5,6},{6,5},{7,8},{8,7},{9,10},{10,... | collective-permute-start | bytes 1622024 | tf_op jit(solution)/shard_map/ppermute | solution.py:547
  4.4 0.0 collective-permute-done.1.near_ref
  4.5 0.6 %broadcast_in_dim.15 = f32[8,1,128]{2,1,0:T(1,128)} broadcast(f32[128]{0:T(128)S(1)} %bitcast_add_fusion), dimensions={2} | broadcast | bytes 4608 | tf_op jit(solution)/shard_map/broadcast_in_dim | solution.py:552
  5.1 6.2 %all-to-all-start = ((f32[8,1,128]{2,1,0:T(1,128)}), f32[8,1,128]{2,1,0:T(1,128)S(1)}, u32[]{:S(2)}, u32[]{:S(2)}) async-start(f32[8,1,128]{2,1,0:T(1,128)} %broadcast_in_dim.15), calls=%async_computation | async-start | bytes 8192 | tf_op jit(solution)/shard_map/all_to_all | solution.py:551
  11.2 3.2 %own_gram.1 = (f32[6,256,256]{2,1,0:T(8,128)S(1)}, f32[2,256,256]{2,1,0:T(8,128)}, f32[8,256]{1,0:T(8,128)S(1)}) custom-call(s32[1]{0:T(128)} %bitcast.refs_0_.odd_ref, bf16[8,4,64,256]{3,2,1,0:T(8,128)(2,1)} %refs_4_.1, bf16[1056,256]{1,0:T(8,128)(2,1)S(1)} %collective-permute-done.1.near_ref, f32[8,256]{1,0:T(8,128)S(1)} %get-tuple-element.14.own_ref), custom_call_target="tpu_custom_call" | custom-call | tf_op jit(solution)/shard_map/own_gram/pallas_call | solution.py:268
  14.5 2.8 %collective-permute-done.refs_1_ = bf16[1056,256]{1,0:T(8,128)(2,1)S(1)} collective-permute-done((bf16[1056,256]{1,0:T(8,128)(2,1)S(1)}, bf16[1056,256]{1,0:T(8,128)(2,1)S(1)}, u32[]{:S(2)}, u32[]{:S(2)}) %collective-permute-start) | collective-permute-done | bytes 540704 | tf_op jit(solution)/shard_map/ppermute | solution.py:547
  17.3 0.1 all-to-all-done
  17.4 13.6 %analyse.1 = bf16[8,4,64,256]{3,2,1,0:T(8,128)(2,1)} custom-call(s32[1]{0:T(128)} %bitcast.refs_0_.odd_ref, bf16[1056,256]{1,0:T(8,128)(2,1)S(1)} %collective-permute-done.refs_1_, f32[6,256,256]{2,1,0:T(8,128)S(1)} %get-tuple-element.15.refs_2_, f32[2,256,256]{2,1,0:T(8,128)} %get-tuple-element.16.refs_3_, bf16[8,4,64,256]{3,2,1,0:T(8,128)(2,1)} %refs_4_.1, ...), custom_call_target="tpu_custom_call" | custom-call | tf_op jit(solution)/shard_map/analyse/pallas_call | solution.py:504
  (2 shorter events, 0.0 us)
Async XLA Ops:
  1.7 2.8 %collective-permute-start.1 = (bf16[1056,256]{1,0:T(8,128)(2,1)S(1)}, bf16[1056,256]{1,0:T(8,128)(2,1)S(1)}, u32[]{:S(2)}, u32[]{:S(2)}) collective-permute-start(bf16[1056,256]{1,0:T(8,128)(2,1)S(1)} %get-tuple-element.13), channel_id=1, source_target_pairs={{0,1},{1,0},{2,3},{3,2},{4,5},{5,4},{6,7},{7,6},{8,9},{9,8},{10,11... | collective-permute-start | bytes 1622024 | tf_op jit(solution)/shard_map/ppermute | solution.py:548
  1.8 15.5 %collective-permute-start = (bf16[1056,256]{1,0:T(8,128)(2,1)S(1)}, bf16[1056,256]{1,0:T(8,128)(2,1)S(1)}, u32[]{:S(2)}, u32[]{:S(2)}) collective-permute-start(bf16[1056,256]{1,0:T(8,128)(2,1)S(1)} %get-tuple-element.12), channel_id=1, source_target_pairs={{0,15},{1,2},{2,1},{3,4},{4,3},{5,6},{6,5},{7,8},{8,7},{9,10},{10,... | collective-permute-start | bytes 1622024 | tf_op jit(solution)/shard_map/ppermute | solution.py:547
  5.1 12.3 %all-to-all-start = ((f32[8,1,128]{2,1,0:T(1,128)}), f32[8,1,128]{2,1,0:T(1,128)S(1)}, u32[]{:S(2)}, u32[]{:S(2)}) async-start(f32[8,1,128]{2,1,0:T(1,128)} %broadcast_in_dim.15), calls=%async_computation | async-start | bytes 8192 | tf_op jit(solution)/shard_map/all_to_all | solution.py:551

commit v23 on v21

--- a/solution.py
+++ b/solution.py
@@ -462,12 +462,11 @@
             gram_ref[region] = first_ref[region] + gram
         else:
             if region == kept:
-                kernel_matrices(range(kept), gram_ref, kernel_ref, mass_ref, scale)
                 fetch_last.wait()
             gram_ref[region] = last_ref[region - kept] + gram
 
     add_grams(slabs, halo, put)
-    kernel_matrices(range(kept, regions), gram_ref, kernel_ref, mass_ref, scale)
+    kernel_matrices(range(regions), gram_ref, kernel_ref, mass_ref, scale)
 
     def use(pair, moves):
         if pair == 0:

time: 31.3 us -> 31.7 us (1.013)
  Pallas kernels: 18.4 us -> 18.8 us
    pallas_call x1, Pallas kernels: 13.5 us -> 13.9 us  [analyse(): pl.pallas_call(functools.partial(analyse_kernel, count, scale), in_specs=...]
where the time goes in v23:
time: 31.7 us; the launch traced here: 31.3 us
  Pallas kernels  18.8 us (59%)
  starting transfers between devices  8.94 us (28%)
  waiting for transfers between devices  2.9 us (9%)
  local copies, waits for them, and re-layouts  0.6 us (2%)
    pallas_call x1, Pallas kernels, analyse(): pl.pallas_call(functools.partial(analyse_kernel, count, scale), in_specs=...  13.9 us
    all_to_all x1, starting transfers between devices, on_device(): lax.all_to_all(jnp.broadcast_to(part, (count // 2, 128)), 'lon', 0, 0, ax...  6.17 us
    pallas_call x1, Pallas kernels, own_gram(): pl.pallas_call(own_gram_kernel, in_specs=[pl.BlockSpec(memory_space=pltpu...  3.23 us
    ppermute x1, waiting for transfers between devices, on_device(): far = lax.ppermute(for_far, 'lon', far_pairs)  2.83 us
    ppermute x1, starting transfers between devices, on_device(): far = lax.ppermute(for_far, 'lon', far_pairs)  2.65 us
    pallas_call x1, Pallas kernels, observe(): pl.pallas_call(observe_kernel, in_specs=[pl.BlockSpec(memory_space=pltpu....  1.65 us
  transfers between devices with their start and end apart: 3, of which 2 were waited for; matrix products, arithmetic and copies ran while one was open for 2% of the time, Pallas kernels for 10%

profile of v23, /device:TPU:1, one launch (start us, length us, event | category | flops | bytes accessed | tf_op | source)
XLA Modules:
  0.0 31.3 jit_solution(14976721241386283123)
XLA Ops:
  0.0 1.7 %observe.1 = (f32[8,256]{1,0:T(8,128)S(1)}, bf16[1056,256]{1,0:T(8,128)(2,1)S(1)}, bf16[1056,256]{1,0:T(8,128)(2,1)S(1)}, f32[8,128]{1,0:T(8,128)S(1)}) custom-call(s32[1]{0:T(128)} %bitcast.refs_0_.odd_ref, bf16[8,4,64,256]{3,2,1,0:T(8,128)(2,1)} %refs_4_.1, bf16[2048,256]{1,0:T(8,128)(2,1)} %bitcast.9, s32[1,256]{1,0:T(1,128)} %bitcast.10, ...), custom_call_target="tpu_custom_call" | custom-call | tf_op jit(solution)/shard_map/observe/pallas_call | solution.py:135
  1.7 0.1 collective-permute-start.1
  1.8 2.7 %collective-permute-start = (bf16[1056,256]{1,0:T(8,128)(2,1)S(1)}, bf16[1056,256]{1,0:T(8,128)(2,1)S(1)}, u32[]{:S(2)}, u32[]{:S(2)}) collective-permute-start(bf16[1056,256]{1,0:T(8,128)(2,1)S(1)} %get-tuple-element.12), channel_id=1, source_target_pairs={{0,15},{1,2},{2,1},{3,4},{4,3},{5,6},{6,5},{7,8},{8,7},{9,10},{10,... | collective-permute-start | bytes 1622024 | tf_op jit(solution)/shard_map/ppermute | solution.py:544
  4.4 0.0 collective-permute-done.1.near_ref
  4.5 0.6 %broadcast_in_dim.15 = f32[8,1,128]{2,1,0:T(1,128)} broadcast(f32[128]{0:T(128)S(1)} %bitcast_add_fusion), dimensions={2} | broadcast | bytes 4608 | tf_op jit(solution)/shard_map/broadcast_in_dim | solution.py:549
  5.1 6.2 %all-to-all-start = ((f32[8,1,128]{2,1,0:T(1,128)}), f32[8,1,128]{2,1,0:T(1,128)S(1)}, u32[]{:S(2)}, u32[]{:S(2)}) async-start(f32[8,1,128]{2,1,0:T(1,128)} %broadcast_in_dim.15), calls=%async_computation | async-start | bytes 8192 | tf_op jit(solution)/shard_map/all_to_all | solution.py:548
  11.2 3.2 %own_gram.1 = (f32[6,256,256]{2,1,0:T(8,128)S(1)}, f32[2,256,256]{2,1,0:T(8,128)}, f32[8,256]{1,0:T(8,128)S(1)}) custom-call(s32[1]{0:T(128)} %bitcast.refs_0_.odd_ref, bf16[8,4,64,256]{3,2,1,0:T(8,128)(2,1)} %refs_4_.1, bf16[1056,256]{1,0:T(8,128)(2,1)S(1)} %collective-permute-done.1.near_ref, f32[8,256]{1,0:T(8,128)S(1)} %get-tuple-element.14.own_ref), custom_call_target="tpu_custom_call" | custom-call | tf_op jit(solution)/shard_map/own_gram/pallas_call | solution.py:268
  14.5 2.8 %collective-permute-done.refs_1_ = bf16[1056,256]{1,0:T(8,128)(2,1)S(1)} collective-permute-done((bf16[1056,256]{1,0:T(8,128)(2,1)S(1)}, bf16[1056,256]{1,0:T(8,128)(2,1)S(1)}, u32[]{:S(2)}, u32[]{:S(2)}) %collective-permute-start) | collective-permute-done | bytes 540704 | tf_op jit(solution)/shard_map/ppermute | solution.py:544
  17.3 0.1 all-to-all-done
  17.4 13.9 %analyse.1 = bf16[8,4,64,256]{3,2,1,0:T(8,128)(2,1)} custom-call(s32[1]{0:T(128)} %bitcast.refs_0_.odd_ref, bf16[1056,256]{1,0:T(8,128)(2,1)S(1)} %collective-permute-done.refs_1_, f32[6,256,256]{2,1,0:T(8,128)S(1)} %get-tuple-element.15.refs_2_, f32[2,256,256]{2,1,0:T(8,128)} %get-tuple-element.16.refs_3_, bf16[8,4,64,256]{3,2,1,0:T(8,128)(2,1)} %refs_4_.1, ...), custom_call_target="tpu_custom_call" | custom-call | tf_op jit(solution)/shard_map/analyse/pallas_call | solution.py:501
  (2 shorter events, 0.0 us)
Async XLA Ops:
  1.7 2.8 %collective-permute-start.1 = (bf16[1056,256]{1,0:T(8,128)(2,1)S(1)}, bf16[1056,256]{1,0:T(8,128)(2,1)S(1)}, u32[]{:S(2)}, u32[]{:S(2)}) collective-permute-start(bf16[1056,256]{1,0:T(8,128)(2,1)S(1)} %get-tuple-element.13), channel_id=1, source_target_pairs={{0,1},{1,0},{2,3},{3,2},{4,5},{5,4},{6,7},{7,6},{8,9},{9,8},{10,11... | collective-permute-start | bytes 1622024 | tf_op jit(solution)/shard_map/ppermute | solution.py:545
  1.8 15.5 %collective-permute-start = (bf16[1056,256]{1,0:T(8,128)(2,1)S(1)}, bf16[1056,256]{1,0:T(8,128)(2,1)S(1)}, u32[]{:S(2)}, u32[]{:S(2)}) collective-permute-start(bf16[1056,256]{1,0:T(8,128)(2,1)S(1)} %get-tuple-element.12), channel_id=1, source_target_pairs={{0,15},{1,2},{2,1},{3,4},{4,3},{5,6},{6,5},{7,8},{8,7},{9,10},{10,... | collective-permute-start | bytes 1622024 | tf_op jit(solution)/shard_map/ppermute | solution.py:544
  5.1 12.3 %all-to-all-start = ((f32[8,1,128]{2,1,0:T(1,128)}), f32[8,1,128]{2,1,0:T(1,128)S(1)}, u32[]{:S(2)}, u32[]{:S(2)}) async-start(f32[8,1,128]{2,1,0:T(1,128)} %broadcast_in_dim.15), calls=%async_computation | async-start | bytes 8192 | tf_op jit(solution)/shard_map/all_to_all | solution.py:548

commit v24 on v21

--- a/solution.py
+++ b/solution.py
@@ -15,7 +15,7 @@
 TILE = 8
 PAIR = 2
 LOG2E = 1.4426950408889634
-ROWS = 32
+ROWS = 64
 LIFT, START, MASS = 20, -10, 60
 
 

time: 31.3 us -> 31.3 us (level)
  no operation moved by 1% of the time
where the time goes in v24:
time: 31.3 us; the launch traced here: 30.9 us
  Pallas kernels  18.4 us (59%)
  starting transfers between devices  8.94 us (29%)
  waiting for transfers between devices  2.9 us (9%)
  local copies, waits for them, and re-layouts  0.6 us (2%)
    pallas_call x1, Pallas kernels, analyse(): pl.pallas_call(functools.partial(analyse_kernel, count, scale), in_specs=...  13.5 us
    all_to_all x1, starting transfers between devices, on_device(): lax.all_to_all(jnp.broadcast_to(part, (count // 2, 128)), 'lon', 0, 0, ax...  6.17 us
    pallas_call x1, Pallas kernels, own_gram(): pl.pallas_call(own_gram_kernel, in_specs=[pl.BlockSpec(memory_space=pltpu...  3.23 us
    ppermute x1, waiting for transfers between devices, on_device(): far = lax.ppermute(for_far, 'lon', far_pairs)  2.83 us
    ppermute x1, starting transfers between devices, on_device(): far = lax.ppermute(for_far, 'lon', far_pairs)  2.65 us
    pallas_call x1, Pallas kernels, observe(): pl.pallas_call(observe_kernel, in_specs=[pl.BlockSpec(memory_space=pltpu....  1.65 us
  transfers between devices with their start and end apart: 3, of which 2 were waited for; matrix products, arithmetic and copies ran while one was open for 2% of the time, Pallas kernels for 10%

profile of v24, /device:TPU:1, one launch (start us, length us, event | category | flops | bytes accessed | tf_op | source)
XLA Modules:
  0.0 30.9 jit_solution(14191898887602845808)
XLA Ops:
  0.0 1.7 %observe.1 = (f32[8,256]{1,0:T(8,128)S(1)}, bf16[1056,256]{1,0:T(8,128)(2,1)S(1)}, bf16[1056,256]{1,0:T(8,128)(2,1)S(1)}, f32[8,128]{1,0:T(8,128)S(1)}) custom-call(s32[1]{0:T(128)} %bitcast.refs_0_.odd_ref, bf16[8,4,64,256]{3,2,1,0:T(8,128)(2,1)} %refs_4_.1, bf16[2048,256]{1,0:T(8,128)(2,1)} %bitcast.9, s32[1,256]{1,0:T(1,128)} %bitcast.10, ...), custom_call_target="tpu_custom_call" | custom-call | tf_op jit(solution)/shard_map/observe/pallas_call | solution.py:135
  1.7 0.1 collective-permute-start.1
  1.8 2.7 %collective-permute-start = (bf16[1056,256]{1,0:T(8,128)(2,1)S(1)}, bf16[1056,256]{1,0:T(8,128)(2,1)S(1)}, u32[]{:S(2)}, u32[]{:S(2)}) collective-permute-start(bf16[1056,256]{1,0:T(8,128)(2,1)S(1)} %get-tuple-element.12), channel_id=1, source_target_pairs={{0,15},{1,2},{2,1},{3,4},{4,3},{5,6},{6,5},{7,8},{8,7},{9,10},{10,... | collective-permute-start | bytes 1622024 | tf_op jit(solution)/shard_map/ppermute | solution.py:545
  4.4 0.0 collective-permute-done.1.near_ref
  4.5 0.6 %broadcast_in_dim.15 = f32[8,1,128]{2,1,0:T(1,128)} broadcast(f32[128]{0:T(128)S(1)} %bitcast_add_fusion), dimensions={2} | broadcast | bytes 4608 | tf_op jit(solution)/shard_map/broadcast_in_dim | solution.py:550
  5.1 6.2 %all-to-all-start = ((f32[8,1,128]{2,1,0:T(1,128)}), f32[8,1,128]{2,1,0:T(1,128)S(1)}, u32[]{:S(2)}, u32[]{:S(2)}) async-start(f32[8,1,128]{2,1,0:T(1,128)} %broadcast_in_dim.15), calls=%async_computation | async-start | bytes 8192 | tf_op jit(solution)/shard_map/all_to_all | solution.py:549
  11.2 3.2 %own_gram.1 = (f32[6,256,256]{2,1,0:T(8,128)S(1)}, f32[2,256,256]{2,1,0:T(8,128)}, f32[8,256]{1,0:T(8,128)S(1)}) custom-call(s32[1]{0:T(128)} %bitcast.refs_0_.odd_ref, bf16[8,4,64,256]{3,2,1,0:T(8,128)(2,1)} %refs_4_.1, bf16[1056,256]{1,0:T(8,128)(2,1)S(1)} %collective-permute-done.1.near_ref, f32[8,256]{1,0:T(8,128)S(1)} %get-tuple-element.14.own_ref), custom_call_target="tpu_custom_call" | custom-call | tf_op jit(solution)/shard_map/own_gram/pallas_call | solution.py:268
  14.5 2.8 %collective-permute-done.refs_1_ = bf16[1056,256]{1,0:T(8,128)(2,1)S(1)} collective-permute-done((bf16[1056,256]{1,0:T(8,128)(2,1)S(1)}, bf16[1056,256]{1,0:T(8,128)(2,1)S(1)}, u32[]{:S(2)}, u32[]{:S(2)}) %collective-permute-start) | collective-permute-done | bytes 540704 | tf_op jit(solution)/shard_map/ppermute | solution.py:545
  17.3 0.1 all-to-all-done
  17.4 13.5 %analyse.1 = bf16[8,4,64,256]{3,2,1,0:T(8,128)(2,1)} custom-call(s32[1]{0:T(128)} %bitcast.refs_0_.odd_ref, bf16[1056,256]{1,0:T(8,128)(2,1)S(1)} %collective-permute-done.refs_1_, f32[6,256,256]{2,1,0:T(8,128)S(1)} %get-tuple-element.15.refs_2_, f32[2,256,256]{2,1,0:T(8,128)} %get-tuple-element.16.refs_3_, bf16[8,4,64,256]{3,2,1,0:T(8,128)(2,1)} %refs_4_.1, ...), custom_call_target="tpu_custom_call" | custom-call | tf_op jit(solution)/shard_map/analyse/pallas_call | solution.py:502
  (2 shorter events, 0.0 us)
Async XLA Ops:
  1.7 2.8 %collective-permute-start.1 = (bf16[1056,256]{1,0:T(8,128)(2,1)S(1)}, bf16[1056,256]{1,0:T(8,128)(2,1)S(1)}, u32[]{:S(2)}, u32[]{:S(2)}) collective-permute-start(bf16[1056,256]{1,0:T(8,128)(2,1)S(1)} %get-tuple-element.13), channel_id=1, source_target_pairs={{0,1},{1,0},{2,3},{3,2},{4,5},{5,4},{6,7},{7,6},{8,9},{9,8},{10,11... | collective-permute-start | bytes 1622024 | tf_op jit(solution)/shard_map/ppermute | solution.py:546
  1.8 15.5 %collective-permute-start = (bf16[1056,256]{1,0:T(8,128)(2,1)S(1)}, bf16[1056,256]{1,0:T(8,128)(2,1)S(1)}, u32[]{:S(2)}, u32[]{:S(2)}) collective-permute-start(bf16[1056,256]{1,0:T(8,128)(2,1)S(1)} %get-tuple-element.12), channel_id=1, source_target_pairs={{0,15},{1,2},{2,1},{3,4},{4,3},{5,6},{6,5},{7,8},{8,7},{9,10},{10,... | collective-permute-start | bytes 1622024 | tf_op jit(solution)/shard_map/ppermute | solution.py:545
  5.1 12.3 %all-to-all-start = ((f32[8,1,128]{2,1,0:T(1,128)}), f32[8,1,128]{2,1,0:T(1,128)S(1)}, u32[]{:S(2)}, u32[]{:S(2)}) async-start(f32[8,1,128]{2,1,0:T(1,128)} %broadcast_in_dim.15), calls=%async_computation | async-start | bytes 8192 | tf_op jit(solution)/shard_map/all_to_all | solution.py:549
